TPU v7x, 32 devices: a whole 2x2x4 slice. The times are simulated.
32 devices in a mesh: groups: 2 (over x), bulk: 16 (over z, y, core).
Axes of the slice: x: 2, y: 2, z: 4, core: 2. Of those that a mesh axis runs over, the one named last changes fastest.
Arguments:
- electrons: float32 [1024, 128], P(('groups', 'bulk')), parts along dimension 0, may hold values from 0.05 to 0.95
- phonons: float32 [512, 128], P(('groups', 'bulk')), parts along dimension 0, may hold values from 0.05 to 2
- phonon_energy: float32 [256, 128], P('bulk'), may hold values from 0.5 to 3
- phonon_decay: float32 [256, 128], P('bulk'), may hold values from 0.5 to 5
- coupling: bfloat16 [4096, 128, 128], P('bulk'), may hold values from 0.00049972534 to 0.019897461
- tile_kblock: int32 [4096], P('bulk'), may hold values from 0 to 31
- tile_partner: int32 [4096], P('bulk'), may hold values from 0 to 31
- tile_qslot: int32 [4096], P('bulk'), may hold values from 0 to 31
- tile_count: int32 [16], P('bulk'), may hold values from 32 to 256, as said below
- partner_need: int32 [16, 32], P('bulk'), may hold values from 0 to 31
- phonon_need: int32 [16, 32], P('bulk'), may hold values from 0 to 15
Outputs:
- electrons_next: float32 [1024, 128], P(('groups', 'bulk')), parts along dimension 0
- phonons_next: float32 [512, 128], P(('groups', 'bulk')), parts along dimension 0
There are 2 independent parts, one for each index of `groups`. A program takes and returns all parts, laid end to end along the dimension named above; an argument that names none is the same for every part. Nothing has to cross between parts.
Inputs may be any that keep to these rules, and one draw needn't show every extreme that they name: The first tile_count[e] of the 256 slots of bulk index e hold tiles, the others are unused. Each count is 256, 128, 64 or 32, and at least one device has 256. `tile_partner`: slot r of a device's partner list names local block partner_need[e, r] of bulk index r // 2; every device lists exactly 2 blocks of every device, itself included, repeats allowed. `tile_qslot`: slot s of a device's phonon list names local q block phonon_need[e, s] of bulk index s // 2; every device lists exactly 2 q blocks of every device, repeats allowed.
All inputs are finite; a program needn't handle non-finite values.
Results may differ from a plain program's by a relative error of at most 0.0003.
Values sent between devices are 32-bit elements; how exact they have to be, the bound alone decides.
No kernel may reach another device: no remote copies, remote signals or barrier semaphores. Data moves between devices by JAX's collectives and lax.ppermute only.
A program may use at most 64 MiB of HBM per device.

v0:
```python
import jax
import jax.numpy as jnp
from jax import lax
from jax.sharding import PartitionSpec as P

STEPS = 2


step_size = 0.05
highest = lax.Precision.HIGHEST


def on_device(
    electrons,
    phonons,
    phonon_energy,
    phonon_decay,
    coupling,
    tile_kblock,
    tile_partner,
    tile_qslot,
    tile_count,
    partner_need,
    phonon_need,
):
    devices = lax.axis_size("bulk")
    kblocks = electrons.shape[0]
    qblocks = phonons.shape[0]
    tile_slots = coupling.shape[0]
    per_peer = partner_need.shape[1] // devices
    qblocks_peer = phonon_need.shape[1] // devices
    in_use = jnp.arange(tile_slots, dtype=jnp.int32) < tile_count[0]
    k_onehot = (jnp.arange(kblocks, dtype=jnp.int32)[:, None] == tile_kblock[None, :]).astype(
        jnp.float32
    )
    thermal = 1.0 / (jnp.exp(phonon_energy) - 1.0)
    served_qblocks = lax.all_to_all(
        phonon_need.reshape(devices, qblocks_peer), "bulk", split_axis=0, concat_axis=0, tiled=True
    )
    k_global = tile_partner // per_peer * kblocks + jnp.take(partner_need[0], tile_partner)
    q_global = tile_qslot // qblocks_peer * qblocks + jnp.take(phonon_need[0], tile_qslot)

    def collision_rates(occupied, bosons):
        own_fill = jnp.take(occupied, tile_kblock, axis=0)
        hole_weights = jnp.stack([1.0 - own_fill, own_fill], axis=1).astype(jnp.bfloat16)
        backward = jnp.einsum(
            "tsi,tij->tsj", hole_weights, coupling, preferred_element_type=jnp.float32
        )
        listed_bosons = jnp.take(bosons, served_qblocks.reshape(-1), axis=0).reshape(
            devices, qblocks_peer, -1
        )
        everything = lax.all_gather(occupied, "bulk", axis=0, tiled=True)
        far_fill = jnp.take(everything, k_global, axis=0)
        phonon_rows_in = lax.all_to_all(
            listed_bosons, "bulk", split_axis=0, concat_axis=0, tiled=True
        )
        far_bose = jnp.take(phonon_rows_in.reshape(devices * qblocks_peer, -1), tile_qslot, axis=0)
        pair_weights = jnp.stack([far_fill * (1.0 + far_bose), far_fill + far_bose], axis=1).astype(
            jnp.bfloat16
        )
        forward = jnp.einsum(
            "tsj,tij->tsi", pair_weights, coupling, preferred_element_type=jnp.float32
        )
        phonon_terms = jnp.where(
            in_use[:, None],
            far_fill * (1.0 + far_bose) * backward[:, 0]
            - far_bose * (1.0 - far_fill) * backward[:, 1],
            0.0,
        )
        electron_terms = jnp.where(in_use[:, None], forward[:, 0] - own_fill * forward[:, 1], 0.0)
        window = (
            jnp.arange(lax.axis_size("bulk") * qblocks, dtype=jnp.int32)[:, None]
            == q_global[None, :]
        )
        phonon_sums = lax.psum_scatter(
            jnp.dot(window.astype(jnp.float32), phonon_terms, precision=highest),
            "bulk",
            scatter_dimension=0,
            tiled=True,
        )
        electron_rate = jnp.dot(k_onehot, electron_terms, precision=highest)
        phonon_rate = phonon_sums - phonon_decay * (bosons - thermal)
        return (electron_rate, phonon_rate)

    occupied = electrons
    bosons = phonons
    for time_step in range(STEPS):
        electron_first, phonon_first = collision_rates(occupied, bosons)
        occupied_mid = occupied + step_size * electron_first
        bosons_mid = bosons + step_size * phonon_first
        electron_second, phonon_second = collision_rates(occupied_mid, bosons_mid)
        occupied = occupied + step_size / 2.0 * (electron_first + electron_second)
        bosons = bosons + step_size / 2.0 * (phonon_first + phonon_second)
    return (occupied, bosons)


def solution(mesh):
    placed = (
        P(("groups", "bulk"), None),
        P(("groups", "bulk"), None),
        P("bulk", None),
        P("bulk", None),
        P("bulk", None, None),
        P("bulk"),
        P("bulk"),
        P("bulk"),
        P("bulk"),
        P("bulk", None),
        P("bulk", None),
    )
    return jax.shard_map(
        on_device,
        mesh=mesh,
        in_specs=placed,
        out_specs=(P(("groups", "bulk"), None), P(("groups", "bulk"), None)),
        check_vma=False,
    )
```

profile of v0, /device:TPU:0, one launch (start us, length us, event | category | flops | bytes accessed | tf_op | source)
XLA Modules:
  0.0 449.2 jit_solution(17292693528886568490)
XLA Ops:
  7.7 1.3 reduce.6
  9.7 7.4 %all-to-all-start = ((s32[16,1,2]{2,1,0:T(1,128)}), s32[16,1,2]{2,1,0:T(1,128)S(1)}, u32[]{:S(2)}, u32[]{:S(2)}) async-start(s32[16,1,2]{2,1,0:T(1,128)} %bitcast.34), calls=%async_computation | async-start | bytes 16384 | tf_op jit(solution)/shard_map/all_to_all | solution.py:37
  18.5 1.8 fusion.179
  20.3 2.1 fusion.178
  22.4 1.8 fusion.177
  24.2 2.1 fusion.176
  28.3 22.7 %all_gather.12 = f32[512,128]{1,0:T(8,128)S(1)} all-gather(f32[32,128]{1,0:T(8,128)} %param.19), channel_id=1, replica_groups=mesh['groups'=2,'bulk'=16] {'bulk'}, dimensions={0}, use_global_device_ids=true | all-gather | bytes 278528 | tf_op jit(solution)/shard_map/all_gather | solution.py:52
  51.0 20.6 %fusion.146 = s32[256]{0:T(256)S(1)} fusion(s32[256]{0:T(256)} %param.26, s32[]{:T(128)} %bitcast.73, s32[]{:T(128)} %bitcast.72, s32[]{:T(128)} %bitcast.71, s32[]{:T(128)} %bitcast.70, s32[]{:T(128)} %bitcast.69, s32[]{:T(128)} %bitcast.68, s32[]{:T(128)} %bitcast.67, s32[]{:T(128)} %bitcast.66, s32[]{:T(128)} %bitcast.65, s32[]{:T(128)} %bitcast.64, ...), kind=kLoop, calls=%fused_computation.286 | loop fusion | flops 21760 | bytes 2176 | tf_op jit(solution)/shard_map/add | solution.py:41
  71.5 20.5 %compare_and_fusion.3 = (pred[256]{0:T(512)(128)(4,1)S(1)}, s32[256]{0:T(256)S(1)}) fusion(s32[]{:T(128)} %bitcast.33, s32[]{:T(128)} %bitcast.32, s32[]{:T(128)} %bitcast.31, s32[]{:T(128)} %bitcast.30, s32[]{:T(128)} %bitcast.29, s32[]{:T(128)} %bitcast.28, s32[]{:T(128)} %bitcast.27, s32[]{:T(128)} %bitcast.26, s32[]{:T(128)} %bitcast.25, s32[]{:T(128)} %bitcast.24, ...), kind=kLoop, calls=%fused_computation.241 | loop fusion | flops 23296 | bytes 2432 | tf_op jit(solution)/shard_map/jit(_take)/and | solution.py:53
  92.9 1.3 gather_fusion.1
  94.8 3.5 all-to-all-start.1
  98.4 1.4 gather_fusion.3
  99.9 0.7 gather_fusion
  100.6 4.2 all-to-all-done.1
  104.8 0.7 gather_fusion.2
  105.9 7.8 %fusion.8 = f32[256,2,128]{2,1,0:T(2,128)S(1)} fusion(bf16[256,128,128]{2,1,0:T(8,128)(2,1)} %param.23, bf16[256,1,128]{2,1,0:T(2,128)(2,1)S(1)} %copy.87, bf16[256,1,128]{2,1,0:T(2,128)(2,1)S(1)} %copy.86), kind=kOutput, calls=%fused_computation.27 | convolution fusion | flops 17039360 | bytes 8781824 | tf_op jit(solution)/shard_map/tsj,tij->tsi/dot_general | solution.py:61
  114.2 0.7 gather_fusion.7
  115.2 5.7 %fusion.24 = f32[256,2,128]{2,1,0:T(2,128)S(1)} fusion(bf16[256,128,128]{2,1,0:T(8,128)(2,1)} %param.23, bf16[256,2,128]{2,0,1:T(8,128)(2,1)S(1)} %pad_maximum_fusion), kind=kOutput, calls=%fused_computation.50 | convolution fusion | flops 16777216 | bytes 8781824 | tf_op jit(solution)/shard_map/tsi,tij->tsj/dot_general | solution.py:46
  121.1 1.1 fusion.7
  122.2 5.7 %fusion.20 = f32[256,2,128]{2,1,0:T(2,128)S(1)} fusion(bf16[256,128,128]{2,1,0:T(8,128)(2,1)} %param.23, bf16[256,2,128]{2,0,1:T(8,128)(2,1)S(1)} %pad_maximum_fusion.2), kind=kOutput, calls=%fused_computation.46 | convolution fusion | flops 16777216 | bytes 8781824 | tf_op jit(solution)/shard_map/tsi,tij->tsj/dot_general | solution.py:46
  128.1 46.6 %reduce-scatter.5.cloned.1.call-done = f32[16,128]{1,0:T(8,128)} async-done(((f32[256,128]{1,0:T(8,128)}), f32[16,128]{1,0:T(8,128)}) %reduce-scatter.5.cloned.1.call-update) | async-done | bytes 8208 | tf_op jit(solution)/shard_map/reduce_scatter | solution.py:75
  174.7 0.8 multiply_add_fusion.5
  176.7 3.7 all-to-all-start.2
  180.6 22.6 %all_gather.13 = f32[512,128]{1,0:T(8,128)S(1)} all-gather(f32[32,128]{1,0:T(8,128)S(1)} %get-tuple-element.104), channel_id=1, replica_groups=mesh['groups'=2,'bulk'=16] {'bulk'}, dimensions={0}, use_global_device_ids=true | all-gather | bytes 278528 | tf_op jit(solution)/shard_map/all_gather | solution.py:52
  203.2 0.7 gather_fusion.4
  203.9 0.7 gather_fusion.6
  204.8 1.1 fusion.6
  205.9 7.8 %fusion.22 = f32[256,2,128]{2,1,0:T(2,128)S(1)} fusion(bf16[256,128,128]{2,1,0:T(8,128)(2,1)} %param.23, bf16[256,2,128]{2,0,1:T(8,128)(2,1)S(1)} %pad_maximum_fusion.1), kind=kOutput, calls=%fused_computation.48 | convolution fusion | flops 16777216 | bytes 8781824 | tf_op jit(solution)/shard_map/tsj,tij->tsi/dot_general | solution.py:61
  214.2 44.1 %reduce-scatter.7.cloned.1.call-done = f32[16,128]{1,0:T(8,128)} async-done(((f32[256,128]{1,0:T(8,128)}), f32[16,128]{1,0:T(8,128)}) %reduce-scatter.7.cloned.1.call-update) | async-done | bytes 8208 | tf_op jit(solution)/shard_map/reduce_scatter | solution.py:75
  260.3 3.8 all-to-all-start.3
  264.1 22.4 %all_gather.14 = f32[512,128]{1,0:T(8,128)S(1)} all-gather(f32[32,128]{1,0:T(8,128)S(1)} %fusion.3), channel_id=1, replica_groups=mesh['groups'=2,'bulk'=16] {'bulk'}, dimensions={0}, use_global_device_ids=true | all-gather | bytes 278528 | tf_op jit(solution)/shard_map/all_gather | solution.py:52
  287.3 0.7 gather_fusion.8
  288.0 0.7 gather_fusion.10
  288.9 7.8 %fusion.18 = f32[256,2,128]{2,1,0:T(2,128)S(1)} fusion(bf16[256,128,128]{2,1,0:T(8,128)(2,1)} %param.23, bf16[256,2,128]{2,0,1:T(8,128)(2,1)S(1)} %pad_maximum_fusion.3), kind=kOutput, calls=%fused_computation.44 | convolution fusion | flops 16777216 | bytes 8781824 | tf_op jit(solution)/shard_map/tsj,tij->tsi/dot_general | solution.py:61
  297.2 0.7 gather_fusion.15
  298.2 5.6 %fusion.16 = f32[256,2,128]{2,1,0:T(2,128)S(1)} fusion(bf16[256,128,128]{2,1,0:T(8,128)(2,1)} %param.23, bf16[256,2,128]{2,0,1:T(8,128)(2,1)S(1)} %pad_maximum_fusion.4), kind=kOutput, calls=%fused_computation.42 | convolution fusion | flops 16777216 | bytes 8781824 | tf_op jit(solution)/shard_map/tsi,tij->tsj/dot_general | solution.py:46
  304.1 1.1 fusion.5
  305.2 5.7 %fusion.12 = f32[256,2,128]{2,1,0:T(2,128)S(1)} fusion(bf16[256,128,128]{2,1,0:T(8,128)(2,1)} %param.23, bf16[256,2,128]{2,0,1:T(8,128)(2,1)S(1)} %pad_maximum_fusion.6), kind=kOutput, calls=%fused_computation.38 | convolution fusion | flops 16777216 | bytes 8781824 | tf_op jit(solution)/shard_map/tsi,tij->tsj/dot_general | solution.py:46
  311.0 46.6 %reduce-scatter.9.cloned.1.call-done = f32[16,128]{1,0:T(8,128)} async-done(((f32[256,128]{1,0:T(8,128)}), f32[16,128]{1,0:T(8,128)}) %reduce-scatter.9.cloned.1.call-update) | async-done | bytes 8208 | tf_op jit(solution)/shard_map/reduce_scatter | solution.py:75
  357.7 0.8 multiply_add_fusion.3
  359.7 3.8 all-to-all-start.4
  363.5 22.6 %all_gather.15 = f32[512,128]{1,0:T(8,128)S(1)} all-gather(f32[32,128]{1,0:T(8,128)S(1)} %get-tuple-element.106), channel_id=1, replica_groups=mesh['groups'=2,'bulk'=16] {'bulk'}, dimensions={0}, use_global_device_ids=true | all-gather | bytes 278528 | tf_op jit(solution)/shard_map/all_gather | solution.py:52
  386.9 0.7 gather_fusion.14
  387.8 1.1 fusion.4
  388.9 7.8 %fusion.14 = f32[256,2,128]{2,1,0:T(2,128)S(1)} fusion(bf16[256,128,128]{2,1,0:T(8,128)(2,1)} %param.23, bf16[256,2,128]{2,0,1:T(8,128)(2,1)S(1)} %pad_maximum_fusion.5), kind=kOutput, calls=%fused_computation.40 | convolution fusion | flops 16777216 | bytes 8781824 | tf_op jit(solution)/shard_map/tsj,tij->tsi/dot_general | solution.py:61
  396.9 0.9 fusion.1
  397.8 43.5 %reduce-scatter.11.cloned.1.call-done = f32[16,128]{1,0:T(8,128)} async-done(((f32[256,128]{1,0:T(8,128)}), f32[16,128]{1,0:T(8,128)}) %reduce-scatter.11.cloned.1.call-update) | async-done | bytes 8208 | tf_op jit(solution)/shard_map/reduce_scatter | solution.py:75
  441.3 1.3 multiply_add_fusion.2
  (78 shorter events, 15.5 us)
Async XLA Ops:
  7.2 106.8 %copy-start.4 = (s32[256]{0:T(256)S(1)}, s32[256]{0:T(256)}, u32[]{:S(2)}) copy-start(s32[256]{0:T(256)} %param.24) | copy-start | bytes 3076
  7.2 106.8 %copy-start = (f32[32,128]{1,0:T(8,128)S(1)}, f32[32,128]{1,0:T(8,128)}, u32[]{:S(2)}) copy-start(f32[32,128]{1,0:T(8,128)} %param.19) | copy-start | bytes 49156
  9.7 82.4 %all-to-all-start = ((s32[16,1,2]{2,1,0:T(1,128)}), s32[16,1,2]{2,1,0:T(1,128)S(1)}, u32[]{:S(2)}, u32[]{:S(2)}) async-start(s32[16,1,2]{2,1,0:T(1,128)} %bitcast.34), calls=%async_computation | async-start | bytes 16384 | tf_op jit(solution)/shard_map/all_to_all | solution.py:37
  94.8 10.0 %all-to-all-start.1 = ((f32[16,2,128]{2,1,0:T(2,128)}), f32[16,2,128]{2,1,0:T(2,128)S(1)}, u32[]{:S(2)}, u32[]{:S(2)}) async-start(f32[16,2,128]{2,1,0:T(2,128)} %bitcast.35), calls=%async_computation.1 | async-start | bytes 32768 | tf_op jit(solution)/shard_map/all_to_all | solution.py:54
  98.3 76.3 %reduce-scatter.5.cloned.1.call-start = ((), (), s32[]{:S(2)}) async-start(), calls=%async_computation.9 | async-start | bytes 139264 | tf_op jit(solution)/shard_map/reduce_scatter | solution.py:75
  115.2 59.5 %copy-start.1 = (f32[16,128]{1,0:T(8,128)S(1)}, f32[16,128]{1,0:T(8,128)}, u32[]{:S(2)}) copy-start(f32[16,128]{1,0:T(8,128)} %param.20) | copy-start | bytes 24580
  115.2 59.5 %copy-start.2 = (f32[16,128]{1,0:T(8,128)S(1)}, f32[16,128]{1,0:T(8,128)}, u32[]{:S(2)}) copy-start(f32[16,128]{1,0:T(8,128)} %param.22) | copy-start | bytes 24580
  115.2 59.5 %copy-start.3 = (f32[16,128]{1,0:T(8,128)S(1)}, f32[16,128]{1,0:T(8,128)}, u32[]{:S(2)}) copy-start(f32[16,128]{1,0:T(8,128)} %param.21) | copy-start | bytes 24580
  174.7 83.6 %copy-start.6 = (f32[16,128]{1,0:T(8,128)S(1)}, f32[16,128]{1,0:T(8,128)}, u32[]{:S(2)}) copy-start(f32[16,128]{1,0:T(8,128)} %reduce-scatter.5.cloned.1.call-done) | copy-start | bytes 24580
  176.7 27.1 %all-to-all-start.2 = ((f32[16,2,128]{2,1,0:T(2,128)}), f32[16,2,128]{2,1,0:T(2,128)S(1)}, u32[]{:S(2)}, u32[]{:S(2)}) async-start(f32[16,2,128]{2,1,0:T(2,128)} %bitcast.78), calls=%async_computation.3 | async-start | bytes 32768 | tf_op jit(solution)/shard_map/all_to_all | solution.py:54
  180.5 77.8 %reduce-scatter.7.cloned.1.call-start = ((), (), s32[]{:S(2)}) async-start(), calls=%async_computation.10 | async-start | bytes 139264 | tf_op jit(solution)/shard_map/reduce_scatter | solution.py:75
  260.3 27.7 %all-to-all-start.3 = ((f32[16,2,128]{2,1,0:T(2,128)}), f32[16,2,128]{2,1,0:T(2,128)S(1)}, u32[]{:S(2)}, u32[]{:S(2)}) async-start(f32[16,2,128]{2,1,0:T(2,128)} %bitcast.88), calls=%async_computation.5 | async-start | bytes 32768 | tf_op jit(solution)/shard_map/all_to_all | solution.py:54
  264.1 93.6 %reduce-scatter.9.cloned.1.call-start = ((), (), s32[]{:S(2)}) async-start(), calls=%async_computation.11 | async-start | bytes 139264 | tf_op jit(solution)/shard_map/reduce_scatter | solution.py:75
  357.7 83.7 %copy-start.5 = (f32[16,128]{1,0:T(8,128)S(1)}, f32[16,128]{1,0:T(8,128)}, u32[]{:S(2)}) copy-start(f32[16,128]{1,0:T(8,128)} %reduce-scatter.9.cloned.1.call-done) | copy-start | bytes 24580
  359.7 27.2 %all-to-all-start.4 = ((f32[16,2,128]{2,1,0:T(2,128)}), f32[16,2,128]{2,1,0:T(2,128)S(1)}, u32[]{:S(2)}, u32[]{:S(2)}) async-start(f32[16,2,128]{2,1,0:T(2,128)} %bitcast.98), calls=%async_computation.7 | async-start | bytes 32768 | tf_op jit(solution)/shard_map/all_to_all | solution.py:54
  363.5 77.9 %reduce-scatter.11.cloned.1.call-start = ((), (), s32[]{:S(2)}) async-start(), calls=%async_computation.12 | async-start | bytes 139264 | tf_op jit(solution)/shard_map/reduce_scatter | solution.py:75
Sparse Core Ops, SparseCore 0:
  122.3 52.3 reduce-scatter.4
  206.0 52.2 reduce-scatter.6
  305.3 52.3 reduce-scatter.8
  389.0 52.3 reduce-scatter.10
where the time goes:
time: 451 us; the launch traced here: 449 us
  waiting for transfers between devices  185 us (41%)
  blocking collectives  90.4 us (20%)
  matrix products  59.8 us (13%)
  other arithmetic  53.2 us (12%)
  local copies, waits for them, and re-layouts  23.5 us (5%)
  starting transfers between devices  22.3 us (5%)
  between operations  14.8 us (3%)
    reduce_scatter x4, waiting for transfers between devices, collision_rates(): lax.psum_scatter(jnp.dot(window.astype(jnp.float32), phonon_terms, precis...  181 us
    all_gather x4, blocking collectives, collision_rates(): everything = lax.all_gather(occupied, 'bulk', axis=0, tiled=True)  90.4 us
    dot_general x4, matrix products, collision_rates(): jnp.einsum('tsj,tij->tsi', pair_weights, coupling, preferred_element_type...  31.2 us
    dot_general x4, matrix products, collision_rates(): jnp.einsum('tsi,tij->tsj', hole_weights, coupling, preferred_element_type...  22.6 us
    add x1, other arithmetic, on_device(): tile_qslot // qblocks_peer * qblocks + jnp.take(phonon_need[0], tile_qslot)  20.6 us
    and x1, other arithmetic, collision_rates(): far_fill = jnp.take(everything, k_global, axis=0)  20.5 us
    all_to_all x4, starting transfers between devices, collision_rates(): lax.all_to_all(listed_bosons, 'bulk', split_axis=0, concat_axis=0, tiled=...  14.8 us
  transfers between devices with their start and end apart: 9, of which 5 were waited for; matrix products, arithmetic and copies ran while one was open for 19% of the time, Pallas kernels for 0%

commit v1 on v0

v1 whole, which is shorter than its diff:
```python
import functools

import jax
import jax.numpy as jnp
from jax import lax
from jax.experimental import pallas as pl
from jax.experimental.pallas import tpu as pltpu
from jax.sharding import PartitionSpec as P

STEPS = 2
DT = 0.05
f32 = jnp.float32
bf16 = jnp.bfloat16
VMEM_LIMIT = 24 * 1024 * 1024


def iota(shape, dim):
    return lax.broadcasted_iota(jnp.int32, shape, dim)


def dot(a, b):
    return lax.dot_general(a, b, (((1,), (0,)), ((), ())), preferred_element_type=f32)


def split(x):
    hi = x.astype(bf16)
    rest = x - hi.astype(f32)
    mid = rest.astype(bf16)
    lo = (rest - mid.astype(f32)).astype(bf16)
    return hi, mid, lo


def pick(onehot, x):
    hi, mid, lo = split(x)
    return dot(onehot, hi) + dot(onehot, mid) + dot(onehot, lo)


def stacked(first, second):
    tiles = first.shape[0]
    return jnp.concatenate(
        [first.reshape(tiles // 8, 8, 128), second.reshape(tiles // 8, 8, 128)], axis=1
    ).astype(bf16)


def row_is(r):
    return iota((16, 128), 0) % 8 == r


def backward_pass(own, c_ref, w_ref, out0, out1):
    groups = c_ref.shape[0] // 8
    w_ref[...] = stacked(1.0 - own, own)

    def body(g, _):
        w = w_ref[g].astype(f32)
        lhs = jnp.concatenate(
            [jnp.where(row_is(r), w, 0.0).astype(bf16) for r in range(8)], axis=1
        )
        rhs = c_ref[pl.ds(g * 8, 8)].reshape(1024, 128)
        res = dot(lhs, rhs)
        out0[g] = res[:8]
        out1[g] = res[8:]
        return 0

    lax.fori_loop(0, groups, body, 0, unroll=4)


def forward_pass(far, bose, c_ref, w_ref, out0, out1):
    groups = c_ref.shape[0] // 8
    w_ref[...] = stacked(far * (1.0 + bose), far + bose)

    def body(g, _):
        rhs = c_ref[pl.ds(g * 8, 8)].reshape(1024, 128)
        full = lax.dot_general(
            w_ref[g], rhs, (((1,), (1,)), ((), ())), preferred_element_type=f32
        )
        res = full[:, :128]
        for r in range(1, 8):
            res = jnp.where(row_is(r), full[:, r * 128 : (r + 1) * 128], res)
        out0[g] = res[:8]
        out1[g] = res[8:]
        return 0

    lax.fori_loop(0, groups, body, 0, unroll=4)


def flat(ref):
    return ref[...].reshape(-1, 128)


def electron_rate(sum_k, far, bose, f, c_ref, w_ref, o0, o1):
    forward_pass(far, bose, c_ref, w_ref, o0, o1)
    return pick(sum_k, flat(o0)) - f * pick(sum_k, flat(o1))


def need_kernel(kb, cap, pneed_ref, qneed_ref, out_ref):
    rows = out_ref.shape[0]
    slots = pneed_ref.shape[1]
    x = iota((rows, slots), 0)
    y = iota((rows, slots), 1)
    peer, r = x // (2 * cap), x % (2 * cap)
    e_here = (r < cap) & (y == peer * cap + r)
    p_here = (r >= cap) & (y == peer * cap + r - cap)
    pn = jnp.broadcast_to(pneed_ref[...].astype(f32), (rows, slots))
    qn = jnp.broadcast_to(qneed_ref[...].astype(f32), (rows, slots)) + float(kb)
    col = jnp.sum(jnp.where(e_here, pn, 0.0) + jnp.where(p_here, qn, 0.0), axis=1, keepdims=True)
    out_ref[...] = (iota((rows, 128), 1).astype(f32) == col).astype(f32)


def tables_kernel(
    cap,
    count_ref,
    kblock_ref,
    partner_ref,
    qslot_ref,
    f_ref,
    c_ref,
    ge4_ref,
    gp4_ref,
    gp8_ref,
    gk_ref,
    sk_ref,
    sp4_ref,
    sp8_ref,
    b0_ref,
    b1_ref,
    w_ref,
):
    tiles = kblock_ref.shape[1]
    kb = f_ref.shape[0]
    used = iota((1, tiles), 1) < count_ref[0]
    k = kblock_ref[...]
    e = partner_ref[...]
    q = qslot_ref[...]
    rows4 = sp4_ref.shape[0]
    rows8 = sp8_ref.shape[0]
    x = iota((kb, tiles), 0)
    ind = lambda m: jnp.where(m, 1.0, 0.0)
    k_hot = ind(x == k)
    sk_ref[...] = jnp.where(used, k_hot, 0.0).astype(bf16)
    gk_ref[...] = k_hot.T.astype(bf16)
    x = iota((rows4, tiles), 0)
    row_e = e // cap * (2 * cap) + e % cap
    row_p = q // cap * (2 * cap) + cap + q % cap
    ge4_ref[...] = ind(x == row_e).T.astype(bf16)
    p_hot = ind(x == row_p)
    gp4_ref[...] = p_hot.T.astype(bf16)
    sp4_ref[...] = jnp.where(used, p_hot, 0.0).astype(bf16)
    x = iota((rows8, tiles), 0)
    row_z = q // cap * (4 * cap) + q % cap
    gp8_ref[...] = ind(x == row_z).T.astype(bf16)
    sp8_ref[...] = jnp.concatenate(
        [
            jnp.where(used, ind(x == row_z + cap), 0.0),
            jnp.where(used, ind(x == row_z + 2 * cap), 0.0),
        ],
        axis=1,
    ).astype(bf16)
    own = pick(gk_ref[...], f_ref[...])
    backward_pass(own, c_ref, w_ref, b0_ref, b1_ref)


def serve_kernel(
    cap, s4_ref, f_ref, n_ref, send_ref, serve_ref, s8_ref, st4_ref, st8a_ref, st8b_ref
):
    kb, qb = f_ref.shape[0], n_ref.shape[0]
    s4 = s4_ref[...]
    rows4 = s4.shape[0]
    rows8 = s8_ref.shape[0]
    hot = s4.astype(bf16)
    serve_ref[...] = hot
    state = jnp.concatenate(
        [f_ref[...], n_ref[...], jnp.zeros((128 - kb - qb, 128), f32)], axis=0
    )
    send_ref[...] = pick(hot, state)
    x = iota((rows8, rows4), 0)
    y = iota((rows8, rows4), 1)
    peer, r = x // (4 * cap), x % (4 * cap)
    source = peer * (2 * cap) + cap + r % cap

    def rows_of(kind):
        here = (y == source) & (r // cap == kind)
        return dot(jnp.where(here, 1.0, 0.0).astype(bf16), hot)

    s8_ref[...] = rows_of(0).astype(bf16)
    st4_ref[...] = s4.T[kb : kb + qb].astype(bf16)
    st8a_ref[...] = rows_of(1).T[kb : kb + qb].astype(bf16)
    st8b_ref[...] = rows_of(2).T[kb : kb + qb].astype(bf16)


def first_kernel(
    recv_ref,
    f_ref,
    ge4_ref,
    gp4_ref,
    sk_ref,
    sp4_ref,
    serve_ref,
    b0_ref,
    b1_ref,
    c_ref,
    send_ref,
    e_ref,
    f1_ref,
    w_ref,
    o0,
    o1,
):
    kb = f_ref.shape[0]
    f = f_ref[...]
    recv = recv_ref[...]
    far = pick(ge4_ref[...], recv)
    bose = pick(gp4_ref[...], recv)
    gain = far * flat(b0_ref)
    terms = gain + bose * (gain - (1.0 - far) * flat(b1_ref))
    rate = electron_rate(sk_ref[...], far, bose, f, c_ref, w_ref, o0, o1)
    f1 = f + DT * rate
    e_ref[...] = rate
    f1_ref[...] = f1
    state = jnp.concatenate([f1, jnp.zeros((128 - kb, 128), f32)], axis=0)
    send_ref[...] = pick(serve_ref[...], state) + pick(sp4_ref[...], terms)


def backward_kernel(f_ref, gk_ref, c_ref, b0_ref, b1_ref, w_ref):
    own = pick(gk_ref[...], f_ref[...])
    backward_pass(own, c_ref, w_ref, b0_ref, b1_ref)


def phonon_kernel(
    recv_ref,
    n_ref,
    energy_ref,
    decay_ref,
    ge4_ref,
    st4_ref,
    sp8_ref,
    s8_ref,
    b0_ref,
    b1_ref,
    kb,
    send_ref,
    p_ref,
    n1_ref,
    far_ref,
):
    n = n_ref[...]
    qb = n.shape[0]
    recv = recv_ref[...]
    thermal = 1.0 / (jnp.exp(energy_ref[...]) - 1.0)
    rate = pick(st4_ref[...], recv) - decay_ref[...] * (n - thermal)
    n1 = n + DT * rate
    p_ref[...] = rate
    n1_ref[...] = n1
    far = pick(ge4_ref[...], recv)
    far_ref[...] = far
    gain = far * flat(b0_ref)
    both = jnp.concatenate([gain, gain - (1.0 - far) * flat(b1_ref)], axis=0)
    state = jnp.concatenate(
        [jnp.zeros((kb, 128), f32), n1, jnp.zeros((128 - kb - qb, 128), f32)], axis=0
    )
    send_ref[...] = pick(s8_ref[...], state) + pick(sp8_ref[...], both)


def second_kernel(
    with_send,
    recv_ref,
    far_ref,
    f_ref,
    f1_ref,
    e_ref,
    n_ref,
    n1_ref,
    p_ref,
    energy_ref,
    decay_ref,
    gp8_ref,
    sk_ref,
    st8a_ref,
    st8b_ref,
    serve_ref,
    c_ref,
    *rest,
):
    if with_send:
        f2_ref, n2_ref, send_ref, w_ref, o0, o1 = rest
    else:
        f2_ref, n2_ref, w_ref, o0, o1 = rest
    recv = recv_ref[...]
    n, n1 = n_ref[...], n1_ref[...]
    kb, qb = f_ref.shape[0], n.shape[0]
    thermal = 1.0 / (jnp.exp(energy_ref[...]) - 1.0)
    p1 = (
        pick(st8a_ref[...], recv)
        + n1 * pick(st8b_ref[...], recv)
        - decay_ref[...] * (n1 - thermal)
    )
    n2 = n + (DT / 2.0) * (p_ref[...] + p1)
    n2_ref[...] = n2
    bose = pick(gp8_ref[...], recv)
    rate = electron_rate(sk_ref[...], far_ref[...], bose, f1_ref[...], c_ref, w_ref, o0, o1)
    f2 = f_ref[...] + (DT / 2.0) * (e_ref[...] + rate)
    f2_ref[...] = f2
    if with_send:
        state = jnp.concatenate([f2, n2, jnp.zeros((128 - kb - qb, 128), f32)], axis=0)
        send_ref[...] = pick(serve_ref[...], state)


def call(kernel, name, outs, scratch=(), smem_first=False, flops=0, seen=0):
    vmem = pl.BlockSpec(memory_space=pltpu.VMEM)

    def run(*args):
        specs = [vmem] * len(args)
        if smem_first:
            specs[0] = pl.BlockSpec(memory_space=pltpu.SMEM)
        return pl.pallas_call(
            kernel,
            out_shape=[jax.ShapeDtypeStruct(s, d) for s, d in outs],
            in_specs=specs,
            out_specs=[vmem] * len(outs),
            scratch_shapes=list(scratch),
            compiler_params=pltpu.CompilerParams(vmem_limit_bytes=VMEM_LIMIT),
            cost_estimate=pl.CostEstimate(
                flops=flops, bytes_accessed=seen, transcendentals=0
            ),
            name=name,
        )(*args)

    return run


def on_device(
    electrons,
    phonons,
    phonon_energy,
    phonon_decay,
    coupling,
    tile_kblock,
    tile_partner,
    tile_qslot,
    tile_count,
    partner_need,
    phonon_need,
):
    devices = lax.axis_size("bulk")
    kb = electrons.shape[0]
    qb = phonons.shape[0]
    tiles = coupling.shape[0]
    cap = partner_need.shape[1] // devices
    assert cap == phonon_need.shape[1] // devices and kb + qb <= 128
    rows4 = devices * 2 * cap
    rows8 = devices * 4 * cap
    groups = tiles // 8
    weights = pltpu.VMEM((groups, 16, 128), bf16)
    partial_sums = pltpu.VMEM((groups, 8, 128), f32)
    pass_out = [((groups, 8, 128), f32)] * 2
    flops = 2 * tiles * 16 * 128 * 128
    c = pltpu.with_memory_space_constraint(coupling, pltpu.VMEM)

    def exchange(x):
        return lax.all_to_all(x, "bulk", split_axis=0, concat_axis=0, tiled=True)

    (need,) = call(functools.partial(need_kernel, kb, cap), "need", [((rows4, 128), f32)])(
        partner_need, phonon_need
    )
    served = exchange(need)
    ge4, gp4, gp8, gk, sk, sp4, sp8, b0, b1 = call(
        functools.partial(tables_kernel, cap),
        "tables",
        [
            ((tiles, rows4), bf16),
            ((tiles, rows4), bf16),
            ((tiles, rows8), bf16),
            ((tiles, kb), bf16),
            ((kb, tiles), bf16),
            ((rows4, tiles), bf16),
            ((rows8, 2 * tiles), bf16),
        ]
        + pass_out,
        [weights],
        smem_first=True,
        flops=flops,
    )(
        tile_count,
        tile_kblock.reshape(1, tiles),
        tile_partner.reshape(1, tiles),
        tile_qslot.reshape(1, tiles),
        electrons,
        c,
    )
    send, serve, s8, st4, st8a, st8b = call(
        functools.partial(serve_kernel, cap),
        "serve",
        [
            ((rows4, 128), f32),
            ((rows4, 128), bf16),
            ((rows8, 128), bf16),
            ((qb, rows4), bf16),
            ((qb, rows8), bf16),
            ((qb, rows8), bf16),
        ],
    )(served, electrons, phonons)

    back = call(backward_kernel, "backward", pass_out, [weights], flops=flops)
    f, n = electrons, phonons
    for step in range(STEPS):
        recv = exchange(send)
        if step:
            b0, b1 = back(f, gk, c)
        send, e0, f1 = call(
            first_kernel,
            "first",
            [((rows4, 128), f32), ((kb, 128), f32), ((kb, 128), f32)],
            [weights, partial_sums, partial_sums],
            flops=flops,
        )(recv, f, ge4, gp4, sk, sp4, serve, b0, b1, c)
        recv = exchange(send)
        b0, b1 = back(f1, gk, c)

        def phonon(*refs):
            phonon_kernel(*refs[:10], kb, *refs[10:])

        send, p0, n1, far = call(
            phonon,
            "phonon",
            [((rows8, 128), f32), ((qb, 128), f32), ((qb, 128), f32), ((tiles, 128), f32)],
        )(recv, n, phonon_energy, phonon_decay, ge4, st4, sp8, s8, b0, b1)
        recv = exchange(send)
        last = step == STEPS - 1
        outs = [((kb, 128), f32), ((qb, 128), f32)]
        if not last:
            outs.append(((rows4, 128), f32))
        f, n, *sent = call(
            functools.partial(second_kernel, not last),
            "second",
            outs,
            [weights, partial_sums, partial_sums],
            flops=flops,
        )(
            recv, far, f, f1, e0, n, n1, p0, phonon_energy, phonon_decay,
            gp8, sk, st8a, st8b, serve, c,
        )
        if not last:
            send = sent[0]
    return (f, n)


def solution(mesh):
    placed = (
        P(("groups", "bulk"), None),
        P(("groups", "bulk"), None),
        P("bulk", None),
        P("bulk", None),
        P("bulk", None, None),
        P("bulk"),
        P("bulk"),
        P("bulk"),
        P("bulk"),
        P("bulk", None),
        P("bulk", None),
    )
    return jax.shard_map(
        on_device,
        mesh=mesh,
        in_specs=placed,
        out_specs=(P(("groups", "bulk"), None), P(("groups", "bulk"), None)),
        check_vma=False,
    )
```

time: 451 us -> 121 us (0.27)
  waiting for transfers between devices: 185 us -> 3.01 us
  matrix products: 59.8 us -> 0 us
  other arithmetic: 53.2 us -> 0 us
  blocking collectives: 90.4 us -> 37.2 us
  Pallas kernels: 0 us -> 28 us
  between operations: 14.8 us -> 1.41 us
  local copies, waits for them, and re-layouts: 23.5 us -> 32.5 us
    reduce_scatter x4 -> x0, waiting for transfers between devices: 181 us -> none  [collision_rates(): lax.psum_scatter(jnp.dot(window.astype(jnp.float32), phonon_terms, precis...]
    all_gather x4 -> x0, blocking collectives: 90.4 us -> none  [collision_rates(): everything = lax.all_gather(occupied, 'bulk', axis=0, tiled=True)]
    dot_general x16 -> x0, matrix products: 59.8 us -> none  [the longest x4 31.2 us: collision_rates(): jnp.einsum('tsj,tij->tsi', pair_weights, coupling, preferred_element_type...]
    all_to_all x0 -> x3, blocking collectives: none -> 37.2 us  [exchange(): return lax.all_to_all(x, 'bulk', split_axis=0, concat_axis=0, tiled=True)]
    unnamed x15 -> x40, local copies, waits for them, and re-layouts: 0.55 us -> 32.5 us
    pallas_call x0 -> x12, Pallas kernels: none -> 28 us  [run(): pl.pallas_call(kernel, out_shape=[jax.ShapeDtypeStruct(s, d) for s, d in...]
    add x5 -> x0, other arithmetic: 24.2 us -> none  [the longest x1 20.6 us: on_device(): tile_qslot // qblocks_peer * qblocks + jnp.take(phonon_need[0], tile_qslot)]
    and x4 -> x0, other arithmetic: 21.9 us -> none  [the longest x1 20.5 us: collision_rates(): far_fill = jnp.take(everything, k_global, axis=0)]
  transfers between devices with their start and end apart: 9 -> 4, of which waited for: 5 -> 3; matrix products, arithmetic and copies ran while one was open for 19% -> 0% of each run, Pallas kernels for 0% -> 8%
where the time goes in v1:
time: 121 us; the launch traced here: 120 us
  blocking collectives  37.2 us (31%)
  local copies, waits for them, and re-layouts  32.5 us (27%)
  Pallas kernels  28 us (23%)
  starting transfers between devices  18 us (15%)
  waiting for transfers between devices  3.01 us (2%)
  between operations  1.41 us (1%)
    all_to_all x3, blocking collectives, exchange(): return lax.all_to_all(x, 'bulk', split_axis=0, concat_axis=0, tiled=True)  37.2 us
    unnamed x40, local copies, waits for them, and re-layouts  32.5 us
    pallas_call x12, Pallas kernels, run(): pl.pallas_call(kernel, out_shape=[jax.ShapeDtypeStruct(s, d) for s, d in...  28 us
    all_to_all x4, starting transfers between devices, exchange(): return lax.all_to_all(x, 'bulk', split_axis=0, concat_axis=0, tiled=True)  18 us
    all_to_all x4, waiting for transfers between devices, exchange(): return lax.all_to_all(x, 'bulk', split_axis=0, concat_axis=0, tiled=True)  3.01 us
  transfers between devices with their start and end apart: 4, of which 3 were waited for; matrix products, arithmetic and copies ran while one was open for 0% of the time, Pallas kernels for 8%

profile of v1, /device:TPU:0, one launch (start us, length us, event | category | flops | bytes accessed | tf_op | source)
XLA Modules:
  0.0 120.2 jit_solution(7838504447272652489)
XLA Ops:
  0.6 0.0 copy-start.10
  0.6 0.0 copy-start.18
  0.7 0.7 copy-done.18
  1.3 0.7 copy-done.19
  2.0 0.1 need.1
  2.1 13.8 %all_to_all.77 = f32[16,4,128]{2,1,0:T(4,128)S(1)} all-to-all(f32[16,4,128]{2,1,0:T(4,128)S(1)} %bitcast.24), channel_id=1, replica_groups=mesh['groups'=2,'bulk'=16] {'bulk'}, dimensions={0} | all-to-all | bytes 65536 | tf_op jit(solution)/shard_map/all_to_all | solution.py:359
  15.9 0.7 copy-done.8
  16.6 0.7 copy-done.13
  17.3 0.8 serve.1
  18.1 3.5 %all-to-all-start.1 = ((f32[16,4,128]{2,1,0:T(4,128)}), f32[16,4,128]{2,1,0:T(4,128)S(1)}, u32[]{:S(2)}, u32[]{:S(2)}) async-start(f32[16,4,128]{2,1,0:T(4,128)} %bitcast.2), calls=%async_computation.1 | async-start | bytes 65536 | tf_op jit(solution)/shard_map/all_to_all | solution.py:359
  22.3 0.0 copy-start
  22.3 3.4 %copy-done = bf16[256,128,128]{2,1,0:T(8,128)(2,1)S(1)} copy-done((bf16[256,128,128]{2,1,0:T(8,128)(2,1)S(1)}, bf16[256,128,128]{2,1,0:T(8,128)(2,1)}, u32[]{:S(2)}) %copy-start) | copy-done | bytes 8388632
  25.6 0.7 copy-done.9
  26.4 0.7 copy-done.15
  27.0 0.7 copy-done.16
  27.7 0.7 copy-done.17
  28.4 2.3 %tables.1 = (bf16[256,64]{1,0:T(8,128)(2,1)S(1)}, bf16[256,64]{1,0:T(8,128)(2,1)S(1)}, bf16[256,128]{1,0:T(8,128)(2,1)S(1)}, bf16[256,32]{1,0:T(8,128)(2,1)S(1)}...) custom-call(s32[1]{0:T(128)S(6)} %copy.13.count_ref, ...), custom_call_target="tpu_custom_call" | custom-call | flops 134217728 | tf_op jit(solution)/shard_map/tables/pallas_call | solution.py:314
  30.7 0.0 all-to-all-done.1
  30.7 0.0 copy-done.10
  30.7 0.0 copy-start.1
  30.8 3.4 %copy-done.1 = bf16[256,128,128]{2,1,0:T(8,128)(2,1)S(1)} copy-done((bf16[256,128,128]{2,1,0:T(8,128)(2,1)S(1)}, bf16[256,128,128]{2,1,0:T(8,128)(2,1)}, u32[]{:S(2)}) %copy-start.1) | copy-done | bytes 8388632
  34.1 4.4 %first.2 = (f32[64,128]{1,0:T(8,128)}, f32[32,128]{1,0:T(8,128)S(1)}, f32[32,128]{1,0:T(8,128)S(1)}) custom-call(f32[64,128]{1,0:T(8,128)S(1)} %bitcast.19, f32[32,128]{1,0:T(8,128)S(1)} %copy-done.10, bf16[256,64]{1,0:T(8,128)(2,1)S(1)} %get-tuple-element.41.ge4_ref.refs_4_, bf16[256,64]{1,0:T(8,128)(2,1)S(1)} %get-tuple-element.42.gp4_ref, ...), custom_call_target="tpu_custom_call" | custom-call | flops 134217728 | tf_op jit(solution)/shard_map/first/pallas_call | solution.py:314
  38.5 6.0 %all-to-all-start.2 = ((f32[16,4,128]{2,1,0:T(4,128)}), f32[16,4,128]{2,1,0:T(4,128)S(1)}, u32[]{:S(2)}, u32[]{:S(2)}) async-start(f32[16,4,128]{2,1,0:T(4,128)} %bitcast.7), calls=%async_computation.2 | async-start | bytes 65536 | tf_op jit(solution)/shard_map/all_to_all | solution.py:359
  44.5 0.0 copy-start.2
  44.5 3.4 %copy-done.2 = bf16[256,128,128]{2,1,0:T(8,128)(2,1)S(1)} copy-done((bf16[256,128,128]{2,1,0:T(8,128)(2,1)S(1)}, bf16[256,128,128]{2,1,0:T(8,128)(2,1)}, u32[]{:S(2)}) %copy-start.2) | copy-done | bytes 8388632
  47.9 2.2 %backward.3 = (f32[32,8,128]{2,1,0:T(8,128)S(1)}, f32[32,8,128]{2,1,0:T(8,128)S(1)}) custom-call(f32[32,128]{1,0:T(8,128)S(1)} %get-tuple-element.52.f_ref.f1_ref, bf16[256,32]{1,0:T(8,128)(2,1)S(1)} %get-tuple-element.53.gk_ref, bf16[256,128,128]{2,1,0:T(8,128)(2,1)S(1)} %copy-done.2), custom_call_target="tpu_custom_call" | custom-call | flops 134217728 | tf_op jit(solution)/shard_map/backward/pallas_call | solution.py:314
  50.1 1.0 all-to-all-done.2
  51.1 0.0 copy-done.11
  51.1 0.5 phonon.2
  51.6 11.7 %all_to_all.78 = f32[16,8,128]{2,1,0:T(8,128)S(1)} all-to-all(f32[16,8,128]{2,1,0:T(8,128)S(1)} %bitcast.26), channel_id=1, replica_groups=mesh['groups'=2,'bulk'=16] {'bulk'}, dimensions={0} | all-to-all | bytes 131072 | tf_op jit(solution)/shard_map/all_to_all | solution.py:359
  63.3 3.4 %copy-done.3 = bf16[256,128,128]{2,1,0:T(8,128)(2,1)S(1)} copy-done((bf16[256,128,128]{2,1,0:T(8,128)(2,1)S(1)}, bf16[256,128,128]{2,1,0:T(8,128)(2,1)}, u32[]{:S(2)}) %copy-start.3) | copy-done | bytes 8388632
  66.7 4.3 %second.2 = (f32[32,128]{1,0:T(8,128)S(1)}, f32[16,128]{1,0:T(8,128)S(1)}, f32[64,128]{1,0:T(8,128)}) custom-call(f32[128,128]{1,0:T(8,128)S(1)} %bitcast.18, f32[256,128]{1,0:T(8,128)S(1)} %get-tuple-element.57.far_ref, f32[32,128]{1,0:T(8,128)S(1)} %copy-done.10, f32[32,128]{1,0:T(8,128)S(1)} %get-tuple-element.52.f_ref.f1_ref, ...), custom_call_target="tpu_custom_call" | custom-call | flops 134217728 | tf_op jit(solution)/shard_map/second/pallas_call | solution.py:314
  71.0 3.5 %all-to-all-start.4 = ((f32[16,4,128]{2,1,0:T(4,128)}), f32[16,4,128]{2,1,0:T(4,128)S(1)}, u32[]{:S(2)}, u32[]{:S(2)}) async-start(f32[16,4,128]{2,1,0:T(4,128)} %bitcast.11), calls=%async_computation.4 | async-start | bytes 65536 | tf_op jit(solution)/shard_map/all_to_all | solution.py:359
  74.5 0.0 copy-start.4
  74.5 3.4 %copy-done.4 = bf16[256,128,128]{2,1,0:T(8,128)(2,1)S(1)} copy-done((bf16[256,128,128]{2,1,0:T(8,128)(2,1)S(1)}, bf16[256,128,128]{2,1,0:T(8,128)(2,1)}, u32[]{:S(2)}) %copy-start.4) | copy-done | bytes 8388632
  77.9 2.2 %backward.4 = (f32[32,8,128]{2,1,0:T(8,128)S(1)}, f32[32,8,128]{2,1,0:T(8,128)S(1)}) custom-call(f32[32,128]{1,0:T(8,128)S(1)} %get-tuple-element.65.f_ref, bf16[256,32]{1,0:T(8,128)(2,1)S(1)} %get-tuple-element.53.gk_ref, bf16[256,128,128]{2,1,0:T(8,128)(2,1)S(1)} %copy-done.4), custom_call_target="tpu_custom_call" | custom-call | flops 134217728 | tf_op jit(solution)/shard_map/backward/pallas_call | solution.py:314
  80.1 1.0 all-to-all-done.4
  81.1 3.4 %copy-done.5 = bf16[256,128,128]{2,1,0:T(8,128)(2,1)S(1)} copy-done((bf16[256,128,128]{2,1,0:T(8,128)(2,1)S(1)}, bf16[256,128,128]{2,1,0:T(8,128)(2,1)}, u32[]{:S(2)}) %copy-start.5) | copy-done | bytes 8388632
  84.5 4.4 %first.3 = (f32[64,128]{1,0:T(8,128)}, f32[32,128]{1,0:T(8,128)S(1)}, f32[32,128]{1,0:T(8,128)S(1)}) custom-call(f32[64,128]{1,0:T(8,128)S(1)} %bitcast.20, f32[32,128]{1,0:T(8,128)S(1)} %get-tuple-element.65.f_ref, bf16[256,64]{1,0:T(8,128)(2,1)S(1)} %get-tuple-element.41.ge4_ref.refs_4_, bf16[256,64]{1,0:T(8,128)(2,1)S(1)} %get-tuple-element.42.gp4_ref, ...), custom_call_target="tpu_custom_call" | custom-call | flops 134217728 | tf_op jit(solution)/shard_map/first/pallas_call | solution.py:314
  88.8 5.0 %all-to-all-start.5 = ((f32[16,4,128]{2,1,0:T(4,128)}), f32[16,4,128]{2,1,0:T(4,128)S(1)}, u32[]{:S(2)}, u32[]{:S(2)}) async-start(f32[16,4,128]{2,1,0:T(4,128)} %bitcast.13), calls=%async_computation.5 | async-start | bytes 65536 | tf_op jit(solution)/shard_map/all_to_all | solution.py:359
  93.9 0.0 copy-start.6
  93.9 3.4 %copy-done.6 = bf16[256,128,128]{2,1,0:T(8,128)(2,1)S(1)} copy-done((bf16[256,128,128]{2,1,0:T(8,128)(2,1)S(1)}, bf16[256,128,128]{2,1,0:T(8,128)(2,1)}, u32[]{:S(2)}) %copy-start.6) | copy-done | bytes 8388632
  97.2 2.2 %backward.5 = (f32[32,8,128]{2,1,0:T(8,128)S(1)}, f32[32,8,128]{2,1,0:T(8,128)S(1)}) custom-call(f32[32,128]{1,0:T(8,128)S(1)} %get-tuple-element.70.f_ref.f1_ref, bf16[256,32]{1,0:T(8,128)(2,1)S(1)} %get-tuple-element.53.gk_ref, bf16[256,128,128]{2,1,0:T(8,128)(2,1)S(1)} %copy-done.6), custom_call_target="tpu_custom_call" | custom-call | flops 134217728 | tf_op jit(solution)/shard_map/backward/pallas_call | solution.py:314
  99.5 1.0 all-to-all-done.5
  100.5 0.5 phonon.3
  101.0 11.7 %all_to_all.79 = f32[16,8,128]{2,1,0:T(8,128)S(1)} all-to-all(f32[16,8,128]{2,1,0:T(8,128)S(1)} %bitcast.25), channel_id=1, replica_groups=mesh['groups'=2,'bulk'=16] {'bulk'}, dimensions={0} | all-to-all | bytes 131072 | tf_op jit(solution)/shard_map/all_to_all | solution.py:359
  112.7 3.4 %copy-done.7 = bf16[256,128,128]{2,1,0:T(8,128)(2,1)S(1)} copy-done((bf16[256,128,128]{2,1,0:T(8,128)(2,1)S(1)}, bf16[256,128,128]{2,1,0:T(8,128)(2,1)}, u32[]{:S(2)}) %copy-start.7) | copy-done | bytes 8388632
  116.0 4.2 %second.3 = (f32[32,128]{1,0:T(8,128)}, f32[16,128]{1,0:T(8,128)}) custom-call(f32[128,128]{1,0:T(8,128)S(1)} %bitcast.17, f32[256,128]{1,0:T(8,128)S(1)} %get-tuple-element.74.far_ref, f32[32,128]{1,0:T(8,128)S(1)} %get-tuple-element.65.f_ref, f32[32,128]{1,0:T(8,128)S(1)} %get-tuple-element.70.f_ref.f1_ref, f32[32,128]{1,0:T(8,128)S(1)} %get-tuple-element.75.e_ref, ...), custom_call_target="tpu_custom_call" | custom-call | flops 134217728 | tf_op jit(solution)/shard_map/second/pallas_call | solution.py:314
  (15 shorter events, 0.0 us)
Async XLA Ops:
  0.6 30.1 %copy-start.10 = (f32[32,128]{1,0:T(8,128)S(1)}, f32[32,128]{1,0:T(8,128)}, u32[]{:S(2)}) copy-start(f32[32,128]{1,0:T(8,128)} %f_ref.7) | copy-start | bytes 49156
  0.6 0.7 copy-start.18
  1.3 0.7 copy-start.19
  15.9 0.7 copy-start.8
  16.6 0.7 copy-start.13
  18.1 12.6 %all-to-all-start.1 = ((f32[16,4,128]{2,1,0:T(4,128)}), f32[16,4,128]{2,1,0:T(4,128)S(1)}, u32[]{:S(2)}, u32[]{:S(2)}) async-start(f32[16,4,128]{2,1,0:T(4,128)} %bitcast.2), calls=%async_computation.1 | async-start | bytes 65536 | tf_op jit(solution)/shard_map/all_to_all | solution.py:359
  22.3 3.4 %copy-start = (bf16[256,128,128]{2,1,0:T(8,128)(2,1)S(1)}, bf16[256,128,128]{2,1,0:T(8,128)(2,1)}, u32[]{:S(2)}) copy-start(bf16[256,128,128]{2,1,0:T(8,128)(2,1)} %c_ref.15) | copy-start | bytes 25165828
  25.6 0.7 copy-start.9
  26.4 0.7 copy-start.15
  27.0 0.7 copy-start.16
  27.7 0.7 copy-start.17
  30.7 3.4 %copy-start.1 = (bf16[256,128,128]{2,1,0:T(8,128)(2,1)S(1)}, bf16[256,128,128]{2,1,0:T(8,128)(2,1)}, u32[]{:S(2)}) copy-start(bf16[256,128,128]{2,1,0:T(8,128)(2,1)} %c_ref.15) | copy-start | bytes 25165828
  34.1 17.0 %copy-start.11 = (f32[16,128]{1,0:T(8,128)S(1)}, f32[16,128]{1,0:T(8,128)}, u32[]{:S(2)}) copy-start(f32[16,128]{1,0:T(8,128)} %energy_ref.3) | copy-start | bytes 24580
  34.1 17.0 %copy-start.12 = (f32[16,128]{1,0:T(8,128)S(1)}, f32[16,128]{1,0:T(8,128)}, u32[]{:S(2)}) copy-start(f32[16,128]{1,0:T(8,128)} %decay_ref.3) | copy-start | bytes 24580
  34.1 17.0 %copy-start.14 = (f32[16,128]{1,0:T(8,128)S(1)}, f32[16,128]{1,0:T(8,128)}, u32[]{:S(2)}) copy-start(f32[16,128]{1,0:T(8,128)} %n_ref.3) | copy-start | bytes 24580
  38.5 12.6 %all-to-all-start.2 = ((f32[16,4,128]{2,1,0:T(4,128)}), f32[16,4,128]{2,1,0:T(4,128)S(1)}, u32[]{:S(2)}, u32[]{:S(2)}) async-start(f32[16,4,128]{2,1,0:T(4,128)} %bitcast.7), calls=%async_computation.2 | async-start | bytes 65536 | tf_op jit(solution)/shard_map/all_to_all | solution.py:359
  44.5 3.4 %copy-start.2 = (bf16[256,128,128]{2,1,0:T(8,128)(2,1)S(1)}, bf16[256,128,128]{2,1,0:T(8,128)(2,1)}, u32[]{:S(2)}) copy-start(bf16[256,128,128]{2,1,0:T(8,128)(2,1)} %c_ref.15) | copy-start | bytes 25165828
  63.3 3.4 %copy-start.3 = (bf16[256,128,128]{2,1,0:T(8,128)(2,1)S(1)}, bf16[256,128,128]{2,1,0:T(8,128)(2,1)}, u32[]{:S(2)}) copy-start(bf16[256,128,128]{2,1,0:T(8,128)(2,1)} %c_ref.15) | copy-start | bytes 25165828
  71.0 10.1 %all-to-all-start.4 = ((f32[16,4,128]{2,1,0:T(4,128)}), f32[16,4,128]{2,1,0:T(4,128)S(1)}, u32[]{:S(2)}, u32[]{:S(2)}) async-start(f32[16,4,128]{2,1,0:T(4,128)} %bitcast.11), calls=%async_computation.4 | async-start | bytes 65536 | tf_op jit(solution)/shard_map/all_to_all | solution.py:359
  74.5 3.4 %copy-start.4 = (bf16[256,128,128]{2,1,0:T(8,128)(2,1)S(1)}, bf16[256,128,128]{2,1,0:T(8,128)(2,1)}, u32[]{:S(2)}) copy-start(bf16[256,128,128]{2,1,0:T(8,128)(2,1)} %c_ref.15) | copy-start | bytes 25165828
  81.1 3.4 %copy-start.5 = (bf16[256,128,128]{2,1,0:T(8,128)(2,1)S(1)}, bf16[256,128,128]{2,1,0:T(8,128)(2,1)}, u32[]{:S(2)}) copy-start(bf16[256,128,128]{2,1,0:T(8,128)(2,1)} %c_ref.15) | copy-start | bytes 25165828
  88.8 11.7 %all-to-all-start.5 = ((f32[16,4,128]{2,1,0:T(4,128)}), f32[16,4,128]{2,1,0:T(4,128)S(1)}, u32[]{:S(2)}, u32[]{:S(2)}) async-start(f32[16,4,128]{2,1,0:T(4,128)} %bitcast.13), calls=%async_computation.5 | async-start | bytes 65536 | tf_op jit(solution)/shard_map/all_to_all | solution.py:359
  93.9 3.4 %copy-start.6 = (bf16[256,128,128]{2,1,0:T(8,128)(2,1)S(1)}, bf16[256,128,128]{2,1,0:T(8,128)(2,1)}, u32[]{:S(2)}) copy-start(bf16[256,128,128]{2,1,0:T(8,128)(2,1)} %c_ref.15) | copy-start | bytes 25165828
  112.7 3.4 %copy-start.7 = (bf16[256,128,128]{2,1,0:T(8,128)(2,1)S(1)}, bf16[256,128,128]{2,1,0:T(8,128)(2,1)}, u32[]{:S(2)}) copy-start(bf16[256,128,128]{2,1,0:T(8,128)(2,1)} %c_ref.15) | copy-start | bytes 25165828

commit v2 on v1

v2 whole, which is shorter than its diff:
```python
import functools

import jax
import jax.numpy as jnp
from jax import lax
from jax.experimental import pallas as pl
from jax.experimental.pallas import tpu as pltpu
from jax.sharding import PartitionSpec as P

STEPS = 2
DT = 0.05
CHUNKS = 8
f32 = jnp.float32
bf16 = jnp.bfloat16
VMEM_LIMIT = 24 * 1024 * 1024


def iota(shape, dim):
    return lax.broadcasted_iota(jnp.int32, shape, dim)


def dot(a, b):
    return lax.dot_general(a, b, (((1,), (0,)), ((), ())), preferred_element_type=f32)


def split(x):
    hi = x.astype(bf16)
    rest = x - hi.astype(f32)
    mid = rest.astype(bf16)
    lo = (rest - mid.astype(f32)).astype(bf16)
    return hi, mid, lo


def pick(onehot, x):
    hi, mid, lo = split(x)
    return dot(onehot, hi) + dot(onehot, mid) + dot(onehot, lo)


def stacked(first, second):
    tiles = first.shape[0]
    return jnp.concatenate(
        [first.reshape(tiles // 8, 8, 128), second.reshape(tiles // 8, 8, 128)], axis=1
    ).astype(bf16)


def row_is(r):
    return iota((16, 128), 0) % 8 == r


def padded(*parts):
    rows = sum(p.shape[0] for p in parts)
    return jnp.concatenate([*parts, jnp.zeros((128 - rows, 128), f32)], axis=0)


def flat(ref):
    return ref[...].reshape(-1, 128)


def chunk_copies(c_hbm, c_ref, sems):
    size = c_ref.shape[0] // CHUNKS
    return [
        pltpu.make_async_copy(
            c_hbm.at[pl.ds(i * size, size)], c_ref.at[pl.ds(i * size, size)], sems.at[i]
        )
        for i in range(CHUNKS)
    ]


def start(copies):
    for copy in copies:
        copy.start()


def over_groups(copies, groups, body):
    size = groups // CHUNKS
    for i, copy in enumerate(copies):
        copy.wait()
        lax.fori_loop(i * size, (i + 1) * size, lambda g, _: body(g), 0, unroll=4)


def backward_pass(own, copies, c_ref, w_ref, out0, out1):
    groups = c_ref.shape[0] // 8
    w_ref[...] = stacked(1.0 - own, own)

    def body(g):
        w = w_ref[g].astype(f32)
        lhs = jnp.concatenate(
            [jnp.where(row_is(r), w, 0.0).astype(bf16) for r in range(8)], axis=1
        )
        rhs = c_ref[pl.ds(g * 8, 8)].reshape(1024, 128)
        res = dot(lhs, rhs)
        out0[g] = res[:8]
        out1[g] = res[8:]
        return 0

    over_groups(copies, groups, body)


def forward_pass(far, bose, copies, c_ref, w_ref, out0, out1):
    groups = c_ref.shape[0] // 8
    w_ref[...] = stacked(far * (1.0 + bose), far + bose)

    def body(g):
        rhs = c_ref[pl.ds(g * 8, 8)].reshape(1024, 128)
        full = lax.dot_general(
            w_ref[g], rhs, (((1,), (1,)), ((), ())), preferred_element_type=f32
        )
        res = full[:, :128]
        for r in range(1, 8):
            res = jnp.where(row_is(r), full[:, r * 128 : (r + 1) * 128], res)
        out0[g] = res[:8]
        out1[g] = res[8:]
        return 0

    over_groups(copies, groups, body)


def electron_rate(sum_k, far, bose, f, copies, c_ref, w_ref, o0, o1):
    forward_pass(far, bose, copies, c_ref, w_ref, o0, o1)
    return pick(sum_k, flat(o0)) - f * pick(sum_k, flat(o1))


def gather_blocks(blocks, into):
    rows = blocks[0].shape[0]
    for s, block in enumerate(blocks):
        into[s * rows : (s + 1) * rows, :] = block[...]
    return into[...]


def put_blocks(value, blocks):
    rows = blocks[0].shape[0]
    for s, block in enumerate(blocks):
        block[...] = value[s * rows : (s + 1) * rows]


def need_kernel(kb, cap, *refs):
    ins, outs = refs[:9], refs[9:]
    small, blocks = outs[:7], outs[7:-3]
    pneed_ref, qneed_ref, sems = outs[-3:]
    copies = [
        pltpu.make_async_copy(src, dst, sems.at[i])
        for i, (src, dst) in enumerate(zip(ins, [*small, pneed_ref, qneed_ref]))
    ]
    start(copies)
    me = lax.axis_index("bulk")
    rows = len(blocks) * 2 * cap
    slots = pneed_ref.shape[1]
    x = iota((rows, slots), 0)
    y = iota((rows, slots), 1)
    peer, r = (x // (2 * cap)) ^ me, x % (2 * cap)
    e_here = (r < cap) & (y == peer * cap + r)
    p_here = (r >= cap) & (y == peer * cap + r - cap)
    for copy in copies:
        copy.wait()
    pn = jnp.broadcast_to(pneed_ref[...].astype(f32), (rows, slots))
    qn = jnp.broadcast_to(qneed_ref[...].astype(f32), (rows, slots)) + float(kb)
    col = jnp.sum(jnp.where(e_here, pn, 0.0) + jnp.where(p_here, qn, 0.0), axis=1, keepdims=True)
    put_blocks((iota((rows, 128), 1).astype(f32) == col).astype(f32), blocks)


def tables_kernel(
    cap,
    count_ref,
    kblock_ref,
    partner_ref,
    qslot_ref,
    f_ref,
    c_hbm,
    ge4_ref,
    gp4_ref,
    gp6_ref,
    gk_ref,
    sk_ref,
    sp4_ref,
    sp6_ref,
    b0_ref,
    b1_ref,
    w_ref,
    c_ref,
    sems,
):
    copies = chunk_copies(c_hbm, c_ref, sems)
    start(copies)
    me = lax.axis_index("bulk")
    tiles = kblock_ref.shape[1]
    kb = f_ref.shape[0]
    used = iota((1, tiles), 1) < count_ref[0]
    k = kblock_ref[...]
    e = partner_ref[...]
    q = qslot_ref[...]
    rows4 = sp4_ref.shape[0]
    rows6 = sp6_ref.shape[0]
    ind = lambda m: jnp.where(m, 1.0, 0.0)
    k_hot = ind(iota((kb, tiles), 0) == k)
    sk_ref[...] = jnp.where(used, k_hot, 0.0).astype(bf16)
    gk_ref[...] = k_hot.T.astype(bf16)
    x = iota((rows4, tiles), 0)
    row_e = ((e // cap) ^ me) * (2 * cap) + e % cap
    row_p = ((q // cap) ^ me) * (2 * cap) + cap + q % cap
    ge4_ref[...] = ind(x == row_e).T.astype(bf16)
    p_hot = ind(x == row_p)
    gp4_ref[...] = p_hot.T.astype(bf16)
    sp4_ref[...] = jnp.where(used, p_hot, 0.0).astype(bf16)
    x = iota((rows6, tiles), 0)
    row_z = ((q // cap) ^ me) * (3 * cap) + q % cap
    gp6_ref[...] = ind(x == row_z).T.astype(bf16)
    sp6_ref[...] = jnp.concatenate(
        [
            jnp.where(used, ind(x == row_z + cap), 0.0),
            jnp.where(used, ind(x == row_z + 2 * cap), 0.0),
        ],
        axis=1,
    ).astype(bf16)
    own = pick(gk_ref[...], f_ref[...])
    backward_pass(own, copies, c_ref, w_ref, b0_ref, b1_ref)


def serve_kernel(devices, cap, *refs):
    recv, (f_ref, n_ref), outs = refs[:devices], refs[devices : devices + 2], refs[devices + 2 :]
    send, rest = outs[:devices], outs[devices:]
    serve_ref, s6_ref, st4_ref, st6a_ref, st6b_ref, into = rest
    kb, qb = f_ref.shape[0], n_ref.shape[0]
    s4 = gather_blocks(recv, into)
    rows4, rows6 = s4.shape[0], s6_ref.shape[0]
    hot = s4.astype(bf16)
    serve_ref[...] = hot
    put_blocks(pick(hot, padded(f_ref[...], n_ref[...])), send)
    x = iota((rows6, rows4), 0)
    y = iota((rows6, rows4), 1)
    peer, r = x // (3 * cap), x % (3 * cap)
    source = peer * (2 * cap) + cap + r % cap

    def rows_of(kind):
        here = (y == source) & (r // cap == kind)
        return dot(jnp.where(here, 1.0, 0.0).astype(bf16), hot)

    s6_ref[...] = rows_of(0).astype(bf16)
    st4_ref[...] = s4.T[kb : kb + qb].astype(bf16)
    st6a_ref[...] = rows_of(1).T[kb : kb + qb].astype(bf16)
    st6b_ref[...] = rows_of(2).T[kb : kb + qb].astype(bf16)


def first_kernel(devices, *refs):
    recv, refs = refs[:devices], refs[devices:]
    (f_ref, ge4_ref, gp4_ref, sk_ref, sp4_ref, serve_ref, b0_ref, b1_ref, c_hbm), refs = (
        refs[:9],
        refs[9:],
    )
    send, (e_ref, f1_ref, w_ref, c_ref, sems, o0, o1, into) = refs[:devices], refs[devices:]
    copies = chunk_copies(c_hbm, c_ref, sems)
    start(copies)
    f = f_ref[...]
    got = gather_blocks(recv, into)
    far = pick(ge4_ref[...], got)
    bose = pick(gp4_ref[...], got)
    rate = electron_rate(sk_ref[...], far, bose, f, copies, c_ref, w_ref, o0, o1)
    gain = far * flat(b0_ref)
    terms = gain + bose * (gain - (1.0 - far) * flat(b1_ref))
    f1 = f + DT * rate
    e_ref[...] = rate
    f1_ref[...] = f1
    put_blocks(pick(serve_ref[...], padded(f1)) + pick(sp4_ref[...], terms), send)


def backward_kernel(f_ref, gk_ref, c_hbm, b0_ref, b1_ref, w_ref, c_ref, sems):
    copies = chunk_copies(c_hbm, c_ref, sems)
    start(copies)
    own = pick(gk_ref[...], f_ref[...])
    backward_pass(own, copies, c_ref, w_ref, b0_ref, b1_ref)


def phonon_kernel(devices, kb, *refs):
    recv, refs = refs[:devices], refs[devices:]
    n_ref, energy_ref, decay_ref, ge4_ref, st4_ref, sp6_ref, s6_ref, b0_ref, b1_ref = refs[:9]
    refs = refs[9:]
    send, (p_ref, n1_ref, far_ref, into) = refs[:devices], refs[devices:]
    n = n_ref[...]
    got = gather_blocks(recv, into)
    thermal = 1.0 / (jnp.exp(energy_ref[...]) - 1.0)
    rate = pick(st4_ref[...], got) - decay_ref[...] * (n - thermal)
    n1 = n + DT * rate
    p_ref[...] = rate
    n1_ref[...] = n1
    far = pick(ge4_ref[...], got)
    far_ref[...] = far
    gain = far * flat(b0_ref)
    both = jnp.concatenate([gain, gain - (1.0 - far) * flat(b1_ref)], axis=0)
    state = padded(jnp.zeros((kb, 128), f32), n1)
    put_blocks(pick(s6_ref[...], state) + pick(sp6_ref[...], both), send)


def second_kernel(devices, with_send, *refs):
    recv, refs = refs[:devices], refs[devices:]
    far_ref, f_ref, f1_ref, e_ref, n_ref, n1_ref, p_ref, energy_ref, decay_ref = refs[:9]
    gp6_ref, sk_ref, st6a_ref, st6b_ref, serve_ref, c_hbm = refs[9:15]
    refs = refs[15:]
    send, refs = (refs[:devices], refs[devices:]) if with_send else ((), refs)
    f2_ref, n2_ref, w_ref, c_ref, sems, o0, o1, into = refs
    copies = chunk_copies(c_hbm, c_ref, sems)
    start(copies)
    got = gather_blocks(recv, into)
    n, n1 = n_ref[...], n1_ref[...]
    bose = pick(gp6_ref[...], got)
    rate = electron_rate(
        sk_ref[...], far_ref[...], bose, f1_ref[...], copies, c_ref, w_ref, o0, o1
    )
    thermal = 1.0 / (jnp.exp(energy_ref[...]) - 1.0)
    p1 = (
        pick(st6a_ref[...], got)
        + n1 * pick(st6b_ref[...], got)
        - decay_ref[...] * (n1 - thermal)
    )
    n2 = n + (DT / 2.0) * (p_ref[...] + p1)
    n2_ref[...] = n2
    f2 = f_ref[...] + (DT / 2.0) * (e_ref[...] + rate)
    f2_ref[...] = f2
    if with_send:
        put_blocks(pick(serve_ref[...], padded(f2, n2)), send)


def call(kernel, name, outs, scratch=(), spaces=None, flops=0, seen=0):
    def run(*args):
        places = dict(spaces or {})
        specs = [
            pl.BlockSpec(memory_space=places.get(i, pltpu.VMEM)) for i in range(len(args))
        ]
        return pl.pallas_call(
            kernel,
            out_shape=[jax.ShapeDtypeStruct(s, d) for s, d in outs],
            in_specs=specs,
            out_specs=[pl.BlockSpec(memory_space=pltpu.VMEM)] * len(outs),
            scratch_shapes=list(scratch),
            compiler_params=pltpu.CompilerParams(vmem_limit_bytes=VMEM_LIMIT),
            cost_estimate=pl.CostEstimate(
                flops=flops, bytes_accessed=seen, transcendentals=0
            ),
            name=name,
        )(*args)

    return run


def on_device(
    electrons,
    phonons,
    phonon_energy,
    phonon_decay,
    coupling,
    tile_kblock,
    tile_partner,
    tile_qslot,
    tile_count,
    partner_need,
    phonon_need,
):
    devices = lax.axis_size("bulk")
    kb = electrons.shape[0]
    qb = phonons.shape[0]
    tiles = coupling.shape[0]
    cap = partner_need.shape[1] // devices
    assert cap == phonon_need.shape[1] // devices and kb + qb <= 128
    assert devices & (devices - 1) == 0
    rows4 = devices * 2 * cap
    rows6 = devices * 3 * cap
    groups = tiles // 8
    streams = [
        pltpu.VMEM((groups, 16, 128), bf16),
        pltpu.VMEM(coupling.shape, bf16),
        pltpu.SemaphoreType.DMA((CHUNKS,)),
    ]
    sums = [pltpu.VMEM((groups, 8, 128), f32)] * 2
    pass_out = [((groups, 8, 128), f32)] * 2
    blocks4 = [((2 * cap, 128), f32)] * devices
    blocks6 = [((3 * cap, 128), f32)] * devices
    into4 = pltpu.VMEM((rows4, 128), f32)
    into6 = pltpu.VMEM((rows6, 128), f32)
    work = dict(flops=2 * tiles * 16 * 128 * 128, seen=tiles * 128 * 128 * 2)

    def exchange(blocks):
        return [blocks[0]] + [
            lax.ppermute(block, "bulk", [(i, i ^ s) for i in range(devices)])
            for s, block in enumerate(blocks)
            if s
        ]

    ints = ((1, tiles), jnp.int32)
    lists = ((1, partner_need.shape[1]), jnp.int32)
    small = [((kb, 128), f32)] + [((qb, 128), f32)] * 3 + [ints] * 3
    f, n, energy, decay, kblock, partner, qslot, *need = call(
        functools.partial(need_kernel, kb, cap),
        "need",
        small + blocks4,
        [pltpu.VMEM(*lists), pltpu.VMEM(*lists), pltpu.SemaphoreType.DMA((9,))],
        spaces={i: pltpu.HBM for i in range(9)},
    )(
        electrons,
        phonons,
        phonon_energy,
        phonon_decay,
        tile_kblock.reshape(1, tiles),
        tile_partner.reshape(1, tiles),
        tile_qslot.reshape(1, tiles),
        partner_need,
        phonon_need,
    )
    served = exchange(need)
    ge4, gp4, gp6, gk, sk, sp4, sp6, b0, b1 = call(
        functools.partial(tables_kernel, cap),
        "tables",
        [
            ((tiles, rows4), bf16),
            ((tiles, rows4), bf16),
            ((tiles, rows6), bf16),
            ((tiles, kb), bf16),
            ((kb, tiles), bf16),
            ((rows4, tiles), bf16),
            ((rows6, 2 * tiles), bf16),
        ]
        + pass_out,
        streams,
        spaces={0: pltpu.SMEM, 5: pltpu.HBM},
        **work,
    )(tile_count, kblock, partner, qslot, f, coupling)
    outs = call(
        functools.partial(serve_kernel, devices, cap),
        "serve",
        blocks4
        + [
            ((rows4, 128), bf16),
            ((rows6, 128), bf16),
            ((qb, rows4), bf16),
            ((qb, rows6), bf16),
            ((qb, rows6), bf16),
        ],
        [into4],
    )(*served, f, n)
    send, (serve, s6, st4, st6a, st6b) = outs[:devices], outs[devices:]

    back = call(backward_kernel, "backward", pass_out, streams, spaces={2: pltpu.HBM}, **work)
    for step in range(STEPS):
        recv = exchange(send)
        if step:
            b0, b1 = back(f, gk, coupling)
        outs = call(
            functools.partial(first_kernel, devices),
            "first",
            blocks4 + [((kb, 128), f32)] * 2,
            streams + sums + [into4],
            spaces={devices + 8: pltpu.HBM},
            **work,
        )(*recv, f, ge4, gp4, sk, sp4, serve, b0, b1, coupling)
        send, (e0, f1) = outs[:devices], outs[devices:]
        recv = exchange(send)
        b0, b1 = back(f1, gk, coupling)
        outs = call(
            functools.partial(phonon_kernel, devices, kb),
            "phonon",
            blocks6 + [((qb, 128), f32)] * 2 + [((tiles, 128), f32)],
            [into4],
        )(*recv, n, energy, decay, ge4, st4, sp6, s6, b0, b1)
        send, (p0, n1, far) = outs[:devices], outs[devices:]
        recv = exchange(send)
        last = step == STEPS - 1
        outs = call(
            functools.partial(second_kernel, devices, not last),
            "second",
            ([] if last else blocks4) + [((kb, 128), f32), ((qb, 128), f32)],
            streams + sums + [into6],
            spaces={devices + 14: pltpu.HBM},
            **work,
        )(
            *recv, far, f, f1, e0, n, n1, p0, energy, decay,
            gp6, sk, st6a, st6b, serve, coupling,
        )
        send, (f, n) = outs[:-2], outs[-2:]
    return (f, n)


def solution(mesh):
    placed = (
        P(("groups", "bulk"), None),
        P(("groups", "bulk"), None),
        P("bulk", None),
        P("bulk", None),
        P("bulk", None, None),
        P("bulk"),
        P("bulk"),
        P("bulk"),
        P("bulk"),
        P("bulk", None),
        P("bulk", None),
    )
    return jax.shard_map(
        on_device,
        mesh=mesh,
        in_specs=placed,
        out_specs=(P(("groups", "bulk"), None), P(("groups", "bulk"), None)),
        check_vma=False,
    )
```

time: 121 us -> 204 us (1.69)
  starting transfers between devices: 18 us -> 146 us
  blocking collectives: 37.2 us -> 0 us
  local copies, waits for them, and re-layouts: 32.5 us -> 9.79 us
  waiting for transfers between devices: 3.01 us -> 14.8 us
  Pallas kernels: 28 us -> 31.5 us
    ppermute x0 -> x105, starting transfers between devices: none -> 146 us  [exchange(): lax.ppermute(block, 'bulk', [(i, i ^ s) for i in range(devices)])]
    all_to_all x3 -> x0, blocking collectives: 37.2 us -> none  [exchange(): return lax.all_to_all(x, 'bulk', split_axis=0, concat_axis=0, tiled=True)]
    unnamed x40 -> x22, local copies, waits for them, and re-layouts: 32.5 us -> 9.79 us
    all_to_all x4 -> x0, starting transfers between devices: 18 us -> none  [exchange(): return lax.all_to_all(x, 'bulk', split_axis=0, concat_axis=0, tiled=True)]
    ppermute x0 -> x105, waiting for transfers between devices: none -> 14.8 us  [exchange(): lax.ppermute(block, 'bulk', [(i, i ^ s) for i in range(devices)])]
    pallas_call x12, Pallas kernels: 28 us -> 31.5 us  [run(): pl.pallas_call(kernel, out_shape=[jax.ShapeDtypeStruct(s, d) for s, d in...]
    all_to_all x4 -> x0, waiting for transfers between devices: 3.01 us -> none  [exchange(): return lax.all_to_all(x, 'bulk', split_axis=0, concat_axis=0, tiled=True)]
  transfers between devices with their start and end apart: 4 -> 105, of which waited for: 3 -> 9; matrix products, arithmetic and copies ran while one was open for 0% -> 0% of each run, Pallas kernels for 8% -> 6%
where the time goes in v2:
time: 204 us; the launch traced here: 203 us
  starting transfers between devices  146 us (72%)
  Pallas kernels  31.5 us (15%)
  waiting for transfers between devices  14.8 us (7%)
  local copies, waits for them, and re-layouts  9.79 us (5%)
    ppermute x105, starting transfers between devices, exchange(): lax.ppermute(block, 'bulk', [(i, i ^ s) for i in range(devices)])  146 us
    pallas_call x12, Pallas kernels, run(): pl.pallas_call(kernel, out_shape=[jax.ShapeDtypeStruct(s, d) for s, d in...  31.5 us
    ppermute x105, waiting for transfers between devices, exchange(): lax.ppermute(block, 'bulk', [(i, i ^ s) for i in range(devices)])  14.8 us
    unnamed x22, local copies, waits for them, and re-layouts  9.79 us
  transfers between devices with their start and end apart: 105, of which 9 were waited for; matrix products, arithmetic and copies ran while one was open for 0% of the time, Pallas kernels for 6%

profile of v2, /device:TPU:0, one launch (start us, length us, event | category | flops | bytes accessed | tf_op | source)
XLA Modules:
  0.0 203.5 jit_solution(7120317988023775880)
XLA Ops:
  7.5 2.6 %collective-permute-start.1 = (f32[4,128]{1,0:T(4,128)S(1)}, f32[4,128]{1,0:T(4,128)S(1)}, u32[]{:S(2)}, u32[]{:S(2)}) collective-permute-start(f32[4,128]{1,0:T(4,128)S(1)} %get-tuple-element.155), channel_id=1, source_target_pairs={{0,2},{1,3},{2,0},{3,1},{4,6},{5,7},{6,4},{7,5},{8,10},{9,11},{10,... | collective-permute-start | bytes 6152 | tf_op jit(solution)/shard_map/ppermute | solution.py:381
  12.0 2.6 %collective-permute-start.5 = (f32[4,128]{1,0:T(4,128)S(1)}, f32[4,128]{1,0:T(4,128)S(1)}, u32[]{:S(2)}, u32[]{:S(2)}) collective-permute-start(f32[4,128]{1,0:T(4,128)S(1)} %get-tuple-element.159), channel_id=1, source_target_pairs={{0,6},{1,7},{2,4},{3,5},{4,2},{5,3},{6,0},{7,1},{8,14},{9,15},{10,... | collective-permute-start | bytes 6152 | tf_op jit(solution)/shard_map/ppermute | solution.py:381
  14.8 2.6 %collective-permute-start.7 = (f32[4,128]{1,0:T(4,128)S(1)}, f32[4,128]{1,0:T(4,128)S(1)}, u32[]{:S(2)}, u32[]{:S(2)}) collective-permute-start(f32[4,128]{1,0:T(4,128)S(1)} %get-tuple-element.161), channel_id=1, source_target_pairs={{0,8},{1,9},{2,10},{3,11},{4,12},{5,13},{6,14},{7,15},{8,0},{9,1},... | collective-permute-start | bytes 6152 | tf_op jit(solution)/shard_map/ppermute | solution.py:381
  17.5 3.5 %collective-permute-start.9 = (f32[4,128]{1,0:T(4,128)S(1)}, f32[4,128]{1,0:T(4,128)S(1)}, u32[]{:S(2)}, u32[]{:S(2)}) collective-permute-start(f32[4,128]{1,0:T(4,128)S(1)} %get-tuple-element.163), channel_id=1, source_target_pairs={{0,10},{1,11},{2,8},{3,9},{4,14},{5,15},{6,12},{7,13},{8,2},{9,3},... | collective-permute-start | bytes 6152 | tf_op jit(solution)/shard_map/ppermute | solution.py:381
  21.1 3.5 %collective-permute-start.11 = (f32[4,128]{1,0:T(4,128)S(1)}, f32[4,128]{1,0:T(4,128)S(1)}, u32[]{:S(2)}, u32[]{:S(2)}) collective-permute-start(f32[4,128]{1,0:T(4,128)S(1)} %get-tuple-element.165), channel_id=1, source_target_pairs={{0,12},{1,13},{2,14},{3,15},{4,8},{5,9},{6,10},{7,11},{8,4},{9,5},... | collective-permute-start | bytes 6152 | tf_op jit(solution)/shard_map/ppermute | solution.py:381
  24.7 4.4 %collective-permute-start.13 = (f32[4,128]{1,0:T(4,128)S(1)}, f32[4,128]{1,0:T(4,128)S(1)}, u32[]{:S(2)}, u32[]{:S(2)}) collective-permute-start(f32[4,128]{1,0:T(4,128)S(1)} %get-tuple-element.167), channel_id=1, source_target_pairs={{0,14},{1,15},{2,12},{3,13},{4,10},{5,11},{6,8},{7,9},{8,6},{9,7},... | collective-permute-start | bytes 6152 | tf_op jit(solution)/shard_map/ppermute | solution.py:381
  31.0 3.8 %collective-permute-done.14.refs_15_ = f32[4,128]{1,0:T(4,128)S(1)} collective-permute-done((f32[4,128]{1,0:T(4,128)S(1)}, f32[4,128]{1,0:T(4,128)S(1)}, u32[]{:S(2)}, u32[]{:S(2)}) %collective-permute-start.14) | collective-permute-done | bytes 2080 | tf_op jit(solution)/shard_map/ppermute | solution.py:381
  39.0 2.3 %collective-permute-start.21 = (f32[4,128]{1,0:T(4,128)S(1)}, f32[4,128]{1,0:T(4,128)S(1)}, u32[]{:S(2)}, u32[]{:S(2)}) collective-permute-start(f32[4,128]{1,0:T(4,128)S(1)} %get-tuple-element.178), channel_id=1, source_target_pairs={{0,7},{1,6},{2,5},{3,4},{4,3},{5,2},{6,1},{7,0},{8,15},{9,14},{10,... | collective-permute-start | bytes 6152 | tf_op jit(solution)/shard_map/ppermute | solution.py:381
  41.4 2.7 %collective-permute-start.23 = (f32[4,128]{1,0:T(4,128)S(1)}, f32[4,128]{1,0:T(4,128)S(1)}, u32[]{:S(2)}, u32[]{:S(2)}) collective-permute-start(f32[4,128]{1,0:T(4,128)S(1)} %get-tuple-element.180), channel_id=1, source_target_pairs={{0,9},{1,8},{2,11},{3,10},{4,13},{5,12},{6,15},{7,14},{8,1},{9,0},... | collective-permute-start | bytes 6152 | tf_op jit(solution)/shard_map/ppermute | solution.py:381
  45.1 3.3 %collective-permute-start.25 = (f32[4,128]{1,0:T(4,128)S(1)}, f32[4,128]{1,0:T(4,128)S(1)}, u32[]{:S(2)}, u32[]{:S(2)}) collective-permute-start(f32[4,128]{1,0:T(4,128)S(1)} %get-tuple-element.182), channel_id=1, source_target_pairs={{0,11},{1,10},{2,9},{3,8},{4,15},{5,14},{6,13},{7,12},{8,3},{9,2},... | collective-permute-start | bytes 6152 | tf_op jit(solution)/shard_map/ppermute | solution.py:381
  48.7 3.2 %collective-permute-start.27 = (f32[4,128]{1,0:T(4,128)S(1)}, f32[4,128]{1,0:T(4,128)S(1)}, u32[]{:S(2)}, u32[]{:S(2)}) collective-permute-start(f32[4,128]{1,0:T(4,128)S(1)} %get-tuple-element.184), channel_id=1, source_target_pairs={{0,13},{1,12},{2,15},{3,14},{4,9},{5,8},{6,11},{7,10},{8,5},{9,4},... | collective-permute-start | bytes 6152 | tf_op jit(solution)/shard_map/ppermute | solution.py:381
  52.4 3.9 %collective-permute-start.29 = (f32[4,128]{1,0:T(4,128)S(1)}, f32[4,128]{1,0:T(4,128)S(1)}, u32[]{:S(2)}, u32[]{:S(2)}) collective-permute-start(f32[4,128]{1,0:T(4,128)S(1)} %get-tuple-element.186), channel_id=1, source_target_pairs={{0,15},{1,14},{2,13},{3,12},{4,11},{5,10},{6,9},{7,8},{8,7},{9,6},... | collective-permute-start | bytes 6152 | tf_op jit(solution)/shard_map/ppermute | solution.py:381
  56.3 3.4 %copy-done = bf16[256,128,128]{2,1,0:T(8,128)(2,1)S(1)} copy-done((bf16[256,128,128]{2,1,0:T(8,128)(2,1)S(1)}, bf16[256,128,128]{2,1,0:T(8,128)(2,1)}, u32[]{:S(2)}) %copy-start) | copy-done | bytes 8388632
  59.7 3.1 %tables.1 = (bf16[256,64]{1,0:T(8,128)(2,1)S(1)}, bf16[256,64]{1,0:T(8,128)(2,1)S(1)}, bf16[256,96]{1,0:T(8,128)(2,1)S(1)}, bf16[256,32]{1,0:T(8,128)(2,1)S(1)},...) custom-call(s32[1]{0:T(128)S(6)} %copy.13.count_ref, ...), custom_call_target="tpu_custom_call" | custom-call | flops 134217728 | bytes 8388608 | tf_op jit(solution)/shard_map/tables/pallas_call | solution.py:327
  63.1 4.4 %first.2 = (f32[4,128]{1,0:T(4,128)S(1)}, f32[4,128]{1,0:T(4,128)S(1)}, f32[4,128]{1,0:T(4,128)S(1)}, f32[4,128]{1,0:T(4,128)S(1)}, f32[4,128]{1,0:T(4,128)S(1)}...) custom-call(f32[4,128]{1,0:T(4,128)S(1)} %get-tuple-element.171.refs, ...), custom_call_target="tpu_custom_call" | custom-call | flops 134217728 | bytes 8388608 | tf_op jit(solution)/shard_map/first/pallas_call | solution.py:327
  69.4 2.1 %collective-permute-start.34 = (f32[4,128]{1,0:T(4,128)S(1)}, f32[4,128]{1,0:T(4,128)S(1)}, u32[]{:S(2)}, u32[]{:S(2)}) collective-permute-start(f32[4,128]{1,0:T(4,128)S(1)} %get-tuple-element.202), channel_id=1, source_target_pairs={{0,5},{1,4},{2,7},{3,6},{4,1},{5,0},{6,3},{7,2},{8,13},{9,12},{10,... | collective-permute-start | bytes 6152 | tf_op jit(solution)/shard_map/ppermute | solution.py:381
  71.7 2.1 %collective-permute-start.36 = (f32[4,128]{1,0:T(4,128)S(1)}, f32[4,128]{1,0:T(4,128)S(1)}, u32[]{:S(2)}, u32[]{:S(2)}) collective-permute-start(f32[4,128]{1,0:T(4,128)S(1)} %get-tuple-element.204), channel_id=1, source_target_pairs={{0,7},{1,6},{2,5},{3,4},{4,3},{5,2},{6,1},{7,0},{8,15},{9,14},{10,... | collective-permute-start | bytes 6152 | tf_op jit(solution)/shard_map/ppermute | solution.py:381
  73.8 3.0 %collective-permute-start.38 = (f32[4,128]{1,0:T(4,128)S(1)}, f32[4,128]{1,0:T(4,128)S(1)}, u32[]{:S(2)}, u32[]{:S(2)}) collective-permute-start(f32[4,128]{1,0:T(4,128)S(1)} %get-tuple-element.206), channel_id=1, source_target_pairs={{0,9},{1,8},{2,11},{3,10},{4,13},{5,12},{6,15},{7,14},{8,1},{9,0},... | collective-permute-start | bytes 6152 | tf_op jit(solution)/shard_map/ppermute | solution.py:381
  77.1 2.9 %collective-permute-start.40 = (f32[4,128]{1,0:T(4,128)S(1)}, f32[4,128]{1,0:T(4,128)S(1)}, u32[]{:S(2)}, u32[]{:S(2)}) collective-permute-start(f32[4,128]{1,0:T(4,128)S(1)} %get-tuple-element.208), channel_id=1, source_target_pairs={{0,11},{1,10},{2,9},{3,8},{4,15},{5,14},{6,13},{7,12},{8,3},{9,2},... | collective-permute-start | bytes 6152 | tf_op jit(solution)/shard_map/ppermute | solution.py:381
  80.4 3.5 %collective-permute-start.42 = (f32[4,128]{1,0:T(4,128)S(1)}, f32[4,128]{1,0:T(4,128)S(1)}, u32[]{:S(2)}, u32[]{:S(2)}) collective-permute-start(f32[4,128]{1,0:T(4,128)S(1)} %get-tuple-element.210), channel_id=1, source_target_pairs={{0,13},{1,12},{2,15},{3,14},{4,9},{5,8},{6,11},{7,10},{8,5},{9,4},... | collective-permute-start | bytes 6152 | tf_op jit(solution)/shard_map/ppermute | solution.py:381
  84.4 3.6 %collective-permute-start.44 = (f32[4,128]{1,0:T(4,128)S(1)}, f32[4,128]{1,0:T(4,128)S(1)}, u32[]{:S(2)}, u32[]{:S(2)}) collective-permute-start(f32[4,128]{1,0:T(4,128)S(1)} %get-tuple-element.212), channel_id=1, source_target_pairs={{0,15},{1,14},{2,13},{3,12},{4,11},{5,10},{6,9},{7,8},{8,7},{9,6},... | collective-permute-start | bytes 6152 | tf_op jit(solution)/shard_map/ppermute | solution.py:381
  88.0 3.0 %backward.3 = (f32[32,8,128]{2,1,0:T(8,128)S(1)}, f32[32,8,128]{2,1,0:T(8,128)S(1)}) custom-call(f32[32,128]{1,0:T(8,128)S(1)} %get-tuple-element.218.f_ref.refs_18_, bf16[256,32]{1,0:T(8,128)(2,1)S(1)} %get-tuple-element.219.gk_ref, bf16[256,128,128]{2,1,0:T(8,128)(2,1)S(1)} %copy-done.1), custom_call_target="tpu_custom_call" | custom-call | flops 134217728 | bytes 8388608 | tf_op jit(solution)/shard_map/backward/pallas_call | solution.py:327
  93.8 2.1 %collective-permute-start.49 = (f32[6,128]{1,0:T(8,128)S(1)}, f32[6,128]{1,0:T(8,128)S(1)}, u32[]{:S(2)}, u32[]{:S(2)}) collective-permute-start(f32[6,128]{1,0:T(8,128)S(1)} %get-tuple-element.227), channel_id=1, source_target_pairs={{0,5},{1,4},{2,7},{3,6},{4,1},{5,0},{6,3},{7,2},{8,13},{9,12},{10,... | collective-permute-start | bytes 9224 | tf_op jit(solution)/shard_map/ppermute | solution.py:381
  96.1 2.1 %collective-permute-start.51 = (f32[6,128]{1,0:T(8,128)S(1)}, f32[6,128]{1,0:T(8,128)S(1)}, u32[]{:S(2)}, u32[]{:S(2)}) collective-permute-start(f32[6,128]{1,0:T(8,128)S(1)} %get-tuple-element.229), channel_id=1, source_target_pairs={{0,7},{1,6},{2,5},{3,4},{4,3},{5,2},{6,1},{7,0},{8,15},{9,14},{10,... | collective-permute-start | bytes 9224 | tf_op jit(solution)/shard_map/ppermute | solution.py:381
  104.4 2.0 %collective-permute-start.56 = (f32[6,128]{1,0:T(8,128)S(1)}, f32[6,128]{1,0:T(8,128)S(1)}, u32[]{:S(2)}, u32[]{:S(2)}) collective-permute-start(f32[6,128]{1,0:T(8,128)S(1)} %get-tuple-element.234), channel_id=1, source_target_pairs={{0,12},{1,13},{2,14},{3,15},{4,8},{5,9},{6,10},{7,11},{8,4},{9,5},... | collective-permute-start | bytes 9224 | tf_op jit(solution)/shard_map/ppermute | solution.py:381
  108.3 2.6 %collective-permute-start.58 = (f32[6,128]{1,0:T(8,128)S(1)}, f32[6,128]{1,0:T(8,128)S(1)}, u32[]{:S(2)}, u32[]{:S(2)}) collective-permute-start(f32[6,128]{1,0:T(8,128)S(1)} %get-tuple-element.236), channel_id=1, source_target_pairs={{0,14},{1,15},{2,12},{3,13},{4,10},{5,11},{6,8},{7,9},{8,6},{9,7},... | collective-permute-start | bytes 9224 | tf_op jit(solution)/shard_map/ppermute | solution.py:381
  112.4 2.2 %collective-permute-done.58.refs_14_ = f32[6,128]{1,0:T(8,128)S(1)} collective-permute-done((f32[6,128]{1,0:T(8,128)S(1)}, f32[6,128]{1,0:T(8,128)S(1)}, u32[]{:S(2)}, u32[]{:S(2)}) %collective-permute-start.58) | collective-permute-done | bytes 3104 | tf_op jit(solution)/shard_map/ppermute | solution.py:381
  114.6 2.0 %collective-permute-done.59.refs_15_ = f32[6,128]{1,0:T(8,128)S(1)} collective-permute-done((f32[6,128]{1,0:T(8,128)S(1)}, f32[6,128]{1,0:T(8,128)S(1)}, u32[]{:S(2)}, u32[]{:S(2)}) %collective-permute-start.59) | collective-permute-done | bytes 3104 | tf_op jit(solution)/shard_map/ppermute | solution.py:381
  116.6 4.6 %second.2 = (f32[4,128]{1,0:T(4,128)S(1)}, f32[4,128]{1,0:T(4,128)S(1)}, f32[4,128]{1,0:T(4,128)S(1)}, f32[4,128]{1,0:T(4,128)S(1)}, f32[4,128]{1,0:T(4,128)S(1)...) custom-call(f32[6,128]{1,0:T(8,128)S(1)} %get-tuple-element.222.refs, ...), custom_call_target="tpu_custom_call" | custom-call | flops 134217728 | bytes 8388608 | tf_op jit(solution)/shard_map/second/pallas_call | solution.py:327
  125.2 2.3 %collective-permute-start.66 = (f32[4,128]{1,0:T(4,128)S(1)}, f32[4,128]{1,0:T(4,128)S(1)}, u32[]{:S(2)}, u32[]{:S(2)}) collective-permute-start(f32[4,128]{1,0:T(4,128)S(1)} %get-tuple-element.252), channel_id=1, source_target_pairs={{0,7},{1,6},{2,5},{3,4},{4,3},{5,2},{6,1},{7,0},{8,15},{9,14},{10,... | collective-permute-start | bytes 6152 | tf_op jit(solution)/shard_map/ppermute | solution.py:381
  127.7 2.6 %collective-permute-start.68 = (f32[4,128]{1,0:T(4,128)S(1)}, f32[4,128]{1,0:T(4,128)S(1)}, u32[]{:S(2)}, u32[]{:S(2)}) collective-permute-start(f32[4,128]{1,0:T(4,128)S(1)} %get-tuple-element.254), channel_id=1, source_target_pairs={{0,9},{1,8},{2,11},{3,10},{4,13},{5,12},{6,15},{7,14},{8,1},{9,0},... | collective-permute-start | bytes 6152 | tf_op jit(solution)/shard_map/ppermute | solution.py:381
  131.2 2.6 %collective-permute-start.70 = (f32[4,128]{1,0:T(4,128)S(1)}, f32[4,128]{1,0:T(4,128)S(1)}, u32[]{:S(2)}, u32[]{:S(2)}) collective-permute-start(f32[4,128]{1,0:T(4,128)S(1)} %get-tuple-element.256), channel_id=1, source_target_pairs={{0,11},{1,10},{2,9},{3,8},{4,15},{5,14},{6,13},{7,12},{8,3},{9,2},... | collective-permute-start | bytes 6152 | tf_op jit(solution)/shard_map/ppermute | solution.py:381
  134.9 2.5 %collective-permute-start.72 = (f32[4,128]{1,0:T(4,128)S(1)}, f32[4,128]{1,0:T(4,128)S(1)}, u32[]{:S(2)}, u32[]{:S(2)}) collective-permute-start(f32[4,128]{1,0:T(4,128)S(1)} %get-tuple-element.258), channel_id=1, source_target_pairs={{0,13},{1,12},{2,15},{3,14},{4,9},{5,8},{6,11},{7,10},{8,5},{9,4},... | collective-permute-start | bytes 6152 | tf_op jit(solution)/shard_map/ppermute | solution.py:381
  137.4 2.0 collective-permute-start.73
  139.4 2.4 %collective-permute-start.74 = (f32[4,128]{1,0:T(4,128)S(1)}, f32[4,128]{1,0:T(4,128)S(1)}, u32[]{:S(2)}, u32[]{:S(2)}) collective-permute-start(f32[4,128]{1,0:T(4,128)S(1)} %get-tuple-element.260), channel_id=1, source_target_pairs={{0,15},{1,14},{2,13},{3,12},{4,11},{5,10},{6,9},{7,8},{8,7},{9,6},... | collective-permute-start | bytes 6152 | tf_op jit(solution)/shard_map/ppermute | solution.py:381
  141.8 3.0 %backward.4 = (f32[32,8,128]{2,1,0:T(8,128)S(1)}, f32[32,8,128]{2,1,0:T(8,128)S(1)}) custom-call(f32[32,128]{1,0:T(8,128)S(1)} %get-tuple-element.261.f_ref.refs_16_.refs_17_, bf16[256,32]{1,0:T(8,128)(2,1)S(1)} %get-tuple-element.219.gk_ref, bf16[256,128,128]{2,1,0:T(8,128)(2,1)S(1)} %copy-done.1), custom_call_target="tpu_custom_call" | custom-call | flops 134217728 | bytes 8388608 | tf_op jit(solution)/shard_map/backward/pallas_call | solution.py:327
  145.1 4.4 %first.3 = (f32[4,128]{1,0:T(4,128)S(1)}, f32[4,128]{1,0:T(4,128)S(1)}, f32[4,128]{1,0:T(4,128)S(1)}, f32[4,128]{1,0:T(4,128)S(1)}, f32[4,128]{1,0:T(4,128)S(1)}...) custom-call(f32[4,128]{1,0:T(4,128)S(1)} %get-tuple-element.245.refs, ...), custom_call_target="tpu_custom_call" | custom-call | flops 134217728 | bytes 8388608 | tf_op jit(solution)/shard_map/first/pallas_call | solution.py:327
  153.5 2.3 %collective-permute-start.81 = (f32[4,128]{1,0:T(4,128)S(1)}, f32[4,128]{1,0:T(4,128)S(1)}, u32[]{:S(2)}, u32[]{:S(2)}) collective-permute-start(f32[4,128]{1,0:T(4,128)S(1)} %get-tuple-element.271), channel_id=1, source_target_pairs={{0,7},{1,6},{2,5},{3,4},{4,3},{5,2},{6,1},{7,0},{8,15},{9,14},{10,... | collective-permute-start | bytes 6152 | tf_op jit(solution)/shard_map/ppermute | solution.py:381
  156.6 2.0 collective-permute-start.83
  165.7 2.6 %collective-permute-start.88 = (f32[4,128]{1,0:T(4,128)S(1)}, f32[4,128]{1,0:T(4,128)S(1)}, u32[]{:S(2)}, u32[]{:S(2)}) collective-permute-start(f32[4,128]{1,0:T(4,128)S(1)} %get-tuple-element.278), channel_id=1, source_target_pairs={{0,14},{1,15},{2,12},{3,13},{4,10},{5,11},{6,8},{7,9},{8,6},{9,7},... | collective-permute-start | bytes 6152 | tf_op jit(solution)/shard_map/ppermute | solution.py:381
  170.0 3.0 %backward.5 = (f32[32,8,128]{2,1,0:T(8,128)S(1)}, f32[32,8,128]{2,1,0:T(8,128)S(1)}) custom-call(f32[32,128]{1,0:T(8,128)S(1)} %get-tuple-element.281.f_ref.refs_18_, bf16[256,32]{1,0:T(8,128)(2,1)S(1)} %get-tuple-element.219.gk_ref, bf16[256,128,128]{2,1,0:T(8,128)(2,1)S(1)} %copy-done.1), custom_call_target="tpu_custom_call" | custom-call | flops 134217728 | bytes 8388608 | tf_op jit(solution)/shard_map/backward/pallas_call | solution.py:327
  178.5 2.3 %collective-permute-start.96 = (f32[6,128]{1,0:T(8,128)S(1)}, f32[6,128]{1,0:T(8,128)S(1)}, u32[]{:S(2)}, u32[]{:S(2)}) collective-permute-start(f32[6,128]{1,0:T(8,128)S(1)} %get-tuple-element.291), channel_id=1, source_target_pairs={{0,7},{1,6},{2,5},{3,4},{4,3},{5,2},{6,1},{7,0},{8,15},{9,14},{10,... | collective-permute-start | bytes 9224 | tf_op jit(solution)/shard_map/ppermute | solution.py:381
  181.0 2.6 %collective-permute-start.98 = (f32[6,128]{1,0:T(8,128)S(1)}, f32[6,128]{1,0:T(8,128)S(1)}, u32[]{:S(2)}, u32[]{:S(2)}) collective-permute-start(f32[6,128]{1,0:T(8,128)S(1)} %get-tuple-element.293), channel_id=1, source_target_pairs={{0,9},{1,8},{2,11},{3,10},{4,13},{5,12},{6,15},{7,14},{8,1},{9,0},... | collective-permute-start | bytes 9224 | tf_op jit(solution)/shard_map/ppermute | solution.py:381
  184.5 2.6 %collective-permute-start.100 = (f32[6,128]{1,0:T(8,128)S(1)}, f32[6,128]{1,0:T(8,128)S(1)}, u32[]{:S(2)}, u32[]{:S(2)}) collective-permute-start(f32[6,128]{1,0:T(8,128)S(1)} %get-tuple-element.295), channel_id=1, source_target_pairs={{0,11},{1,10},{2,9},{3,8},{4,15},{5,14},{6,13},{7,12},{8,3},{9,2},... | collective-permute-start | bytes 9224 | tf_op jit(solution)/shard_map/ppermute | solution.py:381
  188.1 2.5 %collective-permute-start.102 = (f32[6,128]{1,0:T(8,128)S(1)}, f32[6,128]{1,0:T(8,128)S(1)}, u32[]{:S(2)}, u32[]{:S(2)}) collective-permute-start(f32[6,128]{1,0:T(8,128)S(1)} %get-tuple-element.297), channel_id=1, source_target_pairs={{0,13},{1,12},{2,15},{3,14},{4,9},{5,8},{6,11},{7,10},{8,5},{9,4},... | collective-permute-start | bytes 9224 | tf_op jit(solution)/shard_map/ppermute | solution.py:381
  190.7 2.1 %collective-permute-start.103 = (f32[6,128]{1,0:T(8,128)S(1)}, f32[6,128]{1,0:T(8,128)S(1)}, u32[]{:S(2)}, u32[]{:S(2)}) collective-permute-start(f32[6,128]{1,0:T(8,128)S(1)} %get-tuple-element.298), channel_id=1, source_target_pairs={{0,14},{1,15},{2,12},{3,13},{4,10},{5,11},{6,8},{7,9},{8,6},{9,7},... | collective-permute-start | bytes 9224 | tf_op jit(solution)/shard_map/ppermute | solution.py:381
  192.7 2.3 %collective-permute-start.104 = (f32[6,128]{1,0:T(8,128)S(1)}, f32[6,128]{1,0:T(8,128)S(1)}, u32[]{:S(2)}, u32[]{:S(2)}) collective-permute-start(f32[6,128]{1,0:T(8,128)S(1)} %get-tuple-element.299), channel_id=1, source_target_pairs={{0,15},{1,14},{2,13},{3,12},{4,11},{5,10},{6,9},{7,8},{8,7},{9,6},... | collective-permute-start | bytes 9224 | tf_op jit(solution)/shard_map/ppermute | solution.py:381
  198.5 4.8 %second.3 = (f32[32,128]{1,0:T(8,128)}, f32[16,128]{1,0:T(8,128)}) custom-call(f32[6,128]{1,0:T(8,128)S(1)} %get-tuple-element.284.refs_0_, f32[6,128]{1,0:T(8,128)S(1)} %collective-permute-done.90.refs_1_, f32[6,128]{1,0:T(8,128)S(1)} %collective-permute-done.91.refs_2_, f32[6,128]{1,0:T(8,128)S(1)} %collective-permute-done.92.refs_3_, ...), custom_call_target="tpu_custom_call" | custom-call | flops 134217728 | bytes 8388608 | tf_op jit(solution)/shard_map/second/pallas_call | solution.py:327
  (196 shorter events, 63.7 us)
Async XLA Ops:
  12.0 9.0 %collective-permute-start.5 = (f32[4,128]{1,0:T(4,128)S(1)}, f32[4,128]{1,0:T(4,128)S(1)}, u32[]{:S(2)}, u32[]{:S(2)}) collective-permute-start(f32[4,128]{1,0:T(4,128)S(1)} %get-tuple-element.159), channel_id=1, source_target_pairs={{0,6},{1,7},{2,4},{3,5},{4,2},{5,3},{6,0},{7,1},{8,14},{9,15},{10,... | collective-permute-start | bytes 6152 | tf_op jit(solution)/shard_map/ppermute | solution.py:381
  14.8 9.9 %collective-permute-start.7 = (f32[4,128]{1,0:T(4,128)S(1)}, f32[4,128]{1,0:T(4,128)S(1)}, u32[]{:S(2)}, u32[]{:S(2)}) collective-permute-start(f32[4,128]{1,0:T(4,128)S(1)} %get-tuple-element.161), channel_id=1, source_target_pairs={{0,8},{1,9},{2,10},{3,11},{4,12},{5,13},{6,14},{7,15},{8,0},{9,1},... | collective-permute-start | bytes 6152 | tf_op jit(solution)/shard_map/ppermute | solution.py:381
  17.5 11.6 %collective-permute-start.9 = (f32[4,128]{1,0:T(4,128)S(1)}, f32[4,128]{1,0:T(4,128)S(1)}, u32[]{:S(2)}, u32[]{:S(2)}) collective-permute-start(f32[4,128]{1,0:T(4,128)S(1)} %get-tuple-element.163), channel_id=1, source_target_pairs={{0,10},{1,11},{2,8},{3,9},{4,14},{5,15},{6,12},{7,13},{8,2},{9,3},... | collective-permute-start | bytes 6152 | tf_op jit(solution)/shard_map/ppermute | solution.py:381
  21.0 8.2 %collective-permute-start.10 = (f32[4,128]{1,0:T(4,128)S(1)}, f32[4,128]{1,0:T(4,128)S(1)}, u32[]{:S(2)}, u32[]{:S(2)}) collective-permute-start(f32[4,128]{1,0:T(4,128)S(1)} %get-tuple-element.164), channel_id=1, source_target_pairs={{0,11},{1,10},{2,9},{3,8},{4,15},{5,14},{6,13},{7,12},{8,3},{9,2},... | collective-permute-start | bytes 6152 | tf_op jit(solution)/shard_map/ppermute | solution.py:381
  21.1 8.1 %collective-permute-start.11 = (f32[4,128]{1,0:T(4,128)S(1)}, f32[4,128]{1,0:T(4,128)S(1)}, u32[]{:S(2)}, u32[]{:S(2)}) collective-permute-start(f32[4,128]{1,0:T(4,128)S(1)} %get-tuple-element.165), channel_id=1, source_target_pairs={{0,12},{1,13},{2,14},{3,15},{4,8},{5,9},{6,10},{7,11},{8,4},{9,5},... | collective-permute-start | bytes 6152 | tf_op jit(solution)/shard_map/ppermute | solution.py:381
  39.0 9.3 %collective-permute-start.21 = (f32[4,128]{1,0:T(4,128)S(1)}, f32[4,128]{1,0:T(4,128)S(1)}, u32[]{:S(2)}, u32[]{:S(2)}) collective-permute-start(f32[4,128]{1,0:T(4,128)S(1)} %get-tuple-element.178), channel_id=1, source_target_pairs={{0,7},{1,6},{2,5},{3,4},{4,3},{5,2},{6,1},{7,0},{8,15},{9,14},{10,... | collective-permute-start | bytes 6152 | tf_op jit(solution)/shard_map/ppermute | solution.py:381
  41.4 10.5 %collective-permute-start.23 = (f32[4,128]{1,0:T(4,128)S(1)}, f32[4,128]{1,0:T(4,128)S(1)}, u32[]{:S(2)}, u32[]{:S(2)}) collective-permute-start(f32[4,128]{1,0:T(4,128)S(1)} %get-tuple-element.180), channel_id=1, source_target_pairs={{0,9},{1,8},{2,11},{3,10},{4,13},{5,12},{6,15},{7,14},{8,1},{9,0},... | collective-permute-start | bytes 6152 | tf_op jit(solution)/shard_map/ppermute | solution.py:381
  44.1 8.3 %collective-permute-start.24 = (f32[4,128]{1,0:T(4,128)S(1)}, f32[4,128]{1,0:T(4,128)S(1)}, u32[]{:S(2)}, u32[]{:S(2)}) collective-permute-start(f32[4,128]{1,0:T(4,128)S(1)} %get-tuple-element.181), channel_id=1, source_target_pairs={{0,10},{1,11},{2,8},{3,9},{4,14},{5,15},{6,12},{7,13},{8,2},{9,3},... | collective-permute-start | bytes 6152 | tf_op jit(solution)/shard_map/ppermute | solution.py:381
  45.1 17.7 %collective-permute-start.25 = (f32[4,128]{1,0:T(4,128)S(1)}, f32[4,128]{1,0:T(4,128)S(1)}, u32[]{:S(2)}, u32[]{:S(2)}) collective-permute-start(f32[4,128]{1,0:T(4,128)S(1)} %get-tuple-element.182), channel_id=1, source_target_pairs={{0,11},{1,10},{2,9},{3,8},{4,15},{5,14},{6,13},{7,12},{8,3},{9,2},... | collective-permute-start | bytes 6152 | tf_op jit(solution)/shard_map/ppermute | solution.py:381
  48.3 14.5 %collective-permute-start.26 = (f32[4,128]{1,0:T(4,128)S(1)}, f32[4,128]{1,0:T(4,128)S(1)}, u32[]{:S(2)}, u32[]{:S(2)}) collective-permute-start(f32[4,128]{1,0:T(4,128)S(1)} %get-tuple-element.183), channel_id=1, source_target_pairs={{0,12},{1,13},{2,14},{3,15},{4,8},{5,9},{6,10},{7,11},{8,4},{9,5},... | collective-permute-start | bytes 6152 | tf_op jit(solution)/shard_map/ppermute | solution.py:381
  48.7 14.1 %collective-permute-start.27 = (f32[4,128]{1,0:T(4,128)S(1)}, f32[4,128]{1,0:T(4,128)S(1)}, u32[]{:S(2)}, u32[]{:S(2)}) collective-permute-start(f32[4,128]{1,0:T(4,128)S(1)} %get-tuple-element.184), channel_id=1, source_target_pairs={{0,13},{1,12},{2,15},{3,14},{4,9},{5,8},{6,11},{7,10},{8,5},{9,4},... | collective-permute-start | bytes 6152 | tf_op jit(solution)/shard_map/ppermute | solution.py:381
  51.9 10.9 %collective-permute-start.28 = (f32[4,128]{1,0:T(4,128)S(1)}, f32[4,128]{1,0:T(4,128)S(1)}, u32[]{:S(2)}, u32[]{:S(2)}) collective-permute-start(f32[4,128]{1,0:T(4,128)S(1)} %get-tuple-element.185), channel_id=1, source_target_pairs={{0,14},{1,15},{2,12},{3,13},{4,10},{5,11},{6,8},{7,9},{8,6},{9,7},... | collective-permute-start | bytes 6152 | tf_op jit(solution)/shard_map/ppermute | solution.py:381
  52.4 10.4 %collective-permute-start.29 = (f32[4,128]{1,0:T(4,128)S(1)}, f32[4,128]{1,0:T(4,128)S(1)}, u32[]{:S(2)}, u32[]{:S(2)}) collective-permute-start(f32[4,128]{1,0:T(4,128)S(1)} %get-tuple-element.186), channel_id=1, source_target_pairs={{0,15},{1,14},{2,13},{3,12},{4,11},{5,10},{6,9},{7,8},{8,7},{9,6},... | collective-permute-start | bytes 6152 | tf_op jit(solution)/shard_map/ppermute | solution.py:381
  69.4 7.4 %collective-permute-start.34 = (f32[4,128]{1,0:T(4,128)S(1)}, f32[4,128]{1,0:T(4,128)S(1)}, u32[]{:S(2)}, u32[]{:S(2)}) collective-permute-start(f32[4,128]{1,0:T(4,128)S(1)} %get-tuple-element.202), channel_id=1, source_target_pairs={{0,5},{1,4},{2,7},{3,6},{4,1},{5,0},{6,3},{7,2},{8,13},{9,12},{10,... | collective-permute-start | bytes 6152 | tf_op jit(solution)/shard_map/ppermute | solution.py:381
  71.7 8.3 %collective-permute-start.36 = (f32[4,128]{1,0:T(4,128)S(1)}, f32[4,128]{1,0:T(4,128)S(1)}, u32[]{:S(2)}, u32[]{:S(2)}) collective-permute-start(f32[4,128]{1,0:T(4,128)S(1)} %get-tuple-element.204), channel_id=1, source_target_pairs={{0,7},{1,6},{2,5},{3,4},{4,3},{5,2},{6,1},{7,0},{8,15},{9,14},{10,... | collective-permute-start | bytes 6152 | tf_op jit(solution)/shard_map/ppermute | solution.py:381
  73.8 10.1 %collective-permute-start.38 = (f32[4,128]{1,0:T(4,128)S(1)}, f32[4,128]{1,0:T(4,128)S(1)}, u32[]{:S(2)}, u32[]{:S(2)}) collective-permute-start(f32[4,128]{1,0:T(4,128)S(1)} %get-tuple-element.206), channel_id=1, source_target_pairs={{0,9},{1,8},{2,11},{3,10},{4,13},{5,12},{6,15},{7,14},{8,1},{9,0},... | collective-permute-start | bytes 6152 | tf_op jit(solution)/shard_map/ppermute | solution.py:381
  76.8 7.6 %collective-permute-start.39 = (f32[4,128]{1,0:T(4,128)S(1)}, f32[4,128]{1,0:T(4,128)S(1)}, u32[]{:S(2)}, u32[]{:S(2)}) collective-permute-start(f32[4,128]{1,0:T(4,128)S(1)} %get-tuple-element.207), channel_id=1, source_target_pairs={{0,10},{1,11},{2,8},{3,9},{4,14},{5,15},{6,12},{7,13},{8,2},{9,3},... | collective-permute-start | bytes 6152 | tf_op jit(solution)/shard_map/ppermute | solution.py:381
  77.1 13.9 %collective-permute-start.40 = (f32[4,128]{1,0:T(4,128)S(1)}, f32[4,128]{1,0:T(4,128)S(1)}, u32[]{:S(2)}, u32[]{:S(2)}) collective-permute-start(f32[4,128]{1,0:T(4,128)S(1)} %get-tuple-element.208), channel_id=1, source_target_pairs={{0,11},{1,10},{2,9},{3,8},{4,15},{5,14},{6,13},{7,12},{8,3},{9,2},... | collective-permute-start | bytes 6152 | tf_op jit(solution)/shard_map/ppermute | solution.py:381
  80.0 11.0 %collective-permute-start.41 = (f32[4,128]{1,0:T(4,128)S(1)}, f32[4,128]{1,0:T(4,128)S(1)}, u32[]{:S(2)}, u32[]{:S(2)}) collective-permute-start(f32[4,128]{1,0:T(4,128)S(1)} %get-tuple-element.209), channel_id=1, source_target_pairs={{0,12},{1,13},{2,14},{3,15},{4,8},{5,9},{6,10},{7,11},{8,4},{9,5},... | collective-permute-start | bytes 6152 | tf_op jit(solution)/shard_map/ppermute | solution.py:381
  80.4 10.6 %collective-permute-start.42 = (f32[4,128]{1,0:T(4,128)S(1)}, f32[4,128]{1,0:T(4,128)S(1)}, u32[]{:S(2)}, u32[]{:S(2)}) collective-permute-start(f32[4,128]{1,0:T(4,128)S(1)} %get-tuple-element.210), channel_id=1, source_target_pairs={{0,13},{1,12},{2,15},{3,14},{4,9},{5,8},{6,11},{7,10},{8,5},{9,4},... | collective-permute-start | bytes 6152 | tf_op jit(solution)/shard_map/ppermute | solution.py:381
  93.8 7.4 %collective-permute-start.49 = (f32[6,128]{1,0:T(8,128)S(1)}, f32[6,128]{1,0:T(8,128)S(1)}, u32[]{:S(2)}, u32[]{:S(2)}) collective-permute-start(f32[6,128]{1,0:T(8,128)S(1)} %get-tuple-element.227), channel_id=1, source_target_pairs={{0,5},{1,4},{2,7},{3,6},{4,1},{5,0},{6,3},{7,2},{8,13},{9,12},{10,... | collective-permute-start | bytes 9224 | tf_op jit(solution)/shard_map/ppermute | solution.py:381
  96.1 8.3 %collective-permute-start.51 = (f32[6,128]{1,0:T(8,128)S(1)}, f32[6,128]{1,0:T(8,128)S(1)}, u32[]{:S(2)}, u32[]{:S(2)}) collective-permute-start(f32[6,128]{1,0:T(8,128)S(1)} %get-tuple-element.229), channel_id=1, source_target_pairs={{0,7},{1,6},{2,5},{3,4},{4,3},{5,2},{6,1},{7,0},{8,15},{9,14},{10,... | collective-permute-start | bytes 9224 | tf_op jit(solution)/shard_map/ppermute | solution.py:381
  98.2 8.2 %collective-permute-start.52 = (f32[6,128]{1,0:T(8,128)S(1)}, f32[6,128]{1,0:T(8,128)S(1)}, u32[]{:S(2)}, u32[]{:S(2)}) collective-permute-start(f32[6,128]{1,0:T(8,128)S(1)} %get-tuple-element.230), channel_id=1, source_target_pairs={{0,8},{1,9},{2,10},{3,11},{4,12},{5,13},{6,14},{7,15},{8,0},{9,1},... | collective-permute-start | bytes 9224 | tf_op jit(solution)/shard_map/ppermute | solution.py:381
  99.2 9.1 %collective-permute-start.53 = (f32[6,128]{1,0:T(8,128)S(1)}, f32[6,128]{1,0:T(8,128)S(1)}, u32[]{:S(2)}, u32[]{:S(2)}) collective-permute-start(f32[6,128]{1,0:T(8,128)S(1)} %get-tuple-element.231), channel_id=1, source_target_pairs={{0,9},{1,8},{2,11},{3,10},{4,13},{5,12},{6,15},{7,14},{8,1},{9,0},... | collective-permute-start | bytes 9224 | tf_op jit(solution)/shard_map/ppermute | solution.py:381
  101.2 9.7 %collective-permute-start.54 = (f32[6,128]{1,0:T(8,128)S(1)}, f32[6,128]{1,0:T(8,128)S(1)}, u32[]{:S(2)}, u32[]{:S(2)}) collective-permute-start(f32[6,128]{1,0:T(8,128)S(1)} %get-tuple-element.232), channel_id=1, source_target_pairs={{0,10},{1,11},{2,8},{3,9},{4,14},{5,15},{6,12},{7,13},{8,2},{9,3},... | collective-permute-start | bytes 9224 | tf_op jit(solution)/shard_map/ppermute | solution.py:381
  102.7 9.7 %collective-permute-start.55 = (f32[6,128]{1,0:T(8,128)S(1)}, f32[6,128]{1,0:T(8,128)S(1)}, u32[]{:S(2)}, u32[]{:S(2)}) collective-permute-start(f32[6,128]{1,0:T(8,128)S(1)} %get-tuple-element.233), channel_id=1, source_target_pairs={{0,11},{1,10},{2,9},{3,8},{4,15},{5,14},{6,13},{7,12},{8,3},{9,2},... | collective-permute-start | bytes 9224 | tf_op jit(solution)/shard_map/ppermute | solution.py:381
  104.4 8.0 %collective-permute-start.56 = (f32[6,128]{1,0:T(8,128)S(1)}, f32[6,128]{1,0:T(8,128)S(1)}, u32[]{:S(2)}, u32[]{:S(2)}) collective-permute-start(f32[6,128]{1,0:T(8,128)S(1)} %get-tuple-element.234), channel_id=1, source_target_pairs={{0,12},{1,13},{2,14},{3,15},{4,8},{5,9},{6,10},{7,11},{8,4},{9,5},... | collective-permute-start | bytes 9224 | tf_op jit(solution)/shard_map/ppermute | solution.py:381
  125.2 8.6 %collective-permute-start.66 = (f32[4,128]{1,0:T(4,128)S(1)}, f32[4,128]{1,0:T(4,128)S(1)}, u32[]{:S(2)}, u32[]{:S(2)}) collective-permute-start(f32[4,128]{1,0:T(4,128)S(1)} %get-tuple-element.252), channel_id=1, source_target_pairs={{0,7},{1,6},{2,5},{3,4},{4,3},{5,2},{6,1},{7,0},{8,15},{9,14},{10,... | collective-permute-start | bytes 6152 | tf_op jit(solution)/shard_map/ppermute | solution.py:381
  127.6 7.4 %collective-permute-start.67 = (f32[4,128]{1,0:T(4,128)S(1)}, f32[4,128]{1,0:T(4,128)S(1)}, u32[]{:S(2)}, u32[]{:S(2)}) collective-permute-start(f32[4,128]{1,0:T(4,128)S(1)} %get-tuple-element.253), channel_id=1, source_target_pairs={{0,8},{1,9},{2,10},{3,11},{4,12},{5,13},{6,14},{7,15},{8,0},{9,1},... | collective-permute-start | bytes 6152 | tf_op jit(solution)/shard_map/ppermute | solution.py:381
  127.7 9.7 %collective-permute-start.68 = (f32[4,128]{1,0:T(4,128)S(1)}, f32[4,128]{1,0:T(4,128)S(1)}, u32[]{:S(2)}, u32[]{:S(2)}) collective-permute-start(f32[4,128]{1,0:T(4,128)S(1)} %get-tuple-element.254), channel_id=1, source_target_pairs={{0,9},{1,8},{2,11},{3,10},{4,13},{5,12},{6,15},{7,14},{8,1},{9,0},... | collective-permute-start | bytes 6152 | tf_op jit(solution)/shard_map/ppermute | solution.py:381
  130.3 9.1 %collective-permute-start.69 = (f32[4,128]{1,0:T(4,128)S(1)}, f32[4,128]{1,0:T(4,128)S(1)}, u32[]{:S(2)}, u32[]{:S(2)}) collective-permute-start(f32[4,128]{1,0:T(4,128)S(1)} %get-tuple-element.255), channel_id=1, source_target_pairs={{0,10},{1,11},{2,8},{3,9},{4,14},{5,15},{6,12},{7,13},{8,2},{9,3},... | collective-permute-start | bytes 6152 | tf_op jit(solution)/shard_map/ppermute | solution.py:381
  131.2 13.6 %collective-permute-start.70 = (f32[4,128]{1,0:T(4,128)S(1)}, f32[4,128]{1,0:T(4,128)S(1)}, u32[]{:S(2)}, u32[]{:S(2)}) collective-permute-start(f32[4,128]{1,0:T(4,128)S(1)} %get-tuple-element.256), channel_id=1, source_target_pairs={{0,11},{1,10},{2,9},{3,8},{4,15},{5,14},{6,13},{7,12},{8,3},{9,2},... | collective-permute-start | bytes 6152 | tf_op jit(solution)/shard_map/ppermute | solution.py:381
  133.8 11.0 %collective-permute-start.71 = (f32[4,128]{1,0:T(4,128)S(1)}, f32[4,128]{1,0:T(4,128)S(1)}, u32[]{:S(2)}, u32[]{:S(2)}) collective-permute-start(f32[4,128]{1,0:T(4,128)S(1)} %get-tuple-element.257), channel_id=1, source_target_pairs={{0,12},{1,13},{2,14},{3,15},{4,8},{5,9},{6,10},{7,11},{8,4},{9,5},... | collective-permute-start | bytes 6152 | tf_op jit(solution)/shard_map/ppermute | solution.py:381
  134.9 9.8 %collective-permute-start.72 = (f32[4,128]{1,0:T(4,128)S(1)}, f32[4,128]{1,0:T(4,128)S(1)}, u32[]{:S(2)}, u32[]{:S(2)}) collective-permute-start(f32[4,128]{1,0:T(4,128)S(1)} %get-tuple-element.258), channel_id=1, source_target_pairs={{0,13},{1,12},{2,15},{3,14},{4,9},{5,8},{6,11},{7,10},{8,5},{9,4},... | collective-permute-start | bytes 6152 | tf_op jit(solution)/shard_map/ppermute | solution.py:381
  137.4 7.4 %collective-permute-start.73 = (f32[4,128]{1,0:T(4,128)S(1)}, f32[4,128]{1,0:T(4,128)S(1)}, u32[]{:S(2)}, u32[]{:S(2)}) collective-permute-start(f32[4,128]{1,0:T(4,128)S(1)} %get-tuple-element.259), channel_id=1, source_target_pairs={{0,14},{1,15},{2,12},{3,13},{4,10},{5,11},{6,8},{7,9},{8,6},{9,7},... | collective-permute-start | bytes 6152 | tf_op jit(solution)/shard_map/ppermute | solution.py:381
  153.5 8.5 %collective-permute-start.81 = (f32[4,128]{1,0:T(4,128)S(1)}, f32[4,128]{1,0:T(4,128)S(1)}, u32[]{:S(2)}, u32[]{:S(2)}) collective-permute-start(f32[4,128]{1,0:T(4,128)S(1)} %get-tuple-element.271), channel_id=1, source_target_pairs={{0,7},{1,6},{2,5},{3,4},{4,3},{5,2},{6,1},{7,0},{8,15},{9,14},{10,... | collective-permute-start | bytes 6152 | tf_op jit(solution)/shard_map/ppermute | solution.py:381
  155.8 8.0 %collective-permute-start.82 = (f32[4,128]{1,0:T(4,128)S(1)}, f32[4,128]{1,0:T(4,128)S(1)}, u32[]{:S(2)}, u32[]{:S(2)}) collective-permute-start(f32[4,128]{1,0:T(4,128)S(1)} %get-tuple-element.272), channel_id=1, source_target_pairs={{0,8},{1,9},{2,10},{3,11},{4,12},{5,13},{6,14},{7,15},{8,0},{9,1},... | collective-permute-start | bytes 6152 | tf_op jit(solution)/shard_map/ppermute | solution.py:381
  156.6 9.1 %collective-permute-start.83 = (f32[4,128]{1,0:T(4,128)S(1)}, f32[4,128]{1,0:T(4,128)S(1)}, u32[]{:S(2)}, u32[]{:S(2)}) collective-permute-start(f32[4,128]{1,0:T(4,128)S(1)} %get-tuple-element.273), channel_id=1, source_target_pairs={{0,9},{1,8},{2,11},{3,10},{4,13},{5,12},{6,15},{7,14},{8,1},{9,0},... | collective-permute-start | bytes 6152 | tf_op jit(solution)/shard_map/ppermute | solution.py:381
  158.6 9.7 %collective-permute-start.84 = (f32[4,128]{1,0:T(4,128)S(1)}, f32[4,128]{1,0:T(4,128)S(1)}, u32[]{:S(2)}, u32[]{:S(2)}) collective-permute-start(f32[4,128]{1,0:T(4,128)S(1)} %get-tuple-element.274), channel_id=1, source_target_pairs={{0,10},{1,11},{2,8},{3,9},{4,14},{5,15},{6,12},{7,13},{8,2},{9,3},... | collective-permute-start | bytes 6152 | tf_op jit(solution)/shard_map/ppermute | solution.py:381
  160.1 12.9 %collective-permute-start.85 = (f32[4,128]{1,0:T(4,128)S(1)}, f32[4,128]{1,0:T(4,128)S(1)}, u32[]{:S(2)}, u32[]{:S(2)}) collective-permute-start(f32[4,128]{1,0:T(4,128)S(1)} %get-tuple-element.275), channel_id=1, source_target_pairs={{0,11},{1,10},{2,9},{3,8},{4,15},{5,14},{6,13},{7,12},{8,3},{9,2},... | collective-permute-start | bytes 6152 | tf_op jit(solution)/shard_map/ppermute | solution.py:381
  162.0 11.0 %collective-permute-start.86 = (f32[4,128]{1,0:T(4,128)S(1)}, f32[4,128]{1,0:T(4,128)S(1)}, u32[]{:S(2)}, u32[]{:S(2)}) collective-permute-start(f32[4,128]{1,0:T(4,128)S(1)} %get-tuple-element.276), channel_id=1, source_target_pairs={{0,12},{1,13},{2,14},{3,15},{4,8},{5,9},{6,10},{7,11},{8,4},{9,5},... | collective-permute-start | bytes 6152 | tf_op jit(solution)/shard_map/ppermute | solution.py:381
  163.8 9.2 %collective-permute-start.87 = (f32[4,128]{1,0:T(4,128)S(1)}, f32[4,128]{1,0:T(4,128)S(1)}, u32[]{:S(2)}, u32[]{:S(2)}) collective-permute-start(f32[4,128]{1,0:T(4,128)S(1)} %get-tuple-element.277), channel_id=1, source_target_pairs={{0,13},{1,12},{2,15},{3,14},{4,9},{5,8},{6,11},{7,10},{8,5},{9,4},... | collective-permute-start | bytes 6152 | tf_op jit(solution)/shard_map/ppermute | solution.py:381
  165.7 7.3 %collective-permute-start.88 = (f32[4,128]{1,0:T(4,128)S(1)}, f32[4,128]{1,0:T(4,128)S(1)}, u32[]{:S(2)}, u32[]{:S(2)}) collective-permute-start(f32[4,128]{1,0:T(4,128)S(1)} %get-tuple-element.278), channel_id=1, source_target_pairs={{0,14},{1,15},{2,12},{3,13},{4,10},{5,11},{6,8},{7,9},{8,6},{9,7},... | collective-permute-start | bytes 6152 | tf_op jit(solution)/shard_map/ppermute | solution.py:381
  178.5 8.6 %collective-permute-start.96 = (f32[6,128]{1,0:T(8,128)S(1)}, f32[6,128]{1,0:T(8,128)S(1)}, u32[]{:S(2)}, u32[]{:S(2)}) collective-permute-start(f32[6,128]{1,0:T(8,128)S(1)} %get-tuple-element.291), channel_id=1, source_target_pairs={{0,7},{1,6},{2,5},{3,4},{4,3},{5,2},{6,1},{7,0},{8,15},{9,14},{10,... | collective-permute-start | bytes 9224 | tf_op jit(solution)/shard_map/ppermute | solution.py:381
  181.0 9.7 %collective-permute-start.98 = (f32[6,128]{1,0:T(8,128)S(1)}, f32[6,128]{1,0:T(8,128)S(1)}, u32[]{:S(2)}, u32[]{:S(2)}) collective-permute-start(f32[6,128]{1,0:T(8,128)S(1)} %get-tuple-element.293), channel_id=1, source_target_pairs={{0,9},{1,8},{2,11},{3,10},{4,13},{5,12},{6,15},{7,14},{8,1},{9,0},... | collective-permute-start | bytes 9224 | tf_op jit(solution)/shard_map/ppermute | solution.py:381
  183.5 9.2 %collective-permute-start.99 = (f32[6,128]{1,0:T(8,128)S(1)}, f32[6,128]{1,0:T(8,128)S(1)}, u32[]{:S(2)}, u32[]{:S(2)}) collective-permute-start(f32[6,128]{1,0:T(8,128)S(1)} %get-tuple-element.294), channel_id=1, source_target_pairs={{0,10},{1,11},{2,8},{3,9},{4,14},{5,15},{6,12},{7,13},{8,2},{9,3},... | collective-permute-start | bytes 9224 | tf_op jit(solution)/shard_map/ppermute | solution.py:381
  184.5 10.6 %collective-permute-start.100 = (f32[6,128]{1,0:T(8,128)S(1)}, f32[6,128]{1,0:T(8,128)S(1)}, u32[]{:S(2)}, u32[]{:S(2)}) collective-permute-start(f32[6,128]{1,0:T(8,128)S(1)} %get-tuple-element.295), channel_id=1, source_target_pairs={{0,11},{1,10},{2,9},{3,8},{4,15},{5,14},{6,13},{7,12},{8,3},{9,2},... | collective-permute-start | bytes 9224 | tf_op jit(solution)/shard_map/ppermute | solution.py:381
  187.0 8.0 %collective-permute-start.101 = (f32[6,128]{1,0:T(8,128)S(1)}, f32[6,128]{1,0:T(8,128)S(1)}, u32[]{:S(2)}, u32[]{:S(2)}) collective-permute-start(f32[6,128]{1,0:T(8,128)S(1)} %get-tuple-element.296), channel_id=1, source_target_pairs={{0,12},{1,13},{2,14},{3,15},{4,8},{5,9},{6,10},{7,11},{8,4},{9,5},... | collective-permute-start | bytes 9224 | tf_op jit(solution)/shard_map/ppermute | solution.py:381
  (68 other events, 329.9 us)

commit v3 on v2

v3 whole, which is shorter than its diff:
```python
import functools

import jax
import jax.numpy as jnp
from jax import lax
from jax.experimental import pallas as pl
from jax.experimental.pallas import tpu as pltpu
from jax.sharding import PartitionSpec as P

STEPS = 2
DT = 0.05
CHUNKS = 8
f32 = jnp.float32
bf16 = jnp.bfloat16
VMEM_LIMIT = 24 * 1024 * 1024


def iota(shape, dim):
    return lax.broadcasted_iota(jnp.int32, shape, dim)


def dot(a, b):
    return lax.dot_general(a, b, (((1,), (0,)), ((), ())), preferred_element_type=f32)


def split(x):
    hi = x.astype(bf16)
    rest = x - hi.astype(f32)
    mid = rest.astype(bf16)
    lo = (rest - mid.astype(f32)).astype(bf16)
    return hi, mid, lo


def pick(onehot, x):
    hi, mid, lo = split(x)
    return dot(onehot, hi) + dot(onehot, mid) + dot(onehot, lo)


def stacked(first, second):
    tiles = first.shape[0]
    return jnp.concatenate(
        [first.reshape(tiles // 8, 8, 128), second.reshape(tiles // 8, 8, 128)], axis=1
    ).astype(bf16)


def row_is(r):
    return iota((16, 128), 0) % 8 == r


def padded(*parts):
    rows = sum(p.shape[0] for p in parts)
    return jnp.concatenate([*parts, jnp.zeros((128 - rows, 128), f32)], axis=0)


def flat(ref):
    return ref[...].reshape(-1, 128)


def chunk_copies(c_hbm, c_ref, sems):
    size = c_ref.shape[0] // CHUNKS
    return [
        pltpu.make_async_copy(
            c_hbm.at[pl.ds(i * size, size)], c_ref.at[pl.ds(i * size, size)], sems.at[i]
        )
        for i in range(CHUNKS)
    ]


def start(copies):
    for copy in copies:
        copy.start()


def over_groups(copies, groups, body):
    size = groups // CHUNKS
    for i, copy in enumerate(copies):
        copy.wait()
        lax.fori_loop(i * size, (i + 1) * size, lambda g, _: body(g), 0, unroll=4)


def backward_pass(own, copies, c_ref, w_ref, out0, out1):
    groups = c_ref.shape[0] // 8
    w_ref[...] = stacked(1.0 - own, own)

    def body(g):
        w = w_ref[g].astype(f32)
        lhs = jnp.concatenate(
            [jnp.where(row_is(r), w, 0.0).astype(bf16) for r in range(8)], axis=1
        )
        rhs = c_ref[pl.ds(g * 8, 8)].reshape(1024, 128)
        res = dot(lhs, rhs)
        out0[g] = res[:8]
        out1[g] = res[8:]
        return 0

    over_groups(copies, groups, body)


def forward_pass(far, bose, copies, c_ref, w_ref, out0, out1):
    groups = c_ref.shape[0] // 8
    w_ref[...] = stacked(far * (1.0 + bose), far + bose)

    def body(g):
        rhs = c_ref[pl.ds(g * 8, 8)].reshape(1024, 128)
        full = lax.dot_general(
            w_ref[g], rhs, (((1,), (1,)), ((), ())), preferred_element_type=f32
        )
        res = full[:, :128]
        for r in range(1, 8):
            res = jnp.where(row_is(r), full[:, r * 128 : (r + 1) * 128], res)
        out0[g] = res[:8]
        out1[g] = res[8:]
        return 0

    over_groups(copies, groups, body)


def electron_rate(sum_k, far, bose, f, copies, c_ref, w_ref, o0, o1):
    forward_pass(far, bose, copies, c_ref, w_ref, o0, o1)
    return pick(sum_k, flat(o0)) - f * pick(sum_k, flat(o1))


def need_kernel(kb, cap, *refs):
    ins, outs = refs[:9], refs[9:]
    small, out_ref = outs[:7], outs[7]
    pneed_ref, qneed_ref, sems = outs[-3:]
    copies = [
        pltpu.make_async_copy(src, dst, sems.at[i])
        for i, (src, dst) in enumerate(zip(ins, [*small, pneed_ref, qneed_ref]))
    ]
    start(copies)
    rows = out_ref.shape[0]
    slots = pneed_ref.shape[1]
    x = iota((rows, slots), 0)
    y = iota((rows, slots), 1)
    peer, r = x // (2 * cap), x % (2 * cap)
    e_here = (r < cap) & (y == peer * cap + r)
    p_here = (r >= cap) & (y == peer * cap + r - cap)
    for copy in copies:
        copy.wait()
    pn = jnp.broadcast_to(pneed_ref[...].astype(f32), (rows, slots))
    qn = jnp.broadcast_to(qneed_ref[...].astype(f32), (rows, slots)) + float(kb)
    col = jnp.sum(jnp.where(e_here, pn, 0.0) + jnp.where(p_here, qn, 0.0), axis=1, keepdims=True)
    out_ref[...] = (iota((rows, 128), 1).astype(f32) == col).astype(f32)


def tables_kernel(
    cap,
    count_ref,
    kblock_ref,
    partner_ref,
    qslot_ref,
    f_ref,
    c_hbm,
    ge4_ref,
    gp4_ref,
    gp8_ref,
    gk_ref,
    sk_ref,
    sp4_ref,
    sp8_ref,
    b0_ref,
    b1_ref,
    w_ref,
    c_ref,
    sems,
):
    copies = chunk_copies(c_hbm, c_ref, sems)
    start(copies)
    tiles = kblock_ref.shape[1]
    kb = f_ref.shape[0]
    used = iota((1, tiles), 1) < count_ref[0]
    k = kblock_ref[...]
    e = partner_ref[...]
    q = qslot_ref[...]
    rows4 = sp4_ref.shape[0]
    rows8 = sp8_ref.shape[0]
    ind = lambda m: jnp.where(m, 1.0, 0.0)
    k_hot = ind(iota((kb, tiles), 0) == k)
    sk_ref[...] = jnp.where(used, k_hot, 0.0).astype(bf16)
    gk_ref[...] = k_hot.T.astype(bf16)
    x = iota((rows4, tiles), 0)
    row_e = (e // cap) * (2 * cap) + e % cap
    row_p = (q // cap) * (2 * cap) + cap + q % cap
    ge4_ref[...] = ind(x == row_e).T.astype(bf16)
    p_hot = ind(x == row_p)
    gp4_ref[...] = p_hot.T.astype(bf16)
    sp4_ref[...] = jnp.where(used, p_hot, 0.0).astype(bf16)
    x = iota((rows8, tiles), 0)
    row_z = (q // cap) * (4 * cap) + q % cap
    gp8_ref[...] = ind(x == row_z).T.astype(bf16)
    sp8_ref[...] = jnp.concatenate(
        [
            jnp.where(used, ind(x == row_z + cap), 0.0),
            jnp.where(used, ind(x == row_z + 2 * cap), 0.0),
        ],
        axis=1,
    ).astype(bf16)
    own = pick(gk_ref[...], f_ref[...])
    backward_pass(own, copies, c_ref, w_ref, b0_ref, b1_ref)


def serve_kernel(
    cap, recv, f_ref, n_ref, send, serve_ref, s8_ref, st4_ref, st8a_ref, st8b_ref
):
    kb, qb = f_ref.shape[0], n_ref.shape[0]
    s4 = recv[...]
    rows4, rows8 = s4.shape[0], s8_ref.shape[0]
    hot = s4.astype(bf16)
    serve_ref[...] = hot
    send[...] = pick(hot, padded(f_ref[...], n_ref[...]))
    x = iota((rows8, rows4), 0)
    y = iota((rows8, rows4), 1)
    peer, r = x // (4 * cap), x % (4 * cap)
    source = peer * (2 * cap) + cap + r % cap

    def rows_of(kind):
        here = (y == source) & (r // cap == kind)
        return dot(jnp.where(here, 1.0, 0.0).astype(bf16), hot)

    s8_ref[...] = rows_of(0).astype(bf16)
    st4_ref[...] = s4.T[kb : kb + qb].astype(bf16)
    st8a_ref[...] = rows_of(1).T[kb : kb + qb].astype(bf16)
    st8b_ref[...] = rows_of(2).T[kb : kb + qb].astype(bf16)


def first_kernel(
    recv,
    f_ref,
    ge4_ref,
    gp4_ref,
    sk_ref,
    sp4_ref,
    serve_ref,
    b0_ref,
    b1_ref,
    c_hbm,
    send,
    e_ref,
    f1_ref,
    w_ref,
    c_ref,
    sems,
    o0,
    o1,
):
    copies = chunk_copies(c_hbm, c_ref, sems)
    start(copies)
    f = f_ref[...]
    got = recv[...]
    far = pick(ge4_ref[...], got)
    bose = pick(gp4_ref[...], got)
    rate = electron_rate(sk_ref[...], far, bose, f, copies, c_ref, w_ref, o0, o1)
    gain = far * flat(b0_ref)
    terms = gain + bose * (gain - (1.0 - far) * flat(b1_ref))
    f1 = f + DT * rate
    e_ref[...] = rate
    f1_ref[...] = f1
    send[...] = pick(serve_ref[...], padded(f1)) + pick(sp4_ref[...], terms)


def backward_kernel(f_ref, gk_ref, c_hbm, b0_ref, b1_ref, w_ref, c_ref, sems):
    copies = chunk_copies(c_hbm, c_ref, sems)
    start(copies)
    own = pick(gk_ref[...], f_ref[...])
    backward_pass(own, copies, c_ref, w_ref, b0_ref, b1_ref)


def phonon_kernel(
    kb,
    recv,
    n_ref,
    energy_ref,
    decay_ref,
    ge4_ref,
    st4_ref,
    sp8_ref,
    s8_ref,
    b0_ref,
    b1_ref,
    send,
    p_ref,
    n1_ref,
    far_ref,
):
    n = n_ref[...]
    got = recv[...]
    thermal = 1.0 / (jnp.exp(energy_ref[...]) - 1.0)
    rate = pick(st4_ref[...], got) - decay_ref[...] * (n - thermal)
    n1 = n + DT * rate
    p_ref[...] = rate
    n1_ref[...] = n1
    far = pick(ge4_ref[...], got)
    far_ref[...] = far
    gain = far * flat(b0_ref)
    both = jnp.concatenate([gain, gain - (1.0 - far) * flat(b1_ref)], axis=0)
    state = padded(jnp.zeros((kb, 128), f32), n1)
    send[...] = pick(s8_ref[...], state) + pick(sp8_ref[...], both)


def second_kernel(with_send, recv, *refs):
    far_ref, f_ref, f1_ref, e_ref, n_ref, n1_ref, p_ref, energy_ref, decay_ref = refs[:9]
    gp8_ref, sk_ref, st8a_ref, st8b_ref, serve_ref, c_hbm = refs[9:15]
    refs = refs[15:]
    f2_ref, n2_ref, *refs = refs
    send, refs = (refs[0], refs[1:]) if with_send else (None, refs)
    w_ref, c_ref, sems, o0, o1 = refs
    copies = chunk_copies(c_hbm, c_ref, sems)
    start(copies)
    got = recv[...]
    n, n1 = n_ref[...], n1_ref[...]
    bose = pick(gp8_ref[...], got)
    rate = electron_rate(
        sk_ref[...], far_ref[...], bose, f1_ref[...], copies, c_ref, w_ref, o0, o1
    )
    thermal = 1.0 / (jnp.exp(energy_ref[...]) - 1.0)
    p1 = (
        pick(st8a_ref[...], got)
        + n1 * pick(st8b_ref[...], got)
        - decay_ref[...] * (n1 - thermal)
    )
    n2 = n + (DT / 2.0) * (p_ref[...] + p1)
    n2_ref[...] = n2
    f2 = f_ref[...] + (DT / 2.0) * (e_ref[...] + rate)
    f2_ref[...] = f2
    if with_send:
        send[...] = pick(serve_ref[...], padded(f2, n2))


def call(kernel, name, outs, scratch=(), spaces=None, flops=0, seen=0):
    def run(*args):
        places = dict(spaces or {})
        args = [
            pltpu.with_memory_space_constraint(x, pltpu.HBM)
            if places.get(i) is pltpu.HBM
            else x
            for i, x in enumerate(args)
        ]
        specs = [
            pl.BlockSpec(memory_space=places.get(i, pltpu.VMEM)) for i in range(len(args))
        ]
        return pl.pallas_call(
            kernel,
            out_shape=[jax.ShapeDtypeStruct(s, d) for s, d in outs],
            in_specs=specs,
            out_specs=[pl.BlockSpec(memory_space=pltpu.VMEM)] * len(outs),
            scratch_shapes=list(scratch),
            compiler_params=pltpu.CompilerParams(vmem_limit_bytes=VMEM_LIMIT),
            cost_estimate=pl.CostEstimate(
                flops=flops, bytes_accessed=seen, transcendentals=0
            ),
            name=name,
        )(*args)

    return run


def on_device(
    electrons,
    phonons,
    phonon_energy,
    phonon_decay,
    coupling,
    tile_kblock,
    tile_partner,
    tile_qslot,
    tile_count,
    partner_need,
    phonon_need,
):
    devices = lax.axis_size("bulk")
    kb = electrons.shape[0]
    qb = phonons.shape[0]
    tiles = coupling.shape[0]
    cap = partner_need.shape[1] // devices
    assert cap == phonon_need.shape[1] // devices and kb + qb <= 128
    rows4 = devices * 2 * cap
    rows8 = devices * 4 * cap
    groups = tiles // 8
    streams = [
        pltpu.VMEM((groups, 16, 128), bf16),
        pltpu.VMEM(coupling.shape, bf16),
        pltpu.SemaphoreType.DMA((CHUNKS,)),
    ]
    sums = [pltpu.VMEM((groups, 8, 128), f32)] * 2
    pass_out = [((groups, 8, 128), f32)] * 2
    block4 = ((rows4, 128), f32)
    block8 = ((rows8, 128), f32)

    work = dict(flops=2 * tiles * 16 * 128 * 128, seen=tiles * 128 * 128 * 2)

    def exchange(x):
        return lax.all_to_all(x, "bulk", split_axis=0, concat_axis=0, tiled=True)

    ints = ((1, tiles), jnp.int32)
    lists = ((1, partner_need.shape[1]), jnp.int32)
    small = [((kb, 128), f32)] + [((qb, 128), f32)] * 3 + [ints] * 3
    f, n, energy, decay, kblock, partner, qslot, need = call(
        functools.partial(need_kernel, kb, cap),
        "need",
        small + [block4],
        [pltpu.VMEM(*lists), pltpu.VMEM(*lists), pltpu.SemaphoreType.DMA((9,))],
        spaces={i: pltpu.HBM for i in range(9)},
    )(
        electrons,
        phonons,
        phonon_energy,
        phonon_decay,
        tile_kblock.reshape(1, tiles),
        tile_partner.reshape(1, tiles),
        tile_qslot.reshape(1, tiles),
        partner_need,
        phonon_need,
    )
    served = exchange(need)
    ge4, gp4, gp8, gk, sk, sp4, sp8, b0, b1 = call(
        functools.partial(tables_kernel, cap),
        "tables",
        [
            ((tiles, rows4), bf16),
            ((tiles, rows4), bf16),
            ((tiles, rows8), bf16),
            ((tiles, kb), bf16),
            ((kb, tiles), bf16),
            ((rows4, tiles), bf16),
            ((rows8, 2 * tiles), bf16),
        ]
        + pass_out,
        streams,
        spaces={0: pltpu.SMEM, 5: pltpu.HBM},
        **work,
    )(tile_count, kblock, partner, qslot, f, coupling)
    send, serve, s8, st4, st8a, st8b = call(
        functools.partial(serve_kernel, cap),
        "serve",
        [
            block4,
            ((rows4, 128), bf16),
            ((rows8, 128), bf16),
            ((qb, rows4), bf16),
            ((qb, rows8), bf16),
            ((qb, rows8), bf16),
        ],
    )(served, f, n)

    back = call(backward_kernel, "backward", pass_out, streams, spaces={2: pltpu.HBM}, **work)
    for step in range(STEPS):
        recv = exchange(send)
        if step:
            b0, b1 = back(f, gk, coupling)
        send, e0, f1 = call(
            first_kernel,
            "first",
            [block4] + [((kb, 128), f32)] * 2,
            streams + sums,
            spaces={9: pltpu.HBM},
            **work,
        )(recv, f, ge4, gp4, sk, sp4, serve, b0, b1, coupling)
        recv = exchange(send)
        b0, b1 = back(f1, gk, coupling)
        send, p0, n1, far = call(
            functools.partial(phonon_kernel, kb),
            "phonon",
            [block8] + [((qb, 128), f32)] * 2 + [((tiles, 128), f32)],
        )(recv, n, energy, decay, ge4, st4, sp8, s8, b0, b1)
        recv = exchange(send)
        last = step == STEPS - 1
        f, n, *send = call(
            functools.partial(second_kernel, not last),
            "second",
            [((kb, 128), f32), ((qb, 128), f32)] + ([] if last else [block4]),
            streams + sums,
            spaces={15: pltpu.HBM},
            **work,
        )(
            recv, far, f, f1, e0, n, n1, p0, energy, decay,
            gp8, sk, st8a, st8b, serve, coupling,
        )
        send = send[0] if send else None
    return (f, n)


def solution(mesh):
    placed = (
        P(("groups", "bulk"), None),
        P(("groups", "bulk"), None),
        P("bulk", None),
        P("bulk", None),
        P("bulk", None, None),
        P("bulk"),
        P("bulk"),
        P("bulk"),
        P("bulk"),
        P("bulk", None),
        P("bulk", None),
    )
    return jax.shard_map(
        on_device,
        mesh=mesh,
        in_specs=placed,
        out_specs=(P(("groups", "bulk"), None), P(("groups", "bulk"), None)),
        check_vma=False,
    )
```

time: 204 us -> 100 us (0.49)
  starting transfers between devices: 146 us -> 14.5 us
  blocking collectives: 0 us -> 33.5 us
  local copies, waits for them, and re-layouts: 9.79 us -> 0 us
  Pallas kernels: 31.5 us -> 39.3 us
  waiting for transfers between devices: 14.8 us -> 10.6 us
    ppermute x105 -> x0, starting transfers between devices: 146 us -> none  [exchange(): lax.ppermute(block, 'bulk', [(i, i ^ s) for i in range(devices)])]
    all_to_all x0 -> x3, blocking collectives: none -> 33.5 us  [exchange(): return lax.all_to_all(x, 'bulk', split_axis=0, concat_axis=0, tiled=True)]
    ppermute x105 -> x0, waiting for transfers between devices: 14.8 us -> none  [exchange(): lax.ppermute(block, 'bulk', [(i, i ^ s) for i in range(devices)])]
    all_to_all x0 -> x4, starting transfers between devices: none -> 14.5 us  [exchange(): return lax.all_to_all(x, 'bulk', split_axis=0, concat_axis=0, tiled=True)]
    all_to_all x0 -> x4, waiting for transfers between devices: none -> 10.6 us  [exchange(): return lax.all_to_all(x, 'bulk', split_axis=0, concat_axis=0, tiled=True)]
    unnamed x22 -> x0, local copies, waits for them, and re-layouts: 9.79 us -> none
    pallas_call x12, Pallas kernels: 31.5 us -> 39.3 us  [run(): pl.pallas_call(kernel, out_shape=[jax.ShapeDtypeStruct(s, d) for s, d in...]
  transfers between devices with their start and end apart: 105 -> 4, of which waited for: 9 -> 4; matrix products, arithmetic and copies ran while one was open for 0% -> 0% of each run, Pallas kernels for 6% -> 15%
where the time goes in v3:
time: 100 us; the launch traced here: 99.4 us
  Pallas kernels  39.3 us (39%)
  blocking collectives  33.5 us (34%)
  starting transfers between devices  14.5 us (14%)
  waiting for transfers between devices  10.6 us (11%)
  between operations  1.55 us (2%)
    pallas_call x12, Pallas kernels, run(): pl.pallas_call(kernel, out_shape=[jax.ShapeDtypeStruct(s, d) for s, d in...  39.3 us
    all_to_all x3, blocking collectives, exchange(): return lax.all_to_all(x, 'bulk', split_axis=0, concat_axis=0, tiled=True)  33.5 us
    all_to_all x4, starting transfers between devices, exchange(): return lax.all_to_all(x, 'bulk', split_axis=0, concat_axis=0, tiled=True)  14.5 us
    all_to_all x4, waiting for transfers between devices, exchange(): return lax.all_to_all(x, 'bulk', split_axis=0, concat_axis=0, tiled=True)  10.6 us
  transfers between devices with their start and end apart: 4, of which 4 were waited for; matrix products, arithmetic and copies ran while one was open for 0% of the time, Pallas kernels for 15%

profile of v3, /device:TPU:0, one launch (start us, length us, event | category | flops | bytes accessed | tf_op | source)
XLA Modules:
  0.0 99.4 jit_solution(3035535202298619145)
XLA Ops:
  0.6 1.0 need.1
  1.6 13.8 %all_to_all.77 = f32[16,4,128]{2,1,0:T(4,128)S(1)} all-to-all(f32[16,4,128]{2,1,0:T(4,128)S(1)} %bitcast.26), channel_id=1, replica_groups=mesh['groups'=2,'bulk'=16] {'bulk'}, dimensions={0} | all-to-all | bytes 65536 | tf_op jit(solution)/shard_map/all_to_all | solution.py:393
  15.4 0.8 serve.1
  16.2 3.5 %all-to-all-start.1 = ((f32[16,4,128]{2,1,0:T(4,128)}), f32[16,4,128]{2,1,0:T(4,128)S(1)}, u32[]{:S(2)}, u32[]{:S(2)}) async-start(f32[16,4,128]{2,1,0:T(4,128)} %bitcast.5), calls=%async_computation.1 | async-start | bytes 65536 | tf_op jit(solution)/shard_map/all_to_all | solution.py:393
  20.4 3.8 %tables.1 = (bf16[256,64]{1,0:T(8,128)(2,1)S(1)}, bf16[256,64]{1,0:T(8,128)(2,1)S(1)}, bf16[256,128]{1,0:T(8,128)(2,1)S(1)}, bf16[256,32]{1,0:T(8,128)(2,1)S(1)}...) custom-call(s32[1]{0:T(128)S(6)} %copy.13.count_ref, ...), custom_call_target="tpu_custom_call" | custom-call | flops 134217728 | bytes 8388608 | tf_op jit(solution)/shard_map/tables/pallas_call | solution.py:342
  24.2 2.1 %all-to-all-done.1 = f32[16,4,128]{2,1,0:T(4,128)S(1)} async-done(((f32[16,4,128]{2,1,0:T(4,128)}), f32[16,4,128]{2,1,0:T(4,128)S(1)}, u32[]{:S(2)}, u32[]{:S(2)}) %all-to-all-start.1) | async-done | bytes 32800 | tf_op jit(solution)/shard_map/all_to_all | solution.py:393
  26.3 5.4 %first.2 = (f32[64,128]{1,0:T(8,128)}, f32[32,128]{1,0:T(8,128)S(1)}, f32[32,128]{1,0:T(8,128)S(1)}) custom-call(f32[64,128]{1,0:T(8,128)S(1)} %bitcast.19, f32[32,128]{1,0:T(8,128)S(1)} %get-tuple-element.49.f_ref.refs_1_, bf16[256,64]{1,0:T(8,128)(2,1)S(1)} %get-tuple-element.55.ge4_ref, bf16[256,64]{1,0:T(8,128)(2,1)S(1)} %get-tuple-element.56.gp4_ref, ...), custom_call_target="tpu_custom_call" | custom-call | flops 134217728 | bytes 8388608 | tf_op jit(solution)/shard_map/first/pallas_call | solution.py:342
  31.8 3.9 %all-to-all-start.2 = ((f32[16,4,128]{2,1,0:T(4,128)}), f32[16,4,128]{2,1,0:T(4,128)S(1)}, u32[]{:S(2)}, u32[]{:S(2)}) async-start(f32[16,4,128]{2,1,0:T(4,128)} %bitcast.7), calls=%async_computation.2 | async-start | bytes 65536 | tf_op jit(solution)/shard_map/all_to_all | solution.py:393
  35.6 3.7 %backward.3 = (f32[32,8,128]{2,1,0:T(8,128)S(1)}, f32[32,8,128]{2,1,0:T(8,128)S(1)}) custom-call(f32[32,128]{1,0:T(8,128)S(1)} %get-tuple-element.68.f_ref.refs_2_, bf16[256,32]{1,0:T(8,128)(2,1)S(1)} %get-tuple-element.69.gk_ref, bf16[256,128,128]{2,1,0:T(8,128)(2,1)} %refs_14_.3), custom_call_target="tpu_custom_call" | custom-call | flops 134217728 | bytes 8388608 | tf_op jit(solution)/shard_map/backward/pallas_call | solution.py:342
  39.4 2.9 %all-to-all-done.2 = f32[16,4,128]{2,1,0:T(4,128)S(1)} async-done(((f32[16,4,128]{2,1,0:T(4,128)}), f32[16,4,128]{2,1,0:T(4,128)S(1)}, u32[]{:S(2)}, u32[]{:S(2)}) %all-to-all-start.2) | async-done | bytes 32800 | tf_op jit(solution)/shard_map/all_to_all | solution.py:393
  42.3 0.5 phonon.2
  42.7 9.8 %all_to_all.78 = f32[16,8,128]{2,1,0:T(8,128)S(1)} all-to-all(f32[16,8,128]{2,1,0:T(8,128)S(1)} %bitcast.25), channel_id=1, replica_groups=mesh['groups'=2,'bulk'=16] {'bulk'}, dimensions={0} | all-to-all | bytes 131072 | tf_op jit(solution)/shard_map/all_to_all | solution.py:393
  52.6 5.5 %second.2 = (f32[32,128]{1,0:T(8,128)S(1)}, f32[16,128]{1,0:T(8,128)S(1)}, f32[64,128]{1,0:T(8,128)}) custom-call(f32[128,128]{1,0:T(8,128)S(1)} %bitcast.18, f32[256,128]{1,0:T(8,128)S(1)} %get-tuple-element.73.refs_0_, f32[32,128]{1,0:T(8,128)S(1)} %get-tuple-element.49.f_ref.refs_1_, f32[32,128]{1,0:T(8,128)S(1)} %get-tuple-element.68.f_ref.refs_2_, ...), custom_call_target="tpu_custom_call" | custom-call | flops 134217728 | bytes 8388608 | tf_op jit(solution)/shard_map/second/pallas_call | solution.py:342
  58.0 3.5 %all-to-all-start.4 = ((f32[16,4,128]{2,1,0:T(4,128)}), f32[16,4,128]{2,1,0:T(4,128)S(1)}, u32[]{:S(2)}, u32[]{:S(2)}) async-start(f32[16,4,128]{2,1,0:T(4,128)} %bitcast.11), calls=%async_computation.4 | async-start | bytes 65536 | tf_op jit(solution)/shard_map/all_to_all | solution.py:393
  61.6 3.7 %backward.4 = (f32[32,8,128]{2,1,0:T(8,128)S(1)}, f32[32,8,128]{2,1,0:T(8,128)S(1)}) custom-call(f32[32,128]{1,0:T(8,128)S(1)} %get-tuple-element.81.f_ref.refs_1_, bf16[256,32]{1,0:T(8,128)(2,1)S(1)} %get-tuple-element.69.gk_ref, bf16[256,128,128]{2,1,0:T(8,128)(2,1)} %refs_14_.3), custom_call_target="tpu_custom_call" | custom-call | flops 134217728 | bytes 8388608 | tf_op jit(solution)/shard_map/backward/pallas_call | solution.py:342
  65.3 2.9 %all-to-all-done.4 = f32[16,4,128]{2,1,0:T(4,128)S(1)} async-done(((f32[16,4,128]{2,1,0:T(4,128)}), f32[16,4,128]{2,1,0:T(4,128)S(1)}, u32[]{:S(2)}, u32[]{:S(2)}) %all-to-all-start.4) | async-done | bytes 32800 | tf_op jit(solution)/shard_map/all_to_all | solution.py:393
  68.2 5.4 %first.3 = (f32[64,128]{1,0:T(8,128)}, f32[32,128]{1,0:T(8,128)S(1)}, f32[32,128]{1,0:T(8,128)S(1)}) custom-call(f32[64,128]{1,0:T(8,128)S(1)} %bitcast.20, f32[32,128]{1,0:T(8,128)S(1)} %get-tuple-element.81.f_ref.refs_1_, bf16[256,64]{1,0:T(8,128)(2,1)S(1)} %get-tuple-element.55.ge4_ref, bf16[256,64]{1,0:T(8,128)(2,1)S(1)} %get-tuple-element.56.gp4_ref, ...), custom_call_target="tpu_custom_call" | custom-call | flops 134217728 | bytes 8388608 | tf_op jit(solution)/shard_map/first/pallas_call | solution.py:342
  73.6 3.7 %all-to-all-start.5 = ((f32[16,4,128]{2,1,0:T(4,128)}), f32[16,4,128]{2,1,0:T(4,128)S(1)}, u32[]{:S(2)}, u32[]{:S(2)}) async-start(f32[16,4,128]{2,1,0:T(4,128)} %bitcast.13), calls=%async_computation.5 | async-start | bytes 65536 | tf_op jit(solution)/shard_map/all_to_all | solution.py:393
  77.3 3.7 %backward.5 = (f32[32,8,128]{2,1,0:T(8,128)S(1)}, f32[32,8,128]{2,1,0:T(8,128)S(1)}) custom-call(f32[32,128]{1,0:T(8,128)S(1)} %get-tuple-element.86.f_ref.refs_2_, bf16[256,32]{1,0:T(8,128)(2,1)S(1)} %get-tuple-element.69.gk_ref, bf16[256,128,128]{2,1,0:T(8,128)(2,1)} %refs_14_.3), custom_call_target="tpu_custom_call" | custom-call | flops 134217728 | bytes 8388608 | tf_op jit(solution)/shard_map/backward/pallas_call | solution.py:342
  81.0 2.7 %all-to-all-done.5 = f32[16,4,128]{2,1,0:T(4,128)S(1)} async-done(((f32[16,4,128]{2,1,0:T(4,128)}), f32[16,4,128]{2,1,0:T(4,128)S(1)}, u32[]{:S(2)}, u32[]{:S(2)}) %all-to-all-start.5) | async-done | bytes 32800 | tf_op jit(solution)/shard_map/all_to_all | solution.py:393
  83.7 0.5 phonon.3
  84.1 9.8 %all_to_all.79 = f32[16,8,128]{2,1,0:T(8,128)S(1)} all-to-all(f32[16,8,128]{2,1,0:T(8,128)S(1)} %bitcast.24), channel_id=1, replica_groups=mesh['groups'=2,'bulk'=16] {'bulk'}, dimensions={0} | all-to-all | bytes 131072 | tf_op jit(solution)/shard_map/all_to_all | solution.py:393
  94.0 5.3 %second.3 = (f32[32,128]{1,0:T(8,128)}, f32[16,128]{1,0:T(8,128)}) custom-call(f32[128,128]{1,0:T(8,128)S(1)} %bitcast.17, f32[256,128]{1,0:T(8,128)S(1)} %get-tuple-element.90.refs_0_, f32[32,128]{1,0:T(8,128)S(1)} %get-tuple-element.81.f_ref.refs_1_, f32[32,128]{1,0:T(8,128)S(1)} %get-tuple-element.86.f_ref.refs_2_, ...), custom_call_target="tpu_custom_call" | custom-call | flops 134217728 | bytes 8388608 | tf_op jit(solution)/shard_map/second/pallas_call | solution.py:342
Async XLA Ops:
  16.2 10.1 %all-to-all-start.1 = ((f32[16,4,128]{2,1,0:T(4,128)}), f32[16,4,128]{2,1,0:T(4,128)S(1)}, u32[]{:S(2)}, u32[]{:S(2)}) async-start(f32[16,4,128]{2,1,0:T(4,128)} %bitcast.5), calls=%async_computation.1 | async-start | bytes 65536 | tf_op jit(solution)/shard_map/all_to_all | solution.py:393
  31.8 10.5 %all-to-all-start.2 = ((f32[16,4,128]{2,1,0:T(4,128)}), f32[16,4,128]{2,1,0:T(4,128)S(1)}, u32[]{:S(2)}, u32[]{:S(2)}) async-start(f32[16,4,128]{2,1,0:T(4,128)} %bitcast.7), calls=%async_computation.2 | async-start | bytes 65536 | tf_op jit(solution)/shard_map/all_to_all | solution.py:393
  58.0 10.1 %all-to-all-start.4 = ((f32[16,4,128]{2,1,0:T(4,128)}), f32[16,4,128]{2,1,0:T(4,128)S(1)}, u32[]{:S(2)}, u32[]{:S(2)}) async-start(f32[16,4,128]{2,1,0:T(4,128)} %bitcast.11), calls=%async_computation.4 | async-start | bytes 65536 | tf_op jit(solution)/shard_map/all_to_all | solution.py:393
  73.6 10.1 %all-to-all-start.5 = ((f32[16,4,128]{2,1,0:T(4,128)}), f32[16,4,128]{2,1,0:T(4,128)S(1)}, u32[]{:S(2)}, u32[]{:S(2)}) async-start(f32[16,4,128]{2,1,0:T(4,128)} %bitcast.13), calls=%async_computation.5 | async-start | bytes 65536 | tf_op jit(solution)/shard_map/all_to_all | solution.py:393

commit v4 on v3

--- a/solution.py
+++ b/solution.py
@@ -10,6 +10,7 @@
 STEPS = 2
 DT = 0.05
 CHUNKS = 8
+HELD_CHUNKS = 2
 f32 = jnp.float32
 bf16 = jnp.bfloat16
 VMEM_LIMIT = 24 * 1024 * 1024
@@ -56,13 +57,14 @@
     return ref[...].reshape(-1, 128)
 
 
-def chunk_copies(c_hbm, c_ref, sems):
-    size = c_ref.shape[0] // CHUNKS
+def chunk_copies(src, dst, sems):
+    count = sems.shape[0]
+    size = src.shape[0] // count
     return [
         pltpu.make_async_copy(
-            c_hbm.at[pl.ds(i * size, size)], c_ref.at[pl.ds(i * size, size)], sems.at[i]
+            src.at[pl.ds(i * size, size)], dst.at[pl.ds(i * size, size)], sems.at[i]
         )
-        for i in range(CHUNKS)
+        for i in range(count)
     ]
 
 
@@ -71,52 +73,47 @@
         copy.start()
 
 
-def over_groups(copies, groups, body):
-    size = groups // CHUNKS
-    for i, copy in enumerate(copies):
-        copy.wait()
-        lax.fori_loop(i * size, (i + 1) * size, lambda g, _: body(g), 0, unroll=4)
+def block_diagonal(w):
+    w = w.astype(f32)
+    return jnp.concatenate(
+        [jnp.where(row_is(r), w, 0.0).astype(bf16) for r in range(8)], axis=1
+    )
+
+
+def tile_products(w_ref, parts, out0, out1):
+    base = 0
+    for c_ref, copies in parts:
+        groups = c_ref.shape[0] // 8
+        chunks = len(copies) if copies else 1
+        size = groups // chunks
+        for i in range(chunks):
+            if copies:
+                copies[i].wait()
+            for g in range(i * size, (i + 1) * size, 2):
+                lhs = jnp.concatenate(
+                    [block_diagonal(w_ref[base + g]), block_diagonal(w_ref[base + g + 1])],
+                    axis=0,
+                )
+                rhs = jnp.concatenate(
+                    [c_ref[(g + k) * 8 : (g + k + 1) * 8].reshape(1024, 128) for k in (0, 1)],
+                    axis=1,
+                )
+                res = dot(lhs, rhs)
+                for k in (0, 1):
+                    own = res[16 * k : 16 * (k + 1), 128 * k : 128 * (k + 1)]
+                    out0[base + g + k] = own[:8]
+                    out1[base + g + k] = own[8:]
+        base += groups
 
 
 def backward_pass(own, copies, c_ref, w_ref, out0, out1):
-    groups = c_ref.shape[0] // 8
     w_ref[...] = stacked(1.0 - own, own)
-
-    def body(g):
-        w = w_ref[g].astype(f32)
-        lhs = jnp.concatenate(
-            [jnp.where(row_is(r), w, 0.0).astype(bf16) for r in range(8)], axis=1
-        )
-        rhs = c_ref[pl.ds(g * 8, 8)].reshape(1024, 128)
-        res = dot(lhs, rhs)
-        out0[g] = res[:8]
-        out1[g] = res[8:]
-        return 0
-
-    over_groups(copies, groups, body)
-
-
-def forward_pass(far, bose, copies, c_ref, w_ref, out0, out1):
-    groups = c_ref.shape[0] // 8
+    tile_products(w_ref, [(c_ref, copies)], out0, out1)
+
+
+def electron_rate(sum_k, far, bose, f, parts, w_ref, o0, o1):
     w_ref[...] = stacked(far * (1.0 + bose), far + bose)
-
-    def body(g):
-        rhs = c_ref[pl.ds(g * 8, 8)].reshape(1024, 128)
-        full = lax.dot_general(
-            w_ref[g], rhs, (((1,), (1,)), ((), ())), preferred_element_type=f32
-        )
-        res = full[:, :128]
-        for r in range(1, 8):
-            res = jnp.where(row_is(r), full[:, r * 128 : (r + 1) * 128], res)
-        out0[g] = res[:8]
-        out1[g] = res[8:]
-        return 0
-
-    over_groups(copies, groups, body)
-
-
-def electron_rate(sum_k, far, bose, f, copies, c_ref, w_ref, o0, o1):
-    forward_pass(far, bose, copies, c_ref, w_ref, o0, o1)
+    tile_products(w_ref, parts, o0, o1)
     return pick(sum_k, flat(o0)) - f * pick(sum_k, flat(o1))
 
 
@@ -200,8 +197,29 @@
     backward_pass(own, copies, c_ref, w_ref, b0_ref, b1_ref)
 
 
+def transpose_kernel(after_ref, c_hbm, held_ref, t_hbm, c_ref, t_ref, in_sems, out_sems):
+    copies_in = chunk_copies(c_hbm, c_ref, in_sems)
+    copies_out = chunk_copies(t_ref, t_hbm, out_sems)
+    start(copies_in)
+    held = held_ref.shape[0]
+    size = c_ref.shape[0] // len(copies_in)
+    size_out = t_ref.shape[0] // len(copies_out)
+    for i, copy in enumerate(copies_in):
+        copy.wait()
+        for t in range(i * size, (i + 1) * size):
+            turned = c_ref[t].T
+            if t < held:
+                held_ref[t] = turned
+            else:
+                t_ref[t - held] = turned
+                if (t - held + 1) % size_out == 0:
+                    copies_out[(t - held) // size_out].start()
+    for copy in copies_out:
+        copy.wait()
+
+
 def serve_kernel(
-    cap, recv, f_ref, n_ref, send, serve_ref, s8_ref, st4_ref, st8a_ref, st8b_ref
+    cap, recv, f_ref, n_ref, held_ref, send, serve_ref, s8_ref, st4_ref, st8a_ref, st8b_ref
 ):
     kb, qb = f_ref.shape[0], n_ref.shape[0]
     s4 = recv[...]
@@ -234,6 +252,7 @@
     serve_ref,
     b0_ref,
     b1_ref,
+    held_ref,
     c_hbm,
     send,
     e_ref,
@@ -250,7 +269,8 @@
     got = recv[...]
     far = pick(ge4_ref[...], got)
     bose = pick(gp4_ref[...], got)
-    rate = electron_rate(sk_ref[...], far, bose, f, copies, c_ref, w_ref, o0, o1)
+    parts = [(held_ref, None), (c_ref, copies)]
+    rate = electron_rate(sk_ref[...], far, bose, f, parts, w_ref, o0, o1)
     gain = far * flat(b0_ref)
     terms = gain + bose * (gain - (1.0 - far) * flat(b1_ref))
     f1 = f + DT * rate
@@ -300,8 +320,8 @@
 
 def second_kernel(with_send, recv, *refs):
     far_ref, f_ref, f1_ref, e_ref, n_ref, n1_ref, p_ref, energy_ref, decay_ref = refs[:9]
-    gp8_ref, sk_ref, st8a_ref, st8b_ref, serve_ref, c_hbm = refs[9:15]
-    refs = refs[15:]
+    gp8_ref, sk_ref, st8a_ref, st8b_ref, serve_ref, held_ref, c_hbm = refs[9:16]
+    refs = refs[16:]
     f2_ref, n2_ref, *refs = refs
     send, refs = (refs[0], refs[1:]) if with_send else (None, refs)
     w_ref, c_ref, sems, o0, o1 = refs
@@ -310,9 +330,8 @@
     got = recv[...]
     n, n1 = n_ref[...], n1_ref[...]
     bose = pick(gp8_ref[...], got)
-    rate = electron_rate(
-        sk_ref[...], far_ref[...], bose, f1_ref[...], copies, c_ref, w_ref, o0, o1
-    )
+    parts = [(held_ref, None), (c_ref, copies)]
+    rate = electron_rate(sk_ref[...], far_ref[...], bose, f1_ref[...], parts, w_ref, o0, o1)
     thermal = 1.0 / (jnp.exp(energy_ref[...]) - 1.0)
     p1 = (
         pick(st8a_ref[...], got)
@@ -327,7 +346,7 @@
         send[...] = pick(serve_ref[...], padded(f2, n2))
 
 
-def call(kernel, name, outs, scratch=(), spaces=None, flops=0, seen=0):
+def call(kernel, name, outs, scratch=(), spaces=None, out_spaces=None, flops=0, seen=0):
     def run(*args):
         places = dict(spaces or {})
         args = [
@@ -341,9 +360,15 @@
         ]
         return pl.pallas_call(
             kernel,
-            out_shape=[jax.ShapeDtypeStruct(s, d) for s, d in outs],
+            out_shape=[
+                pltpu.HBM(*o) if (out_spaces or {}).get(i) else jax.ShapeDtypeStruct(*o)
+                for i, o in enumerate(outs)
+            ],
             in_specs=specs,
-            out_specs=[pl.BlockSpec(memory_space=pltpu.VMEM)] * len(outs),
+            out_specs=[
+                pl.BlockSpec(memory_space=(out_spaces or {}).get(i, pltpu.VMEM))
+                for i in range(len(outs))
+            ],
             scratch_shapes=list(scratch),
             compiler_params=pltpu.CompilerParams(vmem_limit_bytes=VMEM_LIMIT),
             cost_estimate=pl.CostEstimate(
@@ -377,11 +402,12 @@
     rows4 = devices * 2 * cap
     rows8 = devices * 4 * cap
     groups = tiles // 8
-    streams = [
-        pltpu.VMEM((groups, 16, 128), bf16),
-        pltpu.VMEM(coupling.shape, bf16),
-        pltpu.SemaphoreType.DMA((CHUNKS,)),
-    ]
+    held = HELD_CHUNKS * (tiles // CHUNKS)
+    weights = pltpu.VMEM((groups, 16, 128), bf16)
+    streams = [weights, pltpu.VMEM(coupling.shape, bf16), pltpu.SemaphoreType.DMA((CHUNKS,))]
+    rest = (tiles - held, 128, 128)
+    rest_sems = pltpu.SemaphoreType.DMA((CHUNKS - HELD_CHUNKS,))
+    forward_streams = [weights, pltpu.VMEM(rest, bf16), rest_sems]
     sums = [pltpu.VMEM((groups, 8, 128), f32)] * 2
     pass_out = [((groups, 8, 128), f32)] * 2
     block4 = ((rows4, 128), f32)
@@ -413,6 +439,15 @@
         phonon_need,
     )
     served = exchange(need)
+    c_held, c_rest = call(
+        transpose_kernel,
+        "transpose",
+        [((held, 128, 128), bf16), (rest, bf16)],
+        [pltpu.VMEM(coupling.shape, bf16), pltpu.VMEM(rest, bf16), streams[2], rest_sems],
+        spaces={1: pltpu.HBM},
+        out_spaces={1: pltpu.HBM},
+        **work,
+    )(f, coupling)
     ge4, gp4, gp8, gk, sk, sp4, sp8, b0, b1 = call(
         functools.partial(tables_kernel, cap),
         "tables",
@@ -441,7 +476,7 @@
             ((qb, rows8), bf16),
             ((qb, rows8), bf16),
         ],
-    )(served, f, n)
+    )(served, f, n, c_held)
 
     back = call(backward_kernel, "backward", pass_out, streams, spaces={2: pltpu.HBM}, **work)
     for step in range(STEPS):
@@ -452,10 +487,10 @@
             first_kernel,
             "first",
             [block4] + [((kb, 128), f32)] * 2,
-            streams + sums,
-            spaces={9: pltpu.HBM},
+            forward_streams + sums,
+            spaces={10: pltpu.HBM},
             **work,
-        )(recv, f, ge4, gp4, sk, sp4, serve, b0, b1, coupling)
+        )(recv, f, ge4, gp4, sk, sp4, serve, b0, b1, c_held, c_rest)
         recv = exchange(send)
         b0, b1 = back(f1, gk, coupling)
         send, p0, n1, far = call(
@@ -469,12 +504,12 @@
             functools.partial(second_kernel, not last),
             "second",
             [((kb, 128), f32), ((qb, 128), f32)] + ([] if last else [block4]),
-            streams + sums,
-            spaces={15: pltpu.HBM},
+            forward_streams + sums,
+            spaces={16: pltpu.HBM},
             **work,
         )(
             recv, far, f, f1, e0, n, n1, p0, energy, decay,
-            gp8, sk, st8a, st8b, serve, coupling,
+            gp8, sk, st8a, st8b, serve, c_held, c_rest,
         )
         send = send[0] if send else None
     return (f, n)

time: 100 us -> 99.2 us (level)
  blocking collectives: 33.5 us -> 19.8 us
  starting transfers between devices: 14.5 us -> 23.5 us
  Pallas kernels: 39.3 us -> 42.5 us
    all_to_all x3 -> x2, blocking collectives: 33.5 us -> 19.8 us  [exchange(): return lax.all_to_all(x, 'bulk', split_axis=0, concat_axis=0, tiled=True)]
    all_to_all x4 -> x5, starting transfers between devices: 14.5 us -> 23.5 us  [exchange(): return lax.all_to_all(x, 'bulk', split_axis=0, concat_axis=0, tiled=True)]
    pallas_call x12 -> x13, Pallas kernels: 39.3 us -> 42.5 us  [run(): pl.pallas_call(kernel, out_shape=[pltpu.HBM(*o) if (out_spaces or {}).get...]
    all_to_all x4 -> x5, waiting for transfers between devices: 10.6 us -> 11.4 us  [exchange(): return lax.all_to_all(x, 'bulk', split_axis=0, concat_axis=0, tiled=True)]
  transfers between devices with their start and end apart: 4 -> 5, of which waited for: 4 -> 5; matrix products, arithmetic and copies ran while one was open for 0% -> 0% of each run, Pallas kernels for 15% -> 21%
where the time goes in v4:
time: 99.2 us; the launch traced here: 98.7 us
  Pallas kernels  42.5 us (43%)
  starting transfers between devices  23.5 us (24%)
  blocking collectives  19.8 us (20%)
  waiting for transfers between devices  11.4 us (11%)
  between operations  1.57 us (2%)
    pallas_call x13, Pallas kernels, run(): pl.pallas_call(kernel, out_shape=[pltpu.HBM(*o) if (out_spaces or {}).get...  42.5 us
    all_to_all x5, starting transfers between devices, exchange(): return lax.all_to_all(x, 'bulk', split_axis=0, concat_axis=0, tiled=True)  23.5 us
    all_to_all x2, blocking collectives, exchange(): return lax.all_to_all(x, 'bulk', split_axis=0, concat_axis=0, tiled=True)  19.8 us
    all_to_all x5, waiting for transfers between devices, exchange(): return lax.all_to_all(x, 'bulk', split_axis=0, concat_axis=0, tiled=True)  11.4 us
  transfers between devices with their start and end apart: 5, of which 5 were waited for; matrix products, arithmetic and copies ran while one was open for 0% of the time, Pallas kernels for 21%

profile of v4, /device:TPU:0, one launch (start us, length us, event | category | flops | bytes accessed | tf_op | source)
XLA Modules:
  0.0 98.7 jit_solution(1511863070444388669)
XLA Ops:
  0.6 1.6 %need.1 = (f32[32,128]{1,0:T(8,128)S(1)}, f32[16,128]{1,0:T(8,128)S(1)}, f32[16,128]{1,0:T(8,128)S(1)}, f32[16,128]{1,0:T(8,128)S(1)}, s32[1,256]{1,0:T(1,128)S(...) custom-call(f32[32,128]{1,0:T(8,128)} %refs_0_.1, f32[16,128]{1,0:T(8,128)} %refs_1_.1, ...), custom_call_target="tpu_custom_call" | custom-call | tf_op jit(solution)/shard_map/need/pallas_call | solution.py:361
  2.2 7.4 %all-to-all-start = ((f32[16,4,128]{2,1,0:T(4,128)}), f32[16,4,128]{2,1,0:T(4,128)S(1)}, u32[]{:S(2)}, u32[]{:S(2)}) async-start(f32[16,4,128]{2,1,0:T(4,128)} %bitcast.3), calls=%async_computation | async-start | bytes 65536 | tf_op jit(solution)/shard_map/all_to_all | solution.py:419
  9.6 5.5 %transpose.1 = (bf16[64,128,128]{2,1,0:T(8,128)(2,1)S(1)}, bf16[192,128,128]{2,1,0:T(8,128)(2,1)}) custom-call(f32[32,128]{1,0:T(8,128)S(1)} %get-tuple-element.51.after_ref.f_ref.refs_1_, bf16[256,128,128]{2,1,0:T(8,128)(2,1)} %c_hbm.9), custom_call_target="tpu_custom_call" | custom-call | flops 134217728 | bytes 8388608 | tf_op jit(solution)/shard_map/transpose/pallas_call | solution.py:361
  15.1 1.1 %all-to-all-done = f32[16,4,128]{2,1,0:T(4,128)S(1)} async-done(((f32[16,4,128]{2,1,0:T(4,128)}), f32[16,4,128]{2,1,0:T(4,128)S(1)}, u32[]{:S(2)}, u32[]{:S(2)}) %all-to-all-start) | async-done | bytes 32800 | tf_op jit(solution)/shard_map/all_to_all | solution.py:419
  16.2 0.8 serve.1
  17.1 4.9 %all-to-all-start.1 = ((f32[16,4,128]{2,1,0:T(4,128)}), f32[16,4,128]{2,1,0:T(4,128)S(1)}, u32[]{:S(2)}, u32[]{:S(2)}) async-start(f32[16,4,128]{2,1,0:T(4,128)} %bitcast.5), calls=%async_computation.1 | async-start | bytes 65536 | tf_op jit(solution)/shard_map/all_to_all | solution.py:419
  22.6 3.9 %tables.1 = (bf16[256,64]{1,0:T(8,128)(2,1)S(1)}, bf16[256,64]{1,0:T(8,128)(2,1)S(1)}, bf16[256,128]{1,0:T(8,128)(2,1)S(1)}, bf16[256,32]{1,0:T(8,128)(2,1)S(1)}...) custom-call(s32[1]{0:T(128)S(6)} %copy.13.count_ref, ...), custom_call_target="tpu_custom_call" | custom-call | flops 134217728 | bytes 8388608 | tf_op jit(solution)/shard_map/tables/pallas_call | solution.py:361
  26.5 2.0 %all-to-all-done.1 = f32[16,4,128]{2,1,0:T(4,128)S(1)} async-done(((f32[16,4,128]{2,1,0:T(4,128)}), f32[16,4,128]{2,1,0:T(4,128)S(1)}, u32[]{:S(2)}, u32[]{:S(2)}) %all-to-all-start.1) | async-done | bytes 32800 | tf_op jit(solution)/shard_map/all_to_all | solution.py:419
  28.6 4.6 %first.2 = (f32[64,128]{1,0:T(8,128)}, f32[32,128]{1,0:T(8,128)S(1)}, f32[32,128]{1,0:T(8,128)S(1)}) custom-call(f32[64,128]{1,0:T(8,128)S(1)} %bitcast.19, f32[32,128]{1,0:T(8,128)S(1)} %get-tuple-element.51.after_ref.f_ref.refs_1_, bf16[256,64]{1,0:T(8,128)(2,1)S(1)} %get-tuple-element.58.ge4_ref, bf16[256,64]{1,0:T(8,128)(2,1)S(1)} %get-tuple-element.59.gp4_ref, ...), custom_call_target="tpu_custom_call" | custom-call | flops 134217728 | bytes 8388608 | tf_op jit(solution)/shard_map/first/pallas_call | solution.py:361
  33.2 4.0 %all-to-all-start.2 = ((f32[16,4,128]{2,1,0:T(4,128)}), f32[16,4,128]{2,1,0:T(4,128)S(1)}, u32[]{:S(2)}, u32[]{:S(2)}) async-start(f32[16,4,128]{2,1,0:T(4,128)} %bitcast.7), calls=%async_computation.2 | async-start | bytes 65536 | tf_op jit(solution)/shard_map/all_to_all | solution.py:419
  37.2 3.8 %backward.3 = (f32[32,8,128]{2,1,0:T(8,128)S(1)}, f32[32,8,128]{2,1,0:T(8,128)S(1)}) custom-call(f32[32,128]{1,0:T(8,128)S(1)} %get-tuple-element.72.f_ref.refs_2_, bf16[256,32]{1,0:T(8,128)(2,1)S(1)} %get-tuple-element.73.gk_ref, bf16[256,128,128]{2,1,0:T(8,128)(2,1)} %c_hbm.9), custom_call_target="tpu_custom_call" | custom-call | flops 134217728 | bytes 8388608 | tf_op jit(solution)/shard_map/backward/pallas_call | solution.py:361
  41.0 2.8 %all-to-all-done.2 = f32[16,4,128]{2,1,0:T(4,128)S(1)} async-done(((f32[16,4,128]{2,1,0:T(4,128)}), f32[16,4,128]{2,1,0:T(4,128)S(1)}, u32[]{:S(2)}, u32[]{:S(2)}) %all-to-all-start.2) | async-done | bytes 32800 | tf_op jit(solution)/shard_map/all_to_all | solution.py:419
  43.8 0.5 phonon.2
  44.3 9.9 %all_to_all.77 = f32[16,8,128]{2,1,0:T(8,128)S(1)} all-to-all(f32[16,8,128]{2,1,0:T(8,128)S(1)} %bitcast.25), channel_id=1, replica_groups=mesh['groups'=2,'bulk'=16] {'bulk'}, dimensions={0} | all-to-all | bytes 131072 | tf_op jit(solution)/shard_map/all_to_all | solution.py:419
  54.2 4.7 %second.2 = (f32[32,128]{1,0:T(8,128)S(1)}, f32[16,128]{1,0:T(8,128)S(1)}, f32[64,128]{1,0:T(8,128)}) custom-call(f32[128,128]{1,0:T(8,128)S(1)} %bitcast.18, f32[256,128]{1,0:T(8,128)S(1)} %get-tuple-element.77.refs_0_, f32[32,128]{1,0:T(8,128)S(1)} %get-tuple-element.51.after_ref.f_ref.refs_1_, f32[32,128]{1,0:T(8,128)S(1)} %get-tuple-element.72.f_ref.refs_2_, ...), custom_call_target="tpu_custom_call" | custom-call | flops 134217728 | bytes 8388608 | tf_op jit(solution)/shard_map/second/pallas_call | solution.py:361
  58.9 3.7 %all-to-all-start.4 = ((f32[16,4,128]{2,1,0:T(4,128)}), f32[16,4,128]{2,1,0:T(4,128)S(1)}, u32[]{:S(2)}, u32[]{:S(2)}) async-start(f32[16,4,128]{2,1,0:T(4,128)} %bitcast.11), calls=%async_computation.4 | async-start | bytes 65536 | tf_op jit(solution)/shard_map/all_to_all | solution.py:419
  62.5 3.8 %backward.4 = (f32[32,8,128]{2,1,0:T(8,128)S(1)}, f32[32,8,128]{2,1,0:T(8,128)S(1)}) custom-call(f32[32,128]{1,0:T(8,128)S(1)} %get-tuple-element.85.f_ref.refs_1_, bf16[256,32]{1,0:T(8,128)(2,1)S(1)} %get-tuple-element.73.gk_ref, bf16[256,128,128]{2,1,0:T(8,128)(2,1)} %c_hbm.9), custom_call_target="tpu_custom_call" | custom-call | flops 134217728 | bytes 8388608 | tf_op jit(solution)/shard_map/backward/pallas_call | solution.py:361
  66.4 2.6 %all-to-all-done.4 = f32[16,4,128]{2,1,0:T(4,128)S(1)} async-done(((f32[16,4,128]{2,1,0:T(4,128)}), f32[16,4,128]{2,1,0:T(4,128)S(1)}, u32[]{:S(2)}, u32[]{:S(2)}) %all-to-all-start.4) | async-done | bytes 32800 | tf_op jit(solution)/shard_map/all_to_all | solution.py:419
  69.0 4.6 %first.3 = (f32[64,128]{1,0:T(8,128)}, f32[32,128]{1,0:T(8,128)S(1)}, f32[32,128]{1,0:T(8,128)S(1)}) custom-call(f32[64,128]{1,0:T(8,128)S(1)} %bitcast.21, f32[32,128]{1,0:T(8,128)S(1)} %get-tuple-element.85.f_ref.refs_1_, bf16[256,64]{1,0:T(8,128)(2,1)S(1)} %get-tuple-element.58.ge4_ref, bf16[256,64]{1,0:T(8,128)(2,1)S(1)} %get-tuple-element.59.gp4_ref, ...), custom_call_target="tpu_custom_call" | custom-call | flops 134217728 | bytes 8388608 | tf_op jit(solution)/shard_map/first/pallas_call | solution.py:361
  73.6 3.5 %all-to-all-start.5 = ((f32[16,4,128]{2,1,0:T(4,128)}), f32[16,4,128]{2,1,0:T(4,128)S(1)}, u32[]{:S(2)}, u32[]{:S(2)}) async-start(f32[16,4,128]{2,1,0:T(4,128)} %bitcast.13), calls=%async_computation.5 | async-start | bytes 65536 | tf_op jit(solution)/shard_map/all_to_all | solution.py:419
  77.1 3.8 %backward.5 = (f32[32,8,128]{2,1,0:T(8,128)S(1)}, f32[32,8,128]{2,1,0:T(8,128)S(1)}) custom-call(f32[32,128]{1,0:T(8,128)S(1)} %get-tuple-element.90.f_ref.refs_2_, bf16[256,32]{1,0:T(8,128)(2,1)S(1)} %get-tuple-element.73.gk_ref, bf16[256,128,128]{2,1,0:T(8,128)(2,1)} %c_hbm.9), custom_call_target="tpu_custom_call" | custom-call | flops 134217728 | bytes 8388608 | tf_op jit(solution)/shard_map/backward/pallas_call | solution.py:361
  80.9 2.8 %all-to-all-done.5 = f32[16,4,128]{2,1,0:T(4,128)S(1)} async-done(((f32[16,4,128]{2,1,0:T(4,128)}), f32[16,4,128]{2,1,0:T(4,128)S(1)}, u32[]{:S(2)}, u32[]{:S(2)}) %all-to-all-start.5) | async-done | bytes 32800 | tf_op jit(solution)/shard_map/all_to_all | solution.py:419
  83.7 0.5 phonon.3
  84.2 9.9 %all_to_all.78 = f32[16,8,128]{2,1,0:T(8,128)S(1)} all-to-all(f32[16,8,128]{2,1,0:T(8,128)S(1)} %bitcast.24), channel_id=1, replica_groups=mesh['groups'=2,'bulk'=16] {'bulk'}, dimensions={0} | all-to-all | bytes 131072 | tf_op jit(solution)/shard_map/all_to_all | solution.py:419
  94.1 4.5 %second.3 = (f32[32,128]{1,0:T(8,128)}, f32[16,128]{1,0:T(8,128)}) custom-call(f32[128,128]{1,0:T(8,128)S(1)} %bitcast.17, f32[256,128]{1,0:T(8,128)S(1)} %get-tuple-element.94.refs_0_, f32[32,128]{1,0:T(8,128)S(1)} %get-tuple-element.85.f_ref.refs_1_, f32[32,128]{1,0:T(8,128)S(1)} %get-tuple-element.90.f_ref.refs_2_, ...), custom_call_target="tpu_custom_call" | custom-call | flops 134217728 | bytes 8388608 | tf_op jit(solution)/shard_map/second/pallas_call | solution.py:361
Async XLA Ops:
  2.2 14.0 %all-to-all-start = ((f32[16,4,128]{2,1,0:T(4,128)}), f32[16,4,128]{2,1,0:T(4,128)S(1)}, u32[]{:S(2)}, u32[]{:S(2)}) async-start(f32[16,4,128]{2,1,0:T(4,128)} %bitcast.3), calls=%async_computation | async-start | bytes 65536 | tf_op jit(solution)/shard_map/all_to_all | solution.py:419
  17.1 11.5 %all-to-all-start.1 = ((f32[16,4,128]{2,1,0:T(4,128)}), f32[16,4,128]{2,1,0:T(4,128)S(1)}, u32[]{:S(2)}, u32[]{:S(2)}) async-start(f32[16,4,128]{2,1,0:T(4,128)} %bitcast.5), calls=%async_computation.1 | async-start | bytes 65536 | tf_op jit(solution)/shard_map/all_to_all | solution.py:419
  33.2 10.6 %all-to-all-start.2 = ((f32[16,4,128]{2,1,0:T(4,128)}), f32[16,4,128]{2,1,0:T(4,128)S(1)}, u32[]{:S(2)}, u32[]{:S(2)}) async-start(f32[16,4,128]{2,1,0:T(4,128)} %bitcast.7), calls=%async_computation.2 | async-start | bytes 65536 | tf_op jit(solution)/shard_map/all_to_all | solution.py:419
  58.9 10.1 %all-to-all-start.4 = ((f32[16,4,128]{2,1,0:T(4,128)}), f32[16,4,128]{2,1,0:T(4,128)S(1)}, u32[]{:S(2)}, u32[]{:S(2)}) async-start(f32[16,4,128]{2,1,0:T(4,128)} %bitcast.11), calls=%async_computation.4 | async-start | bytes 65536 | tf_op jit(solution)/shard_map/all_to_all | solution.py:419
  73.6 10.1 %all-to-all-start.5 = ((f32[16,4,128]{2,1,0:T(4,128)}), f32[16,4,128]{2,1,0:T(4,128)S(1)}, u32[]{:S(2)}, u32[]{:S(2)}) async-start(f32[16,4,128]{2,1,0:T(4,128)} %bitcast.13), calls=%async_computation.5 | async-start | bytes 65536 | tf_op jit(solution)/shard_map/all_to_all | solution.py:419

commit v5 on v4

--- a/solution.py
+++ b/solution.py
@@ -10,7 +10,7 @@
 STEPS = 2
 DT = 0.05
 CHUNKS = 8
-HELD_CHUNKS = 2
+HELD_CHUNKS = 3
 f32 = jnp.float32
 bf16 = jnp.bfloat16
 VMEM_LIMIT = 24 * 1024 * 1024
@@ -80,13 +80,12 @@
     )
 
 
-def tile_products(w_ref, parts, out0, out1):
+def tile_products(w_ref, parts, out0, out1, after=None):
+    size = w_ref.shape[0] // CHUNKS
     base = 0
     for c_ref, copies in parts:
         groups = c_ref.shape[0] // 8
-        chunks = len(copies) if copies else 1
-        size = groups // chunks
-        for i in range(chunks):
+        for i in range(groups // size):
             if copies:
                 copies[i].wait()
             for g in range(i * size, (i + 1) * size, 2):
@@ -103,6 +102,8 @@
                     own = res[16 * k : 16 * (k + 1), 128 * k : 128 * (k + 1)]
                     out0[base + g + k] = own[:8]
                     out1[base + g + k] = own[8:]
+            if after:
+                after(base // size + i)
         base += groups
 
 
@@ -111,23 +112,33 @@
     tile_products(w_ref, [(c_ref, copies)], out0, out1)
 
 
-def electron_rate(sum_k, far, bose, f, parts, w_ref, o0, o1):
+def electron_rate(sum_k_ref, far, bose, f, parts, w_ref, o0, o1):
     w_ref[...] = stacked(far * (1.0 + bose), far + bose)
-    tile_products(w_ref, parts, o0, o1)
-    return pick(sum_k, flat(o0)) - f * pick(sum_k, flat(o1))
-
-
-def need_kernel(kb, cap, *refs):
+    totals = [jnp.zeros_like(f), jnp.zeros_like(f)]
+    size = w_ref.shape[0] // CHUNKS
+
+    def after(chunk):
+        for k, out in enumerate((o0, o1)):
+            rows = out[chunk * size : (chunk + 1) * size].reshape(-1, 128)
+            totals[k] = totals[k] + pick(sum_k_ref[chunk], rows)
+
+    tile_products(w_ref, parts, o0, o1, after)
+    return totals[0] - f * totals[1]
+
+
+def need_kernel(cap, *refs):
     ins, outs = refs[:9], refs[9:]
-    small, out_ref = outs[:7], outs[7]
+    small, send_ref, list_ref = outs[:7], outs[7], outs[8]
     pneed_ref, qneed_ref, sems = outs[-3:]
     copies = [
         pltpu.make_async_copy(src, dst, sems.at[i])
         for i, (src, dst) in enumerate(zip(ins, [*small, pneed_ref, qneed_ref]))
     ]
     start(copies)
-    rows = out_ref.shape[0]
+    rows, sent = list_ref.shape
     slots = pneed_ref.shape[1]
+    peers = slots // cap
+    step = sent // peers
     x = iota((rows, slots), 0)
     y = iota((rows, slots), 1)
     peer, r = x // (2 * cap), x % (2 * cap)
@@ -135,10 +146,20 @@
     p_here = (r >= cap) & (y == peer * cap + r - cap)
     for copy in copies:
         copy.wait()
+    f, n = small[0][...], small[1][...]
+    kb, qb = f.shape[0], n.shape[0]
     pn = jnp.broadcast_to(pneed_ref[...].astype(f32), (rows, slots))
     qn = jnp.broadcast_to(qneed_ref[...].astype(f32), (rows, slots)) + float(kb)
     col = jnp.sum(jnp.where(e_here, pn, 0.0) + jnp.where(p_here, qn, 0.0), axis=1, keepdims=True)
-    out_ref[...] = (iota((rows, 128), 1).astype(f32) == col).astype(f32)
+    hot = (iota((rows, 128), 1).astype(f32) == col).astype(f32)
+    start_of = (iota((rows, 1), 0) // (2 * cap) * step).astype(f32)
+    list_ref[...] = jnp.where(iota((rows, sent), 1).astype(f32) == col + start_of, 1.0, 0.0).astype(
+        bf16
+    )
+    blank = jnp.zeros((step - kb - qb - 2 * cap, 128), f32)
+    for p in range(peers):
+        lists = jnp.concatenate([hot[p * 2 * cap : (p + 1) * 2 * cap], blank], axis=0)
+        send_ref[p * step : (p + 1) * step] = jnp.concatenate([f, n, lists], axis=0)
 
 
 def tables_kernel(
@@ -174,7 +195,10 @@
     rows8 = sp8_ref.shape[0]
     ind = lambda m: jnp.where(m, 1.0, 0.0)
     k_hot = ind(iota((kb, tiles), 0) == k)
-    sk_ref[...] = jnp.where(used, k_hot, 0.0).astype(bf16)
+    sums = jnp.where(used, k_hot, 0.0)
+    width = tiles // CHUNKS
+    for i in range(CHUNKS):
+        sk_ref[i] = sums[:, i * width : (i + 1) * width].astype(bf16)
     gk_ref[...] = k_hot.T.astype(bf16)
     x = iota((rows4, tiles), 0)
     row_e = (e // cap) * (2 * cap) + e % cap
@@ -218,15 +242,9 @@
         copy.wait()
 
 
-def serve_kernel(
-    cap, recv, f_ref, n_ref, held_ref, send, serve_ref, s8_ref, st4_ref, st8a_ref, st8b_ref
-):
-    kb, qb = f_ref.shape[0], n_ref.shape[0]
-    s4 = recv[...]
-    rows4, rows8 = s4.shape[0], s8_ref.shape[0]
-    hot = s4.astype(bf16)
-    serve_ref[...] = hot
-    send[...] = pick(hot, padded(f_ref[...], n_ref[...]))
+def serve_kernel(cap, kb, qb, hot_ref, s8_ref, st4_ref, st8a_ref, st8b_ref):
+    hot = hot_ref[...]
+    rows4, rows8 = hot.shape[0], s8_ref.shape[0]
     x = iota((rows8, rows4), 0)
     y = iota((rows8, rows4), 1)
     peer, r = x // (4 * cap), x % (4 * cap)
@@ -237,19 +255,21 @@
         return dot(jnp.where(here, 1.0, 0.0).astype(bf16), hot)
 
     s8_ref[...] = rows_of(0).astype(bf16)
-    st4_ref[...] = s4.T[kb : kb + qb].astype(bf16)
+    st4_ref[...] = hot.astype(f32).T[kb : kb + qb].astype(bf16)
     st8a_ref[...] = rows_of(1).T[kb : kb + qb].astype(bf16)
     st8b_ref[...] = rows_of(2).T[kb : kb + qb].astype(bf16)
 
 
 def first_kernel(
+    cap,
+    state_rows,
     recv,
+    list_ref,
     f_ref,
     ge4_ref,
     gp4_ref,
     sk_ref,
     sp4_ref,
-    serve_ref,
     b0_ref,
     b1_ref,
     held_ref,
@@ -257,26 +277,35 @@
     send,
     e_ref,
     f1_ref,
-    w_ref,
-    c_ref,
-    sems,
-    o0,
-    o1,
+    *refs,
 ):
+    starts = len(refs) == 6
+    w_ref, c_ref, sems, o0, o1 = refs[-5:]
     copies = chunk_copies(c_hbm, c_ref, sems)
     start(copies)
     f = f_ref[...]
     got = recv[...]
+    serve = list_ref[...]
+    if starts:
+        rows, sent = serve.shape
+        got, every = pick(serve, got), got
+        x = iota((rows, sent), 0)
+        step = sent // (rows // (2 * cap))
+        lists_at = x // (2 * cap) * step + state_rows + x % (2 * cap)
+        at = jnp.where(iota((rows, sent), 1) == lists_at, 1.0, 0.0).astype(bf16)
+        serve = dot(at, every.astype(bf16)).astype(bf16)
+        refs[0][...] = serve
     far = pick(ge4_ref[...], got)
     bose = pick(gp4_ref[...], got)
-    parts = [(held_ref, None), (c_ref, copies)]
-    rate = electron_rate(sk_ref[...], far, bose, f, parts, w_ref, o0, o1)
     gain = far * flat(b0_ref)
     terms = gain + bose * (gain - (1.0 - far) * flat(b1_ref))
+    phonon_rows = pick(sp4_ref[...], terms)
+    parts = [(held_ref, None), (c_ref, copies)]
+    rate = electron_rate(sk_ref, far, bose, f, parts, w_ref, o0, o1)
     f1 = f + DT * rate
     e_ref[...] = rate
     f1_ref[...] = f1
-    send[...] = pick(serve_ref[...], padded(f1)) + pick(sp4_ref[...], terms)
+    send[...] = pick(serve, padded(f1)) + phonon_rows
 
 
 def backward_kernel(f_ref, gk_ref, c_hbm, b0_ref, b1_ref, w_ref, c_ref, sems):
@@ -330,8 +359,6 @@
     got = recv[...]
     n, n1 = n_ref[...], n1_ref[...]
     bose = pick(gp8_ref[...], got)
-    parts = [(held_ref, None), (c_ref, copies)]
-    rate = electron_rate(sk_ref[...], far_ref[...], bose, f1_ref[...], parts, w_ref, o0, o1)
     thermal = 1.0 / (jnp.exp(energy_ref[...]) - 1.0)
     p1 = (
         pick(st8a_ref[...], got)
@@ -340,6 +367,8 @@
     )
     n2 = n + (DT / 2.0) * (p_ref[...] + p1)
     n2_ref[...] = n2
+    parts = [(held_ref, None), (c_ref, copies)]
+    rate = electron_rate(sk_ref, far_ref[...], bose, f1_ref[...], parts, w_ref, o0, o1)
     f2 = f_ref[...] + (DT / 2.0) * (e_ref[...] + rate)
     f2_ref[...] = f2
     if with_send:
@@ -421,10 +450,11 @@
     ints = ((1, tiles), jnp.int32)
     lists = ((1, partner_need.shape[1]), jnp.int32)
     small = [((kb, 128), f32)] + [((qb, 128), f32)] * 3 + [ints] * 3
-    f, n, energy, decay, kblock, partner, qslot, need = call(
-        functools.partial(need_kernel, kb, cap),
+    step_rows = -(-(kb + qb + 2 * cap) // 8) * 8
+    f, n, energy, decay, kblock, partner, qslot, send, lists_in = call(
+        functools.partial(need_kernel, cap),
         "need",
-        small + [block4],
+        small + [((devices * step_rows, 128), f32), ((rows4, devices * step_rows), bf16)],
         [pltpu.VMEM(*lists), pltpu.VMEM(*lists), pltpu.SemaphoreType.DMA((9,))],
         spaces={i: pltpu.HBM for i in range(9)},
     )(
@@ -438,7 +468,7 @@
         partner_need,
         phonon_need,
     )
-    served = exchange(need)
+    recv = exchange(send)
     c_held, c_rest = call(
         transpose_kernel,
         "transpose",
@@ -456,7 +486,7 @@
             ((tiles, rows4), bf16),
             ((tiles, rows8), bf16),
             ((tiles, kb), bf16),
-            ((kb, tiles), bf16),
+            ((CHUNKS, kb, tiles // CHUNKS), bf16),
             ((rows4, tiles), bf16),
             ((rows8, 2 * tiles), bf16),
         ]
@@ -465,32 +495,31 @@
         spaces={0: pltpu.SMEM, 5: pltpu.HBM},
         **work,
     )(tile_count, kblock, partner, qslot, f, coupling)
-    send, serve, s8, st4, st8a, st8b = call(
-        functools.partial(serve_kernel, cap),
-        "serve",
-        [
-            block4,
-            ((rows4, 128), bf16),
-            ((rows8, 128), bf16),
-            ((qb, rows4), bf16),
-            ((qb, rows8), bf16),
-            ((qb, rows8), bf16),
-        ],
-    )(served, f, n, c_held)
-
     back = call(backward_kernel, "backward", pass_out, streams, spaces={2: pltpu.HBM}, **work)
     for step in range(STEPS):
-        recv = exchange(send)
         if step:
+            recv = exchange(send)
             b0, b1 = back(f, gk, coupling)
-        send, e0, f1 = call(
-            first_kernel,
+        send, e0, f1, *hot = call(
+            functools.partial(first_kernel, cap, kb + qb),
             "first",
-            [block4] + [((kb, 128), f32)] * 2,
+            [block4] + [((kb, 128), f32)] * 2 + ([] if step else [((rows4, 128), bf16)]),
             forward_streams + sums,
             spaces={10: pltpu.HBM},
             **work,
-        )(recv, f, ge4, gp4, sk, sp4, serve, b0, b1, c_held, c_rest)
+        )(recv, serve if step else lists_in, f, ge4, gp4, sk, sp4, b0, b1, c_held, c_rest)
+        if not step:
+            serve = hot[0]
+            s8, st4, st8a, st8b = call(
+                functools.partial(serve_kernel, cap, kb, qb),
+                "serve",
+                [
+                    ((rows8, 128), bf16),
+                    ((qb, rows4), bf16),
+                    ((qb, rows8), bf16),
+                    ((qb, rows8), bf16),
+                ],
+            )(serve)
         recv = exchange(send)
         b0, b1 = back(f1, gk, coupling)
         send, p0, n1, far = call(

time: 99.2 us -> 143 us (1.44); the launches traced: 98.7 us -> 140 us
  local copies, waits for them, and re-layouts: 0 us -> 47.6 us
  waiting for transfers between devices: 11.4 us -> 2.59 us
  blocking collectives: 19.8 us -> 24.4 us
  starting transfers between devices: 23.5 us -> 22 us
    unnamed x0 -> x152, local copies, waits for them, and re-layouts: none -> 47.6 us
    all_to_all x5 -> x4, waiting for transfers between devices: 11.4 us -> 2.59 us  [exchange(): return lax.all_to_all(x, 'bulk', split_axis=0, concat_axis=0, tiled=True)]
    all_to_all x2, blocking collectives: 19.8 us -> 24.4 us  [exchange(): return lax.all_to_all(x, 'bulk', split_axis=0, concat_axis=0, tiled=True)]
    all_to_all x5 -> x4, starting transfers between devices: 23.5 us -> 22 us  [exchange(): return lax.all_to_all(x, 'bulk', split_axis=0, concat_axis=0, tiled=True)]
  transfers between devices with their start and end apart: 5 -> 4, of which waited for: 5 -> 3; matrix products, arithmetic and copies ran while one was open for 0% -> 0% of each run, Pallas kernels for 21% -> 15%
where the time goes in v5:
time: 143 us; the launch traced here: 140 us
  local copies, waits for them, and re-layouts  47.6 us (33%)
  Pallas kernels  41.5 us (29%)
  blocking collectives  24.4 us (17%)
  starting transfers between devices  22 us (15%)
  waiting for transfers between devices  2.59 us (2%)
  between operations  1.81 us (1%)
    unnamed x152, local copies, waits for them, and re-layouts  47.6 us
    pallas_call x13, Pallas kernels, run(): pl.pallas_call(kernel, out_shape=[pltpu.HBM(*o) if (out_spaces or {}).get...  41.5 us
    all_to_all x2, blocking collectives, exchange(): return lax.all_to_all(x, 'bulk', split_axis=0, concat_axis=0, tiled=True)  24.4 us
    all_to_all x4, starting transfers between devices, exchange(): return lax.all_to_all(x, 'bulk', split_axis=0, concat_axis=0, tiled=True)  22 us
  transfers between devices with their start and end apart: 4, of which 3 were waited for; matrix products, arithmetic and copies ran while one was open for 0% of the time, Pallas kernels for 15%

profile of v5, /device:TPU:0, one launch (start us, length us, event | category | flops | bytes accessed | tf_op | source)
XLA Modules:
  0.0 140.0 jit_solution(9665913518995475126)
XLA Ops:
  0.6 1.8 %need.1 = (f32[32,128]{1,0:T(8,128)S(1)}, f32[16,128]{1,0:T(8,128)S(1)}, f32[16,128]{1,0:T(8,128)S(1)}, f32[16,128]{1,0:T(8,128)S(1)}, s32[1,256]{1,0:T(1,128)S(...) custom-call(f32[32,128]{1,0:T(8,128)} %refs_0_.1, ...), custom_call_target="tpu_custom_call" | custom-call | tf_op jit(solution)/shard_map/need/pallas_call | solution.py:390
  4.3 7.4 %all-to-all-start = ((f32[16,56,128]{2,1,0:T(8,128)}), f32[16,56,128]{2,1,0:T(8,128)}, u32[]{:S(2)}, u32[]{:S(2)}) async-start(f32[16,56,128]{2,1,0:T(8,128)} %bitcast.3), calls=%async_computation | async-start | bytes 917504 | tf_op jit(solution)/shard_map/all_to_all | solution.py:448
  12.4 5.0 %transpose.1 = (bf16[96,128,128]{2,1,0:T(8,128)(2,1)S(1)}, bf16[160,128,128]{2,1,0:T(8,128)(2,1)}) custom-call(f32[32,128]{1,0:T(8,128)S(1)} %get-tuple-element.52.f_ref.after_ref.refs_1_, bf16[256,128,128]{2,1,0:T(8,128)(2,1)} %c_hbm.9), custom_call_target="tpu_custom_call" | custom-call | flops 134217728 | bytes 8388608 | tf_op jit(solution)/shard_map/transpose/pallas_call | solution.py:390
  17.5 4.0 %tables.1 = (bf16[256,64]{1,0:T(8,128)(2,1)S(1)}, bf16[256,64]{1,0:T(8,128)(2,1)S(1)}, bf16[256,128]{1,0:T(8,128)(2,1)S(1)}, bf16[256,32]{1,0:T(8,128)(2,1)S(1)}...) custom-call(s32[1]{0:T(128)S(6)} %copy.13.count_ref, ...), custom_call_target="tpu_custom_call" | custom-call | flops 134217728 | bytes 8388608 | tf_op jit(solution)/shard_map/tables/pallas_call | solution.py:390
  23.9 1.1 all-to-all-done
  25.0 0.8 copy-done.1
  25.9 0.9 copy-done.12
  26.8 0.9 copy-done.14
  27.7 0.8 copy-done.20
  28.4 0.9 copy-done.42
  29.3 4.7 %first.2 = (f32[64,128]{1,0:T(8,128)S(1)}, f32[32,128]{1,0:T(8,128)S(1)}, f32[32,128]{1,0:T(8,128)S(1)}, bf16[64,128]{1,0:T(8,128)(2,1)S(1)}) custom-call(f32[896,128]{1,0:T(8,128)} %bitcast.4.recv, bf16[64,896]{1,0:T(8,128)(2,1)S(1)} %copy-done.42, f32[32,128]{1,0:T(8,128)S(1)} %get-tuple-element.52.f_ref.after_ref.refs_1_, ...), custom_call_target="tpu_custom_call" | custom-call | flops 134217728 | bytes 8388608 | tf_op jit(solution)/shard_map/first/pallas_call | solution.py:390
  36.5 4.9 %all-to-all-start.1 = ((f32[16,4,128]{2,1,0:T(4,128)}), f32[16,4,128]{2,1,0:T(4,128)}, u32[]{:S(2)}, u32[]{:S(2)}) async-start(f32[16,4,128]{2,1,0:T(4,128)} %bitcast.19), calls=%async_computation.1 | async-start | bytes 65536 | tf_op jit(solution)/shard_map/all_to_all | solution.py:448
  41.4 0.7 copy-done.4
  44.8 0.7 copy-done.47
  45.5 3.8 %backward.3 = (f32[32,8,128]{2,1,0:T(8,128)S(1)}, f32[32,8,128]{2,1,0:T(8,128)S(1)}) custom-call(f32[32,128]{1,0:T(8,128)S(1)} %copy-done.47, bf16[256,32]{1,0:T(8,128)(2,1)S(1)} %get-tuple-element.73.gk_ref, bf16[256,128,128]{2,1,0:T(8,128)(2,1)} %c_hbm.9), custom_call_target="tpu_custom_call" | custom-call | flops 134217728 | bytes 8388608 | tf_op jit(solution)/shard_map/backward/pallas_call | solution.py:390
  50.6 0.8 copy-done.23
  51.3 0.9 copy-done.30
  52.2 0.9 copy-done.32
  53.1 0.7 copy-done.34
  53.8 0.7 copy-done.38
  55.9 1.2 phonon.2
  57.1 12.7 %all_to_all.66 = f32[16,8,128]{2,1,0:T(8,128)S(1)} all-to-all(f32[16,8,128]{2,1,0:T(8,128)S(1)} %bitcast.18), channel_id=1, replica_groups=mesh['groups'=2,'bulk'=16] {'bulk'}, dimensions={0} | all-to-all | bytes 131072 | tf_op jit(solution)/shard_map/all_to_all | solution.py:448
  69.8 0.7 copy-done.5
  71.9 0.7 copy-done.48
  72.6 0.7 copy-done.60
  74.7 3.5 %second.2 = (f32[32,128]{1,0:T(8,128)S(1)}, f32[16,128]{1,0:T(8,128)S(1)}, f32[64,128]{1,0:T(8,128)S(1)}) custom-call(f32[128,128]{1,0:T(8,128)S(1)} %bitcast.16, f32[256,128]{1,0:T(8,128)S(1)} %get-tuple-element.77.refs_0_, f32[32,128]{1,0:T(8,128)S(1)} %get-tuple-element.52.f_ref.after_ref.refs_1_, f32[32,128]{1,0:T(8,128)S(1)} %copy-done.48, ...), custom_call_target="tpu_custom_call" | custom-call | flops 134217728 | bytes 8388608 | tf_op jit(solution)/shard_map/second/pallas_call | solution.py:390
  80.0 4.5 %all-to-all-start.3 = ((f32[16,4,128]{2,1,0:T(4,128)}), f32[16,4,128]{2,1,0:T(4,128)}, u32[]{:S(2)}, u32[]{:S(2)}) async-start(f32[16,4,128]{2,1,0:T(4,128)} %bitcast.20), calls=%async_computation.3 | async-start | bytes 65536 | tf_op jit(solution)/shard_map/all_to_all | solution.py:448
  84.5 0.7 copy-done.8
  85.2 3.8 %backward.4 = (f32[32,8,128]{2,1,0:T(8,128)S(1)}, f32[32,8,128]{2,1,0:T(8,128)S(1)}) custom-call(f32[32,128]{1,0:T(8,128)S(1)} %copy-done.8, bf16[256,32]{1,0:T(8,128)(2,1)S(1)} %get-tuple-element.73.gk_ref, bf16[256,128,128]{2,1,0:T(8,128)(2,1)} %c_hbm.9), custom_call_target="tpu_custom_call" | custom-call | flops 134217728 | bytes 8388608 | tf_op jit(solution)/shard_map/backward/pallas_call | solution.py:390
  90.9 0.8 copy-done.2
  91.8 0.7 copy-done.9
  92.5 0.9 copy-done.16
  93.4 0.9 copy-done.18
  94.3 0.8 copy-done.21
  95.0 4.3 %first.3 = (f32[64,128]{1,0:T(8,128)S(1)}, f32[32,128]{1,0:T(8,128)S(1)}, f32[32,128]{1,0:T(8,128)S(1)}) custom-call(f32[64,128]{1,0:T(8,128)} %bitcast.10.recv, bf16[64,128]{1,0:T(8,128)(2,1)S(1)} %copy-done.6, f32[32,128]{1,0:T(8,128)S(1)} %copy-done.9, bf16[256,64]{1,0:T(8,128)(2,1)S(1)} %get-tuple-element.56.ge4_ref, bf16[256,64]{1,0:T(8,128)(2,1)S(1)} %copy-done.2, ...), custom_call_target="tpu_custom_call" | custom-call | flops 134217728 | bytes 8388608 | tf_op jit(solution)/shard_map/first/pallas_call | solution.py:390
  101.2 5.1 %all-to-all-start.4 = ((f32[16,4,128]{2,1,0:T(4,128)}), f32[16,4,128]{2,1,0:T(4,128)}, u32[]{:S(2)}, u32[]{:S(2)}) async-start(f32[16,4,128]{2,1,0:T(4,128)} %bitcast.21), calls=%async_computation.4 | async-start | bytes 65536 | tf_op jit(solution)/shard_map/all_to_all | solution.py:448
  106.3 0.7 copy-done.44
  107.0 3.8 %backward.5 = (f32[32,8,128]{2,1,0:T(8,128)S(1)}, f32[32,8,128]{2,1,0:T(8,128)S(1)}) custom-call(f32[32,128]{1,0:T(8,128)S(1)} %copy-done.44, bf16[256,32]{1,0:T(8,128)(2,1)S(1)} %get-tuple-element.73.gk_ref, bf16[256,128,128]{2,1,0:T(8,128)(2,1)} %c_hbm.9), custom_call_target="tpu_custom_call" | custom-call | flops 134217728 | bytes 8388608 | tf_op jit(solution)/shard_map/backward/pallas_call | solution.py:390
  112.1 0.9 all-to-all-done.4
  113.0 0.8 copy-done.24
  113.8 0.9 copy-done.26
  114.7 0.9 copy-done.28
  118.3 1.2 phonon.3
  119.6 11.8 %all_to_all.67 = f32[16,8,128]{2,1,0:T(8,128)S(1)} all-to-all(f32[16,8,128]{2,1,0:T(8,128)S(1)} %bitcast.17), channel_id=1, replica_groups=mesh['groups'=2,'bulk'=16] {'bulk'}, dimensions={0} | all-to-all | bytes 131072 | tf_op jit(solution)/shard_map/all_to_all | solution.py:448
  131.4 0.7 copy-done.10
  132.1 0.7 copy-done.45
  133.5 0.7 copy-done.58
  135.6 4.3 %second.3 = (f32[32,128]{1,0:T(8,128)}, f32[16,128]{1,0:T(8,128)}) custom-call(f32[128,128]{1,0:T(8,128)S(1)} %bitcast.15, f32[256,128]{1,0:T(8,128)S(1)} %get-tuple-element.94.refs_0_, f32[32,128]{1,0:T(8,128)S(1)} %copy-done.10, f32[32,128]{1,0:T(8,128)S(1)} %copy-done.45, f32[32,128]{1,0:T(8,128)S(1)} %copy-done.58, f32[16,128]{1,0:T(8,128)S(1)} %copy-done.56, ...), custom_call_target="tpu_custom_call" | custom-call | flops 134217728 | bytes 8388608 | tf_op jit(solution)/shard_map/second/pallas_call | solution.py:390
  (127 shorter events, 26.4 us)
Async XLA Ops:
  4.2 8.1 %copy-start.52 = (f32[16,128]{1,0:T(8,128)}, f32[16,128]{1,0:T(8,128)S(1)}, u32[]{:S(2)}) copy-start(f32[16,128]{1,0:T(8,128)S(1)} %get-tuple-element.65.n_ref.refs_4_) | copy-start | bytes 24580
  4.2 8.1 %copy-start.70 = (s32[1,256]{1,0:T(1,128)}, s32[1,256]{1,0:T(1,128)S(1)}, u32[]{:S(2)}) copy-start(s32[1,256]{1,0:T(1,128)S(1)} %get-tuple-element.53.kblock_ref) | copy-start | bytes 3076
  4.2 8.1 %copy-start.72 = (s32[1,256]{1,0:T(1,128)}, s32[1,256]{1,0:T(1,128)S(1)}, u32[]{:S(2)}) copy-start(s32[1,256]{1,0:T(1,128)S(1)} %get-tuple-element.54.partner_ref) | copy-start | bytes 3076
  4.2 8.1 %copy-start.74 = (s32[1,256]{1,0:T(1,128)}, s32[1,256]{1,0:T(1,128)S(1)}, u32[]{:S(2)}) copy-start(s32[1,256]{1,0:T(1,128)S(1)} %get-tuple-element.55.qslot_ref) | copy-start | bytes 3076
  4.3 20.8 %all-to-all-start = ((f32[16,56,128]{2,1,0:T(8,128)}), f32[16,56,128]{2,1,0:T(8,128)}, u32[]{:S(2)}, u32[]{:S(2)}) async-start(f32[16,56,128]{2,1,0:T(8,128)} %bitcast.3), calls=%async_computation | async-start | bytes 917504 | tf_op jit(solution)/shard_map/all_to_all | solution.py:448
  12.4 5.0 %copy-start.71 = (s32[1,256]{1,0:T(1,128)S(1)}, s32[1,256]{1,0:T(1,128)}, u32[]{:S(2)}) copy-start(s32[1,256]{1,0:T(1,128)} %copy-done.70) | copy-start | bytes 3076
  12.4 5.0 %copy-start.73 = (s32[1,256]{1,0:T(1,128)S(1)}, s32[1,256]{1,0:T(1,128)}, u32[]{:S(2)}) copy-start(s32[1,256]{1,0:T(1,128)} %copy-done.72) | copy-start | bytes 3076
  12.4 5.0 %copy-start.75 = (s32[1,256]{1,0:T(1,128)S(1)}, s32[1,256]{1,0:T(1,128)}, u32[]{:S(2)}) copy-start(s32[1,256]{1,0:T(1,128)} %copy-done.74) | copy-start | bytes 3076
  25.0 0.8 copy-start.1
  25.9 0.9 copy-start.12
  26.8 0.9 copy-start.14
  27.7 0.8 copy-start.20
  28.4 0.9 copy-start.42
  36.5 14.1 %all-to-all-start.1 = ((f32[16,4,128]{2,1,0:T(4,128)}), f32[16,4,128]{2,1,0:T(4,128)}, u32[]{:S(2)}, u32[]{:S(2)}) async-start(f32[16,4,128]{2,1,0:T(4,128)} %bitcast.19), calls=%async_computation.1 | async-start | bytes 65536 | tf_op jit(solution)/shard_map/all_to_all | solution.py:448
  41.4 0.7 copy-start.4
  44.8 0.7 copy-start.47
  50.6 0.8 copy-start.23
  51.3 0.9 copy-start.30
  52.2 0.9 copy-start.32
  53.1 0.7 copy-start.34
  53.8 0.7 copy-start.38
  54.5 0.7 copy-start.53
  69.8 0.7 copy-start.5
  70.5 0.7 copy-start.35
  71.2 0.7 copy-start.39
  71.9 0.7 copy-start.48
  72.6 0.7 copy-start.60
  80.0 10.9 %copy-start.6 = (bf16[64,128]{1,0:T(8,128)(2,1)S(1)}, bf16[64,128]{1,0:T(8,128)(2,1)}, u32[]{:S(2)}) copy-start(bf16[64,128]{1,0:T(8,128)(2,1)} %copy-done.3) | copy-start | bytes 49156
  80.0 10.9 %all-to-all-start.3 = ((f32[16,4,128]{2,1,0:T(4,128)}), f32[16,4,128]{2,1,0:T(4,128)}, u32[]{:S(2)}, u32[]{:S(2)}) async-start(f32[16,4,128]{2,1,0:T(4,128)} %bitcast.20), calls=%async_computation.3 | async-start | bytes 65536 | tf_op jit(solution)/shard_map/all_to_all | solution.py:448
  84.4 0.7 copy-start.8
  90.9 0.8 copy-start.2
  91.8 0.7 copy-start.9
  92.5 0.9 copy-start.16
  93.4 0.9 copy-start.18
  94.3 0.8 copy-start.21
  101.2 11.8 %all-to-all-start.4 = ((f32[16,4,128]{2,1,0:T(4,128)}), f32[16,4,128]{2,1,0:T(4,128)}, u32[]{:S(2)}, u32[]{:S(2)}) async-start(f32[16,4,128]{2,1,0:T(4,128)} %bitcast.21), calls=%async_computation.4 | async-start | bytes 65536 | tf_op jit(solution)/shard_map/all_to_all | solution.py:448
  106.3 0.7 copy-start.44
  113.0 0.8 copy-start.24
  113.8 0.9 copy-start.26
  114.7 0.9 copy-start.28
  115.6 0.7 copy-start.36
  116.3 0.7 copy-start.40
  117.0 0.7 copy-start.55
  131.3 0.7 copy-start.10
  132.1 0.7 copy-start.45
  132.8 0.7 copy-start.56
  133.5 0.7 copy-start.58
  134.9 0.7 copy-start.66
  (32 other events, 20.0 us)

commit v6 on v5

--- a/solution.py
+++ b/solution.py
@@ -10,7 +10,7 @@
 STEPS = 2
 DT = 0.05
 CHUNKS = 8
-HELD_CHUNKS = 3
+HELD_CHUNKS = 2
 f32 = jnp.float32
 bf16 = jnp.bfloat16
 VMEM_LIMIT = 24 * 1024 * 1024

time: 143 us -> 93.6 us (0.65); the launches traced: 140 us -> 93 us
  local copies, waits for them, and re-layouts: 47.6 us -> 0 us
  waiting for transfers between devices: 2.59 us -> 11.1 us
  blocking collectives: 24.4 us -> 20 us
  starting transfers between devices: 22 us -> 18.4 us
    unnamed x152 -> x0, local copies, waits for them, and re-layouts: 47.6 us -> none
    all_to_all x4, waiting for transfers between devices: 2.59 us -> 11.1 us  [exchange(): return lax.all_to_all(x, 'bulk', split_axis=0, concat_axis=0, tiled=True)]
    all_to_all x2, blocking collectives: 24.4 us -> 20 us  [exchange(): return lax.all_to_all(x, 'bulk', split_axis=0, concat_axis=0, tiled=True)]
    all_to_all x4, starting transfers between devices: 22 us -> 18.4 us  [exchange(): return lax.all_to_all(x, 'bulk', split_axis=0, concat_axis=0, tiled=True)]
  transfers between devices with their start and end apart: 4 -> 4, of which waited for: 3 -> 4; matrix products, arithmetic and copies ran while one was open for 0% -> 0% of each run, Pallas kernels for 15% -> 23%
where the time goes in v6:
time: 93.6 us; the launch traced here: 93 us
  Pallas kernels  41.9 us (45%)
  blocking collectives  20 us (21%)
  starting transfers between devices  18.4 us (20%)
  waiting for transfers between devices  11.1 us (12%)
  between operations  1.57 us (2%)
    pallas_call x13, Pallas kernels, run(): pl.pallas_call(kernel, out_shape=[pltpu.HBM(*o) if (out_spaces or {}).get...  41.9 us
    all_to_all x2, blocking collectives, exchange(): return lax.all_to_all(x, 'bulk', split_axis=0, concat_axis=0, tiled=True)  20 us
    all_to_all x4, starting transfers between devices, exchange(): return lax.all_to_all(x, 'bulk', split_axis=0, concat_axis=0, tiled=True)  18.4 us
    all_to_all x4, waiting for transfers between devices, exchange(): return lax.all_to_all(x, 'bulk', split_axis=0, concat_axis=0, tiled=True)  11.1 us
  transfers between devices with their start and end apart: 4, of which 4 were waited for; matrix products, arithmetic and copies ran while one was open for 0% of the time, Pallas kernels for 23%

profile of v6, /device:TPU:0, one launch (start us, length us, event | category | flops | bytes accessed | tf_op | source)
XLA Modules:
  0.0 93.0 jit_solution(16833243771514137683)
XLA Ops:
  0.6 1.8 %need.1 = (f32[32,128]{1,0:T(8,128)S(1)}, f32[16,128]{1,0:T(8,128)S(1)}, f32[16,128]{1,0:T(8,128)S(1)}, f32[16,128]{1,0:T(8,128)S(1)}, s32[1,256]{1,0:T(1,128)S(...) custom-call(f32[32,128]{1,0:T(8,128)} %refs_0_.1, ...), custom_call_target="tpu_custom_call" | custom-call | tf_op jit(solution)/shard_map/need/pallas_call | solution.py:390
  2.4 7.4 %all-to-all-start = ((f32[16,56,128]{2,1,0:T(8,128)}), f32[16,56,128]{2,1,0:T(8,128)S(1)}, u32[]{:S(2)}, u32[]{:S(2)}) async-start(f32[16,56,128]{2,1,0:T(8,128)} %bitcast.3), calls=%async_computation | async-start | bytes 917504 | tf_op jit(solution)/shard_map/all_to_all | solution.py:448
  10.4 5.5 %transpose.1 = (bf16[64,128,128]{2,1,0:T(8,128)(2,1)S(1)}, bf16[192,128,128]{2,1,0:T(8,128)(2,1)}) custom-call(f32[32,128]{1,0:T(8,128)S(1)} %get-tuple-element.52.f_ref.after_ref.refs_1_, bf16[256,128,128]{2,1,0:T(8,128)(2,1)} %c_hbm.9), custom_call_target="tpu_custom_call" | custom-call | flops 134217728 | bytes 8388608 | tf_op jit(solution)/shard_map/transpose/pallas_call | solution.py:390
  16.0 4.0 %tables.1 = (bf16[256,64]{1,0:T(8,128)(2,1)S(1)}, bf16[256,64]{1,0:T(8,128)(2,1)S(1)}, bf16[256,128]{1,0:T(8,128)(2,1)S(1)}, bf16[256,32]{1,0:T(8,128)(2,1)S(1)}...) custom-call(s32[1]{0:T(128)S(6)} %copy.13.count_ref, ...), custom_call_target="tpu_custom_call" | custom-call | flops 134217728 | bytes 8388608 | tf_op jit(solution)/shard_map/tables/pallas_call | solution.py:390
  19.9 3.1 %all-to-all-done = f32[16,56,128]{2,1,0:T(8,128)S(1)} async-done(((f32[16,56,128]{2,1,0:T(8,128)}), f32[16,56,128]{2,1,0:T(8,128)S(1)}, u32[]{:S(2)}, u32[]{:S(2)}) %all-to-all-start) | async-done | bytes 458784 | tf_op jit(solution)/shard_map/all_to_all | solution.py:448
  23.1 4.5 %first.2 = (f32[64,128]{1,0:T(8,128)}, f32[32,128]{1,0:T(8,128)S(1)}, f32[32,128]{1,0:T(8,128)S(1)}, bf16[64,128]{1,0:T(8,128)(2,1)S(1)}) custom-call(f32[896,128]{1,0:T(8,128)S(1)} %bitcast.15, bf16[64,896]{1,0:T(8,128)(2,1)S(1)} %get-tuple-element.51.list_ref, f32[32,128]{1,0:T(8,128)S(1)} %get-tuple-element.52.f_ref.after_ref.refs_1_, ...), custom_call_target="tpu_custom_call" | custom-call | flops 134217728 | bytes 8388608 | tf_op jit(solution)/shard_map/first/pallas_call | solution.py:390
  27.6 3.9 %all-to-all-start.1 = ((f32[16,4,128]{2,1,0:T(4,128)}), f32[16,4,128]{2,1,0:T(4,128)S(1)}, u32[]{:S(2)}, u32[]{:S(2)}) async-start(f32[16,4,128]{2,1,0:T(4,128)} %bitcast.5), calls=%async_computation.1 | async-start | bytes 65536 | tf_op jit(solution)/shard_map/all_to_all | solution.py:448
  31.5 0.2 serve.1
  31.7 3.8 %backward.3 = (f32[32,8,128]{2,1,0:T(8,128)S(1)}, f32[32,8,128]{2,1,0:T(8,128)S(1)}) custom-call(f32[32,128]{1,0:T(8,128)S(1)} %get-tuple-element.72.f_ref.refs_2_, bf16[256,32]{1,0:T(8,128)(2,1)S(1)} %get-tuple-element.73.gk_ref, bf16[256,128,128]{2,1,0:T(8,128)(2,1)} %c_hbm.9), custom_call_target="tpu_custom_call" | custom-call | flops 134217728 | bytes 8388608 | tf_op jit(solution)/shard_map/backward/pallas_call | solution.py:390
  35.6 2.6 %all-to-all-done.1 = f32[16,4,128]{2,1,0:T(4,128)S(1)} async-done(((f32[16,4,128]{2,1,0:T(4,128)}), f32[16,4,128]{2,1,0:T(4,128)S(1)}, u32[]{:S(2)}, u32[]{:S(2)}) %all-to-all-start.1) | async-done | bytes 32800 | tf_op jit(solution)/shard_map/all_to_all | solution.py:448
  38.1 0.5 phonon.2
  38.6 10.1 %all_to_all.66 = f32[16,8,128]{2,1,0:T(8,128)S(1)} all-to-all(f32[16,8,128]{2,1,0:T(8,128)S(1)} %bitcast.22), channel_id=1, replica_groups=mesh['groups'=2,'bulk'=16] {'bulk'}, dimensions={0} | all-to-all | bytes 131072 | tf_op jit(solution)/shard_map/all_to_all | solution.py:448
  48.7 4.6 %second.2 = (f32[32,128]{1,0:T(8,128)S(1)}, f32[16,128]{1,0:T(8,128)S(1)}, f32[64,128]{1,0:T(8,128)}) custom-call(f32[128,128]{1,0:T(8,128)S(1)} %bitcast.17, f32[256,128]{1,0:T(8,128)S(1)} %get-tuple-element.77.refs_0_, f32[32,128]{1,0:T(8,128)S(1)} %get-tuple-element.52.f_ref.after_ref.refs_1_, f32[32,128]{1,0:T(8,128)S(1)} %get-tuple-element.72.f_ref.refs_2_, ...), custom_call_target="tpu_custom_call" | custom-call | flops 134217728 | bytes 8388608 | tf_op jit(solution)/shard_map/second/pallas_call | solution.py:390
  53.3 3.7 %all-to-all-start.3 = ((f32[16,4,128]{2,1,0:T(4,128)}), f32[16,4,128]{2,1,0:T(4,128)S(1)}, u32[]{:S(2)}, u32[]{:S(2)}) async-start(f32[16,4,128]{2,1,0:T(4,128)} %bitcast.9), calls=%async_computation.3 | async-start | bytes 65536 | tf_op jit(solution)/shard_map/all_to_all | solution.py:448
  57.0 3.8 %backward.4 = (f32[32,8,128]{2,1,0:T(8,128)S(1)}, f32[32,8,128]{2,1,0:T(8,128)S(1)}) custom-call(f32[32,128]{1,0:T(8,128)S(1)} %get-tuple-element.85.f_ref.refs_1_, bf16[256,32]{1,0:T(8,128)(2,1)S(1)} %get-tuple-element.73.gk_ref, bf16[256,128,128]{2,1,0:T(8,128)(2,1)} %c_hbm.9), custom_call_target="tpu_custom_call" | custom-call | flops 134217728 | bytes 8388608 | tf_op jit(solution)/shard_map/backward/pallas_call | solution.py:390
  60.8 2.6 %all-to-all-done.3 = f32[16,4,128]{2,1,0:T(4,128)S(1)} async-done(((f32[16,4,128]{2,1,0:T(4,128)}), f32[16,4,128]{2,1,0:T(4,128)S(1)}, u32[]{:S(2)}, u32[]{:S(2)}) %all-to-all-start.3) | async-done | bytes 32800 | tf_op jit(solution)/shard_map/all_to_all | solution.py:448
  63.4 4.5 %first.3 = (f32[64,128]{1,0:T(8,128)}, f32[32,128]{1,0:T(8,128)S(1)}, f32[32,128]{1,0:T(8,128)S(1)}) custom-call(f32[64,128]{1,0:T(8,128)S(1)} %bitcast.18, bf16[64,128]{1,0:T(8,128)(2,1)S(1)} %get-tuple-element.68.hot_ref.refs_13_.list_ref, f32[32,128]{1,0:T(8,128)S(1)} %get-tuple-element.85.f_ref.refs_1_, bf16[256,64]{1,0:T(8,128)(2,1)S(1)} %get-tuple-element.56.ge4_ref, ...), custom_call_target="tpu_custom_call" | custom-call | flops 134217728 | bytes 8388608 | tf_op jit(solution)/shard_map/first/pallas_call | solution.py:390
  67.9 3.5 %all-to-all-start.4 = ((f32[16,4,128]{2,1,0:T(4,128)}), f32[16,4,128]{2,1,0:T(4,128)S(1)}, u32[]{:S(2)}, u32[]{:S(2)}) async-start(f32[16,4,128]{2,1,0:T(4,128)} %bitcast.11), calls=%async_computation.4 | async-start | bytes 65536 | tf_op jit(solution)/shard_map/all_to_all | solution.py:448
  71.4 3.8 %backward.5 = (f32[32,8,128]{2,1,0:T(8,128)S(1)}, f32[32,8,128]{2,1,0:T(8,128)S(1)}) custom-call(f32[32,128]{1,0:T(8,128)S(1)} %get-tuple-element.90.f_ref.refs_2_, bf16[256,32]{1,0:T(8,128)(2,1)S(1)} %get-tuple-element.73.gk_ref, bf16[256,128,128]{2,1,0:T(8,128)(2,1)} %c_hbm.9), custom_call_target="tpu_custom_call" | custom-call | flops 134217728 | bytes 8388608 | tf_op jit(solution)/shard_map/backward/pallas_call | solution.py:390
  75.2 2.8 %all-to-all-done.4 = f32[16,4,128]{2,1,0:T(4,128)S(1)} async-done(((f32[16,4,128]{2,1,0:T(4,128)}), f32[16,4,128]{2,1,0:T(4,128)S(1)}, u32[]{:S(2)}, u32[]{:S(2)}) %all-to-all-start.4) | async-done | bytes 32800 | tf_op jit(solution)/shard_map/all_to_all | solution.py:448
  78.0 0.5 phonon.3
  78.5 9.9 %all_to_all.67 = f32[16,8,128]{2,1,0:T(8,128)S(1)} all-to-all(f32[16,8,128]{2,1,0:T(8,128)S(1)} %bitcast.21), channel_id=1, replica_groups=mesh['groups'=2,'bulk'=16] {'bulk'}, dimensions={0} | all-to-all | bytes 131072 | tf_op jit(solution)/shard_map/all_to_all | solution.py:448
  88.4 4.5 %second.3 = (f32[32,128]{1,0:T(8,128)}, f32[16,128]{1,0:T(8,128)}) custom-call(f32[128,128]{1,0:T(8,128)S(1)} %bitcast.16, f32[256,128]{1,0:T(8,128)S(1)} %get-tuple-element.94.refs_0_, f32[32,128]{1,0:T(8,128)S(1)} %get-tuple-element.85.f_ref.refs_1_, f32[32,128]{1,0:T(8,128)S(1)} %get-tuple-element.90.f_ref.refs_2_, ...), custom_call_target="tpu_custom_call" | custom-call | flops 134217728 | bytes 8388608 | tf_op jit(solution)/shard_map/second/pallas_call | solution.py:390
Async XLA Ops:
  2.4 20.7 %all-to-all-start = ((f32[16,56,128]{2,1,0:T(8,128)}), f32[16,56,128]{2,1,0:T(8,128)S(1)}, u32[]{:S(2)}, u32[]{:S(2)}) async-start(f32[16,56,128]{2,1,0:T(8,128)} %bitcast.3), calls=%async_computation | async-start | bytes 917504 | tf_op jit(solution)/shard_map/all_to_all | solution.py:448
  27.6 10.5 %all-to-all-start.1 = ((f32[16,4,128]{2,1,0:T(4,128)}), f32[16,4,128]{2,1,0:T(4,128)S(1)}, u32[]{:S(2)}, u32[]{:S(2)}) async-start(f32[16,4,128]{2,1,0:T(4,128)} %bitcast.5), calls=%async_computation.1 | async-start | bytes 65536 | tf_op jit(solution)/shard_map/all_to_all | solution.py:448
  53.3 10.1 %all-to-all-start.3 = ((f32[16,4,128]{2,1,0:T(4,128)}), f32[16,4,128]{2,1,0:T(4,128)S(1)}, u32[]{:S(2)}, u32[]{:S(2)}) async-start(f32[16,4,128]{2,1,0:T(4,128)} %bitcast.9), calls=%async_computation.3 | async-start | bytes 65536 | tf_op jit(solution)/shard_map/all_to_all | solution.py:448
  67.9 10.1 %all-to-all-start.4 = ((f32[16,4,128]{2,1,0:T(4,128)}), f32[16,4,128]{2,1,0:T(4,128)S(1)}, u32[]{:S(2)}, u32[]{:S(2)}) async-start(f32[16,4,128]{2,1,0:T(4,128)} %bitcast.11), calls=%async_computation.4 | async-start | bytes 65536 | tf_op jit(solution)/shard_map/all_to_all | solution.py:448

commit v7 on v6

--- a/solution.py
+++ b/solution.py
@@ -57,15 +57,15 @@
     return ref[...].reshape(-1, 128)
 
 
-def chunk_copies(src, dst, sems):
-    count = sems.shape[0]
-    size = src.shape[0] // count
-    return [
-        pltpu.make_async_copy(
-            src.at[pl.ds(i * size, size)], dst.at[pl.ds(i * size, size)], sems.at[i]
-        )
-        for i in range(count)
-    ]
+def chunk_copy(src, dst, sems, i):
+    size = src.shape[0] // sems.shape[0]
+    here = pl.ds(i * size, size)
+    return pltpu.make_async_copy(src.at[here], dst.at[here], sems.at[i])
+
+
+def start_chunks(src, dst, sems):
+    for i in range(sems.shape[0]):
+        chunk_copy(src, dst, sems, i).start()
 
 
 def start(copies):
@@ -80,50 +80,44 @@
     )
 
 
-def tile_products(w_ref, parts, out0, out1, after=None):
+def tile_products(w_ref, parts, out0, out1):
     size = w_ref.shape[0] // CHUNKS
     base = 0
-    for c_ref, copies in parts:
+    for c_ref, c_hbm, sems in parts:
         groups = c_ref.shape[0] // 8
-        for i in range(groups // size):
-            if copies:
-                copies[i].wait()
-            for g in range(i * size, (i + 1) * size, 2):
+
+        def chunk(i, _):
+            if c_hbm is not None:
+                chunk_copy(c_hbm, c_ref, sems, i).wait()
+            for k in range(0, size, 2):
+                g = i * size + k
+                at = base + g
                 lhs = jnp.concatenate(
-                    [block_diagonal(w_ref[base + g]), block_diagonal(w_ref[base + g + 1])],
-                    axis=0,
+                    [block_diagonal(w_ref[at]), block_diagonal(w_ref[at + 1])], axis=0
                 )
                 rhs = jnp.concatenate(
-                    [c_ref[(g + k) * 8 : (g + k + 1) * 8].reshape(1024, 128) for k in (0, 1)],
-                    axis=1,
+                    [c_ref[pl.ds((g + j) * 8, 8)].reshape(1024, 128) for j in (0, 1)], axis=1
                 )
                 res = dot(lhs, rhs)
-                for k in (0, 1):
-                    own = res[16 * k : 16 * (k + 1), 128 * k : 128 * (k + 1)]
-                    out0[base + g + k] = own[:8]
-                    out1[base + g + k] = own[8:]
-            if after:
-                after(base // size + i)
+                for j in (0, 1):
+                    own = res[16 * j : 16 * (j + 1), 128 * j : 128 * (j + 1)]
+                    out0[at + j] = own[:8]
+                    out1[at + j] = own[8:]
+            return 0
+
+        lax.fori_loop(0, groups // size, chunk, 0)
         base += groups
 
 
-def backward_pass(own, copies, c_ref, w_ref, out0, out1):
+def backward_pass(own, c_hbm, c_ref, sems, w_ref, out0, out1):
     w_ref[...] = stacked(1.0 - own, own)
-    tile_products(w_ref, [(c_ref, copies)], out0, out1)
-
-
-def electron_rate(sum_k_ref, far, bose, f, parts, w_ref, o0, o1):
+    tile_products(w_ref, [(c_ref, c_hbm, sems)], out0, out1)
+
+
+def electron_rate(sum_k, far, bose, f, parts, w_ref, o0, o1):
     w_ref[...] = stacked(far * (1.0 + bose), far + bose)
-    totals = [jnp.zeros_like(f), jnp.zeros_like(f)]
-    size = w_ref.shape[0] // CHUNKS
-
-    def after(chunk):
-        for k, out in enumerate((o0, o1)):
-            rows = out[chunk * size : (chunk + 1) * size].reshape(-1, 128)
-            totals[k] = totals[k] + pick(sum_k_ref[chunk], rows)
-
-    tile_products(w_ref, parts, o0, o1, after)
-    return totals[0] - f * totals[1]
+    tile_products(w_ref, parts, o0, o1)
+    return pick(sum_k, flat(o0)) - f * pick(sum_k, flat(o1))
 
 
 def need_kernel(cap, *refs):
@@ -152,14 +146,15 @@
     qn = jnp.broadcast_to(qneed_ref[...].astype(f32), (rows, slots)) + float(kb)
     col = jnp.sum(jnp.where(e_here, pn, 0.0) + jnp.where(p_here, qn, 0.0), axis=1, keepdims=True)
     hot = (iota((rows, 128), 1).astype(f32) == col).astype(f32)
-    start_of = (iota((rows, 1), 0) // (2 * cap) * step).astype(f32)
-    list_ref[...] = jnp.where(iota((rows, sent), 1).astype(f32) == col + start_of, 1.0, 0.0).astype(
-        bf16
-    )
-    blank = jnp.zeros((step - kb - qb - 2 * cap, 128), f32)
-    for p in range(peers):
-        lists = jnp.concatenate([hot[p * 2 * cap : (p + 1) * 2 * cap], blank], axis=0)
-        send_ref[p * step : (p + 1) * step] = jnp.concatenate([f, n, lists], axis=0)
+    core = lax.rem(lax.axis_index("bulk"), 2)
+    peer1 = iota((rows, 1), 0) // (2 * cap)
+    start_of = (peer1 // 2 + jnp.where(peer1 % 2 == core, 0, peers // 2)) * step
+    list_ref[...] = jnp.where(
+        iota((rows, sent), 1).astype(f32) == col + start_of.astype(f32), 1.0, 0.0
+    ).astype(bf16)
+    for chip in range(peers // 2):
+        lists = hot[chip * 4 * cap : (chip + 1) * 4 * cap]
+        send_ref[chip * step : (chip + 1) * step] = jnp.concatenate([f, n, lists], axis=0)
 
 
 def tables_kernel(
@@ -183,8 +178,7 @@
     c_ref,
     sems,
 ):
-    copies = chunk_copies(c_hbm, c_ref, sems)
-    start(copies)
+    start_chunks(c_hbm, c_ref, sems)
     tiles = kblock_ref.shape[1]
     kb = f_ref.shape[0]
     used = iota((1, tiles), 1) < count_ref[0]
@@ -195,10 +189,7 @@
     rows8 = sp8_ref.shape[0]
     ind = lambda m: jnp.where(m, 1.0, 0.0)
     k_hot = ind(iota((kb, tiles), 0) == k)
-    sums = jnp.where(used, k_hot, 0.0)
-    width = tiles // CHUNKS
-    for i in range(CHUNKS):
-        sk_ref[i] = sums[:, i * width : (i + 1) * width].astype(bf16)
+    sk_ref[...] = jnp.where(used, k_hot, 0.0).astype(bf16)
     gk_ref[...] = k_hot.T.astype(bf16)
     x = iota((rows4, tiles), 0)
     row_e = (e // cap) * (2 * cap) + e % cap
@@ -218,28 +209,31 @@
         axis=1,
     ).astype(bf16)
     own = pick(gk_ref[...], f_ref[...])
-    backward_pass(own, copies, c_ref, w_ref, b0_ref, b1_ref)
+    backward_pass(own, c_hbm, c_ref, sems, w_ref, b0_ref, b1_ref)
 
 
 def transpose_kernel(after_ref, c_hbm, held_ref, t_hbm, c_ref, t_ref, in_sems, out_sems):
-    copies_in = chunk_copies(c_hbm, c_ref, in_sems)
-    copies_out = chunk_copies(t_ref, t_hbm, out_sems)
-    start(copies_in)
-    held = held_ref.shape[0]
-    size = c_ref.shape[0] // len(copies_in)
-    size_out = t_ref.shape[0] // len(copies_out)
-    for i, copy in enumerate(copies_in):
-        copy.wait()
-        for t in range(i * size, (i + 1) * size):
-            turned = c_ref[t].T
-            if t < held:
-                held_ref[t] = turned
-            else:
-                t_ref[t - held] = turned
-                if (t - held + 1) % size_out == 0:
-                    copies_out[(t - held) // size_out].start()
-    for copy in copies_out:
-        copy.wait()
+    start_chunks(c_hbm, c_ref, in_sems)
+    size = c_ref.shape[0] // in_sems.shape[0]
+    held = held_ref.shape[0] // size
+
+    def to_held(i, _):
+        chunk_copy(c_hbm, c_ref, in_sems, i).wait()
+        for t in range(size):
+            held_ref[i * size + t] = c_ref[i * size + t].T
+        return 0
+
+    def to_rest(i, _):
+        chunk_copy(c_hbm, c_ref, in_sems, held + i).wait()
+        for t in range(size):
+            t_ref[i * size + t] = c_ref[(held + i) * size + t].T
+        chunk_copy(t_ref, t_hbm, out_sems, i).start()
+        return 0
+
+    lax.fori_loop(0, held, to_held, 0)
+    lax.fori_loop(0, out_sems.shape[0], to_rest, 0)
+    for i in range(out_sems.shape[0]):
+        chunk_copy(t_ref, t_hbm, out_sems, i).wait()
 
 
 def serve_kernel(cap, kb, qb, hot_ref, s8_ref, st4_ref, st8a_ref, st8b_ref):
@@ -260,48 +254,37 @@
     st8b_ref[...] = rows_of(2).T[kb : kb + qb].astype(bf16)
 
 
-def first_kernel(
-    cap,
-    state_rows,
-    recv,
-    list_ref,
-    f_ref,
-    ge4_ref,
-    gp4_ref,
-    sk_ref,
-    sp4_ref,
-    b0_ref,
-    b1_ref,
-    held_ref,
-    c_hbm,
-    send,
-    e_ref,
-    f1_ref,
-    *refs,
-):
-    starts = len(refs) == 6
+def first_kernel(cap, state_rows, starts, recv, *refs):
+    other, refs = (refs[0], refs[1:]) if starts else (None, refs)
+    list_ref, f_ref, ge4_ref, gp4_ref, sk_ref, sp4_ref, b0_ref, b1_ref, held_ref, c_hbm = refs[:10]
+    send, e_ref, f1_ref = refs[10:13]
+    hot_ref = refs[13] if starts else None
     w_ref, c_ref, sems, o0, o1 = refs[-5:]
-    copies = chunk_copies(c_hbm, c_ref, sems)
-    start(copies)
+    start_chunks(c_hbm, c_ref, sems)
     f = f_ref[...]
     got = recv[...]
     serve = list_ref[...]
     if starts:
         rows, sent = serve.shape
-        got, every = pick(serve, got), got
+        every = jnp.concatenate([got, other[...]], axis=0)
+        got = pick(serve, every)
         x = iota((rows, sent), 0)
-        step = sent // (rows // (2 * cap))
-        lists_at = x // (2 * cap) * step + state_rows + x % (2 * cap)
+        peers = rows // (2 * cap)
+        step = sent // peers
+        core = lax.rem(lax.axis_index("bulk"), 2)
+        peer = x // (2 * cap)
+        chip_row = (peer // 2 + jnp.where(peer % 2 == core, 0, peers // 2)) * step
+        lists_at = chip_row + state_rows + 2 * cap * core + x % (2 * cap)
         at = jnp.where(iota((rows, sent), 1) == lists_at, 1.0, 0.0).astype(bf16)
         serve = dot(at, every.astype(bf16)).astype(bf16)
-        refs[0][...] = serve
+        hot_ref[...] = serve
     far = pick(ge4_ref[...], got)
     bose = pick(gp4_ref[...], got)
     gain = far * flat(b0_ref)
     terms = gain + bose * (gain - (1.0 - far) * flat(b1_ref))
     phonon_rows = pick(sp4_ref[...], terms)
-    parts = [(held_ref, None), (c_ref, copies)]
-    rate = electron_rate(sk_ref, far, bose, f, parts, w_ref, o0, o1)
+    parts = [(held_ref, None, None), (c_ref, c_hbm, sems)]
+    rate = electron_rate(sk_ref[...], far, bose, f, parts, w_ref, o0, o1)
     f1 = f + DT * rate
     e_ref[...] = rate
     f1_ref[...] = f1
@@ -309,10 +292,9 @@
 
 
 def backward_kernel(f_ref, gk_ref, c_hbm, b0_ref, b1_ref, w_ref, c_ref, sems):
-    copies = chunk_copies(c_hbm, c_ref, sems)
-    start(copies)
+    start_chunks(c_hbm, c_ref, sems)
     own = pick(gk_ref[...], f_ref[...])
-    backward_pass(own, copies, c_ref, w_ref, b0_ref, b1_ref)
+    backward_pass(own, c_hbm, c_ref, sems, w_ref, b0_ref, b1_ref)
 
 
 def phonon_kernel(
@@ -354,8 +336,7 @@
     f2_ref, n2_ref, *refs = refs
     send, refs = (refs[0], refs[1:]) if with_send else (None, refs)
     w_ref, c_ref, sems, o0, o1 = refs
-    copies = chunk_copies(c_hbm, c_ref, sems)
-    start(copies)
+    start_chunks(c_hbm, c_ref, sems)
     got = recv[...]
     n, n1 = n_ref[...], n1_ref[...]
     bose = pick(gp8_ref[...], got)
@@ -367,8 +348,8 @@
     )
     n2 = n + (DT / 2.0) * (p_ref[...] + p1)
     n2_ref[...] = n2
-    parts = [(held_ref, None), (c_ref, copies)]
-    rate = electron_rate(sk_ref, far_ref[...], bose, f1_ref[...], parts, w_ref, o0, o1)
+    parts = [(held_ref, None, None), (c_ref, c_hbm, sems)]
+    rate = electron_rate(sk_ref[...], far_ref[...], bose, f1_ref[...], parts, w_ref, o0, o1)
     f2 = f_ref[...] + (DT / 2.0) * (e_ref[...] + rate)
     f2_ref[...] = f2
     if with_send:
@@ -450,11 +431,12 @@
     ints = ((1, tiles), jnp.int32)
     lists = ((1, partner_need.shape[1]), jnp.int32)
     small = [((kb, 128), f32)] + [((qb, 128), f32)] * 3 + [ints] * 3
-    step_rows = -(-(kb + qb + 2 * cap) // 8) * 8
+    step_rows = kb + qb + 4 * cap
+    assert step_rows % 8 == 0 and devices % 2 == 0
     f, n, energy, decay, kblock, partner, qslot, send, lists_in = call(
         functools.partial(need_kernel, cap),
         "need",
-        small + [((devices * step_rows, 128), f32), ((rows4, devices * step_rows), bf16)],
+        small + [((devices // 2 * step_rows, 128), f32), ((rows4, devices * step_rows), bf16)],
         [pltpu.VMEM(*lists), pltpu.VMEM(*lists), pltpu.SemaphoreType.DMA((9,))],
         spaces={i: pltpu.HBM for i in range(9)},
     )(
@@ -468,7 +450,11 @@
         partner_need,
         phonon_need,
     )
-    recv = exchange(send)
+    same_core = [list(range(core, devices, 2)) for core in (0, 1)]
+    recv = lax.all_to_all(
+        send, "bulk", split_axis=0, concat_axis=0, tiled=True, axis_index_groups=same_core
+    )
+    other = lax.ppermute(recv, "bulk", [(i, i ^ 1) for i in range(devices)])
     c_held, c_rest = call(
         transpose_kernel,
         "transpose",
@@ -486,7 +472,7 @@
             ((tiles, rows4), bf16),
             ((tiles, rows8), bf16),
             ((tiles, kb), bf16),
-            ((CHUNKS, kb, tiles // CHUNKS), bf16),
+            ((kb, tiles), bf16),
             ((rows4, tiles), bf16),
             ((rows8, 2 * tiles), bf16),
         ]
@@ -500,14 +486,15 @@
         if step:
             recv = exchange(send)
             b0, b1 = back(f, gk, coupling)
+        lists = (serve,) if step else (other, lists_in)
         send, e0, f1, *hot = call(
-            functools.partial(first_kernel, cap, kb + qb),
+            functools.partial(first_kernel, cap, kb + qb, not step),
             "first",
             [block4] + [((kb, 128), f32)] * 2 + ([] if step else [((rows4, 128), bf16)]),
             forward_streams + sums,
-            spaces={10: pltpu.HBM},
+            spaces={9 + len(lists): pltpu.HBM},
             **work,
-        )(recv, serve if step else lists_in, f, ge4, gp4, sk, sp4, b0, b1, c_held, c_rest)
+        )(recv, *lists, f, ge4, gp4, sk, sp4, b0, b1, c_held, c_rest)
         if not step:
             serve = hot[0]
             s8, st4, st8a, st8b = call(

time: 93.6 us -> 96.2 us (1.028)
  blocking collectives: 20 us -> 35.5 us
  starting transfers between devices: 18.4 us -> 10.5 us
  waiting for transfers between devices: 11.1 us -> 8.24 us
  Pallas kernels: 41.9 us -> 40.1 us
    all_to_all x0 -> x1, blocking collectives: none -> 15.5 us  [on_device(): lax.all_to_all(send, 'bulk', split_axis=0, concat_axis=0, tiled=True, axi...]
    all_to_all x4 -> x3, starting transfers between devices: 18.4 us -> 10.5 us  [exchange(): return lax.all_to_all(x, 'bulk', split_axis=0, concat_axis=0, tiled=True)]
    all_to_all x4 -> x3, waiting for transfers between devices: 11.1 us -> 8.24 us  [exchange(): return lax.all_to_all(x, 'bulk', split_axis=0, concat_axis=0, tiled=True)]
    pallas_call x13, Pallas kernels: 41.9 us -> 40.1 us  [run(): pl.pallas_call(kernel, out_shape=[pltpu.HBM(*o) if (out_spaces or {}).get...]
  transfers between devices with their start and end apart: 4 -> 4, of which waited for: 4 -> 3; matrix products, arithmetic and copies ran while one was open for 0% -> 0% of each run, Pallas kernels for 23% -> 22%
where the time goes in v7:
time: 96.2 us; the launch traced here: 95.8 us
  Pallas kernels  40.1 us (42%)
  blocking collectives  35.5 us (37%)
  starting transfers between devices  10.5 us (11%)
  waiting for transfers between devices  8.24 us (9%)
  between operations  1.41 us (1%)
    pallas_call x13, Pallas kernels, run(): pl.pallas_call(kernel, out_shape=[pltpu.HBM(*o) if (out_spaces or {}).get...  40.1 us
    all_to_all x2, blocking collectives, exchange(): return lax.all_to_all(x, 'bulk', split_axis=0, concat_axis=0, tiled=True)  20 us
    all_to_all x1, blocking collectives, on_device(): lax.all_to_all(send, 'bulk', split_axis=0, concat_axis=0, tiled=True, axi...  15.5 us
    all_to_all x3, starting transfers between devices, exchange(): return lax.all_to_all(x, 'bulk', split_axis=0, concat_axis=0, tiled=True)  10.5 us
    all_to_all x3, waiting for transfers between devices, exchange(): return lax.all_to_all(x, 'bulk', split_axis=0, concat_axis=0, tiled=True)  8.24 us
  transfers between devices with their start and end apart: 4, of which 3 were waited for; matrix products, arithmetic and copies ran while one was open for 0% of the time, Pallas kernels for 22%

profile of v7, /device:TPU:0, one launch (start us, length us, event | category | flops | bytes accessed | tf_op | source)
XLA Modules:
  0.0 95.8 jit_solution(13377996972882485306)
XLA Ops:
  0.6 1.0 %need.1 = (f32[32,128]{1,0:T(8,128)S(1)}, f32[16,128]{1,0:T(8,128)S(1)}, f32[16,128]{1,0:T(8,128)S(1)}, f32[16,128]{1,0:T(8,128)S(1)}, s32[1,256]{1,0:T(1,128)S(...) custom-call(f32[32,128]{1,0:T(8,128)} %refs_0_.1, ...), custom_call_target="tpu_custom_call" | custom-call | tf_op jit(solution)/shard_map/need/pallas_call | solution.py:371
  1.6 15.5 %all_to_all.66 = f32[8,56,128]{2,1,0:T(8,128)S(1)} all-to-all(f32[8,56,128]{2,1,0:T(8,128)S(1)} %bitcast.19), channel_id=1, replica_groups={{0,2,4,6,8,10,12,14},{1,3,5,7,9,11,13,15},{16,18,20,22,24,26,28,30},{17..., dimensions={0} | all-to-all | bytes 458752 | tf_op jit(solution)/shard_map/all_to_all | solution.py:454
  17.1 0.0 collective-permute-start
  17.8 5.5 %transpose.1 = (bf16[64,128,128]{2,1,0:T(8,128)(2,1)S(1)}, bf16[192,128,128]{2,1,0:T(8,128)(2,1)}) custom-call(f32[32,128]{1,0:T(8,128)S(1)} %get-tuple-element.52.f_ref.after_ref.refs_2_.refs_1_, bf16[256,128,128]{2,1,0:T(8,128)(2,1)} %c_hbm.9), custom_call_target="tpu_custom_call" | custom-call | flops 134217728 | bytes 8388608 | tf_op jit(solution)/shard_map/transpose/pallas_call | solution.py:371
  23.3 3.9 %tables.1 = (bf16[256,64]{1,0:T(8,128)(2,1)S(1)}, bf16[256,64]{1,0:T(8,128)(2,1)S(1)}, bf16[256,128]{1,0:T(8,128)(2,1)S(1)}, bf16[256,32]{1,0:T(8,128)(2,1)S(1)}...) custom-call(s32[1]{0:T(128)S(6)} %copy.13.count_ref, ...), custom_call_target="tpu_custom_call" | custom-call | flops 134217728 | bytes 8388608 | tf_op jit(solution)/shard_map/tables/pallas_call | solution.py:371
  27.2 0.0 collective-permute-done.refs_0_
  27.2 4.7 %first.2 = (f32[64,128]{1,0:T(8,128)}, f32[32,128]{1,0:T(8,128)S(1)}, f32[32,128]{1,0:T(8,128)S(1)}, bf16[64,128]{1,0:T(8,128)(2,1)S(1)}) custom-call(f32[448,128]{1,0:T(8,128)S(1)} %bitcast.16, f32[448,128]{1,0:T(8,128)S(1)} %collective-permute-done.refs_0_, bf16[64,896]{1,0:T(8,128)(2,1)S(1)} %get-tuple-element.51.refs_1_, ...), custom_call_target="tpu_custom_call" | custom-call | flops 134217728 | bytes 8388608 | tf_op jit(solution)/shard_map/first/pallas_call | solution.py:371
  31.9 3.6 %all-to-all-start.1 = ((f32[16,4,128]{2,1,0:T(4,128)}), f32[16,4,128]{2,1,0:T(4,128)S(1)}, u32[]{:S(2)}, u32[]{:S(2)}) async-start(f32[16,4,128]{2,1,0:T(4,128)} %bitcast.5), calls=%async_computation.1 | async-start | bytes 65536 | tf_op jit(solution)/shard_map/all_to_all | solution.py:429
  35.5 0.2 serve.1
  35.7 3.8 %backward.3 = (f32[32,8,128]{2,1,0:T(8,128)S(1)}, f32[32,8,128]{2,1,0:T(8,128)S(1)}) custom-call(f32[32,128]{1,0:T(8,128)S(1)} %get-tuple-element.72.f_ref.refs_2_, bf16[256,32]{1,0:T(8,128)(2,1)S(1)} %get-tuple-element.73.gk_ref, bf16[256,128,128]{2,1,0:T(8,128)(2,1)} %c_hbm.9), custom_call_target="tpu_custom_call" | custom-call | flops 134217728 | bytes 8388608 | tf_op jit(solution)/shard_map/backward/pallas_call | solution.py:371
  39.5 2.6 %all-to-all-done.1 = f32[16,4,128]{2,1,0:T(4,128)S(1)} async-done(((f32[16,4,128]{2,1,0:T(4,128)}), f32[16,4,128]{2,1,0:T(4,128)S(1)}, u32[]{:S(2)}, u32[]{:S(2)}) %all-to-all-start.1) | async-done | bytes 32800 | tf_op jit(solution)/shard_map/all_to_all | solution.py:429
  42.1 0.5 phonon.2
  42.6 10.1 %all_to_all.67 = f32[16,8,128]{2,1,0:T(8,128)S(1)} all-to-all(f32[16,8,128]{2,1,0:T(8,128)S(1)} %bitcast.24), channel_id=1, replica_groups=mesh['groups'=2,'bulk'=16] {'bulk'}, dimensions={0} | all-to-all | bytes 131072 | tf_op jit(solution)/shard_map/all_to_all | solution.py:429
  52.7 4.2 %second.2 = (f32[32,128]{1,0:T(8,128)S(1)}, f32[16,128]{1,0:T(8,128)S(1)}, f32[64,128]{1,0:T(8,128)}) custom-call(f32[128,128]{1,0:T(8,128)S(1)} %bitcast.18, f32[256,128]{1,0:T(8,128)S(1)} %get-tuple-element.77.refs_0_, f32[32,128]{1,0:T(8,128)S(1)} %get-tuple-element.52.f_ref.after_ref.refs_2_.refs_1_, f32[32,128]{1,0:T(8,128)S(1)} %get-tuple-element.72.f_ref.refs_2_, ...), custom_call_target="tpu_custom_call" | custom-call | flops 134217728 | bytes 8388608 | tf_op jit(solution)/shard_map/second/pallas_call | solution.py:371
  56.9 3.5 %all-to-all-start.3 = ((f32[16,4,128]{2,1,0:T(4,128)}), f32[16,4,128]{2,1,0:T(4,128)S(1)}, u32[]{:S(2)}, u32[]{:S(2)}) async-start(f32[16,4,128]{2,1,0:T(4,128)} %bitcast.9), calls=%async_computation.3 | async-start | bytes 65536 | tf_op jit(solution)/shard_map/all_to_all | solution.py:429
  60.4 3.8 %backward.4 = (f32[32,8,128]{2,1,0:T(8,128)S(1)}, f32[32,8,128]{2,1,0:T(8,128)S(1)}) custom-call(f32[32,128]{1,0:T(8,128)S(1)} %get-tuple-element.85.f_ref.refs_1_, bf16[256,32]{1,0:T(8,128)(2,1)S(1)} %get-tuple-element.73.gk_ref, bf16[256,128,128]{2,1,0:T(8,128)(2,1)} %c_hbm.9), custom_call_target="tpu_custom_call" | custom-call | flops 134217728 | bytes 8388608 | tf_op jit(solution)/shard_map/backward/pallas_call | solution.py:371
  64.1 2.8 %all-to-all-done.3 = f32[16,4,128]{2,1,0:T(4,128)S(1)} async-done(((f32[16,4,128]{2,1,0:T(4,128)}), f32[16,4,128]{2,1,0:T(4,128)S(1)}, u32[]{:S(2)}, u32[]{:S(2)}) %all-to-all-start.3) | async-done | bytes 32800 | tf_op jit(solution)/shard_map/all_to_all | solution.py:429
  67.0 4.4 %first.3 = (f32[64,128]{1,0:T(8,128)}, f32[32,128]{1,0:T(8,128)S(1)}, f32[32,128]{1,0:T(8,128)S(1)}) custom-call(f32[64,128]{1,0:T(8,128)S(1)} %bitcast.20, bf16[64,128]{1,0:T(8,128)(2,1)S(1)} %get-tuple-element.68.hot_ref.refs_13_.refs_0_, f32[32,128]{1,0:T(8,128)S(1)} %get-tuple-element.85.f_ref.refs_1_, ...), custom_call_target="tpu_custom_call" | custom-call | flops 134217728 | bytes 8388608 | tf_op jit(solution)/shard_map/first/pallas_call | solution.py:371
  71.4 3.5 %all-to-all-start.4 = ((f32[16,4,128]{2,1,0:T(4,128)}), f32[16,4,128]{2,1,0:T(4,128)S(1)}, u32[]{:S(2)}, u32[]{:S(2)}) async-start(f32[16,4,128]{2,1,0:T(4,128)} %bitcast.11), calls=%async_computation.4 | async-start | bytes 65536 | tf_op jit(solution)/shard_map/all_to_all | solution.py:429
  74.8 3.8 %backward.5 = (f32[32,8,128]{2,1,0:T(8,128)S(1)}, f32[32,8,128]{2,1,0:T(8,128)S(1)}) custom-call(f32[32,128]{1,0:T(8,128)S(1)} %get-tuple-element.90.f_ref.refs_2_, bf16[256,32]{1,0:T(8,128)(2,1)S(1)} %get-tuple-element.73.gk_ref, bf16[256,128,128]{2,1,0:T(8,128)(2,1)} %c_hbm.9), custom_call_target="tpu_custom_call" | custom-call | flops 134217728 | bytes 8388608 | tf_op jit(solution)/shard_map/backward/pallas_call | solution.py:371
  78.6 2.8 %all-to-all-done.4 = f32[16,4,128]{2,1,0:T(4,128)S(1)} async-done(((f32[16,4,128]{2,1,0:T(4,128)}), f32[16,4,128]{2,1,0:T(4,128)S(1)}, u32[]{:S(2)}, u32[]{:S(2)}) %all-to-all-start.4) | async-done | bytes 32800 | tf_op jit(solution)/shard_map/all_to_all | solution.py:429
  81.4 0.5 phonon.3
  81.9 9.9 %all_to_all.68 = f32[16,8,128]{2,1,0:T(8,128)S(1)} all-to-all(f32[16,8,128]{2,1,0:T(8,128)S(1)} %bitcast.23), channel_id=1, replica_groups=mesh['groups'=2,'bulk'=16] {'bulk'}, dimensions={0} | all-to-all | bytes 131072 | tf_op jit(solution)/shard_map/all_to_all | solution.py:429
  91.7 4.0 %second.3 = (f32[32,128]{1,0:T(8,128)}, f32[16,128]{1,0:T(8,128)}) custom-call(f32[128,128]{1,0:T(8,128)S(1)} %bitcast.17, f32[256,128]{1,0:T(8,128)S(1)} %get-tuple-element.94.refs_0_, f32[32,128]{1,0:T(8,128)S(1)} %get-tuple-element.85.f_ref.refs_1_, f32[32,128]{1,0:T(8,128)S(1)} %get-tuple-element.90.f_ref.refs_2_, ...), custom_call_target="tpu_custom_call" | custom-call | flops 134217728 | bytes 8388608 | tf_op jit(solution)/shard_map/second/pallas_call | solution.py:371
Async XLA Ops:
  17.1 10.1 %collective-permute-start = (f32[448,128]{1,0:T(8,128)S(1)}, f32[448,128]{1,0:T(8,128)S(1)}, u32[]{:S(2)}, u32[]{:S(2)}) collective-permute-start(f32[448,128]{1,0:T(8,128)S(1)} %bitcast.15), channel_id=1, source_target_pairs={{0,1},{1,0},{2,3},{3,2},{4,5},{5,4},{6,7},{7,6},{8,9},{9,8},{10,11... | collective-permute-start | bytes 688136 | tf_op jit(solution)/shard_map/ppermute | solution.py:457
  31.9 10.2 %all-to-all-start.1 = ((f32[16,4,128]{2,1,0:T(4,128)}), f32[16,4,128]{2,1,0:T(4,128)S(1)}, u32[]{:S(2)}, u32[]{:S(2)}) async-start(f32[16,4,128]{2,1,0:T(4,128)} %bitcast.5), calls=%async_computation.1 | async-start | bytes 65536 | tf_op jit(solution)/shard_map/all_to_all | solution.py:429
  56.9 10.1 %all-to-all-start.3 = ((f32[16,4,128]{2,1,0:T(4,128)}), f32[16,4,128]{2,1,0:T(4,128)S(1)}, u32[]{:S(2)}, u32[]{:S(2)}) async-start(f32[16,4,128]{2,1,0:T(4,128)} %bitcast.9), calls=%async_computation.3 | async-start | bytes 65536 | tf_op jit(solution)/shard_map/all_to_all | solution.py:429
  71.4 10.1 %all-to-all-start.4 = ((f32[16,4,128]{2,1,0:T(4,128)}), f32[16,4,128]{2,1,0:T(4,128)S(1)}, u32[]{:S(2)}, u32[]{:S(2)}) async-start(f32[16,4,128]{2,1,0:T(4,128)} %bitcast.11), calls=%async_computation.4 | async-start | bytes 65536 | tf_op jit(solution)/shard_map/all_to_all | solution.py:429

commit v8 on v7

--- a/solution.py
+++ b/solution.py
@@ -80,8 +80,17 @@
     )
 
 
+def left_sides(first, second, w_ref):
+    tiles = first.shape[0]
+    w = stacked(first, second)
+    for p in range(tiles // 16):
+        w_ref[p] = jnp.concatenate(
+            [block_diagonal(w[2 * p]), block_diagonal(w[2 * p + 1])], axis=0
+        )
+
+
 def tile_products(w_ref, parts, out0, out1):
-    size = w_ref.shape[0] // CHUNKS
+    size = 2 * w_ref.shape[0] // CHUNKS
     base = 0
     for c_ref, c_hbm, sems in parts:
         groups = c_ref.shape[0] // 8
@@ -92,13 +101,10 @@
             for k in range(0, size, 2):
                 g = i * size + k
                 at = base + g
-                lhs = jnp.concatenate(
-                    [block_diagonal(w_ref[at]), block_diagonal(w_ref[at + 1])], axis=0
-                )
                 rhs = jnp.concatenate(
                     [c_ref[pl.ds((g + j) * 8, 8)].reshape(1024, 128) for j in (0, 1)], axis=1
                 )
-                res = dot(lhs, rhs)
+                res = dot(w_ref[at // 2], rhs)
                 for j in (0, 1):
                     own = res[16 * j : 16 * (j + 1), 128 * j : 128 * (j + 1)]
                     out0[at + j] = own[:8]
@@ -110,12 +116,12 @@
 
 
 def backward_pass(own, c_hbm, c_ref, sems, w_ref, out0, out1):
-    w_ref[...] = stacked(1.0 - own, own)
+    left_sides(1.0 - own, own, w_ref)
     tile_products(w_ref, [(c_ref, c_hbm, sems)], out0, out1)
 
 
 def electron_rate(sum_k, far, bose, f, parts, w_ref, o0, o1):
-    w_ref[...] = stacked(far * (1.0 + bose), far + bose)
+    left_sides(far * (1.0 + bose), far + bose, w_ref)
     tile_products(w_ref, parts, o0, o1)
     return pick(sum_k, flat(o0)) - f * pick(sum_k, flat(o1))
 
@@ -413,7 +419,7 @@
     rows8 = devices * 4 * cap
     groups = tiles // 8
     held = HELD_CHUNKS * (tiles // CHUNKS)
-    weights = pltpu.VMEM((groups, 16, 128), bf16)
+    weights = pltpu.VMEM((groups // 2, 32, 1024), bf16)
     streams = [weights, pltpu.VMEM(coupling.shape, bf16), pltpu.SemaphoreType.DMA((CHUNKS,))]
     rest = (tiles - held, 128, 128)
     rest_sems = pltpu.SemaphoreType.DMA((CHUNKS - HELD_CHUNKS,))
@@ -454,7 +460,6 @@
     recv = lax.all_to_all(
         send, "bulk", split_axis=0, concat_axis=0, tiled=True, axis_index_groups=same_core
     )
-    other = lax.ppermute(recv, "bulk", [(i, i ^ 1) for i in range(devices)])
     c_held, c_rest = call(
         transpose_kernel,
         "transpose",
@@ -481,6 +486,8 @@
         spaces={0: pltpu.SMEM, 5: pltpu.HBM},
         **work,
     )(tile_count, kblock, partner, qslot, f, coupling)
+    recv, c_held, b0 = lax.optimization_barrier((recv, c_held, b0))
+    other = lax.ppermute(recv, "bulk", [(i, i ^ 1) for i in range(devices)])
     back = call(backward_kernel, "backward", pass_out, streams, spaces={2: pltpu.HBM}, **work)
     for step in range(STEPS):
         if step:

time: 96.2 us -> 93 us (0.967)
  blocking collectives: 35.5 us -> 20 us
  starting transfers between devices: 10.5 us -> 20.5 us
  waiting for transfers between devices: 8.24 us -> 9.72 us
    all_to_all x1 -> x0, blocking collectives: 15.5 us -> none  [on_device(): lax.all_to_all(send, 'bulk', split_axis=0, concat_axis=0, tiled=True, axi...]
    all_to_all x0 -> x1, starting transfers between devices: none -> 7.29 us  [on_device(): lax.all_to_all(send, 'bulk', split_axis=0, concat_axis=0, tiled=True, axi...]
    all_to_all x3, starting transfers between devices: 10.5 us -> 13.1 us  [exchange(): return lax.all_to_all(x, 'bulk', split_axis=0, concat_axis=0, tiled=True)]
    ppermute x1, waiting for transfers between devices: 0.01 us -> 1.48 us  [on_device(): other = lax.ppermute(recv, 'bulk', [(i, i ^ 1) for i in range(devices)])]
  transfers between devices with their start and end apart: 4 -> 5, of which waited for: 3 -> 4; matrix products, arithmetic and copies ran while one was open for 0% -> 0% of each run, Pallas kernels for 22% -> 23%
where the time goes in v8:
time: 93 us; the launch traced here: 92.5 us
  Pallas kernels  40.9 us (44%)
  starting transfers between devices  20.5 us (22%)
  blocking collectives  20 us (22%)
  waiting for transfers between devices  9.72 us (10%)
  between operations  1.42 us (2%)
    pallas_call x13, Pallas kernels, run(): pl.pallas_call(kernel, out_shape=[pltpu.HBM(*o) if (out_spaces or {}).get...  40.9 us
    all_to_all x2, blocking collectives, exchange(): return lax.all_to_all(x, 'bulk', split_axis=0, concat_axis=0, tiled=True)  20 us
    all_to_all x3, starting transfers between devices, exchange(): return lax.all_to_all(x, 'bulk', split_axis=0, concat_axis=0, tiled=True)  13.1 us
    all_to_all x3, waiting for transfers between devices, exchange(): return lax.all_to_all(x, 'bulk', split_axis=0, concat_axis=0, tiled=True)  8.24 us
    all_to_all x1, starting transfers between devices, on_device(): lax.all_to_all(send, 'bulk', split_axis=0, concat_axis=0, tiled=True, axi...  7.29 us
  transfers between devices with their start and end apart: 5, of which 4 were waited for; matrix products, arithmetic and copies ran while one was open for 0% of the time, Pallas kernels for 23%

profile of v8, /device:TPU:0, one launch (start us, length us, event | category | flops | bytes accessed | tf_op | source)
XLA Modules:
  0.0 92.5 jit_solution(885381897348049973)
XLA Ops:
  0.6 1.7 %need.1 = (f32[32,128]{1,0:T(8,128)S(1)}, f32[16,128]{1,0:T(8,128)S(1)}, f32[16,128]{1,0:T(8,128)S(1)}, f32[16,128]{1,0:T(8,128)S(1)}, s32[1,256]{1,0:T(1,128)S(...) custom-call(f32[32,128]{1,0:T(8,128)} %refs_0_.1, ...), custom_call_target="tpu_custom_call" | custom-call | tf_op jit(solution)/shard_map/need/pallas_call | solution.py:377
  2.3 7.3 %all-to-all-start = ((f32[8,56,128]{2,1,0:T(8,128)}), f32[8,56,128]{2,1,0:T(8,128)S(1)}, u32[]{:S(2)}, u32[]{:S(2)}) async-start(f32[8,56,128]{2,1,0:T(8,128)} %bitcast.3), calls=%async_computation | async-start | bytes 458752 | tf_op jit(solution)/shard_map/all_to_all | solution.py:460
  10.3 5.5 %transpose.1 = (bf16[64,128,128]{2,1,0:T(8,128)(2,1)S(1)}, bf16[192,128,128]{2,1,0:T(8,128)(2,1)}) custom-call(f32[32,128]{1,0:T(8,128)S(1)} %get-tuple-element.54.after_ref.f_ref.refs_2_.refs_1_, bf16[256,128,128]{2,1,0:T(8,128)(2,1)} %c_hbm.9), custom_call_target="tpu_custom_call" | custom-call | flops 134217728 | bytes 8388608 | tf_op jit(solution)/shard_map/transpose/pallas_call | solution.py:377
  15.8 3.8 %tables.1 = (bf16[256,64]{1,0:T(8,128)(2,1)S(1)}, bf16[256,64]{1,0:T(8,128)(2,1)S(1)}, bf16[256,128]{1,0:T(8,128)(2,1)S(1)}, bf16[256,32]{1,0:T(8,128)(2,1)S(1)}...) custom-call(s32[1]{0:T(128)S(6)} %copy.13.count_ref, ...), custom_call_target="tpu_custom_call" | custom-call | flops 134217728 | bytes 8388608 | tf_op jit(solution)/shard_map/tables/pallas_call | solution.py:377
  19.6 0.0 all-to-all-done
  19.6 0.1 collective-permute-start
  19.7 1.5 %collective-permute-done.refs_0_ = f32[448,128]{1,0:T(8,128)S(1)} collective-permute-done((f32[448,128]{1,0:T(8,128)S(1)}, f32[448,128]{1,0:T(8,128)S(1)}, u32[]{:S(2)}, u32[]{:S(2)}) %collective-permute-start) | collective-permute-done | bytes 229408 | tf_op jit(solution)/shard_map/ppermute | solution.py:490
  21.1 4.8 %first.2 = (f32[64,128]{1,0:T(8,128)}, f32[32,128]{1,0:T(8,128)S(1)}, f32[32,128]{1,0:T(8,128)S(1)}, bf16[64,128]{1,0:T(8,128)(2,1)S(1)}) custom-call(f32[448,128]{1,0:T(8,128)S(1)} %bitcast.16, f32[448,128]{1,0:T(8,128)S(1)} %collective-permute-done.refs_0_, bf16[64,896]{1,0:T(8,128)(2,1)S(1)} %get-tuple-element.61.refs_1_, ...), custom_call_target="tpu_custom_call" | custom-call | flops 134217728 | bytes 8388608 | tf_op jit(solution)/shard_map/first/pallas_call | solution.py:377
  25.9 6.1 %all-to-all-start.1 = ((f32[16,4,128]{2,1,0:T(4,128)}), f32[16,4,128]{2,1,0:T(4,128)S(1)}, u32[]{:S(2)}, u32[]{:S(2)}) async-start(f32[16,4,128]{2,1,0:T(4,128)} %bitcast.5), calls=%async_computation.1 | async-start | bytes 65536 | tf_op jit(solution)/shard_map/all_to_all | solution.py:435
  32.0 0.2 serve.1
  32.2 3.8 %backward.3 = (f32[32,8,128]{2,1,0:T(8,128)S(1)}, f32[32,8,128]{2,1,0:T(8,128)S(1)}) custom-call(f32[32,128]{1,0:T(8,128)S(1)} %get-tuple-element.78.f_ref.refs_2_, bf16[256,32]{1,0:T(8,128)(2,1)S(1)} %get-tuple-element.79.gk_ref, bf16[256,128,128]{2,1,0:T(8,128)(2,1)} %c_hbm.9), custom_call_target="tpu_custom_call" | custom-call | flops 134217728 | bytes 8388608 | tf_op jit(solution)/shard_map/backward/pallas_call | solution.py:377
  36.1 2.6 %all-to-all-done.1 = f32[16,4,128]{2,1,0:T(4,128)S(1)} async-done(((f32[16,4,128]{2,1,0:T(4,128)}), f32[16,4,128]{2,1,0:T(4,128)S(1)}, u32[]{:S(2)}, u32[]{:S(2)}) %all-to-all-start.1) | async-done | bytes 32800 | tf_op jit(solution)/shard_map/all_to_all | solution.py:435
  38.7 0.5 phonon.2
  39.1 10.1 %all_to_all.67 = f32[16,8,128]{2,1,0:T(8,128)S(1)} all-to-all(f32[16,8,128]{2,1,0:T(8,128)S(1)} %bitcast.23), channel_id=1, replica_groups=mesh['groups'=2,'bulk'=16] {'bulk'}, dimensions={0} | all-to-all | bytes 131072 | tf_op jit(solution)/shard_map/all_to_all | solution.py:435
  49.2 4.2 %second.2 = (f32[32,128]{1,0:T(8,128)S(1)}, f32[16,128]{1,0:T(8,128)S(1)}, f32[64,128]{1,0:T(8,128)}) custom-call(f32[128,128]{1,0:T(8,128)S(1)} %bitcast.18, f32[256,128]{1,0:T(8,128)S(1)} %get-tuple-element.83.refs_0_, f32[32,128]{1,0:T(8,128)S(1)} %get-tuple-element.54.after_ref.f_ref.refs_2_.refs_1_, f32[32,128]{1,0:T(8,128)S(1)} %get-tuple-element.78.f_ref.refs_2_, ...), custom_call_target="tpu_custom_call" | custom-call | flops 134217728 | bytes 8388608 | tf_op jit(solution)/shard_map/second/pallas_call | solution.py:377
  53.5 3.5 %all-to-all-start.3 = ((f32[16,4,128]{2,1,0:T(4,128)}), f32[16,4,128]{2,1,0:T(4,128)S(1)}, u32[]{:S(2)}, u32[]{:S(2)}) async-start(f32[16,4,128]{2,1,0:T(4,128)} %bitcast.9), calls=%async_computation.3 | async-start | bytes 65536 | tf_op jit(solution)/shard_map/all_to_all | solution.py:435
  57.0 3.8 %backward.4 = (f32[32,8,128]{2,1,0:T(8,128)S(1)}, f32[32,8,128]{2,1,0:T(8,128)S(1)}) custom-call(f32[32,128]{1,0:T(8,128)S(1)} %get-tuple-element.91.f_ref.refs_1_, bf16[256,32]{1,0:T(8,128)(2,1)S(1)} %get-tuple-element.79.gk_ref, bf16[256,128,128]{2,1,0:T(8,128)(2,1)} %c_hbm.9), custom_call_target="tpu_custom_call" | custom-call | flops 134217728 | bytes 8388608 | tf_op jit(solution)/shard_map/backward/pallas_call | solution.py:377
  60.7 2.8 %all-to-all-done.3 = f32[16,4,128]{2,1,0:T(4,128)S(1)} async-done(((f32[16,4,128]{2,1,0:T(4,128)}), f32[16,4,128]{2,1,0:T(4,128)S(1)}, u32[]{:S(2)}, u32[]{:S(2)}) %all-to-all-start.3) | async-done | bytes 32800 | tf_op jit(solution)/shard_map/all_to_all | solution.py:435
  63.5 4.5 %first.3 = (f32[64,128]{1,0:T(8,128)}, f32[32,128]{1,0:T(8,128)S(1)}, f32[32,128]{1,0:T(8,128)S(1)}) custom-call(f32[64,128]{1,0:T(8,128)S(1)} %bitcast.19, bf16[64,128]{1,0:T(8,128)(2,1)S(1)} %get-tuple-element.74.hot_ref.refs_13_.refs_0_, f32[32,128]{1,0:T(8,128)S(1)} %get-tuple-element.91.f_ref.refs_1_, ...), custom_call_target="tpu_custom_call" | custom-call | flops 134217728 | bytes 8388608 | tf_op jit(solution)/shard_map/first/pallas_call | solution.py:377
  68.0 3.5 %all-to-all-start.4 = ((f32[16,4,128]{2,1,0:T(4,128)}), f32[16,4,128]{2,1,0:T(4,128)S(1)}, u32[]{:S(2)}, u32[]{:S(2)}) async-start(f32[16,4,128]{2,1,0:T(4,128)} %bitcast.11), calls=%async_computation.4 | async-start | bytes 65536 | tf_op jit(solution)/shard_map/all_to_all | solution.py:435
  71.5 3.8 %backward.5 = (f32[32,8,128]{2,1,0:T(8,128)S(1)}, f32[32,8,128]{2,1,0:T(8,128)S(1)}) custom-call(f32[32,128]{1,0:T(8,128)S(1)} %get-tuple-element.96.f_ref.refs_2_, bf16[256,32]{1,0:T(8,128)(2,1)S(1)} %get-tuple-element.79.gk_ref, bf16[256,128,128]{2,1,0:T(8,128)(2,1)} %c_hbm.9), custom_call_target="tpu_custom_call" | custom-call | flops 134217728 | bytes 8388608 | tf_op jit(solution)/shard_map/backward/pallas_call | solution.py:377
  75.3 2.8 %all-to-all-done.4 = f32[16,4,128]{2,1,0:T(4,128)S(1)} async-done(((f32[16,4,128]{2,1,0:T(4,128)}), f32[16,4,128]{2,1,0:T(4,128)S(1)}, u32[]{:S(2)}, u32[]{:S(2)}) %all-to-all-start.4) | async-done | bytes 32800 | tf_op jit(solution)/shard_map/all_to_all | solution.py:435
  78.1 0.5 phonon.3
  78.6 9.9 %all_to_all.68 = f32[16,8,128]{2,1,0:T(8,128)S(1)} all-to-all(f32[16,8,128]{2,1,0:T(8,128)S(1)} %bitcast.22), channel_id=1, replica_groups=mesh['groups'=2,'bulk'=16] {'bulk'}, dimensions={0} | all-to-all | bytes 131072 | tf_op jit(solution)/shard_map/all_to_all | solution.py:435
  88.5 4.0 %second.3 = (f32[32,128]{1,0:T(8,128)}, f32[16,128]{1,0:T(8,128)}) custom-call(f32[128,128]{1,0:T(8,128)S(1)} %bitcast.17, f32[256,128]{1,0:T(8,128)S(1)} %get-tuple-element.100.refs_0_, f32[32,128]{1,0:T(8,128)S(1)} %get-tuple-element.91.f_ref.refs_1_, f32[32,128]{1,0:T(8,128)S(1)} %get-tuple-element.96.f_ref.refs_2_, ...), custom_call_target="tpu_custom_call" | custom-call | flops 134217728 | bytes 8388608 | tf_op jit(solution)/shard_map/second/pallas_call | solution.py:377
Async XLA Ops:
  2.3 17.3 %all-to-all-start = ((f32[8,56,128]{2,1,0:T(8,128)}), f32[8,56,128]{2,1,0:T(8,128)S(1)}, u32[]{:S(2)}, u32[]{:S(2)}) async-start(f32[8,56,128]{2,1,0:T(8,128)} %bitcast.3), calls=%async_computation | async-start | bytes 458752 | tf_op jit(solution)/shard_map/all_to_all | solution.py:460
  19.6 1.6 %collective-permute-start = (f32[448,128]{1,0:T(8,128)S(1)}, f32[448,128]{1,0:T(8,128)S(1)}, u32[]{:S(2)}, u32[]{:S(2)}) collective-permute-start(f32[448,128]{1,0:T(8,128)S(1)} %bitcast.15), channel_id=1, source_target_pairs={{0,1},{1,0},{2,3},{3,2},{4,5},{5,4},{6,7},{7,6},{8,9},{9,8},{10,11... | collective-permute-start | bytes 688136 | tf_op jit(solution)/shard_map/ppermute | solution.py:490
  25.9 12.8 %all-to-all-start.1 = ((f32[16,4,128]{2,1,0:T(4,128)}), f32[16,4,128]{2,1,0:T(4,128)S(1)}, u32[]{:S(2)}, u32[]{:S(2)}) async-start(f32[16,4,128]{2,1,0:T(4,128)} %bitcast.5), calls=%async_computation.1 | async-start | bytes 65536 | tf_op jit(solution)/shard_map/all_to_all | solution.py:435
  53.5 10.1 %all-to-all-start.3 = ((f32[16,4,128]{2,1,0:T(4,128)}), f32[16,4,128]{2,1,0:T(4,128)S(1)}, u32[]{:S(2)}, u32[]{:S(2)}) async-start(f32[16,4,128]{2,1,0:T(4,128)} %bitcast.9), calls=%async_computation.3 | async-start | bytes 65536 | tf_op jit(solution)/shard_map/all_to_all | solution.py:435
  68.0 10.1 %all-to-all-start.4 = ((f32[16,4,128]{2,1,0:T(4,128)}), f32[16,4,128]{2,1,0:T(4,128)S(1)}, u32[]{:S(2)}, u32[]{:S(2)}) async-start(f32[16,4,128]{2,1,0:T(4,128)} %bitcast.11), calls=%async_computation.4 | async-start | bytes 65536 | tf_op jit(solution)/shard_map/all_to_all | solution.py:435

commit v9 on v8

--- a/solution.py
+++ b/solution.py
@@ -7,13 +7,12 @@
 from jax.experimental.pallas import tpu as pltpu
 from jax.sharding import PartitionSpec as P
 
-STEPS = 2
 DT = 0.05
 CHUNKS = 8
 HELD_CHUNKS = 2
 f32 = jnp.float32
 bf16 = jnp.bfloat16
-VMEM_LIMIT = 24 * 1024 * 1024
+VMEM_LIMIT = 48 * 1024 * 1024
 
 
 def iota(shape, dim):
@@ -89,6 +88,21 @@
         )
 
 
+def chunk_products(w_ref, c_ref, i, base, out0, out1):
+    size = 2 * w_ref.shape[0] // CHUNKS
+    for k in range(0, size, 2):
+        g = i * size + k
+        at = base + g
+        rhs = jnp.concatenate(
+            [c_ref[pl.ds((g + j) * 8, 8)].reshape(1024, 128) for j in (0, 1)], axis=1
+        )
+        res = dot(w_ref[at // 2], rhs)
+        for j in (0, 1):
+            own = res[16 * j : 16 * (j + 1), 128 * j : 128 * (j + 1)]
+            out0[at + j] = own[:8]
+            out1[at + j] = own[8:]
+
+
 def tile_products(w_ref, parts, out0, out1):
     size = 2 * w_ref.shape[0] // CHUNKS
     base = 0
@@ -98,17 +112,7 @@
         def chunk(i, _):
             if c_hbm is not None:
                 chunk_copy(c_hbm, c_ref, sems, i).wait()
-            for k in range(0, size, 2):
-                g = i * size + k
-                at = base + g
-                rhs = jnp.concatenate(
-                    [c_ref[pl.ds((g + j) * 8, 8)].reshape(1024, 128) for j in (0, 1)], axis=1
-                )
-                res = dot(w_ref[at // 2], rhs)
-                for j in (0, 1):
-                    own = res[16 * j : 16 * (j + 1), 128 * j : 128 * (j + 1)]
-                    out0[at + j] = own[:8]
-                    out1[at + j] = own[8:]
+            chunk_products(w_ref, c_ref, i, base, out0, out1)
             return 0
 
         lax.fori_loop(0, groups // size, chunk, 0)
@@ -126,9 +130,17 @@
     return pick(sum_k, flat(o0)) - f * pick(sum_k, flat(o1))
 
 
+def my_core():
+    return lax.rem(lax.axis_index("bulk"), 2)
+
+
+def block_of(peer, peers):
+    return peer // 2 + jnp.where(peer % 2 == my_core(), 0, peers // 2)
+
+
 def need_kernel(cap, *refs):
     ins, outs = refs[:9], refs[9:]
-    small, send_ref, list_ref = outs[:7], outs[7], outs[8]
+    small, send_ref, list_ref, mine_ref = outs[:7], outs[7], outs[8], outs[9]
     pneed_ref, qneed_ref, sems = outs[-3:]
     copies = [
         pltpu.make_async_copy(src, dst, sems.at[i])
@@ -148,22 +160,25 @@
         copy.wait()
     f, n = small[0][...], small[1][...]
     kb, qb = f.shape[0], n.shape[0]
-    pn = jnp.broadcast_to(pneed_ref[...].astype(f32), (rows, slots))
-    qn = jnp.broadcast_to(qneed_ref[...].astype(f32), (rows, slots)) + float(kb)
+    own_p, own_q = pneed_ref[...].astype(f32), qneed_ref[...].astype(f32)
+    pn = jnp.broadcast_to(own_p, (rows, slots))
+    qn = jnp.broadcast_to(own_q, (rows, slots)) + float(kb)
     col = jnp.sum(jnp.where(e_here, pn, 0.0) + jnp.where(p_here, qn, 0.0), axis=1, keepdims=True)
-    hot = (iota((rows, 128), 1).astype(f32) == col).astype(f32)
-    core = lax.rem(lax.axis_index("bulk"), 2)
-    peer1 = iota((rows, 1), 0) // (2 * cap)
-    start_of = (peer1 // 2 + jnp.where(peer1 % 2 == core, 0, peers // 2)) * step
+    mine_ref[...] = jnp.broadcast_to(col, (rows, 128))
+    start_of = block_of(iota((rows, 1), 0) // (2 * cap), peers) * step
     list_ref[...] = jnp.where(
         iota((rows, sent), 1).astype(f32) == col + start_of.astype(f32), 1.0, 0.0
     ).astype(bf16)
+    row = iota((8, slots), 0)
+    lists = jnp.where(row == 0, own_p, jnp.where(row == 1, own_q, 0.0))
+    if slots < 128:
+        lists = jnp.concatenate([lists, jnp.zeros((8, 128 - slots), f32)], axis=1)
+    block = jnp.concatenate([f, n, lists], axis=0)
     for chip in range(peers // 2):
-        lists = hot[chip * 4 * cap : (chip + 1) * 4 * cap]
-        send_ref[chip * step : (chip + 1) * step] = jnp.concatenate([f, n, lists], axis=0)
-
-
-def tables_kernel(
+        send_ref[chip * step : (chip + 1) * step] = block
+
+
+def prepare_kernel(
     cap,
     count_ref,
     kblock_ref,
@@ -171,20 +186,25 @@
     qslot_ref,
     f_ref,
     c_hbm,
+    held_ref,
+    t_hbm,
     ge4_ref,
     gp4_ref,
     gp8_ref,
     gk_ref,
     sk_ref,
+    sp_ref,
     sp4_ref,
     sp8_ref,
     b0_ref,
     b1_ref,
     w_ref,
     c_ref,
-    sems,
+    in_sems,
+    t_ref,
+    out_sems,
 ):
-    start_chunks(c_hbm, c_ref, sems)
+    start_chunks(c_hbm, c_ref, in_sems)
     tiles = kblock_ref.shape[1]
     kb = f_ref.shape[0]
     used = iota((1, tiles), 1) < count_ref[0]
@@ -195,8 +215,10 @@
     rows8 = sp8_ref.shape[0]
     ind = lambda m: jnp.where(m, 1.0, 0.0)
     k_hot = ind(iota((kb, tiles), 0) == k)
+    gk_ref[...] = k_hot.T.astype(bf16)
+    own = pick(gk_ref[...], f_ref[...])
+    left_sides(1.0 - own, own, w_ref)
     sk_ref[...] = jnp.where(used, k_hot, 0.0).astype(bf16)
-    gk_ref[...] = k_hot.T.astype(bf16)
     x = iota((rows4, tiles), 0)
     row_e = (e // cap) * (2 * cap) + e % cap
     row_p = (q // cap) * (2 * cap) + cap + q % cap
@@ -204,6 +226,7 @@
     p_hot = ind(x == row_p)
     gp4_ref[...] = p_hot.T.astype(bf16)
     sp4_ref[...] = jnp.where(used, p_hot, 0.0).astype(bf16)
+    sp_ref[...] = jnp.where(used, ind(iota(sp_ref.shape, 0) == q), 0.0).astype(bf16)
     x = iota((rows8, tiles), 0)
     row_z = (q // cap) * (4 * cap) + q % cap
     gp8_ref[...] = ind(x == row_z).T.astype(bf16)
@@ -214,23 +237,20 @@
         ],
         axis=1,
     ).astype(bf16)
-    own = pick(gk_ref[...], f_ref[...])
-    backward_pass(own, c_hbm, c_ref, sems, w_ref, b0_ref, b1_ref)
-
-
-def transpose_kernel(after_ref, c_hbm, held_ref, t_hbm, c_ref, t_ref, in_sems, out_sems):
-    start_chunks(c_hbm, c_ref, in_sems)
-    size = c_ref.shape[0] // in_sems.shape[0]
+
+    size = c_ref.shape[0] // CHUNKS
     held = held_ref.shape[0] // size
 
     def to_held(i, _):
         chunk_copy(c_hbm, c_ref, in_sems, i).wait()
+        chunk_products(w_ref, c_ref, i, 0, b0_ref, b1_ref)
         for t in range(size):
             held_ref[i * size + t] = c_ref[i * size + t].T
         return 0
 
     def to_rest(i, _):
         chunk_copy(c_hbm, c_ref, in_sems, held + i).wait()
+        chunk_products(w_ref, c_ref, held + i, 0, b0_ref, b1_ref)
         for t in range(size):
             t_ref[i * size + t] = c_ref[(held + i) * size + t].T
         chunk_copy(t_ref, t_hbm, out_sems, i).start()
@@ -242,7 +262,31 @@
         chunk_copy(t_ref, t_hbm, out_sems, i).wait()
 
 
-def serve_kernel(cap, kb, qb, hot_ref, s8_ref, st4_ref, st8a_ref, st8b_ref):
+def blocks(same_ref, other_ref, peers, first, count):
+    step = 2 * same_ref.shape[0] // peers
+    parts = [
+        ref[b * step + first : b * step + first + count]
+        for ref in (same_ref, other_ref)
+        for b in range(peers // 2)
+    ]
+    return jnp.concatenate(parts, axis=0)
+
+
+def serve_kernel(
+    cap,
+    kb,
+    qb,
+    same_ref,
+    other_ref,
+    hot_ref,
+    mine_ref,
+    share_ref,
+    owner_ref,
+    s8_ref,
+    st4_ref,
+    st8a_ref,
+    st8b_ref,
+):
     hot = hot_ref[...]
     rows4, rows8 = hot.shape[0], s8_ref.shape[0]
     x = iota((rows8, rows4), 0)
@@ -259,42 +303,168 @@
     st8a_ref[...] = rows_of(1).T[kb : kb + qb].astype(bf16)
     st8b_ref[...] = rows_of(2).T[kb : kb + qb].astype(bf16)
 
-
-def first_kernel(cap, state_rows, starts, recv, *refs):
-    other, refs = (refs[0], refs[1:]) if starts else (None, refs)
-    list_ref, f_ref, ge4_ref, gp4_ref, sk_ref, sp4_ref, b0_ref, b1_ref, held_ref, c_hbm = refs[:10]
-    send, e_ref, f1_ref = refs[10:13]
-    hot_ref = refs[13] if starts else None
-    w_ref, c_ref, sems, o0, o1 = refs[-5:]
+    peers = rows4 // (2 * cap)
+    slots = peers * cap
+    wide = peers * slots
+    lists = blocks(same_ref, other_ref, peers, kb + qb, 8).astype(bf16)
+    pick_q = iota((peers, 8 * peers), 1) == 8 * iota((peers, 8 * peers), 0) + 1
+    every_q = dot(jnp.where(pick_q, 1.0, 0.0).astype(bf16), lists).astype(bf16)
+    tiled = iota((128, wide), 0) == iota((128, wide), 1) % slots
+    spread = dot(every_q, jnp.where(tiled, 1.0, 0.0).astype(bf16))
+    lane = iota((1, wide), 1)
+    here = iota((peers, wide), 0) == lane // slots
+    q = jnp.sum(jnp.where(here, spread, 0.0), axis=0, keepdims=True)
+    ids = q + (lane % slots // cap * qb).astype(f32)
+    row = iota((rows4, 1), 0)
+    col = mine_ref[...][:, :1]
+    my_ids = col - float(kb) + (row // (2 * cap) * qb).astype(f32)
+    my_ids = jnp.where(row % (2 * cap) >= cap, my_ids, -1.0)
+    share_ref[...] = jnp.where(ids == my_ids, 1.0, 0.0).astype(bf16)
+    owned = (lax.axis_index("bulk") * qb + iota((qb, 1), 0)).astype(f32)
+    owner_ref[...] = jnp.where(ids == owned, 1.0, 0.0).astype(bf16)
+
+
+def thermal_of(energy_ref):
+    return 1.0 / (jnp.exp(energy_ref[...]) - 1.0)
+
+
+def put_broadcast(send, served, contributions):
+    slots = contributions.shape[0]
+    for chip in range(served.shape[0] // 8):
+        at = chip * (8 + slots)
+        send[at : at + 8] = served[chip * 8 : chip * 8 + 8]
+        send[at + 8 : at + 8 + slots] = contributions
+
+
+def phonon_terms(far, bose, b0_ref, b1_ref):
+    gain = far * flat(b0_ref)
+    return gain + bose * (gain - (1.0 - far) * flat(b1_ref))
+
+
+def first_kernel(
+    cap,
+    same_ref,
+    other_ref,
+    list_ref,
+    f_ref,
+    n_ref,
+    energy_ref,
+    decay_ref,
+    ge4_ref,
+    gp4_ref,
+    sk_ref,
+    sp_ref,
+    b0_ref,
+    b1_ref,
+    held_ref,
+    c_hbm,
+    send,
+    e_ref,
+    f1_ref,
+    hot_ref,
+    w_ref,
+    c_ref,
+    sems,
+    o0,
+    o1,
+):
     start_chunks(c_hbm, c_ref, sems)
-    f = f_ref[...]
-    got = recv[...]
-    serve = list_ref[...]
-    if starts:
-        rows, sent = serve.shape
-        every = jnp.concatenate([got, other[...]], axis=0)
-        got = pick(serve, every)
-        x = iota((rows, sent), 0)
-        peers = rows // (2 * cap)
-        step = sent // peers
-        core = lax.rem(lax.axis_index("bulk"), 2)
-        peer = x // (2 * cap)
-        chip_row = (peer // 2 + jnp.where(peer % 2 == core, 0, peers // 2)) * step
-        lists_at = chip_row + state_rows + 2 * cap * core + x % (2 * cap)
-        at = jnp.where(iota((rows, sent), 1) == lists_at, 1.0, 0.0).astype(bf16)
-        serve = dot(at, every.astype(bf16)).astype(bf16)
-        hot_ref[...] = serve
+    f, n = f_ref[...], n_ref[...]
+    kb, qb = f.shape[0], n.shape[0]
+    rows4 = list_ref.shape[0]
+    peers = rows4 // (2 * cap)
+    got = pick(list_ref[...], jnp.concatenate([same_ref[...], other_ref[...]], axis=0))
     far = pick(ge4_ref[...], got)
     bose = pick(gp4_ref[...], got)
-    gain = far * flat(b0_ref)
-    terms = gain + bose * (gain - (1.0 - far) * flat(b1_ref))
-    phonon_rows = pick(sp4_ref[...], terms)
+    contributions = pick(sp_ref[...], phonon_terms(far, bose, b0_ref, b1_ref))
+    lists = blocks(same_ref, other_ref, peers, kb + qb, 8).astype(bf16)
+    x = iota((rows4, 8 * peers), 0)
+    r = x % (2 * cap)
+    kind = jnp.where(r < cap, 0, 1)
+    at = iota((rows4, 8 * peers), 1) == 8 * block_of(x // (2 * cap), peers) + kind
+    asked = dot(jnp.where(at, 1.0, 0.0).astype(bf16), lists)
+    r = iota((rows4, 128), 0) % (2 * cap)
+    lane = iota((rows4, 128), 1)
+    wanted = lane == lax.axis_index("bulk") * cap + r % cap
+    col = jnp.sum(jnp.where(wanted, asked, 0.0), axis=1, keepdims=True)
+    col = col + jnp.where(r[:, :1] < cap, 0.0, float(kb))
+    hot = jnp.where(lane.astype(f32) == col, 1.0, 0.0).astype(bf16)
+    hot_ref[...] = hot
+    base = n - DT * decay_ref[...] * (n - thermal_of(energy_ref))
     parts = [(held_ref, None, None), (c_ref, c_hbm, sems)]
     rate = electron_rate(sk_ref[...], far, bose, f, parts, w_ref, o0, o1)
     f1 = f + DT * rate
     e_ref[...] = rate
     f1_ref[...] = f1
-    send[...] = pick(serve, padded(f1)) + phonon_rows
+    put_broadcast(send, pick(hot, padded(f1, base)), contributions)
+
+
+def middle_kernel(
+    cap,
+    ends,
+    same_ref,
+    other_ref,
+    share_ref,
+    owner_ref,
+    serve_ref,
+    f_ref,
+    e_ref,
+    own_ref,
+    n_ref,
+    energy_ref,
+    decay_ref,
+    ge4_ref,
+    gp4_ref,
+    sk_ref,
+    sp_ref,
+    b0_ref,
+    b1_ref,
+    held_ref,
+    c_hbm,
+    send,
+    *refs,
+):
+    w_ref, c_ref, sems, o0, o1 = refs[-5:]
+    start_chunks(c_hbm, c_ref, sems)
+    rows4 = serve_ref.shape[0]
+    peers = rows4 // (2 * cap)
+    slots = peers * cap
+    x = iota((rows4, 8 * peers), 0)
+    source = 8 * block_of(x // (2 * cap), peers) + 2 * cap * my_core() + x % (2 * cap)
+    at = jnp.where(iota((rows4, 8 * peers), 1) == source, 1.0, 0.0).astype(bf16)
+    heads = blocks(same_ref, other_ref, peers, 0, 8)
+    tails = split(blocks(same_ref, other_ref, peers, 8, slots))
+    weight = DT / 2.0 if ends else DT
+    shares = sum(dot(share_ref[...], part) for part in tails)
+    got = pick(at, heads) + weight * shares
+    far = pick(ge4_ref[...], got)
+    bose = pick(gp4_ref[...], got)
+    terms = phonon_terms(far, bose, b0_ref, b1_ref)
+    contributions = pick(sp_ref[...], terms)
+    total = sum(dot(owner_ref[...], part) for part in tails)
+    n = n_ref[...]
+    own = own_ref[...]
+    parts = [(held_ref, None, None), (c_ref, c_hbm, sems)]
+    if ends:
+        n2_ref, e2_ref, f3_ref = refs[:3]
+        n2_ref[...] = n + (DT / 2.0) * total
+        rate = electron_rate(sk_ref[...], far, bose, own, parts, w_ref, o0, o1)
+        f3 = own + DT * rate
+        e2_ref[...] = rate
+        f3_ref[...] = f3
+        send[...] = pick(serve_ref[...], padded(f3)) + contributions
+    else:
+        base_ref, f2_ref = refs[:2]
+        thermal = thermal_of(energy_ref)
+        decay = decay_ref[...]
+        p0 = total - decay * (n - thermal)
+        n1 = n + DT * p0
+        base = n + (DT / 2.0) * (p0 - decay * (n1 - thermal))
+        base_ref[...] = base
+        rate = electron_rate(sk_ref[...], far, bose, own, parts, w_ref, o0, o1)
+        f2 = f_ref[...] + (DT / 2.0) * (e_ref[...] + rate)
+        f2_ref[...] = f2
+        put_broadcast(send, pick(serve_ref[...], padded(f2, base)), contributions)
 
 
 def backward_kernel(f_ref, gk_ref, c_hbm, b0_ref, b1_ref, w_ref, c_ref, sems):
@@ -322,7 +492,7 @@
 ):
     n = n_ref[...]
     got = recv[...]
-    thermal = 1.0 / (jnp.exp(energy_ref[...]) - 1.0)
+    thermal = thermal_of(energy_ref)
     rate = pick(st4_ref[...], got) - decay_ref[...] * (n - thermal)
     n1 = n + DT * rate
     p_ref[...] = rate
@@ -335,18 +505,16 @@
     send[...] = pick(s8_ref[...], state) + pick(sp8_ref[...], both)
 
 
-def second_kernel(with_send, recv, *refs):
+def last_kernel(recv, *refs):
     far_ref, f_ref, f1_ref, e_ref, n_ref, n1_ref, p_ref, energy_ref, decay_ref = refs[:9]
-    gp8_ref, sk_ref, st8a_ref, st8b_ref, serve_ref, held_ref, c_hbm = refs[9:16]
-    refs = refs[16:]
-    f2_ref, n2_ref, *refs = refs
-    send, refs = (refs[0], refs[1:]) if with_send else (None, refs)
-    w_ref, c_ref, sems, o0, o1 = refs
+    gp8_ref, sk_ref, st8a_ref, st8b_ref, held_ref, c_hbm = refs[9:15]
+    refs = refs[15:]
+    f2_ref, n2_ref, w_ref, c_ref, sems, o0, o1 = refs
     start_chunks(c_hbm, c_ref, sems)
     got = recv[...]
     n, n1 = n_ref[...], n1_ref[...]
     bose = pick(gp8_ref[...], got)
-    thermal = 1.0 / (jnp.exp(energy_ref[...]) - 1.0)
+    thermal = thermal_of(energy_ref)
     p1 = (
         pick(st8a_ref[...], got)
         + n1 * pick(st8b_ref[...], got)
@@ -358,8 +526,6 @@
     rate = electron_rate(sk_ref[...], far_ref[...], bose, f1_ref[...], parts, w_ref, o0, o1)
     f2 = f_ref[...] + (DT / 2.0) * (e_ref[...] + rate)
     f2_ref[...] = f2
-    if with_send:
-        send[...] = pick(serve_ref[...], padded(f2, n2))
 
 
 def call(kernel, name, outs, scratch=(), spaces=None, out_spaces=None, flops=0, seen=0):
@@ -437,13 +603,36 @@
     ints = ((1, tiles), jnp.int32)
     lists = ((1, partner_need.shape[1]), jnp.int32)
     small = [((kb, 128), f32)] + [((qb, 128), f32)] * 3 + [ints] * 3
-    step_rows = kb + qb + 4 * cap
-    assert step_rows % 8 == 0 and devices % 2 == 0
-    f, n, energy, decay, kblock, partner, qslot, send, lists_in = call(
+    step_rows = kb + qb + 8
+    slots = devices * cap
+    wide = 8 + slots
+    assert step_rows % 8 == 0 and slots % 8 == 0 and slots <= 128
+    assert devices % 2 == 0 and cap == 2
+    chips = devices // 2
+    same_core = [list(range(core, devices, 2)) for core in (0, 1)]
+
+    def to_chips(x):
+        return lax.all_to_all(
+            x, "bulk", split_axis=0, concat_axis=0, tiled=True, axis_index_groups=same_core
+        )
+
+    def between_cores(x):
+        return lax.ppermute(x, "bulk", [(i, i ^ 1) for i in range(devices)])
+
+    f, n, energy, decay, kblock, partner, qslot, send, lists, mine = call(
         functools.partial(need_kernel, cap),
         "need",
-        small + [((devices // 2 * step_rows, 128), f32), ((rows4, devices * step_rows), bf16)],
-        [pltpu.VMEM(*lists), pltpu.VMEM(*lists), pltpu.SemaphoreType.DMA((9,))],
+        small
+        + [
+            ((chips * step_rows, 128), f32),
+            ((rows4, devices * step_rows), bf16),
+            ((rows4, 128), f32),
+        ],
+        [
+            pltpu.VMEM(*lists),
+            pltpu.VMEM((1, phonon_need.shape[1]), jnp.int32),
+            pltpu.SemaphoreType.DMA((9,)),
+        ],
         spaces={i: pltpu.HBM for i in range(9)},
     )(
         electrons,
@@ -456,85 +645,95 @@
         partner_need,
         phonon_need,
     )
-    same_core = [list(range(core, devices, 2)) for core in (0, 1)]
-    recv = lax.all_to_all(
-        send, "bulk", split_axis=0, concat_axis=0, tiled=True, axis_index_groups=same_core
-    )
-    c_held, c_rest = call(
-        transpose_kernel,
-        "transpose",
-        [((held, 128, 128), bf16), (rest, bf16)],
-        [pltpu.VMEM(coupling.shape, bf16), pltpu.VMEM(rest, bf16), streams[2], rest_sems],
-        spaces={1: pltpu.HBM},
-        out_spaces={1: pltpu.HBM},
-        **work,
-    )(f, coupling)
-    ge4, gp4, gp8, gk, sk, sp4, sp8, b0, b1 = call(
-        functools.partial(tables_kernel, cap),
-        "tables",
+    same = to_chips(send)
+    c_held, c_rest, ge4, gp4, gp8, gk, sk, sp, sp4, sp8, b0, b1 = call(
+        functools.partial(prepare_kernel, cap),
+        "prepare",
         [
+            ((held, 128, 128), bf16),
+            (rest, bf16),
             ((tiles, rows4), bf16),
             ((tiles, rows4), bf16),
             ((tiles, rows8), bf16),
             ((tiles, kb), bf16),
             ((kb, tiles), bf16),
+            ((slots, tiles), bf16),
             ((rows4, tiles), bf16),
             ((rows8, 2 * tiles), bf16),
         ]
         + pass_out,
-        streams,
+        [*streams, pltpu.VMEM(rest, bf16), rest_sems],
         spaces={0: pltpu.SMEM, 5: pltpu.HBM},
+        out_spaces={1: pltpu.HBM},
         **work,
     )(tile_count, kblock, partner, qslot, f, coupling)
-    recv, c_held, b0 = lax.optimization_barrier((recv, c_held, b0))
-    other = lax.ppermute(recv, "bulk", [(i, i ^ 1) for i in range(devices)])
+    same, c_held, b0 = lax.optimization_barrier((same, c_held, b0))
+    other = between_cores(same)
+    wide_block = ((chips * wide, 128), f32)
+    k_rows, q_rows = ((kb, 128), f32), ((qb, 128), f32)
+    forward_scratch = forward_streams + sums
+    send, e0, f1, serve = call(
+        functools.partial(first_kernel, cap),
+        "first",
+        [wide_block, k_rows, k_rows, ((rows4, 128), bf16)],
+        forward_scratch,
+        spaces={14: pltpu.HBM},
+        **work,
+    )(same, other, lists, f, n, energy, decay, ge4, gp4, sk, sp, b0, b1, c_held, c_rest)
+    share, owner, s8, st4, st8a, st8b = call(
+        functools.partial(serve_kernel, cap, kb, qb),
+        "serve",
+        [
+            ((rows4, devices * slots), bf16),
+            ((qb, devices * slots), bf16),
+            ((rows8, 128), bf16),
+            ((qb, rows4), bf16),
+            ((qb, rows8), bf16),
+            ((qb, rows8), bf16),
+        ],
+    )(same, other, serve, mine)
     back = call(backward_kernel, "backward", pass_out, streams, spaces={2: pltpu.HBM}, **work)
-    for step in range(STEPS):
-        if step:
-            recv = exchange(send)
-            b0, b1 = back(f, gk, coupling)
-        lists = (serve,) if step else (other, lists_in)
-        send, e0, f1, *hot = call(
-            functools.partial(first_kernel, cap, kb + qb, not step),
-            "first",
-            [block4] + [((kb, 128), f32)] * 2 + ([] if step else [((rows4, 128), bf16)]),
-            forward_streams + sums,
-            spaces={9 + len(lists): pltpu.HBM},
-            **work,
-        )(recv, *lists, f, ge4, gp4, sk, sp4, b0, b1, c_held, c_rest)
-        if not step:
-            serve = hot[0]
-            s8, st4, st8a, st8b = call(
-                functools.partial(serve_kernel, cap, kb, qb),
-                "serve",
-                [
-                    ((rows8, 128), bf16),
-                    ((qb, rows4), bf16),
-                    ((qb, rows8), bf16),
-                    ((qb, rows8), bf16),
-                ],
-            )(serve)
-        recv = exchange(send)
-        b0, b1 = back(f1, gk, coupling)
-        send, p0, n1, far = call(
-            functools.partial(phonon_kernel, kb),
-            "phonon",
-            [block8] + [((qb, 128), f32)] * 2 + [((tiles, 128), f32)],
-        )(recv, n, energy, decay, ge4, st4, sp8, s8, b0, b1)
-        recv = exchange(send)
-        last = step == STEPS - 1
-        f, n, *send = call(
-            functools.partial(second_kernel, not last),
-            "second",
-            [((kb, 128), f32), ((qb, 128), f32)] + ([] if last else [block4]),
-            forward_streams + sums,
-            spaces={16: pltpu.HBM},
+
+    def middle(ends, send, outs, f, e, own, n, contributions):
+        same = to_chips(send)
+        b0, b1 = back(own, gk, coupling)
+        same, b0 = lax.optimization_barrier((same, b0))
+        other = between_cores(same)
+        return call(
+            functools.partial(middle_kernel, cap, ends),
+            "middle",
+            outs,
+            forward_scratch,
+            spaces={18: pltpu.HBM},
             **work,
         )(
-            recv, far, f, f1, e0, n, n1, p0, energy, decay,
-            gp8, sk, st8a, st8b, serve, c_held, c_rest,
+            same, other, share, owner, serve, f, e, own, n, energy, decay,
+            ge4, gp4, sk, contributions, b0, b1, c_held, c_rest,
         )
-        send = send[0] if send else None
+
+    send, base, f2 = middle(False, send, [wide_block, q_rows, k_rows], f, e0, f1, n, sp)
+    send, n2, e2, f3 = middle(
+        True, send, [block4, q_rows, k_rows, k_rows], f2, e0, f2, base, sp4
+    )
+    recv = exchange(send)
+    b0, b1 = back(f3, gk, coupling)
+    send, p2, n3, far = call(
+        functools.partial(phonon_kernel, kb),
+        "phonon",
+        [block8, q_rows, q_rows, ((tiles, 128), f32)],
+    )(recv, n2, energy, decay, ge4, st4, sp8, s8, b0, b1)
+    recv = exchange(send)
+    f, n = call(
+        last_kernel,
+        "last",
+        [k_rows, q_rows],
+        forward_scratch,
+        spaces={15: pltpu.HBM},
+        **work,
+    )(
+        recv, far, f2, f3, e2, n2, n3, p2, energy, decay,
+        gp8, sk, st8a, st8b, c_held, c_rest,
+    )
     return (f, n)
 
 

time: 93 us -> 86.5 us (0.930)
  blocking collectives: 20 us -> 9.88 us
  waiting for transfers between devices: 9.72 us -> 16.6 us
  Pallas kernels: 40.9 us -> 36.9 us
  local copies, waits for them, and re-layouts: 0 us -> 2.83 us
  starting transfers between devices: 20.5 us -> 18 us
    all_to_all x1 -> x3, waiting for transfers between devices: 0.01 us -> 10.6 us  [to_chips(): lax.all_to_all(x, 'bulk', split_axis=0, concat_axis=0, tiled=True, axis_i...]
    all_to_all x2 -> x1, blocking collectives: 20 us -> 9.88 us  [exchange(): return lax.all_to_all(x, 'bulk', split_axis=0, concat_axis=0, tiled=True)]
    all_to_all x3 -> x1, starting transfers between devices: 13.1 us -> 3.49 us  [exchange(): return lax.all_to_all(x, 'bulk', split_axis=0, concat_axis=0, tiled=True)]
    all_to_all x1 -> x3, starting transfers between devices: 7.29 us -> 14.5 us  [to_chips(): lax.all_to_all(x, 'bulk', split_axis=0, concat_axis=0, tiled=True, axis_i...]
    all_to_all x3 -> x1, waiting for transfers between devices: 8.24 us -> 2.82 us  [exchange(): return lax.all_to_all(x, 'bulk', split_axis=0, concat_axis=0, tiled=True)]
    pallas_call x13 -> x11, Pallas kernels: 40.9 us -> 36.9 us  [run(): pl.pallas_call(kernel, out_shape=[pltpu.HBM(*o) if (out_spaces or {}).get...]
    unnamed x0 -> x36, local copies, waits for them, and re-layouts: none -> 2.83 us
    ppermute x1 -> x3, waiting for transfers between devices: 1.48 us -> 3.15 us  [between_cores(): return lax.ppermute(x, 'bulk', [(i, i ^ 1) for i in range(devices)])]
  transfers between devices with their start and end apart: 5 -> 7, of which waited for: 4 -> 7; matrix products, arithmetic and copies ran while one was open for 0% -> 0% of each run, Pallas kernels for 23% -> 20%
where the time goes in v9:
time: 86.5 us; the launch traced here: 85.7 us
  Pallas kernels  36.9 us (43%)
  starting transfers between devices  18 us (21%)
  waiting for transfers between devices  16.6 us (19%)
  blocking collectives  9.88 us (11%)
  local copies, waits for them, and re-layouts  2.83 us (3%)
  between operations  1.54 us (2%)
    pallas_call x11, Pallas kernels, run(): pl.pallas_call(kernel, out_shape=[pltpu.HBM(*o) if (out_spaces or {}).get...  36.9 us
    all_to_all x3, starting transfers between devices, to_chips(): lax.all_to_all(x, 'bulk', split_axis=0, concat_axis=0, tiled=True, axis_i...  14.5 us
    all_to_all x3, waiting for transfers between devices, to_chips(): lax.all_to_all(x, 'bulk', split_axis=0, concat_axis=0, tiled=True, axis_i...  10.6 us
    all_to_all x1, blocking collectives, exchange(): return lax.all_to_all(x, 'bulk', split_axis=0, concat_axis=0, tiled=True)  9.88 us
    all_to_all x1, starting transfers between devices, exchange(): return lax.all_to_all(x, 'bulk', split_axis=0, concat_axis=0, tiled=True)  3.49 us
    ppermute x3, waiting for transfers between devices, between_cores(): return lax.ppermute(x, 'bulk', [(i, i ^ 1) for i in range(devices)])  3.15 us
    unnamed x36, local copies, waits for them, and re-layouts  2.83 us
    all_to_all x1, waiting for transfers between devices, exchange(): return lax.all_to_all(x, 'bulk', split_axis=0, concat_axis=0, tiled=True)  2.82 us
  transfers between devices with their start and end apart: 7, of which 7 were waited for; matrix products, arithmetic and copies ran while one was open for 0% of the time, Pallas kernels for 20%

profile of v9, /device:TPU:0, one launch (start us, length us, event | category | flops | bytes accessed | tf_op | source)
XLA Modules:
  0.0 85.7 jit_solution(8800378955911546782)
XLA Ops:
  0.6 1.6 %need.1 = (f32[32,128]{1,0:T(8,128)S(1)}, f32[16,128]{1,0:T(8,128)S(1)}, f32[16,128]{1,0:T(8,128)S(1)}, f32[16,128]{1,0:T(8,128)S(1)}, s32[1,256]{1,0:T(1,128)S(...) custom-call(f32[32,128]{1,0:T(8,128)} %refs_0_.1, ...), custom_call_target="tpu_custom_call" | custom-call | tf_op jit(solution)/shard_map/need/pallas_call | solution.py:543
  2.2 0.0 copy-start.6
  2.2 0.0 copy-start.8
  2.2 7.3 %all-to-all-start = ((f32[8,56,128]{2,1,0:T(8,128)}), f32[8,56,128]{2,1,0:T(8,128)S(1)}, u32[]{:S(2)}, u32[]{:S(2)}) async-start(f32[8,56,128]{2,1,0:T(8,128)} %bitcast.3), calls=%async_computation | async-start | bytes 458752 | tf_op jit(solution)/shard_map/all_to_all | solution.py:615
  10.2 0.0 copy-done.6
  10.2 5.5 %prepare.1 = (bf16[64,128,128]{2,1,0:T(8,128)(2,1)S(1)}, bf16[192,128,128]{2,1,0:T(8,128)(2,1)}, bf16[256,64]{1,0:T(8,128)(2,1)S(1)}, bf16[256,64]{1,0:T(8,128)(...) custom-call(s32[1]{0:T(128)S(6)} %copy.13.count_ref, ...), custom_call_target="tpu_custom_call" | custom-call | flops 134217728 | bytes 8388608 | tf_op jit(solution)/shard_map/prepare/pallas_call | solution.py:543
  15.7 0.0 copy-start.2
  15.7 2.3 %all-to-all-done = f32[8,56,128]{2,1,0:T(8,128)S(1)} async-done(((f32[8,56,128]{2,1,0:T(8,128)}), f32[8,56,128]{2,1,0:T(8,128)S(1)}, u32[]{:S(2)}, u32[]{:S(2)}) %all-to-all-start) | async-done | bytes 229408 | tf_op jit(solution)/shard_map/all_to_all | solution.py:615
  18.0 0.0 collective-permute-start
  18.0 1.5 %collective-permute-done.other_ref = f32[448,128]{1,0:T(8,128)S(1)} collective-permute-done((f32[448,128]{1,0:T(8,128)S(1)}, f32[448,128]{1,0:T(8,128)S(1)}, u32[]{:S(2)}, u32[]{:S(2)}) %collective-permute-start) | collective-permute-done | bytes 229408 | tf_op jit(solution)/shard_map/ppermute | solution.py:620
  19.5 4.8 %first.1 = (f32[320,128]{1,0:T(8,128)}, f32[32,128]{1,0:T(8,128)S(1)}, f32[32,128]{1,0:T(8,128)S(1)}, bf16[64,128]{1,0:T(8,128)(2,1)S(1)}) custom-call(f32[448,128]{1,0:T(8,128)S(1)} %bitcast.14, f32[448,128]{1,0:T(8,128)S(1)} %collective-permute-done.other_ref, bf16[64,896]{1,0:T(8,128)(2,1)S(1)} %get-tuple-element.66.list_ref, ...), custom_call_target="tpu_custom_call" | custom-call | flops 134217728 | bytes 8388608 | tf_op jit(solution)/shard_map/first/pallas_call | solution.py:543
  24.2 0.0 copy-done.8
  24.2 0.0 copy-start
  24.3 0.0 copy-done.2
  24.3 3.8 %all-to-all-start.1 = ((f32[8,40,128]{2,1,0:T(8,128)}), f32[8,40,128]{2,1,0:T(8,128)S(1)}, u32[]{:S(2)}, u32[]{:S(2)}) async-start(f32[8,40,128]{2,1,0:T(8,128)} %bitcast.5), calls=%async_computation.1 | async-start | bytes 327680 | tf_op jit(solution)/shard_map/all_to_all | solution.py:615
  28.1 3.8 %backward.3 = (f32[32,8,128]{2,1,0:T(8,128)S(1)}, f32[32,8,128]{2,1,0:T(8,128)S(1)}) custom-call(f32[32,128]{1,0:T(8,128)S(1)} %get-tuple-element.79.f_ref.own_ref, bf16[256,32]{1,0:T(8,128)(2,1)S(1)} %get-tuple-element.80.gk_ref, bf16[256,128,128]{2,1,0:T(8,128)(2,1)} %c_hbm.7), custom_call_target="tpu_custom_call" | custom-call | flops 134217728 | bytes 8388608 | tf_op jit(solution)/shard_map/backward/pallas_call | solution.py:543
  31.8 4.0 %all-to-all-done.1 = f32[8,40,128]{2,1,0:T(8,128)S(1)} async-done(((f32[8,40,128]{2,1,0:T(8,128)}), f32[8,40,128]{2,1,0:T(8,128)S(1)}, u32[]{:S(2)}, u32[]{:S(2)}) %all-to-all-start.1) | async-done | bytes 163872 | tf_op jit(solution)/shard_map/all_to_all | solution.py:615
  35.8 0.0 collective-permute-start.1
  35.8 0.0 copy-done
  35.8 0.8 copy-done.7
  36.6 0.3 serve.1
  36.9 0.0 copy-start.4
  36.9 0.0 copy-start.12
  36.9 0.0 copy-start.14
  36.9 0.0 copy-start.16
  37.0 0.3 collective-permute-done.1.other_ref
  37.2 0.7 copy-done.1
  38.0 0.7 copy-done.9
  38.6 4.4 %middle.2 = (f32[320,128]{1,0:T(8,128)}, f32[16,128]{1,0:T(8,128)S(1)}, f32[32,128]{1,0:T(8,128)S(1)}) custom-call(f32[320,128]{1,0:T(8,128)S(1)} %bitcast.17, f32[320,128]{1,0:T(8,128)S(1)} %collective-permute-done.1.other_ref, bf16[64,512]{1,0:T(8,128)(2,1)S(1)} %get-tuple-element.85.share_ref, bf16[16,512]{1,0:T(8,128)(2,1)S(1)} %get-tuple-element.86.owner_ref, ...), custom_call_target="tpu_custom_call" | custom-call | flops 134217728 | bytes 8388608 | tf_op jit(solution)/shard_map/middle/pallas_call | solution.py:543
  43.0 0.0 copy-done.4
  43.0 0.0 copy-start.10
  43.1 0.6 copy-done.10
  43.6 0.0 copy-done.12
  43.7 0.0 copy-done.14
  43.7 0.0 copy-done.16
  43.7 0.0 copy-start.11
  43.7 3.4 %all-to-all-start.2 = ((f32[8,40,128]{2,1,0:T(8,128)}), f32[8,40,128]{2,1,0:T(8,128)S(1)}, u32[]{:S(2)}, u32[]{:S(2)}) async-start(f32[8,40,128]{2,1,0:T(8,128)} %bitcast.7), calls=%async_computation.2 | async-start | bytes 327680 | tf_op jit(solution)/shard_map/all_to_all | solution.py:615
  47.1 3.8 %backward.4 = (f32[32,8,128]{2,1,0:T(8,128)S(1)}, f32[32,8,128]{2,1,0:T(8,128)S(1)}) custom-call(f32[32,128]{1,0:T(8,128)S(1)} %get-tuple-element.91.f_ref.own_ref.refs_1_, bf16[256,32]{1,0:T(8,128)(2,1)S(1)} %get-tuple-element.80.gk_ref, bf16[256,128,128]{2,1,0:T(8,128)(2,1)} %c_hbm.7), custom_call_target="tpu_custom_call" | custom-call | flops 134217728 | bytes 8388608 | tf_op jit(solution)/shard_map/backward/pallas_call | solution.py:543
  50.8 4.3 %all-to-all-done.2 = f32[8,40,128]{2,1,0:T(8,128)S(1)} async-done(((f32[8,40,128]{2,1,0:T(8,128)}), f32[8,40,128]{2,1,0:T(8,128)S(1)}, u32[]{:S(2)}, u32[]{:S(2)}) %all-to-all-start.2) | async-done | bytes 163872 | tf_op jit(solution)/shard_map/all_to_all | solution.py:615
  55.2 0.0 collective-permute-start.2
  55.2 1.4 %collective-permute-done.2.other_ref = f32[320,128]{1,0:T(8,128)S(1)} collective-permute-done((f32[320,128]{1,0:T(8,128)S(1)}, f32[320,128]{1,0:T(8,128)S(1)}, u32[]{:S(2)}, u32[]{:S(2)}) %collective-permute-start.2) | collective-permute-done | bytes 163872 | tf_op jit(solution)/shard_map/ppermute | solution.py:620
  56.6 4.5 %middle.3 = (f32[64,128]{1,0:T(8,128)}, f32[16,128]{1,0:T(8,128)S(1)}, f32[32,128]{1,0:T(8,128)S(1)}, f32[32,128]{1,0:T(8,128)S(1)}) custom-call(f32[320,128]{1,0:T(8,128)S(1)} %bitcast.19, f32[320,128]{1,0:T(8,128)S(1)} %collective-permute-done.2.other_ref, bf16[64,512]{1,0:T(8,128)(2,1)S(1)} %get-tuple-element.85.share_ref, ...), custom_call_target="tpu_custom_call" | custom-call | flops 134217728 | bytes 8388608 | tf_op jit(solution)/shard_map/middle/pallas_call | solution.py:543
  61.1 3.5 %all-to-all-start.3 = ((f32[16,4,128]{2,1,0:T(4,128)}), f32[16,4,128]{2,1,0:T(4,128)S(1)}, u32[]{:S(2)}, u32[]{:S(2)}) async-start(f32[16,4,128]{2,1,0:T(4,128)} %bitcast.9), calls=%async_computation.3 | async-start | bytes 65536 | tf_op jit(solution)/shard_map/all_to_all | solution.py:601
  64.6 3.8 %backward.5 = (f32[32,8,128]{2,1,0:T(8,128)S(1)}, f32[32,8,128]{2,1,0:T(8,128)S(1)}) custom-call(f32[32,128]{1,0:T(8,128)S(1)} %get-tuple-element.103.f_ref.refs_2_, bf16[256,32]{1,0:T(8,128)(2,1)S(1)} %get-tuple-element.80.gk_ref, bf16[256,128,128]{2,1,0:T(8,128)(2,1)} %c_hbm.7), custom_call_target="tpu_custom_call" | custom-call | flops 134217728 | bytes 8388608 | tf_op jit(solution)/shard_map/backward/pallas_call | solution.py:543
  68.4 2.8 %all-to-all-done.3 = f32[16,4,128]{2,1,0:T(4,128)S(1)} async-done(((f32[16,4,128]{2,1,0:T(4,128)}), f32[16,4,128]{2,1,0:T(4,128)S(1)}, u32[]{:S(2)}, u32[]{:S(2)}) %all-to-all-start.3) | async-done | bytes 32800 | tf_op jit(solution)/shard_map/all_to_all | solution.py:601
  71.2 0.5 phonon.1
  71.7 9.9 %all_to_all.58 = f32[16,8,128]{2,1,0:T(8,128)S(1)} all-to-all(f32[16,8,128]{2,1,0:T(8,128)S(1)} %bitcast.22), channel_id=1, replica_groups=mesh['groups'=2,'bulk'=16] {'bulk'}, dimensions={0} | all-to-all | bytes 131072 | tf_op jit(solution)/shard_map/all_to_all | solution.py:601
  81.6 4.1 %last.1 = (f32[32,128]{1,0:T(8,128)}, f32[16,128]{1,0:T(8,128)}) custom-call(f32[128,128]{1,0:T(8,128)S(1)} %bitcast.20, f32[256,128]{1,0:T(8,128)S(1)} %get-tuple-element.107.refs_0_, f32[32,128]{1,0:T(8,128)S(1)} %get-tuple-element.91.f_ref.own_ref.refs_1_, f32[32,128]{1,0:T(8,128)S(1)} %get-tuple-element.103.f_ref.refs_2_, ...), custom_call_target="tpu_custom_call" | custom-call | flops 134217728 | bytes 8388608 | tf_op jit(solution)/shard_map/last/pallas_call | solution.py:543
  (14 shorter events, 0.0 us)
Async XLA Ops:
  2.2 8.0 %copy-start.6 = (f32[64,128]{1,0:T(8,128)}, f32[64,128]{1,0:T(8,128)S(1)}, u32[]{:S(2)}) copy-start(f32[64,128]{1,0:T(8,128)S(1)} %get-tuple-element.84.mine_ref) | copy-start | bytes 98308
  2.2 22.0 %copy-start.8 = (f32[16,128]{1,0:T(8,128)}, f32[16,128]{1,0:T(8,128)S(1)}, u32[]{:S(2)}) copy-start(f32[16,128]{1,0:T(8,128)S(1)} %get-tuple-element.67.n_ref) | copy-start | bytes 24580
  2.2 15.7 %all-to-all-start = ((f32[8,56,128]{2,1,0:T(8,128)}), f32[8,56,128]{2,1,0:T(8,128)S(1)}, u32[]{:S(2)}, u32[]{:S(2)}) async-start(f32[8,56,128]{2,1,0:T(8,128)} %bitcast.3), calls=%async_computation | async-start | bytes 458752 | tf_op jit(solution)/shard_map/all_to_all | solution.py:615
  15.7 8.6 %copy-start.2 = (bf16[64,256]{1,0:T(8,128)(2,1)}, bf16[64,256]{1,0:T(8,128)(2,1)S(1)}, u32[]{:S(2)}) copy-start(bf16[64,256]{1,0:T(8,128)(2,1)S(1)} %get-tuple-element.95.sp_ref) | copy-start | bytes 98308
  18.0 1.5 %collective-permute-start = (f32[448,128]{1,0:T(8,128)S(1)}, f32[448,128]{1,0:T(8,128)S(1)}, u32[]{:S(2)}, u32[]{:S(2)}) collective-permute-start(f32[448,128]{1,0:T(8,128)S(1)} %bitcast.13), channel_id=1, source_target_pairs={{0,1},{1,0},{2,3},{3,2},{4,5},{5,4},{6,7},{7,6},{8,9},{9,8},{10,11... | collective-permute-start | bytes 688136 | tf_op jit(solution)/shard_map/ppermute | solution.py:620
  24.2 11.6 %copy-start = (f32[32,128]{1,0:T(8,128)}, f32[32,128]{1,0:T(8,128)S(1)}, u32[]{:S(2)}) copy-start(f32[32,128]{1,0:T(8,128)S(1)} %get-tuple-element.79.f_ref.own_ref) | copy-start | bytes 49156
  24.3 11.6 %all-to-all-start.1 = ((f32[8,40,128]{2,1,0:T(8,128)}), f32[8,40,128]{2,1,0:T(8,128)S(1)}, u32[]{:S(2)}, u32[]{:S(2)}) async-start(f32[8,40,128]{2,1,0:T(8,128)} %bitcast.5), calls=%async_computation.1 | async-start | bytes 327680 | tf_op jit(solution)/shard_map/all_to_all | solution.py:615
  35.8 1.4 %collective-permute-start.1 = (f32[320,128]{1,0:T(8,128)S(1)}, f32[320,128]{1,0:T(8,128)S(1)}, u32[]{:S(2)}, u32[]{:S(2)}) collective-permute-start(f32[320,128]{1,0:T(8,128)S(1)} %bitcast.16), channel_id=1, source_target_pairs={{0,1},{1,0},{2,3},{3,2},{4,5},{5,4},{6,7},{7,6},{8,9},{9,8},{10,11... | collective-permute-start | bytes 491528 | tf_op jit(solution)/shard_map/ppermute | solution.py:620
  35.8 0.8 copy-start.7
  36.9 6.1 %copy-start.4 = (bf16[128,128]{1,0:T(8,128)(2,1)}, bf16[128,128]{1,0:T(8,128)(2,1)S(1)}, u32[]{:S(2)}) copy-start(bf16[128,128]{1,0:T(8,128)(2,1)S(1)} %get-tuple-element.102.s8_ref) | copy-start | bytes 98308
  36.9 6.7 %copy-start.12 = (bf16[16,128]{1,0:T(8,128)(2,1)}, bf16[16,128]{1,0:T(8,128)(2,1)S(1)}, u32[]{:S(2)}) copy-start(bf16[16,128]{1,0:T(8,128)(2,1)S(1)} %get-tuple-element.112.refs_11_) | copy-start | bytes 12292
  36.9 6.7 %copy-start.14 = (bf16[16,128]{1,0:T(8,128)(2,1)}, bf16[16,128]{1,0:T(8,128)(2,1)S(1)}, u32[]{:S(2)}) copy-start(bf16[16,128]{1,0:T(8,128)(2,1)S(1)} %get-tuple-element.113.refs_12_) | copy-start | bytes 12292
  36.9 6.7 %copy-start.16 = (bf16[16,64]{1,0:T(8,128)(2,1)}, bf16[16,64]{1,0:T(8,128)(2,1)S(1)}, u32[]{:S(2)}) copy-start(bf16[16,64]{1,0:T(8,128)(2,1)S(1)} %get-tuple-element.100.st4_ref) | copy-start | bytes 6148
  37.2 0.7 copy-start.1
  37.9 0.7 copy-start.9
  43.0 0.6 copy-start.10
  43.6 12.9 %copy-start.3 = (bf16[64,256]{1,0:T(8,128)(2,1)S(1)}, bf16[64,256]{1,0:T(8,128)(2,1)}, u32[]{:S(2)}) copy-start(bf16[64,256]{1,0:T(8,128)(2,1)} %copy-done.2) | copy-start | bytes 98308
  43.7 12.9 %copy-start.11 = (f32[16,128]{1,0:T(8,128)S(1)}, f32[16,128]{1,0:T(8,128)}, u32[]{:S(2)}) copy-start(f32[16,128]{1,0:T(8,128)} %copy-done.10) | copy-start | bytes 24580
  43.7 11.5 %all-to-all-start.2 = ((f32[8,40,128]{2,1,0:T(8,128)}), f32[8,40,128]{2,1,0:T(8,128)S(1)}, u32[]{:S(2)}, u32[]{:S(2)}) async-start(f32[8,40,128]{2,1,0:T(8,128)} %bitcast.7), calls=%async_computation.2 | async-start | bytes 327680 | tf_op jit(solution)/shard_map/all_to_all | solution.py:615
  55.2 1.4 %collective-permute-start.2 = (f32[320,128]{1,0:T(8,128)S(1)}, f32[320,128]{1,0:T(8,128)S(1)}, u32[]{:S(2)}, u32[]{:S(2)}) collective-permute-start(f32[320,128]{1,0:T(8,128)S(1)} %bitcast.18), channel_id=1, source_target_pairs={{0,1},{1,0},{2,3},{3,2},{4,5},{5,4},{6,7},{7,6},{8,9},{9,8},{10,11... | collective-permute-start | bytes 491528 | tf_op jit(solution)/shard_map/ppermute | solution.py:620
  61.1 10.1 %copy-start.5 = (bf16[128,128]{1,0:T(8,128)(2,1)S(1)}, bf16[128,128]{1,0:T(8,128)(2,1)}, u32[]{:S(2)}) copy-start(bf16[128,128]{1,0:T(8,128)(2,1)} %copy-done.4) | copy-start | bytes 98308
  61.1 10.1 %copy-start.17 = (bf16[16,64]{1,0:T(8,128)(2,1)S(1)}, bf16[16,64]{1,0:T(8,128)(2,1)}, u32[]{:S(2)}) copy-start(bf16[16,64]{1,0:T(8,128)(2,1)} %copy-done.16) | copy-start | bytes 6148
  61.1 20.5 %copy-start.13 = (bf16[16,128]{1,0:T(8,128)(2,1)S(1)}, bf16[16,128]{1,0:T(8,128)(2,1)}, u32[]{:S(2)}) copy-start(bf16[16,128]{1,0:T(8,128)(2,1)} %copy-done.12) | copy-start | bytes 12292
  61.1 20.5 %copy-start.15 = (bf16[16,128]{1,0:T(8,128)(2,1)S(1)}, bf16[16,128]{1,0:T(8,128)(2,1)}, u32[]{:S(2)}) copy-start(bf16[16,128]{1,0:T(8,128)(2,1)} %copy-done.14) | copy-start | bytes 12292
  61.1 10.1 %all-to-all-start.3 = ((f32[16,4,128]{2,1,0:T(4,128)}), f32[16,4,128]{2,1,0:T(4,128)S(1)}, u32[]{:S(2)}, u32[]{:S(2)}) async-start(f32[16,4,128]{2,1,0:T(4,128)} %bitcast.9), calls=%async_computation.3 | async-start | bytes 65536 | tf_op jit(solution)/shard_map/all_to_all | solution.py:601

commit v10 on v9

--- a/solution.py
+++ b/solution.py
@@ -33,7 +33,15 @@
 
 def pick(onehot, x):
     hi, mid, lo = split(x)
-    return dot(onehot, hi) + dot(onehot, mid) + dot(onehot, lo)
+    both = dot(onehot, jnp.concatenate([hi, mid], axis=1))
+    return both[:, :128] + both[:, 128:] + dot(onehot, lo)
+
+
+def add_rows(onehot, x):
+    hi = x.astype(bf16)
+    mid = (x - hi.astype(f32)).astype(bf16)
+    both = dot(onehot, jnp.concatenate([hi, mid], axis=1))
+    return both[:, :128] + both[:, 128:]
 
 
 def stacked(first, second):
@@ -80,31 +88,22 @@
 
 
 def left_sides(first, second, w_ref):
-    tiles = first.shape[0]
     w = stacked(first, second)
-    for p in range(tiles // 16):
-        w_ref[p] = jnp.concatenate(
-            [block_diagonal(w[2 * p]), block_diagonal(w[2 * p + 1])], axis=0
-        )
+    for g in range(w.shape[0]):
+        w_ref[g] = block_diagonal(w[g])
 
 
 def chunk_products(w_ref, c_ref, i, base, out0, out1):
-    size = 2 * w_ref.shape[0] // CHUNKS
-    for k in range(0, size, 2):
+    size = w_ref.shape[0] // CHUNKS
+    for k in range(size):
         g = i * size + k
-        at = base + g
-        rhs = jnp.concatenate(
-            [c_ref[pl.ds((g + j) * 8, 8)].reshape(1024, 128) for j in (0, 1)], axis=1
-        )
-        res = dot(w_ref[at // 2], rhs)
-        for j in (0, 1):
-            own = res[16 * j : 16 * (j + 1), 128 * j : 128 * (j + 1)]
-            out0[at + j] = own[:8]
-            out1[at + j] = own[8:]
+        res = dot(w_ref[base + g], c_ref[pl.ds(g * 8, 8)].reshape(1024, 128))
+        out0[base + g] = res[:8]
+        out1[base + g] = res[8:]
 
 
 def tile_products(w_ref, parts, out0, out1):
-    size = 2 * w_ref.shape[0] // CHUNKS
+    size = w_ref.shape[0] // CHUNKS
     base = 0
     for c_ref, c_hbm, sems in parts:
         groups = c_ref.shape[0] // 8
@@ -127,7 +126,7 @@
 def electron_rate(sum_k, far, bose, f, parts, w_ref, o0, o1):
     left_sides(far * (1.0 + bose), far + bose, w_ref)
     tile_products(w_ref, parts, o0, o1)
-    return pick(sum_k, flat(o0)) - f * pick(sum_k, flat(o1))
+    return add_rows(sum_k, flat(o0)) - f * add_rows(sum_k, flat(o1))
 
 
 def my_core():
@@ -140,41 +139,24 @@
 
 def need_kernel(cap, *refs):
     ins, outs = refs[:9], refs[9:]
-    small, send_ref, list_ref, mine_ref = outs[:7], outs[7], outs[8], outs[9]
-    pneed_ref, qneed_ref, sems = outs[-3:]
+    *small, pneed_ref, qneed_ref, send_ref, sems = outs
     copies = [
         pltpu.make_async_copy(src, dst, sems.at[i])
         for i, (src, dst) in enumerate(zip(ins, [*small, pneed_ref, qneed_ref]))
     ]
     start(copies)
-    rows, sent = list_ref.shape
     slots = pneed_ref.shape[1]
-    peers = slots // cap
-    step = sent // peers
-    x = iota((rows, slots), 0)
-    y = iota((rows, slots), 1)
-    peer, r = x // (2 * cap), x % (2 * cap)
-    e_here = (r < cap) & (y == peer * cap + r)
-    p_here = (r >= cap) & (y == peer * cap + r - cap)
+    step = send_ref.shape[0] // (slots // cap // 2)
     for copy in copies:
         copy.wait()
     f, n = small[0][...], small[1][...]
-    kb, qb = f.shape[0], n.shape[0]
     own_p, own_q = pneed_ref[...].astype(f32), qneed_ref[...].astype(f32)
-    pn = jnp.broadcast_to(own_p, (rows, slots))
-    qn = jnp.broadcast_to(own_q, (rows, slots)) + float(kb)
-    col = jnp.sum(jnp.where(e_here, pn, 0.0) + jnp.where(p_here, qn, 0.0), axis=1, keepdims=True)
-    mine_ref[...] = jnp.broadcast_to(col, (rows, 128))
-    start_of = block_of(iota((rows, 1), 0) // (2 * cap), peers) * step
-    list_ref[...] = jnp.where(
-        iota((rows, sent), 1).astype(f32) == col + start_of.astype(f32), 1.0, 0.0
-    ).astype(bf16)
     row = iota((8, slots), 0)
     lists = jnp.where(row == 0, own_p, jnp.where(row == 1, own_q, 0.0))
     if slots < 128:
         lists = jnp.concatenate([lists, jnp.zeros((8, 128 - slots), f32)], axis=1)
     block = jnp.concatenate([f, n, lists], axis=0)
-    for chip in range(peers // 2):
+    for chip in range(slots // cap // 2):
         send_ref[chip * step : (chip + 1) * step] = block
 
 
@@ -185,6 +167,8 @@
     partner_ref,
     qslot_ref,
     f_ref,
+    pneed_ref,
+    qneed_ref,
     c_hbm,
     held_ref,
     t_hbm,
@@ -196,6 +180,8 @@
     sp_ref,
     sp4_ref,
     sp8_ref,
+    list_ref,
+    mine_ref,
     b0_ref,
     b1_ref,
     w_ref,
@@ -216,7 +202,7 @@
     ind = lambda m: jnp.where(m, 1.0, 0.0)
     k_hot = ind(iota((kb, tiles), 0) == k)
     gk_ref[...] = k_hot.T.astype(bf16)
-    own = pick(gk_ref[...], f_ref[...])
+    own = add_rows(gk_ref[...], f_ref[...])
     left_sides(1.0 - own, own, w_ref)
     sk_ref[...] = jnp.where(used, k_hot, 0.0).astype(bf16)
     x = iota((rows4, tiles), 0)
@@ -238,6 +224,23 @@
         axis=1,
     ).astype(bf16)
 
+    rows, sent = list_ref.shape
+    slots = pneed_ref.shape[1]
+    peers = slots // cap
+    x = iota((rows, slots), 0)
+    y = iota((rows, slots), 1)
+    peer, r = x // (2 * cap), x % (2 * cap)
+    e_here = (r < cap) & (y == peer * cap + r)
+    p_here = (r >= cap) & (y == peer * cap + r - cap)
+    pn = jnp.broadcast_to(pneed_ref[...].astype(f32), (rows, slots))
+    qn = jnp.broadcast_to(qneed_ref[...].astype(f32), (rows, slots)) + float(kb)
+    col = jnp.sum(jnp.where(e_here, pn, 0.0) + jnp.where(p_here, qn, 0.0), axis=1, keepdims=True)
+    mine_ref[...] = jnp.broadcast_to(col, (rows, 128))
+    start_of = block_of(iota((rows, 1), 0) // (2 * cap), peers) * (sent // peers)
+    list_ref[...] = jnp.where(
+        iota((rows, sent), 1).astype(f32) == col + start_of.astype(f32), 1.0, 0.0
+    ).astype(bf16)
+
     size = c_ref.shape[0] // CHUNKS
     held = held_ref.shape[0] // size
 
@@ -276,12 +279,10 @@
     cap,
     kb,
     qb,
-    same_ref,
-    other_ref,
+    asked_ref,
     hot_ref,
     mine_ref,
     share_ref,
-    owner_ref,
     s8_ref,
     st4_ref,
     st8a_ref,
@@ -306,7 +307,7 @@
     peers = rows4 // (2 * cap)
     slots = peers * cap
     wide = peers * slots
-    lists = blocks(same_ref, other_ref, peers, kb + qb, 8).astype(bf16)
+    lists = asked_ref[...]
     pick_q = iota((peers, 8 * peers), 1) == 8 * iota((peers, 8 * peers), 0) + 1
     every_q = dot(jnp.where(pick_q, 1.0, 0.0).astype(bf16), lists).astype(bf16)
     tiled = iota((128, wide), 0) == iota((128, wide), 1) % slots
@@ -319,9 +320,9 @@
     col = mine_ref[...][:, :1]
     my_ids = col - float(kb) + (row // (2 * cap) * qb).astype(f32)
     my_ids = jnp.where(row % (2 * cap) >= cap, my_ids, -1.0)
-    share_ref[...] = jnp.where(ids == my_ids, 1.0, 0.0).astype(bf16)
     owned = (lax.axis_index("bulk") * qb + iota((qb, 1), 0)).astype(f32)
-    owner_ref[...] = jnp.where(ids == owned, 1.0, 0.0).astype(bf16)
+    wanted = jnp.concatenate([my_ids, owned], axis=0)
+    share_ref[...] = jnp.where(ids == wanted, 1.0, 0.0).astype(bf16)
 
 
 def thermal_of(energy_ref):
@@ -362,6 +363,7 @@
     e_ref,
     f1_ref,
     hot_ref,
+    asked_ref,
     w_ref,
     c_ref,
     sems,
@@ -374,10 +376,11 @@
     rows4 = list_ref.shape[0]
     peers = rows4 // (2 * cap)
     got = pick(list_ref[...], jnp.concatenate([same_ref[...], other_ref[...]], axis=0))
-    far = pick(ge4_ref[...], got)
-    bose = pick(gp4_ref[...], got)
-    contributions = pick(sp_ref[...], phonon_terms(far, bose, b0_ref, b1_ref))
+    far = add_rows(ge4_ref[...], got)
+    bose = add_rows(gp4_ref[...], got)
+    contributions = add_rows(sp_ref[...], phonon_terms(far, bose, b0_ref, b1_ref))
     lists = blocks(same_ref, other_ref, peers, kb + qb, 8).astype(bf16)
+    asked_ref[...] = lists
     x = iota((rows4, 8 * peers), 0)
     r = x % (2 * cap)
     kind = jnp.where(r < cap, 0, 1)
@@ -405,7 +408,6 @@
     same_ref,
     other_ref,
     share_ref,
-    owner_ref,
     serve_ref,
     f_ref,
     e_ref,
@@ -433,15 +435,15 @@
     source = 8 * block_of(x // (2 * cap), peers) + 2 * cap * my_core() + x % (2 * cap)
     at = jnp.where(iota((rows4, 8 * peers), 1) == source, 1.0, 0.0).astype(bf16)
     heads = blocks(same_ref, other_ref, peers, 0, 8)
-    tails = split(blocks(same_ref, other_ref, peers, 8, slots))
+    tails = blocks(same_ref, other_ref, peers, 8, slots)
     weight = DT / 2.0 if ends else DT
-    shares = sum(dot(share_ref[...], part) for part in tails)
+    both = add_rows(share_ref[...], tails)
+    shares, total = both[:rows4], both[rows4:]
     got = pick(at, heads) + weight * shares
-    far = pick(ge4_ref[...], got)
-    bose = pick(gp4_ref[...], got)
+    far = add_rows(ge4_ref[...], got)
+    bose = add_rows(gp4_ref[...], got)
     terms = phonon_terms(far, bose, b0_ref, b1_ref)
-    contributions = pick(sp_ref[...], terms)
-    total = sum(dot(owner_ref[...], part) for part in tails)
+    contributions = add_rows(sp_ref[...], terms)
     n = n_ref[...]
     own = own_ref[...]
     parts = [(held_ref, None, None), (c_ref, c_hbm, sems)]
@@ -469,7 +471,7 @@
 
 def backward_kernel(f_ref, gk_ref, c_hbm, b0_ref, b1_ref, w_ref, c_ref, sems):
     start_chunks(c_hbm, c_ref, sems)
-    own = pick(gk_ref[...], f_ref[...])
+    own = add_rows(gk_ref[...], f_ref[...])
     backward_pass(own, c_hbm, c_ref, sems, w_ref, b0_ref, b1_ref)
 
 
@@ -493,16 +495,16 @@
     n = n_ref[...]
     got = recv[...]
     thermal = thermal_of(energy_ref)
-    rate = pick(st4_ref[...], got) - decay_ref[...] * (n - thermal)
+    rate = add_rows(st4_ref[...], got) - decay_ref[...] * (n - thermal)
     n1 = n + DT * rate
     p_ref[...] = rate
     n1_ref[...] = n1
-    far = pick(ge4_ref[...], got)
+    far = add_rows(ge4_ref[...], got)
     far_ref[...] = far
     gain = far * flat(b0_ref)
     both = jnp.concatenate([gain, gain - (1.0 - far) * flat(b1_ref)], axis=0)
     state = padded(jnp.zeros((kb, 128), f32), n1)
-    send[...] = pick(s8_ref[...], state) + pick(sp8_ref[...], both)
+    send[...] = pick(s8_ref[...], state) + add_rows(sp8_ref[...], both)
 
 
 def last_kernel(recv, *refs):
@@ -513,11 +515,11 @@
     start_chunks(c_hbm, c_ref, sems)
     got = recv[...]
     n, n1 = n_ref[...], n1_ref[...]
-    bose = pick(gp8_ref[...], got)
+    bose = add_rows(gp8_ref[...], got)
     thermal = thermal_of(energy_ref)
     p1 = (
-        pick(st8a_ref[...], got)
-        + n1 * pick(st8b_ref[...], got)
+        add_rows(st8a_ref[...], got)
+        + n1 * add_rows(st8b_ref[...], got)
         - decay_ref[...] * (n1 - thermal)
     )
     n2 = n + (DT / 2.0) * (p_ref[...] + p1)
@@ -585,7 +587,7 @@
     rows8 = devices * 4 * cap
     groups = tiles // 8
     held = HELD_CHUNKS * (tiles // CHUNKS)
-    weights = pltpu.VMEM((groups // 2, 32, 1024), bf16)
+    weights = pltpu.VMEM((groups, 16, 1024), bf16)
     streams = [weights, pltpu.VMEM(coupling.shape, bf16), pltpu.SemaphoreType.DMA((CHUNKS,))]
     rest = (tiles - held, 128, 128)
     rest_sems = pltpu.SemaphoreType.DMA((CHUNKS - HELD_CHUNKS,))
@@ -619,20 +621,11 @@
     def between_cores(x):
         return lax.ppermute(x, "bulk", [(i, i ^ 1) for i in range(devices)])
 
-    f, n, energy, decay, kblock, partner, qslot, send, lists, mine = call(
+    f, n, energy, decay, kblock, partner, qslot, pneed, qneed, send = call(
         functools.partial(need_kernel, cap),
         "need",
-        small
-        + [
-            ((chips * step_rows, 128), f32),
-            ((rows4, devices * step_rows), bf16),
-            ((rows4, 128), f32),
-        ],
-        [
-            pltpu.VMEM(*lists),
-            pltpu.VMEM((1, phonon_need.shape[1]), jnp.int32),
-            pltpu.SemaphoreType.DMA((9,)),
-        ],
+        small + [lists, lists, ((chips * step_rows, 128), f32)],
+        [pltpu.SemaphoreType.DMA((9,))],
         spaces={i: pltpu.HBM for i in range(9)},
     )(
         electrons,
@@ -646,7 +639,7 @@
         phonon_need,
     )
     same = to_chips(send)
-    c_held, c_rest, ge4, gp4, gp8, gk, sk, sp, sp4, sp8, b0, b1 = call(
+    c_held, c_rest, ge4, gp4, gp8, gk, sk, sp, sp4, sp8, picks, mine, b0, b1 = call(
         functools.partial(prepare_kernel, cap),
         "prepare",
         [
@@ -660,38 +653,39 @@
             ((slots, tiles), bf16),
             ((rows4, tiles), bf16),
             ((rows8, 2 * tiles), bf16),
+            ((rows4, devices * step_rows), bf16),
+            ((rows4, 128), f32),
         ]
         + pass_out,
         [*streams, pltpu.VMEM(rest, bf16), rest_sems],
-        spaces={0: pltpu.SMEM, 5: pltpu.HBM},
+        spaces={0: pltpu.SMEM, 7: pltpu.HBM},
         out_spaces={1: pltpu.HBM},
         **work,
-    )(tile_count, kblock, partner, qslot, f, coupling)
+    )(tile_count, kblock, partner, qslot, f, pneed, qneed, coupling)
     same, c_held, b0 = lax.optimization_barrier((same, c_held, b0))
     other = between_cores(same)
     wide_block = ((chips * wide, 128), f32)
     k_rows, q_rows = ((kb, 128), f32), ((qb, 128), f32)
     forward_scratch = forward_streams + sums
-    send, e0, f1, serve = call(
+    send, e0, f1, serve, asked = call(
         functools.partial(first_kernel, cap),
         "first",
-        [wide_block, k_rows, k_rows, ((rows4, 128), bf16)],
+        [wide_block, k_rows, k_rows, ((rows4, 128), bf16), ((8 * devices, 128), bf16)],
         forward_scratch,
         spaces={14: pltpu.HBM},
         **work,
-    )(same, other, lists, f, n, energy, decay, ge4, gp4, sk, sp, b0, b1, c_held, c_rest)
-    share, owner, s8, st4, st8a, st8b = call(
+    )(same, other, picks, f, n, energy, decay, ge4, gp4, sk, sp, b0, b1, c_held, c_rest)
+    share, s8, st4, st8a, st8b = call(
         functools.partial(serve_kernel, cap, kb, qb),
         "serve",
         [
-            ((rows4, devices * slots), bf16),
-            ((qb, devices * slots), bf16),
+            ((rows4 + qb, devices * slots), bf16),
             ((rows8, 128), bf16),
             ((qb, rows4), bf16),
             ((qb, rows8), bf16),
             ((qb, rows8), bf16),
         ],
-    )(same, other, serve, mine)
+    )(asked, serve, mine)
     back = call(backward_kernel, "backward", pass_out, streams, spaces={2: pltpu.HBM}, **work)
 
     def middle(ends, send, outs, f, e, own, n, contributions):
@@ -704,10 +698,10 @@
             "middle",
             outs,
             forward_scratch,
-            spaces={18: pltpu.HBM},
+            spaces={17: pltpu.HBM},
             **work,
         )(
-            same, other, share, owner, serve, f, e, own, n, energy, decay,
+            same, other, share, serve, f, e, own, n, energy, decay,
             ge4, gp4, sk, contributions, b0, b1, c_held, c_rest,
         )
 

time: 86.5 us -> 83.1 us (0.961)
  local copies, waits for them, and re-layouts: 2.83 us -> 0 us
  Pallas kernels: 36.9 us -> 36 us
    unnamed x36 -> x0, local copies, waits for them, and re-layouts: 2.83 us -> none
    pallas_call x11, Pallas kernels: 36.9 us -> 36 us  [run(): pl.pallas_call(kernel, out_shape=[pltpu.HBM(*o) if (out_spaces or {}).get...]
  transfers between devices with their start and end apart: 7 -> 7, of which waited for: 7 -> 7; matrix products, arithmetic and copies ran while one was open for 0% -> 0% of each run, Pallas kernels for 20% -> 21%
where the time goes in v10:
time: 83.1 us; the launch traced here: 82.5 us
  Pallas kernels  36 us (43%)
  starting transfers between devices  18 us (22%)
  waiting for transfers between devices  17.3 us (21%)
  blocking collectives  9.83 us (12%)
  between operations  1.39 us (2%)
    pallas_call x11, Pallas kernels, run(): pl.pallas_call(kernel, out_shape=[pltpu.HBM(*o) if (out_spaces or {}).get...  36 us
    all_to_all x3, starting transfers between devices, to_chips(): lax.all_to_all(x, 'bulk', split_axis=0, concat_axis=0, tiled=True, axis_i...  14.5 us
    all_to_all x3, waiting for transfers between devices, to_chips(): lax.all_to_all(x, 'bulk', split_axis=0, concat_axis=0, tiled=True, axis_i...  10.5 us
    all_to_all x1, blocking collectives, exchange(): return lax.all_to_all(x, 'bulk', split_axis=0, concat_axis=0, tiled=True)  9.83 us
    ppermute x3, waiting for transfers between devices, between_cores(): return lax.ppermute(x, 'bulk', [(i, i ^ 1) for i in range(devices)])  3.95 us
    all_to_all x1, starting transfers between devices, exchange(): return lax.all_to_all(x, 'bulk', split_axis=0, concat_axis=0, tiled=True)  3.49 us
    all_to_all x1, waiting for transfers between devices, exchange(): return lax.all_to_all(x, 'bulk', split_axis=0, concat_axis=0, tiled=True)  2.85 us
  transfers between devices with their start and end apart: 7, of which 7 were waited for; matrix products, arithmetic and copies ran while one was open for 0% of the time, Pallas kernels for 21%

profile of v10, /device:TPU:0, one launch (start us, length us, event | category | flops | bytes accessed | tf_op | source)
XLA Modules:
  0.0 82.5 jit_solution(45289460668915793)
XLA Ops:
  0.6 1.6 %need.1 = (f32[32,128]{1,0:T(8,128)S(1)}, f32[16,128]{1,0:T(8,128)S(1)}, f32[16,128]{1,0:T(8,128)S(1)}, f32[16,128]{1,0:T(8,128)S(1)}, s32[1,256]{1,0:T(1,128)S(...) custom-call(f32[32,128]{1,0:T(8,128)} %refs_0_.1, ...), custom_call_target="tpu_custom_call" | custom-call | tf_op jit(solution)/shard_map/need/pallas_call | solution.py:545
  2.2 7.3 %all-to-all-start = ((f32[8,56,128]{2,1,0:T(8,128)}), f32[8,56,128]{2,1,0:T(8,128)S(1)}, u32[]{:S(2)}, u32[]{:S(2)}) async-start(f32[8,56,128]{2,1,0:T(8,128)} %bitcast.3), calls=%async_computation | async-start | bytes 458752 | tf_op jit(solution)/shard_map/all_to_all | solution.py:617
  10.2 5.5 %prepare.1 = (bf16[64,128,128]{2,1,0:T(8,128)(2,1)S(1)}, bf16[192,128,128]{2,1,0:T(8,128)(2,1)}, bf16[256,64]{1,0:T(8,128)(2,1)S(1)}, bf16[256,64]{1,0:T(8,128)(...) custom-call(s32[1]{0:T(128)S(6)} %copy.13.count_ref, ...), custom_call_target="tpu_custom_call" | custom-call | flops 134217728 | bytes 8388608 | tf_op jit(solution)/shard_map/prepare/pallas_call | solution.py:545
  15.7 2.3 %all-to-all-done = f32[8,56,128]{2,1,0:T(8,128)S(1)} async-done(((f32[8,56,128]{2,1,0:T(8,128)}), f32[8,56,128]{2,1,0:T(8,128)S(1)}, u32[]{:S(2)}, u32[]{:S(2)}) %all-to-all-start) | async-done | bytes 229408 | tf_op jit(solution)/shard_map/all_to_all | solution.py:617
  18.0 0.0 collective-permute-start
  18.0 1.5 %collective-permute-done.other_ref = f32[448,128]{1,0:T(8,128)S(1)} collective-permute-done((f32[448,128]{1,0:T(8,128)S(1)}, f32[448,128]{1,0:T(8,128)S(1)}, u32[]{:S(2)}, u32[]{:S(2)}) %collective-permute-start) | collective-permute-done | bytes 229408 | tf_op jit(solution)/shard_map/ppermute | solution.py:622
  19.4 4.6 %first.1 = (f32[320,128]{1,0:T(8,128)}, f32[32,128]{1,0:T(8,128)S(1)}, f32[32,128]{1,0:T(8,128)S(1)}, bf16[64,128]{1,0:T(8,128)(2,1)S(1)}, bf16[128,128]{1,0:T(8,128)(2,1)S(1)}) custom-call(f32[448,128]{1,0:T(8,128)S(1)} %bitcast.14, f32[448,128]{1,0:T(8,128)S(1)} %collective-permute-done.other_ref, bf16[64,896]{1,0:T(8,128)(2,1)S(1)} %get-tuple-element.70.list_ref, ...), custom_call_target="tpu_custom_call" | custom-call | flops 134217728 | bytes 8388608 | tf_op jit(solution)/shard_map/first/pallas_call | solution.py:545
  24.0 3.8 %all-to-all-start.1 = ((f32[8,40,128]{2,1,0:T(8,128)}), f32[8,40,128]{2,1,0:T(8,128)S(1)}, u32[]{:S(2)}, u32[]{:S(2)}) async-start(f32[8,40,128]{2,1,0:T(8,128)} %bitcast.5), calls=%async_computation.1 | async-start | bytes 327680 | tf_op jit(solution)/shard_map/all_to_all | solution.py:617
  27.9 3.7 %backward.3 = (f32[32,8,128]{2,1,0:T(8,128)S(1)}, f32[32,8,128]{2,1,0:T(8,128)S(1)}) custom-call(f32[32,128]{1,0:T(8,128)S(1)} %get-tuple-element.83.f_ref.own_ref, bf16[256,32]{1,0:T(8,128)(2,1)S(1)} %get-tuple-element.84.gk_ref, bf16[256,128,128]{2,1,0:T(8,128)(2,1)} %c_hbm.7), custom_call_target="tpu_custom_call" | custom-call | flops 134217728 | bytes 8388608 | tf_op jit(solution)/shard_map/backward/pallas_call | solution.py:545
  31.6 4.0 %all-to-all-done.1 = f32[8,40,128]{2,1,0:T(8,128)S(1)} async-done(((f32[8,40,128]{2,1,0:T(8,128)}), f32[8,40,128]{2,1,0:T(8,128)S(1)}, u32[]{:S(2)}, u32[]{:S(2)}) %all-to-all-start.1) | async-done | bytes 163872 | tf_op jit(solution)/shard_map/all_to_all | solution.py:617
  35.6 0.0 collective-permute-start.1
  35.6 0.3 serve.1
  36.0 1.1 %collective-permute-done.1.other_ref = f32[320,128]{1,0:T(8,128)S(1)} collective-permute-done((f32[320,128]{1,0:T(8,128)S(1)}, f32[320,128]{1,0:T(8,128)S(1)}, u32[]{:S(2)}, u32[]{:S(2)}) %collective-permute-start.1) | collective-permute-done | bytes 163872 | tf_op jit(solution)/shard_map/ppermute | solution.py:622
  37.0 4.3 %middle.2 = (f32[320,128]{1,0:T(8,128)}, f32[16,128]{1,0:T(8,128)S(1)}, f32[32,128]{1,0:T(8,128)S(1)}) custom-call(f32[320,128]{1,0:T(8,128)S(1)} %bitcast.16, f32[320,128]{1,0:T(8,128)S(1)} %collective-permute-done.1.other_ref, bf16[80,512]{1,0:T(8,128)(2,1)S(1)} %get-tuple-element.90.share_ref, bf16[64,128]{1,0:T(8,128)(2,1)S(1)} %get-tuple-element.88.hot_ref.serve_ref, ...), custom_call_target="tpu_custom_call" | custom-call | flops 134217728 | bytes 8388608 | tf_op jit(solution)/shard_map/middle/pallas_call | solution.py:545
  41.3 3.4 %all-to-all-start.2 = ((f32[8,40,128]{2,1,0:T(8,128)}), f32[8,40,128]{2,1,0:T(8,128)S(1)}, u32[]{:S(2)}, u32[]{:S(2)}) async-start(f32[8,40,128]{2,1,0:T(8,128)} %bitcast.7), calls=%async_computation.2 | async-start | bytes 327680 | tf_op jit(solution)/shard_map/all_to_all | solution.py:617
  44.7 3.7 %backward.4 = (f32[32,8,128]{2,1,0:T(8,128)S(1)}, f32[32,8,128]{2,1,0:T(8,128)S(1)}) custom-call(f32[32,128]{1,0:T(8,128)S(1)} %get-tuple-element.95.f_ref.own_ref.refs_1_, bf16[256,32]{1,0:T(8,128)(2,1)S(1)} %get-tuple-element.84.gk_ref, bf16[256,128,128]{2,1,0:T(8,128)(2,1)} %c_hbm.7), custom_call_target="tpu_custom_call" | custom-call | flops 134217728 | bytes 8388608 | tf_op jit(solution)/shard_map/backward/pallas_call | solution.py:545
  48.4 4.2 %all-to-all-done.2 = f32[8,40,128]{2,1,0:T(8,128)S(1)} async-done(((f32[8,40,128]{2,1,0:T(8,128)}), f32[8,40,128]{2,1,0:T(8,128)S(1)}, u32[]{:S(2)}, u32[]{:S(2)}) %all-to-all-start.2) | async-done | bytes 163872 | tf_op jit(solution)/shard_map/all_to_all | solution.py:617
  52.7 0.0 collective-permute-start.2
  52.7 1.4 %collective-permute-done.2.other_ref = f32[320,128]{1,0:T(8,128)S(1)} collective-permute-done((f32[320,128]{1,0:T(8,128)S(1)}, f32[320,128]{1,0:T(8,128)S(1)}, u32[]{:S(2)}, u32[]{:S(2)}) %collective-permute-start.2) | collective-permute-done | bytes 163872 | tf_op jit(solution)/shard_map/ppermute | solution.py:622
  54.1 4.2 %middle.3 = (f32[64,128]{1,0:T(8,128)}, f32[16,128]{1,0:T(8,128)S(1)}, f32[32,128]{1,0:T(8,128)S(1)}, f32[32,128]{1,0:T(8,128)S(1)}) custom-call(f32[320,128]{1,0:T(8,128)S(1)} %bitcast.18, f32[320,128]{1,0:T(8,128)S(1)} %collective-permute-done.2.other_ref, bf16[80,512]{1,0:T(8,128)(2,1)S(1)} %get-tuple-element.90.share_ref, ...), custom_call_target="tpu_custom_call" | custom-call | flops 134217728 | bytes 8388608 | tf_op jit(solution)/shard_map/middle/pallas_call | solution.py:545
  58.3 3.5 %all-to-all-start.3 = ((f32[16,4,128]{2,1,0:T(4,128)}), f32[16,4,128]{2,1,0:T(4,128)S(1)}, u32[]{:S(2)}, u32[]{:S(2)}) async-start(f32[16,4,128]{2,1,0:T(4,128)} %bitcast.9), calls=%async_computation.3 | async-start | bytes 65536 | tf_op jit(solution)/shard_map/all_to_all | solution.py:603
  61.8 3.7 %backward.5 = (f32[32,8,128]{2,1,0:T(8,128)S(1)}, f32[32,8,128]{2,1,0:T(8,128)S(1)}) custom-call(f32[32,128]{1,0:T(8,128)S(1)} %get-tuple-element.107.f_ref.refs_2_, bf16[256,32]{1,0:T(8,128)(2,1)S(1)} %get-tuple-element.84.gk_ref, bf16[256,128,128]{2,1,0:T(8,128)(2,1)} %c_hbm.7), custom_call_target="tpu_custom_call" | custom-call | flops 134217728 | bytes 8388608 | tf_op jit(solution)/shard_map/backward/pallas_call | solution.py:545
  65.5 2.9 %all-to-all-done.3 = f32[16,4,128]{2,1,0:T(4,128)S(1)} async-done(((f32[16,4,128]{2,1,0:T(4,128)}), f32[16,4,128]{2,1,0:T(4,128)S(1)}, u32[]{:S(2)}, u32[]{:S(2)}) %all-to-all-start.3) | async-done | bytes 32800 | tf_op jit(solution)/shard_map/all_to_all | solution.py:603
  68.4 0.4 phonon.1
  68.8 9.8 %all_to_all.58 = f32[16,8,128]{2,1,0:T(8,128)S(1)} all-to-all(f32[16,8,128]{2,1,0:T(8,128)S(1)} %bitcast.21), channel_id=1, replica_groups=mesh['groups'=2,'bulk'=16] {'bulk'}, dimensions={0} | all-to-all | bytes 131072 | tf_op jit(solution)/shard_map/all_to_all | solution.py:603
  78.6 3.9 %last.1 = (f32[32,128]{1,0:T(8,128)}, f32[16,128]{1,0:T(8,128)}) custom-call(f32[128,128]{1,0:T(8,128)S(1)} %bitcast.19, f32[256,128]{1,0:T(8,128)S(1)} %get-tuple-element.111.refs_0_, f32[32,128]{1,0:T(8,128)S(1)} %get-tuple-element.95.f_ref.own_ref.refs_1_, f32[32,128]{1,0:T(8,128)S(1)} %get-tuple-element.107.f_ref.refs_2_, ...), custom_call_target="tpu_custom_call" | custom-call | flops 134217728 | bytes 8388608 | tf_op jit(solution)/shard_map/last/pallas_call | solution.py:545
Async XLA Ops:
  2.2 15.7 %all-to-all-start = ((f32[8,56,128]{2,1,0:T(8,128)}), f32[8,56,128]{2,1,0:T(8,128)S(1)}, u32[]{:S(2)}, u32[]{:S(2)}) async-start(f32[8,56,128]{2,1,0:T(8,128)} %bitcast.3), calls=%async_computation | async-start | bytes 458752 | tf_op jit(solution)/shard_map/all_to_all | solution.py:617
  18.0 1.5 %collective-permute-start = (f32[448,128]{1,0:T(8,128)S(1)}, f32[448,128]{1,0:T(8,128)S(1)}, u32[]{:S(2)}, u32[]{:S(2)}) collective-permute-start(f32[448,128]{1,0:T(8,128)S(1)} %bitcast.13), channel_id=1, source_target_pairs={{0,1},{1,0},{2,3},{3,2},{4,5},{5,4},{6,7},{7,6},{8,9},{9,8},{10,11... | collective-permute-start | bytes 688136 | tf_op jit(solution)/shard_map/ppermute | solution.py:622
  24.0 11.6 %all-to-all-start.1 = ((f32[8,40,128]{2,1,0:T(8,128)}), f32[8,40,128]{2,1,0:T(8,128)S(1)}, u32[]{:S(2)}, u32[]{:S(2)}) async-start(f32[8,40,128]{2,1,0:T(8,128)} %bitcast.5), calls=%async_computation.1 | async-start | bytes 327680 | tf_op jit(solution)/shard_map/all_to_all | solution.py:617
  35.6 1.4 %collective-permute-start.1 = (f32[320,128]{1,0:T(8,128)S(1)}, f32[320,128]{1,0:T(8,128)S(1)}, u32[]{:S(2)}, u32[]{:S(2)}) collective-permute-start(f32[320,128]{1,0:T(8,128)S(1)} %bitcast.15), channel_id=1, source_target_pairs={{0,1},{1,0},{2,3},{3,2},{4,5},{5,4},{6,7},{7,6},{8,9},{9,8},{10,11... | collective-permute-start | bytes 491528 | tf_op jit(solution)/shard_map/ppermute | solution.py:622
  41.3 11.4 %all-to-all-start.2 = ((f32[8,40,128]{2,1,0:T(8,128)}), f32[8,40,128]{2,1,0:T(8,128)S(1)}, u32[]{:S(2)}, u32[]{:S(2)}) async-start(f32[8,40,128]{2,1,0:T(8,128)} %bitcast.7), calls=%async_computation.2 | async-start | bytes 327680 | tf_op jit(solution)/shard_map/all_to_all | solution.py:617
  52.7 1.4 %collective-permute-start.2 = (f32[320,128]{1,0:T(8,128)S(1)}, f32[320,128]{1,0:T(8,128)S(1)}, u32[]{:S(2)}, u32[]{:S(2)}) collective-permute-start(f32[320,128]{1,0:T(8,128)S(1)} %bitcast.17), channel_id=1, source_target_pairs={{0,1},{1,0},{2,3},{3,2},{4,5},{5,4},{6,7},{7,6},{8,9},{9,8},{10,11... | collective-permute-start | bytes 491528 | tf_op jit(solution)/shard_map/ppermute | solution.py:622
  58.3 10.1 %all-to-all-start.3 = ((f32[16,4,128]{2,1,0:T(4,128)}), f32[16,4,128]{2,1,0:T(4,128)S(1)}, u32[]{:S(2)}, u32[]{:S(2)}) async-start(f32[16,4,128]{2,1,0:T(4,128)} %bitcast.9), calls=%async_computation.3 | async-start | bytes 65536 | tf_op jit(solution)/shard_map/all_to_all | solution.py:603

commit v11 on v10

--- a/solution.py
+++ b/solution.py
@@ -44,6 +44,21 @@
     return both[:, :128] + both[:, 128:]
 
 
+def gather_pair(table, x):
+    rows = x.shape[0]
+    hi = x.astype(bf16)
+    mid = (x - hi.astype(f32)).astype(bf16)
+    blank = jnp.zeros((rows, 128), bf16)
+
+    def both(part):
+        upper = jnp.concatenate([part, blank], axis=1)
+        lower = jnp.concatenate([blank, part], axis=1)
+        return dot(table, jnp.concatenate([upper, lower], axis=0))
+
+    res = both(hi) + both(mid)
+    return res[:, :128], res[:, 128:]
+
+
 def stacked(first, second):
     tiles = first.shape[0]
     return jnp.concatenate(
@@ -72,7 +87,7 @@
 
 def start_chunks(src, dst, sems):
     for i in range(sems.shape[0]):
-        chunk_copy(src, dst, sems, i).start()
+        chunk_copy(src, dst, sems, i).start(priority=i % 2)
 
 
 def start(copies):
@@ -172,8 +187,7 @@
     c_hbm,
     held_ref,
     t_hbm,
-    ge4_ref,
-    gp4_ref,
+    pair_ref,
     gp8_ref,
     gk_ref,
     sk_ref,
@@ -208,9 +222,8 @@
     x = iota((rows4, tiles), 0)
     row_e = (e // cap) * (2 * cap) + e % cap
     row_p = (q // cap) * (2 * cap) + cap + q % cap
-    ge4_ref[...] = ind(x == row_e).T.astype(bf16)
     p_hot = ind(x == row_p)
-    gp4_ref[...] = p_hot.T.astype(bf16)
+    pair_ref[...] = jnp.concatenate([ind(x == row_e), p_hot], axis=0).T.astype(bf16)
     sp4_ref[...] = jnp.where(used, p_hot, 0.0).astype(bf16)
     sp_ref[...] = jnp.where(used, ind(iota(sp_ref.shape, 0) == q), 0.0).astype(bf16)
     x = iota((rows8, tiles), 0)
@@ -351,8 +364,7 @@
     n_ref,
     energy_ref,
     decay_ref,
-    ge4_ref,
-    gp4_ref,
+    pair_ref,
     sk_ref,
     sp_ref,
     b0_ref,
@@ -376,8 +388,7 @@
     rows4 = list_ref.shape[0]
     peers = rows4 // (2 * cap)
     got = pick(list_ref[...], jnp.concatenate([same_ref[...], other_ref[...]], axis=0))
-    far = add_rows(ge4_ref[...], got)
-    bose = add_rows(gp4_ref[...], got)
+    far, bose = gather_pair(pair_ref[...], got)
     contributions = add_rows(sp_ref[...], phonon_terms(far, bose, b0_ref, b1_ref))
     lists = blocks(same_ref, other_ref, peers, kb + qb, 8).astype(bf16)
     asked_ref[...] = lists
@@ -415,8 +426,7 @@
     n_ref,
     energy_ref,
     decay_ref,
-    ge4_ref,
-    gp4_ref,
+    pair_ref,
     sk_ref,
     sp_ref,
     b0_ref,
@@ -440,8 +450,7 @@
     both = add_rows(share_ref[...], tails)
     shares, total = both[:rows4], both[rows4:]
     got = pick(at, heads) + weight * shares
-    far = add_rows(ge4_ref[...], got)
-    bose = add_rows(gp4_ref[...], got)
+    far, bose = gather_pair(pair_ref[...], got)
     terms = phonon_terms(far, bose, b0_ref, b1_ref)
     contributions = add_rows(sp_ref[...], terms)
     n = n_ref[...]
@@ -481,7 +490,7 @@
     n_ref,
     energy_ref,
     decay_ref,
-    ge4_ref,
+    pair_ref,
     st4_ref,
     sp8_ref,
     s8_ref,
@@ -499,7 +508,7 @@
     n1 = n + DT * rate
     p_ref[...] = rate
     n1_ref[...] = n1
-    far = add_rows(ge4_ref[...], got)
+    far = add_rows(pair_ref[:, : got.shape[0]], got)
     far_ref[...] = far
     gain = far * flat(b0_ref)
     both = jnp.concatenate([gain, gain - (1.0 - far) * flat(b1_ref)], axis=0)
@@ -639,14 +648,13 @@
         phonon_need,
     )
     same = to_chips(send)
-    c_held, c_rest, ge4, gp4, gp8, gk, sk, sp, sp4, sp8, picks, mine, b0, b1 = call(
+    c_held, c_rest, pair, gp8, gk, sk, sp, sp4, sp8, picks, mine, b0, b1 = call(
         functools.partial(prepare_kernel, cap),
         "prepare",
         [
             ((held, 128, 128), bf16),
             (rest, bf16),
-            ((tiles, rows4), bf16),
-            ((tiles, rows4), bf16),
+            ((tiles, 2 * rows4), bf16),
             ((tiles, rows8), bf16),
             ((tiles, kb), bf16),
             ((kb, tiles), bf16),
@@ -672,9 +680,9 @@
         "first",
         [wide_block, k_rows, k_rows, ((rows4, 128), bf16), ((8 * devices, 128), bf16)],
         forward_scratch,
-        spaces={14: pltpu.HBM},
+        spaces={13: pltpu.HBM},
         **work,
-    )(same, other, picks, f, n, energy, decay, ge4, gp4, sk, sp, b0, b1, c_held, c_rest)
+    )(same, other, picks, f, n, energy, decay, pair, sk, sp, b0, b1, c_held, c_rest)
     share, s8, st4, st8a, st8b = call(
         functools.partial(serve_kernel, cap, kb, qb),
         "serve",
@@ -698,11 +706,11 @@
             "middle",
             outs,
             forward_scratch,
-            spaces={17: pltpu.HBM},
+            spaces={16: pltpu.HBM},
             **work,
         )(
             same, other, share, serve, f, e, own, n, energy, decay,
-            ge4, gp4, sk, contributions, b0, b1, c_held, c_rest,
+            pair, sk, contributions, b0, b1, c_held, c_rest,
         )
 
     send, base, f2 = middle(False, send, [wide_block, q_rows, k_rows], f, e0, f1, n, sp)
@@ -715,7 +723,7 @@
         functools.partial(phonon_kernel, kb),
         "phonon",
         [block8, q_rows, q_rows, ((tiles, 128), f32)],
-    )(recv, n2, energy, decay, ge4, st4, sp8, s8, b0, b1)
+    )(recv, n2, energy, decay, pair, st4, sp8, s8, b0, b1)
     recv = exchange(send)
     f, n = call(
         last_kernel,

time: 83.1 us -> 85.4 us (1.028)
  Pallas kernels: 36 us -> 39.6 us
  waiting for transfers between devices: 17.3 us -> 15 us
    pallas_call x11, Pallas kernels: 36 us -> 39.6 us  [run(): pl.pallas_call(kernel, out_shape=[pltpu.HBM(*o) if (out_spaces or {}).get...]
    all_to_all x3, waiting for transfers between devices: 10.5 us -> 8.82 us  [to_chips(): lax.all_to_all(x, 'bulk', split_axis=0, concat_axis=0, tiled=True, axis_i...]
  transfers between devices with their start and end apart: 7 -> 7, of which waited for: 7 -> 7; matrix products, arithmetic and copies ran while one was open for 0% -> 0% of each run, Pallas kernels for 21% -> 23%
where the time goes in v11:
time: 85.4 us; the launch traced here: 84.9 us
  Pallas kernels  39.6 us (46%)
  starting transfers between devices  18.5 us (22%)
  waiting for transfers between devices  15 us (18%)
  blocking collectives  10.5 us (12%)
  between operations  1.39 us (2%)
    pallas_call x11, Pallas kernels, run(): pl.pallas_call(kernel, out_shape=[pltpu.HBM(*o) if (out_spaces or {}).get...  39.6 us
    all_to_all x3, starting transfers between devices, to_chips(): lax.all_to_all(x, 'bulk', split_axis=0, concat_axis=0, tiled=True, axis_i...  15 us
    all_to_all x1, blocking collectives, exchange(): return lax.all_to_all(x, 'bulk', split_axis=0, concat_axis=0, tiled=True)  10.5 us
    all_to_all x3, waiting for transfers between devices, to_chips(): lax.all_to_all(x, 'bulk', split_axis=0, concat_axis=0, tiled=True, axis_i...  8.82 us
    ppermute x3, waiting for transfers between devices, between_cores(): return lax.ppermute(x, 'bulk', [(i, i ^ 1) for i in range(devices)])  3.95 us
    all_to_all x1, starting transfers between devices, exchange(): return lax.all_to_all(x, 'bulk', split_axis=0, concat_axis=0, tiled=True)  3.49 us
    all_to_all x1, waiting for transfers between devices, exchange(): return lax.all_to_all(x, 'bulk', split_axis=0, concat_axis=0, tiled=True)  2.22 us
  transfers between devices with their start and end apart: 7, of which 7 were waited for; matrix products, arithmetic and copies ran while one was open for 0% of the time, Pallas kernels for 23%

profile of v11, /device:TPU:0, one launch (start us, length us, event | category | flops | bytes accessed | tf_op | source)
XLA Modules:
  0.0 84.9 jit_solution(8175928687411938814)
XLA Ops:
  0.6 1.6 %need.1 = (f32[32,128]{1,0:T(8,128)S(1)}, f32[16,128]{1,0:T(8,128)S(1)}, f32[16,128]{1,0:T(8,128)S(1)}, f32[16,128]{1,0:T(8,128)S(1)}, s32[1,256]{1,0:T(1,128)S(...) custom-call(f32[32,128]{1,0:T(8,128)} %refs_0_.1, ...), custom_call_target="tpu_custom_call" | custom-call | tf_op jit(solution)/shard_map/need/pallas_call | solution.py:554
  2.2 7.3 %all-to-all-start = ((f32[8,56,128]{2,1,0:T(8,128)}), f32[8,56,128]{2,1,0:T(8,128)S(1)}, u32[]{:S(2)}, u32[]{:S(2)}) async-start(f32[8,56,128]{2,1,0:T(8,128)} %bitcast.3), calls=%async_computation | async-start | bytes 458752 | tf_op jit(solution)/shard_map/all_to_all | solution.py:626
  10.2 6.0 %prepare.1 = (bf16[64,128,128]{2,1,0:T(8,128)(2,1)S(1)}, bf16[192,128,128]{2,1,0:T(8,128)(2,1)}, bf16[256,128]{1,0:T(8,128)(2,1)S(1)}, bf16[256,128]{1,0:T(8,128...) custom-call(s32[1]{0:T(128)S(6)} %copy.13.count_ref, ...), custom_call_target="tpu_custom_call" | custom-call | flops 134217728 | bytes 8388608 | tf_op jit(solution)/shard_map/prepare/pallas_call | solution.py:554
  16.1 1.8 %all-to-all-done = f32[8,56,128]{2,1,0:T(8,128)S(1)} async-done(((f32[8,56,128]{2,1,0:T(8,128)}), f32[8,56,128]{2,1,0:T(8,128)S(1)}, u32[]{:S(2)}, u32[]{:S(2)}) %all-to-all-start) | async-done | bytes 229408 | tf_op jit(solution)/shard_map/all_to_all | solution.py:626
  18.0 0.0 collective-permute-start
  18.0 1.5 %collective-permute-done.other_ref = f32[448,128]{1,0:T(8,128)S(1)} collective-permute-done((f32[448,128]{1,0:T(8,128)S(1)}, f32[448,128]{1,0:T(8,128)S(1)}, u32[]{:S(2)}, u32[]{:S(2)}) %collective-permute-start) | collective-permute-done | bytes 229408 | tf_op jit(solution)/shard_map/ppermute | solution.py:631
  19.4 4.8 %first.1 = (f32[320,128]{1,0:T(8,128)}, f32[32,128]{1,0:T(8,128)S(1)}, f32[32,128]{1,0:T(8,128)S(1)}, bf16[64,128]{1,0:T(8,128)(2,1)S(1)}, bf16[128,128]{1,0:T(8,128)(2,1)S(1)}) custom-call(f32[448,128]{1,0:T(8,128)S(1)} %bitcast.14, f32[448,128]{1,0:T(8,128)S(1)} %collective-permute-done.other_ref, bf16[64,896]{1,0:T(8,128)(2,1)S(1)} %get-tuple-element.69.list_ref, ...), custom_call_target="tpu_custom_call" | custom-call | flops 134217728 | bytes 8388608 | tf_op jit(solution)/shard_map/first/pallas_call | solution.py:554
  24.2 4.3 %all-to-all-start.1 = ((f32[8,40,128]{2,1,0:T(8,128)}), f32[8,40,128]{2,1,0:T(8,128)S(1)}, u32[]{:S(2)}, u32[]{:S(2)}) async-start(f32[8,40,128]{2,1,0:T(8,128)} %bitcast.5), calls=%async_computation.1 | async-start | bytes 327680 | tf_op jit(solution)/shard_map/all_to_all | solution.py:626
  28.5 4.4 %backward.3 = (f32[32,8,128]{2,1,0:T(8,128)S(1)}, f32[32,8,128]{2,1,0:T(8,128)S(1)}) custom-call(f32[32,128]{1,0:T(8,128)S(1)} %get-tuple-element.81.f_ref.own_ref, bf16[256,32]{1,0:T(8,128)(2,1)S(1)} %get-tuple-element.82.gk_ref, bf16[256,128,128]{2,1,0:T(8,128)(2,1)} %c_hbm.7), custom_call_target="tpu_custom_call" | custom-call | flops 134217728 | bytes 8388608 | tf_op jit(solution)/shard_map/backward/pallas_call | solution.py:554
  32.9 3.4 %all-to-all-done.1 = f32[8,40,128]{2,1,0:T(8,128)S(1)} async-done(((f32[8,40,128]{2,1,0:T(8,128)}), f32[8,40,128]{2,1,0:T(8,128)S(1)}, u32[]{:S(2)}, u32[]{:S(2)}) %all-to-all-start.1) | async-done | bytes 163872 | tf_op jit(solution)/shard_map/all_to_all | solution.py:626
  36.3 0.0 collective-permute-start.1
  36.3 0.3 serve.1
  36.6 1.1 %collective-permute-done.1.other_ref = f32[320,128]{1,0:T(8,128)S(1)} collective-permute-done((f32[320,128]{1,0:T(8,128)S(1)}, f32[320,128]{1,0:T(8,128)S(1)}, u32[]{:S(2)}, u32[]{:S(2)}) %collective-permute-start.1) | collective-permute-done | bytes 163872 | tf_op jit(solution)/shard_map/ppermute | solution.py:631
  37.7 4.7 %middle.2 = (f32[320,128]{1,0:T(8,128)}, f32[16,128]{1,0:T(8,128)S(1)}, f32[32,128]{1,0:T(8,128)S(1)}) custom-call(f32[320,128]{1,0:T(8,128)S(1)} %bitcast.16, f32[320,128]{1,0:T(8,128)S(1)} %collective-permute-done.1.other_ref, bf16[80,512]{1,0:T(8,128)(2,1)S(1)} %get-tuple-element.88.share_ref, bf16[64,128]{1,0:T(8,128)(2,1)S(1)} %get-tuple-element.86.hot_ref.serve_ref, ...), custom_call_target="tpu_custom_call" | custom-call | flops 134217728 | bytes 8388608 | tf_op jit(solution)/shard_map/middle/pallas_call | solution.py:554
  42.4 3.4 %all-to-all-start.2 = ((f32[8,40,128]{2,1,0:T(8,128)}), f32[8,40,128]{2,1,0:T(8,128)S(1)}, u32[]{:S(2)}, u32[]{:S(2)}) async-start(f32[8,40,128]{2,1,0:T(8,128)} %bitcast.7), calls=%async_computation.2 | async-start | bytes 327680 | tf_op jit(solution)/shard_map/all_to_all | solution.py:626
  45.8 4.4 %backward.4 = (f32[32,8,128]{2,1,0:T(8,128)S(1)}, f32[32,8,128]{2,1,0:T(8,128)S(1)}) custom-call(f32[32,128]{1,0:T(8,128)S(1)} %get-tuple-element.93.f_ref.own_ref.refs_1_, bf16[256,32]{1,0:T(8,128)(2,1)S(1)} %get-tuple-element.82.gk_ref, bf16[256,128,128]{2,1,0:T(8,128)(2,1)} %c_hbm.7), custom_call_target="tpu_custom_call" | custom-call | flops 134217728 | bytes 8388608 | tf_op jit(solution)/shard_map/backward/pallas_call | solution.py:554
  50.1 3.6 %all-to-all-done.2 = f32[8,40,128]{2,1,0:T(8,128)S(1)} async-done(((f32[8,40,128]{2,1,0:T(8,128)}), f32[8,40,128]{2,1,0:T(8,128)S(1)}, u32[]{:S(2)}, u32[]{:S(2)}) %all-to-all-start.2) | async-done | bytes 163872 | tf_op jit(solution)/shard_map/all_to_all | solution.py:626
  53.8 0.0 collective-permute-start.2
  53.8 1.4 %collective-permute-done.2.other_ref = f32[320,128]{1,0:T(8,128)S(1)} collective-permute-done((f32[320,128]{1,0:T(8,128)S(1)}, f32[320,128]{1,0:T(8,128)S(1)}, u32[]{:S(2)}, u32[]{:S(2)}) %collective-permute-start.2) | collective-permute-done | bytes 163872 | tf_op jit(solution)/shard_map/ppermute | solution.py:631
  55.2 4.5 %middle.3 = (f32[64,128]{1,0:T(8,128)}, f32[16,128]{1,0:T(8,128)S(1)}, f32[32,128]{1,0:T(8,128)S(1)}, f32[32,128]{1,0:T(8,128)S(1)}) custom-call(f32[320,128]{1,0:T(8,128)S(1)} %bitcast.18, f32[320,128]{1,0:T(8,128)S(1)} %collective-permute-done.2.other_ref, bf16[80,512]{1,0:T(8,128)(2,1)S(1)} %get-tuple-element.88.share_ref, ...), custom_call_target="tpu_custom_call" | custom-call | flops 134217728 | bytes 8388608 | tf_op jit(solution)/shard_map/middle/pallas_call | solution.py:554
  59.6 3.5 %all-to-all-start.3 = ((f32[16,4,128]{2,1,0:T(4,128)}), f32[16,4,128]{2,1,0:T(4,128)S(1)}, u32[]{:S(2)}, u32[]{:S(2)}) async-start(f32[16,4,128]{2,1,0:T(4,128)} %bitcast.9), calls=%async_computation.3 | async-start | bytes 65536 | tf_op jit(solution)/shard_map/all_to_all | solution.py:612
  63.1 4.4 %backward.5 = (f32[32,8,128]{2,1,0:T(8,128)S(1)}, f32[32,8,128]{2,1,0:T(8,128)S(1)}) custom-call(f32[32,128]{1,0:T(8,128)S(1)} %get-tuple-element.105.f_ref.refs_2_, bf16[256,32]{1,0:T(8,128)(2,1)S(1)} %get-tuple-element.82.gk_ref, bf16[256,128,128]{2,1,0:T(8,128)(2,1)} %c_hbm.7), custom_call_target="tpu_custom_call" | custom-call | flops 134217728 | bytes 8388608 | tf_op jit(solution)/shard_map/backward/pallas_call | solution.py:554
  67.5 2.2 %all-to-all-done.3 = f32[16,4,128]{2,1,0:T(4,128)S(1)} async-done(((f32[16,4,128]{2,1,0:T(4,128)}), f32[16,4,128]{2,1,0:T(4,128)S(1)}, u32[]{:S(2)}, u32[]{:S(2)}) %all-to-all-start.3) | async-done | bytes 32800 | tf_op jit(solution)/shard_map/all_to_all | solution.py:612
  69.7 0.4 phonon.1
  70.1 10.5 %all_to_all.58 = f32[16,8,128]{2,1,0:T(8,128)S(1)} all-to-all(f32[16,8,128]{2,1,0:T(8,128)S(1)} %bitcast.21), channel_id=1, replica_groups=mesh['groups'=2,'bulk'=16] {'bulk'}, dimensions={0} | all-to-all | bytes 131072 | tf_op jit(solution)/shard_map/all_to_all | solution.py:612
  80.6 4.3 %last.1 = (f32[32,128]{1,0:T(8,128)}, f32[16,128]{1,0:T(8,128)}) custom-call(f32[128,128]{1,0:T(8,128)S(1)} %bitcast.19, f32[256,128]{1,0:T(8,128)S(1)} %get-tuple-element.109.refs_0_, f32[32,128]{1,0:T(8,128)S(1)} %get-tuple-element.93.f_ref.own_ref.refs_1_, f32[32,128]{1,0:T(8,128)S(1)} %get-tuple-element.105.f_ref.refs_2_, ...), custom_call_target="tpu_custom_call" | custom-call | flops 134217728 | bytes 8388608 | tf_op jit(solution)/shard_map/last/pallas_call | solution.py:554
Async XLA Ops:
  2.2 15.7 %all-to-all-start = ((f32[8,56,128]{2,1,0:T(8,128)}), f32[8,56,128]{2,1,0:T(8,128)S(1)}, u32[]{:S(2)}, u32[]{:S(2)}) async-start(f32[8,56,128]{2,1,0:T(8,128)} %bitcast.3), calls=%async_computation | async-start | bytes 458752 | tf_op jit(solution)/shard_map/all_to_all | solution.py:626
  18.0 1.5 %collective-permute-start = (f32[448,128]{1,0:T(8,128)S(1)}, f32[448,128]{1,0:T(8,128)S(1)}, u32[]{:S(2)}, u32[]{:S(2)}) collective-permute-start(f32[448,128]{1,0:T(8,128)S(1)} %bitcast.13), channel_id=1, source_target_pairs={{0,1},{1,0},{2,3},{3,2},{4,5},{5,4},{6,7},{7,6},{8,9},{9,8},{10,11... | collective-permute-start | bytes 688136 | tf_op jit(solution)/shard_map/ppermute | solution.py:631
  24.2 12.0 %all-to-all-start.1 = ((f32[8,40,128]{2,1,0:T(8,128)}), f32[8,40,128]{2,1,0:T(8,128)S(1)}, u32[]{:S(2)}, u32[]{:S(2)}) async-start(f32[8,40,128]{2,1,0:T(8,128)} %bitcast.5), calls=%async_computation.1 | async-start | bytes 327680 | tf_op jit(solution)/shard_map/all_to_all | solution.py:626
  36.3 1.4 %collective-permute-start.1 = (f32[320,128]{1,0:T(8,128)S(1)}, f32[320,128]{1,0:T(8,128)S(1)}, u32[]{:S(2)}, u32[]{:S(2)}) collective-permute-start(f32[320,128]{1,0:T(8,128)S(1)} %bitcast.15), channel_id=1, source_target_pairs={{0,1},{1,0},{2,3},{3,2},{4,5},{5,4},{6,7},{7,6},{8,9},{9,8},{10,11... | collective-permute-start | bytes 491528 | tf_op jit(solution)/shard_map/ppermute | solution.py:631
  42.4 11.4 %all-to-all-start.2 = ((f32[8,40,128]{2,1,0:T(8,128)}), f32[8,40,128]{2,1,0:T(8,128)S(1)}, u32[]{:S(2)}, u32[]{:S(2)}) async-start(f32[8,40,128]{2,1,0:T(8,128)} %bitcast.7), calls=%async_computation.2 | async-start | bytes 327680 | tf_op jit(solution)/shard_map/all_to_all | solution.py:626
  53.8 1.4 %collective-permute-start.2 = (f32[320,128]{1,0:T(8,128)S(1)}, f32[320,128]{1,0:T(8,128)S(1)}, u32[]{:S(2)}, u32[]{:S(2)}) collective-permute-start(f32[320,128]{1,0:T(8,128)S(1)} %bitcast.17), channel_id=1, source_target_pairs={{0,1},{1,0},{2,3},{3,2},{4,5},{5,4},{6,7},{7,6},{8,9},{9,8},{10,11... | collective-permute-start | bytes 491528 | tf_op jit(solution)/shard_map/ppermute | solution.py:631
  59.6 10.1 %all-to-all-start.3 = ((f32[16,4,128]{2,1,0:T(4,128)}), f32[16,4,128]{2,1,0:T(4,128)S(1)}, u32[]{:S(2)}, u32[]{:S(2)}) async-start(f32[16,4,128]{2,1,0:T(4,128)} %bitcast.9), calls=%async_computation.3 | async-start | bytes 65536 | tf_op jit(solution)/shard_map/all_to_all | solution.py:612

commit v12 on v11

--- a/solution.py
+++ b/solution.py
@@ -10,6 +10,7 @@
 DT = 0.05
 CHUNKS = 8
 HELD_CHUNKS = 2
+FETCHED_CHUNKS = 2
 f32 = jnp.float32
 bf16 = jnp.bfloat16
 VMEM_LIMIT = 48 * 1024 * 1024
@@ -79,15 +80,16 @@
     return ref[...].reshape(-1, 128)
 
 
-def chunk_copy(src, dst, sems, i):
-    size = src.shape[0] // sems.shape[0]
-    here = pl.ds(i * size, size)
-    return pltpu.make_async_copy(src.at[here], dst.at[here], sems.at[i])
-
-
-def start_chunks(src, dst, sems):
+def chunk_copy(src, dst, sems, i, skip=0):
+    size = dst.shape[0] // sems.shape[0]
+    return pltpu.make_async_copy(
+        src.at[pl.ds(skip + i * size, size)], dst.at[pl.ds(i * size, size)], sems.at[i]
+    )
+
+
+def start_chunks(src, dst, sems, skip=0):
     for i in range(sems.shape[0]):
-        chunk_copy(src, dst, sems, i).start(priority=i % 2)
+        chunk_copy(src, dst, sems, i, skip).start()
 
 
 def start(copies):
@@ -117,20 +119,21 @@
         out1[base + g] = res[8:]
 
 
-def tile_products(w_ref, parts, out0, out1):
+def tile_products(w_ref, parts, out0, out1, after=None, carry=0):
     size = w_ref.shape[0] // CHUNKS
     base = 0
     for c_ref, c_hbm, sems in parts:
         groups = c_ref.shape[0] // 8
 
-        def chunk(i, _):
+        def chunk(i, carry):
             if c_hbm is not None:
                 chunk_copy(c_hbm, c_ref, sems, i).wait()
             chunk_products(w_ref, c_ref, i, base, out0, out1)
-            return 0
-
-        lax.fori_loop(0, groups // size, chunk, 0)
+            return after(base // size + i, carry) if after else carry
+
+        carry = lax.fori_loop(0, groups // size, chunk, carry)
         base += groups
+    return carry
 
 
 def backward_pass(own, c_hbm, c_ref, sems, w_ref, out0, out1):
@@ -138,10 +141,20 @@
     tile_products(w_ref, [(c_ref, c_hbm, sems)], out0, out1)
 
 
-def electron_rate(sum_k, far, bose, f, parts, w_ref, o0, o1):
+def electron_rate(sum_k_ref, far, bose, f, parts, w_ref, o0, o1):
     left_sides(far * (1.0 + bose), far + bose, w_ref)
-    tile_products(w_ref, parts, o0, o1)
-    return add_rows(sum_k, flat(o0)) - f * add_rows(sum_k, flat(o1))
+    size = w_ref.shape[0] // CHUNKS
+
+    def after(i, totals):
+        sums = sum_k_ref[i]
+        return tuple(
+            total + add_rows(sums, out[pl.ds(i * size, size)].reshape(-1, 128))
+            for total, out in zip(totals, (o0, o1))
+        )
+
+    nothing = jnp.zeros_like(f)
+    gain, loss = tile_products(w_ref, parts, o0, o1, after, (nothing, nothing))
+    return gain - f * loss
 
 
 def my_core():
@@ -218,7 +231,10 @@
     gk_ref[...] = k_hot.T.astype(bf16)
     own = add_rows(gk_ref[...], f_ref[...])
     left_sides(1.0 - own, own, w_ref)
-    sk_ref[...] = jnp.where(used, k_hot, 0.0).astype(bf16)
+    sums = jnp.where(used, k_hot, 0.0)
+    width = tiles // CHUNKS
+    for i in range(CHUNKS):
+        sk_ref[i] = sums[:, i * width : (i + 1) * width].astype(bf16)
     x = iota((rows4, tiles), 0)
     row_e = (e // cap) * (2 * cap) + e % cap
     row_p = (q // cap) * (2 * cap) + cap + q % cap
@@ -370,6 +386,7 @@
     b0_ref,
     b1_ref,
     held_ref,
+    fetched_ref,
     c_hbm,
     send,
     e_ref,
@@ -382,12 +399,12 @@
     o0,
     o1,
 ):
-    start_chunks(c_hbm, c_ref, sems)
+    start_chunks(c_hbm, c_ref, sems, fetched_ref.shape[0])
     f, n = f_ref[...], n_ref[...]
     kb, qb = f.shape[0], n.shape[0]
     rows4 = list_ref.shape[0]
     peers = rows4 // (2 * cap)
-    got = pick(list_ref[...], jnp.concatenate([same_ref[...], other_ref[...]], axis=0))
+    got = add_rows(list_ref[...], jnp.concatenate([same_ref[...], other_ref[...]], axis=0))
     far, bose = gather_pair(pair_ref[...], got)
     contributions = add_rows(sp_ref[...], phonon_terms(far, bose, b0_ref, b1_ref))
     lists = blocks(same_ref, other_ref, peers, kb + qb, 8).astype(bf16)
@@ -405,8 +422,8 @@
     hot = jnp.where(lane.astype(f32) == col, 1.0, 0.0).astype(bf16)
     hot_ref[...] = hot
     base = n - DT * decay_ref[...] * (n - thermal_of(energy_ref))
-    parts = [(held_ref, None, None), (c_ref, c_hbm, sems)]
-    rate = electron_rate(sk_ref[...], far, bose, f, parts, w_ref, o0, o1)
+    parts = [(held_ref, None, None), (fetched_ref, None, None), (c_ref, c_hbm, sems)]
+    rate = electron_rate(sk_ref, far, bose, f, parts, w_ref, o0, o1)
     f1 = f + DT * rate
     e_ref[...] = rate
     f1_ref[...] = f1
@@ -432,12 +449,13 @@
     b0_ref,
     b1_ref,
     held_ref,
+    fetched_ref,
     c_hbm,
     send,
     *refs,
 ):
     w_ref, c_ref, sems, o0, o1 = refs[-5:]
-    start_chunks(c_hbm, c_ref, sems)
+    start_chunks(c_hbm, c_ref, sems, fetched_ref.shape[0])
     rows4 = serve_ref.shape[0]
     peers = rows4 // (2 * cap)
     slots = peers * cap
@@ -449,17 +467,17 @@
     weight = DT / 2.0 if ends else DT
     both = add_rows(share_ref[...], tails)
     shares, total = both[:rows4], both[rows4:]
-    got = pick(at, heads) + weight * shares
+    got = add_rows(at, heads) + weight * shares
     far, bose = gather_pair(pair_ref[...], got)
     terms = phonon_terms(far, bose, b0_ref, b1_ref)
     contributions = add_rows(sp_ref[...], terms)
     n = n_ref[...]
     own = own_ref[...]
-    parts = [(held_ref, None, None), (c_ref, c_hbm, sems)]
+    parts = [(held_ref, None, None), (fetched_ref, None, None), (c_ref, c_hbm, sems)]
     if ends:
         n2_ref, e2_ref, f3_ref = refs[:3]
         n2_ref[...] = n + (DT / 2.0) * total
-        rate = electron_rate(sk_ref[...], far, bose, own, parts, w_ref, o0, o1)
+        rate = electron_rate(sk_ref, far, bose, own, parts, w_ref, o0, o1)
         f3 = own + DT * rate
         e2_ref[...] = rate
         f3_ref[...] = f3
@@ -472,7 +490,7 @@
         n1 = n + DT * p0
         base = n + (DT / 2.0) * (p0 - decay * (n1 - thermal))
         base_ref[...] = base
-        rate = electron_rate(sk_ref[...], far, bose, own, parts, w_ref, o0, o1)
+        rate = electron_rate(sk_ref, far, bose, own, parts, w_ref, o0, o1)
         f2 = f_ref[...] + (DT / 2.0) * (e_ref[...] + rate)
         f2_ref[...] = f2
         put_broadcast(send, pick(serve_ref[...], padded(f2, base)), contributions)
@@ -482,6 +500,12 @@
     start_chunks(c_hbm, c_ref, sems)
     own = add_rows(gk_ref[...], f_ref[...])
     backward_pass(own, c_hbm, c_ref, sems, w_ref, b0_ref, b1_ref)
+
+
+def fetch_kernel(after_ref, c_hbm, fetched_ref, sems):
+    start_chunks(c_hbm, fetched_ref, sems)
+    for i in range(sems.shape[0]):
+        chunk_copy(c_hbm, fetched_ref, sems, i).wait()
 
 
 def phonon_kernel(
@@ -534,7 +558,7 @@
     n2 = n + (DT / 2.0) * (p_ref[...] + p1)
     n2_ref[...] = n2
     parts = [(held_ref, None, None), (c_ref, c_hbm, sems)]
-    rate = electron_rate(sk_ref[...], far_ref[...], bose, f1_ref[...], parts, w_ref, o0, o1)
+    rate = electron_rate(sk_ref, far_ref[...], bose, f1_ref[...], parts, w_ref, o0, o1)
     f2 = f_ref[...] + (DT / 2.0) * (e_ref[...] + rate)
     f2_ref[...] = f2
 
@@ -554,8 +578,7 @@
         return pl.pallas_call(
             kernel,
             out_shape=[
-                pltpu.HBM(*o) if (out_spaces or {}).get(i) else jax.ShapeDtypeStruct(*o)
-                for i, o in enumerate(outs)
+                (out_spaces or {}).get(i, jax.ShapeDtypeStruct)(*o) for i, o in enumerate(outs)
             ],
             in_specs=specs,
             out_specs=[
@@ -601,6 +624,9 @@
     rest = (tiles - held, 128, 128)
     rest_sems = pltpu.SemaphoreType.DMA((CHUNKS - HELD_CHUNKS,))
     forward_streams = [weights, pltpu.VMEM(rest, bf16), rest_sems]
+    fetched = (FETCHED_CHUNKS * (tiles // CHUNKS), 128, 128)
+    short = (rest[0] - fetched[0], 128, 128)
+    short_sems = pltpu.SemaphoreType.DMA((CHUNKS - HELD_CHUNKS - FETCHED_CHUNKS,))
     sums = [pltpu.VMEM((groups, 8, 128), f32)] * 2
     pass_out = [((groups, 8, 128), f32)] * 2
     block4 = ((rows4, 128), f32)
@@ -657,7 +683,7 @@
             ((tiles, 2 * rows4), bf16),
             ((tiles, rows8), bf16),
             ((tiles, kb), bf16),
-            ((kb, tiles), bf16),
+            ((CHUNKS, kb, tiles // CHUNKS), bf16),
             ((slots, tiles), bf16),
             ((rows4, tiles), bf16),
             ((rows8, 2 * tiles), bf16),
@@ -671,18 +697,31 @@
         **work,
     )(tile_count, kblock, partner, qslot, f, pneed, qneed, coupling)
     same, c_held, b0 = lax.optimization_barrier((same, c_held, b0))
-    other = between_cores(same)
     wide_block = ((chips * wide, 128), f32)
     k_rows, q_rows = ((kb, 128), f32), ((qb, 128), f32)
-    forward_scratch = forward_streams + sums
+    forward_scratch = [weights, pltpu.VMEM(short, bf16), short_sems] + sums
+
+    def fetch(after):
+        return call(
+            fetch_kernel,
+            "fetch",
+            [(fetched, bf16)],
+            [pltpu.SemaphoreType.DMA((FETCHED_CHUNKS,))],
+            spaces={0: pl.ANY, 1: pltpu.HBM},
+            out_spaces={0: pltpu.VMEM},
+            seen=fetched[0] * 128 * 128 * 2,
+        )(after, c_rest)[0]
+
+    other = between_cores(same)
+    c_fetched = fetch(same)
     send, e0, f1, serve, asked = call(
         functools.partial(first_kernel, cap),
         "first",
         [wide_block, k_rows, k_rows, ((rows4, 128), bf16), ((8 * devices, 128), bf16)],
         forward_scratch,
-        spaces={13: pltpu.HBM},
+        spaces={14: pltpu.HBM},
         **work,
-    )(same, other, picks, f, n, energy, decay, pair, sk, sp, b0, b1, c_held, c_rest)
+    )(same, other, picks, f, n, energy, decay, pair, sk, sp, b0, b1, c_held, c_fetched, c_rest)
     share, s8, st4, st8a, st8b = call(
         functools.partial(serve_kernel, cap, kb, qb),
         "serve",
@@ -701,16 +740,17 @@
         b0, b1 = back(own, gk, coupling)
         same, b0 = lax.optimization_barrier((same, b0))
         other = between_cores(same)
+        c_fetched = fetch(same)
         return call(
             functools.partial(middle_kernel, cap, ends),
             "middle",
             outs,
             forward_scratch,
-            spaces={16: pltpu.HBM},
+            spaces={17: pltpu.HBM},
             **work,
         )(
             same, other, share, serve, f, e, own, n, energy, decay,
-            pair, sk, contributions, b0, b1, c_held, c_rest,
+            pair, sk, contributions, b0, b1, c_held, c_fetched, c_rest,
         )
 
     send, base, f2 = middle(False, send, [wide_block, q_rows, k_rows], f, e0, f1, n, sp)
@@ -729,7 +769,7 @@
         last_kernel,
         "last",
         [k_rows, q_rows],
-        forward_scratch,
+        forward_streams + sums,
         spaces={15: pltpu.HBM},
         **work,
     )(

time: 85.4 us -> 85.9 us (level)
  Pallas kernels: 39.6 us -> 41.9 us
  waiting for transfers between devices: 15 us -> 14 us
    ppermute x3, waiting for transfers between devices: 3.95 us -> 0.01 us  [between_cores(): return lax.ppermute(x, 'bulk', [(i, i ^ 1) for i in range(devices)])]
    all_to_all x3, waiting for transfers between devices: 8.82 us -> 11.2 us  [to_chips(): lax.all_to_all(x, 'bulk', split_axis=0, concat_axis=0, tiled=True, axis_i...]
    pallas_call x11 -> x14, Pallas kernels: 39.6 us -> 41.9 us  [run(): pl.pallas_call(kernel, out_shape=[(out_spaces or {}).get(i, jax.ShapeDtyp...]
  transfers between devices with their start and end apart: 7 -> 7, of which waited for: 7 -> 4; matrix products, arithmetic and copies ran while one was open for 0% -> 0% of each run, Pallas kernels for 23% -> 26%
where the time goes in v12:
time: 85.9 us; the launch traced here: 85.3 us
  Pallas kernels  41.9 us (49%)
  starting transfers between devices  18.1 us (21%)
  waiting for transfers between devices  14 us (16%)
  blocking collectives  9.82 us (11%)
  between operations  1.43 us (2%)
    pallas_call x14, Pallas kernels, run(): pl.pallas_call(kernel, out_shape=[(out_spaces or {}).get(i, jax.ShapeDtyp...  41.9 us
    all_to_all x3, starting transfers between devices, to_chips(): lax.all_to_all(x, 'bulk', split_axis=0, concat_axis=0, tiled=True, axis_i...  14.6 us
    all_to_all x3, waiting for transfers between devices, to_chips(): lax.all_to_all(x, 'bulk', split_axis=0, concat_axis=0, tiled=True, axis_i...  11.2 us
    all_to_all x1, blocking collectives, exchange(): return lax.all_to_all(x, 'bulk', split_axis=0, concat_axis=0, tiled=True)  9.82 us
    all_to_all x1, starting transfers between devices, exchange(): return lax.all_to_all(x, 'bulk', split_axis=0, concat_axis=0, tiled=True)  3.49 us
    all_to_all x1, waiting for transfers between devices, exchange(): return lax.all_to_all(x, 'bulk', split_axis=0, concat_axis=0, tiled=True)  2.85 us
  transfers between devices with their start and end apart: 7, of which 4 were waited for; matrix products, arithmetic and copies ran while one was open for 0% of the time, Pallas kernels for 26%

profile of v12, /device:TPU:0, one launch (start us, length us, event | category | flops | bytes accessed | tf_op | source)
XLA Modules:
  0.0 85.3 jit_solution(4260006732368716134)
XLA Ops:
  0.6 1.6 %need.1 = (f32[32,128]{1,0:T(8,128)S(1)}, f32[16,128]{1,0:T(8,128)S(1)}, f32[16,128]{1,0:T(8,128)S(1)}, f32[16,128]{1,0:T(8,128)S(1)}, s32[1,256]{1,0:T(1,128)S(...) custom-call(f32[32,128]{1,0:T(8,128)} %refs_0_.1, ...), custom_call_target="tpu_custom_call" | custom-call | tf_op jit(solution)/shard_map/need/pallas_call | solution.py:578
  2.2 7.3 %all-to-all-start = ((f32[8,56,128]{2,1,0:T(8,128)}), f32[8,56,128]{2,1,0:T(8,128)S(1)}, u32[]{:S(2)}, u32[]{:S(2)}) async-start(f32[8,56,128]{2,1,0:T(8,128)} %bitcast.3), calls=%async_computation | async-start | bytes 458752 | tf_op jit(solution)/shard_map/all_to_all | solution.py:652
  10.2 5.6 %prepare.1 = (bf16[64,128,128]{2,1,0:T(8,128)(2,1)S(1)}, bf16[192,128,128]{2,1,0:T(8,128)(2,1)}, bf16[256,128]{1,0:T(8,128)(2,1)S(1)}, bf16[256,128]{1,0:T(8,128...) custom-call(s32[1]{0:T(128)S(6)} %copy.13.count_ref, ...), custom_call_target="tpu_custom_call" | custom-call | flops 134217728 | bytes 8388608 | tf_op jit(solution)/shard_map/prepare/pallas_call | solution.py:578
  15.8 2.2 %all-to-all-done = f32[8,56,128]{2,1,0:T(8,128)S(1)} async-done(((f32[8,56,128]{2,1,0:T(8,128)}), f32[8,56,128]{2,1,0:T(8,128)S(1)}, u32[]{:S(2)}, u32[]{:S(2)}) %all-to-all-start) | async-done | bytes 229408 | tf_op jit(solution)/shard_map/all_to_all | solution.py:652
  18.0 0.0 collective-permute-start
  18.0 1.6 %fetch.3.fetched_ref = bf16[64,128,128]{2,1,0:T(8,128)(2,1)S(1)} custom-call(f32[448,128]{1,0:T(8,128)S(1)} %bitcast.14, bf16[192,128,128]{2,1,0:T(8,128)(2,1)} %get-tuple-element.79.c_hbm.refs_14_), custom_call_target="tpu_custom_call" | custom-call | bytes 2097152 | tf_op jit(solution)/shard_map/fetch/pallas_call | solution.py:578
  19.5 0.0 collective-permute-done.other_ref
  19.5 4.7 %first.1 = (f32[320,128]{1,0:T(8,128)}, f32[32,128]{1,0:T(8,128)S(1)}, f32[32,128]{1,0:T(8,128)S(1)}, bf16[64,128]{1,0:T(8,128)(2,1)S(1)}, bf16[128,128]{1,0:T(8,128)(2,1)S(1)}) custom-call(f32[448,128]{1,0:T(8,128)S(1)} %bitcast.15, f32[448,128]{1,0:T(8,128)S(1)} %collective-permute-done.other_ref, bf16[64,896]{1,0:T(8,128)(2,1)S(1)} %get-tuple-element.69.list_ref, ...), custom_call_target="tpu_custom_call" | custom-call | flops 134217728 | bytes 8388608 | tf_op jit(solution)/shard_map/first/pallas_call | solution.py:578
  24.2 3.9 %all-to-all-start.1 = ((f32[8,40,128]{2,1,0:T(8,128)}), f32[8,40,128]{2,1,0:T(8,128)S(1)}, u32[]{:S(2)}, u32[]{:S(2)}) async-start(f32[8,40,128]{2,1,0:T(8,128)} %bitcast.5), calls=%async_computation.1 | async-start | bytes 327680 | tf_op jit(solution)/shard_map/all_to_all | solution.py:652
  28.1 3.7 %backward.3 = (f32[32,8,128]{2,1,0:T(8,128)S(1)}, f32[32,8,128]{2,1,0:T(8,128)S(1)}) custom-call(f32[32,128]{1,0:T(8,128)S(1)} %get-tuple-element.81.f_ref.own_ref, bf16[256,32]{1,0:T(8,128)(2,1)S(1)} %get-tuple-element.82.gk_ref, bf16[256,128,128]{2,1,0:T(8,128)(2,1)} %c_hbm.7), custom_call_target="tpu_custom_call" | custom-call | flops 134217728 | bytes 8388608 | tf_op jit(solution)/shard_map/backward/pallas_call | solution.py:578
  31.9 4.4 %all-to-all-done.1 = f32[8,40,128]{2,1,0:T(8,128)S(1)} async-done(((f32[8,40,128]{2,1,0:T(8,128)}), f32[8,40,128]{2,1,0:T(8,128)S(1)}, u32[]{:S(2)}, u32[]{:S(2)}) %all-to-all-start.1) | async-done | bytes 163872 | tf_op jit(solution)/shard_map/all_to_all | solution.py:652
  36.3 0.0 collective-permute-start.1
  36.3 0.3 serve.1
  36.6 1.6 %fetch.4.fetched_ref = bf16[64,128,128]{2,1,0:T(8,128)(2,1)S(1)} custom-call(f32[320,128]{1,0:T(8,128)S(1)} %bitcast.17, bf16[192,128,128]{2,1,0:T(8,128)(2,1)} %get-tuple-element.79.c_hbm.refs_14_), custom_call_target="tpu_custom_call" | custom-call | bytes 2097152 | tf_op jit(solution)/shard_map/fetch/pallas_call | solution.py:578
  38.2 0.0 collective-permute-done.1.other_ref
  38.2 4.6 %middle.2 = (f32[320,128]{1,0:T(8,128)}, f32[16,128]{1,0:T(8,128)S(1)}, f32[32,128]{1,0:T(8,128)S(1)}) custom-call(f32[320,128]{1,0:T(8,128)S(1)} %bitcast.18, f32[320,128]{1,0:T(8,128)S(1)} %collective-permute-done.1.other_ref, bf16[80,512]{1,0:T(8,128)(2,1)S(1)} %get-tuple-element.88.share_ref, bf16[64,128]{1,0:T(8,128)(2,1)S(1)} %get-tuple-element.86.hot_ref.serve_ref, ...), custom_call_target="tpu_custom_call" | custom-call | flops 134217728 | bytes 8388608 | tf_op jit(solution)/shard_map/middle/pallas_call | solution.py:578
  42.8 3.4 %all-to-all-start.2 = ((f32[8,40,128]{2,1,0:T(8,128)}), f32[8,40,128]{2,1,0:T(8,128)S(1)}, u32[]{:S(2)}, u32[]{:S(2)}) async-start(f32[8,40,128]{2,1,0:T(8,128)} %bitcast.7), calls=%async_computation.2 | async-start | bytes 327680 | tf_op jit(solution)/shard_map/all_to_all | solution.py:652
  46.2 3.7 %backward.4 = (f32[32,8,128]{2,1,0:T(8,128)S(1)}, f32[32,8,128]{2,1,0:T(8,128)S(1)}) custom-call(f32[32,128]{1,0:T(8,128)S(1)} %get-tuple-element.93.f_ref.own_ref.refs_1_, bf16[256,32]{1,0:T(8,128)(2,1)S(1)} %get-tuple-element.82.gk_ref, bf16[256,128,128]{2,1,0:T(8,128)(2,1)} %c_hbm.7), custom_call_target="tpu_custom_call" | custom-call | flops 134217728 | bytes 8388608 | tf_op jit(solution)/shard_map/backward/pallas_call | solution.py:578
  49.9 4.6 %all-to-all-done.2 = f32[8,40,128]{2,1,0:T(8,128)S(1)} async-done(((f32[8,40,128]{2,1,0:T(8,128)}), f32[8,40,128]{2,1,0:T(8,128)S(1)}, u32[]{:S(2)}, u32[]{:S(2)}) %all-to-all-start.2) | async-done | bytes 163872 | tf_op jit(solution)/shard_map/all_to_all | solution.py:652
  54.6 0.0 collective-permute-start.2
  54.6 1.6 %fetch.5.fetched_ref = bf16[64,128,128]{2,1,0:T(8,128)(2,1)S(1)} custom-call(f32[320,128]{1,0:T(8,128)S(1)} %bitcast.20, bf16[192,128,128]{2,1,0:T(8,128)(2,1)} %get-tuple-element.79.c_hbm.refs_14_), custom_call_target="tpu_custom_call" | custom-call | bytes 2097152 | tf_op jit(solution)/shard_map/fetch/pallas_call | solution.py:578
  56.1 0.0 collective-permute-done.2.other_ref
  56.1 4.6 %middle.3 = (f32[64,128]{1,0:T(8,128)}, f32[16,128]{1,0:T(8,128)S(1)}, f32[32,128]{1,0:T(8,128)S(1)}, f32[32,128]{1,0:T(8,128)S(1)}) custom-call(f32[320,128]{1,0:T(8,128)S(1)} %bitcast.21, f32[320,128]{1,0:T(8,128)S(1)} %collective-permute-done.2.other_ref, bf16[80,512]{1,0:T(8,128)(2,1)S(1)} %get-tuple-element.88.share_ref, ...), custom_call_target="tpu_custom_call" | custom-call | flops 134217728 | bytes 8388608 | tf_op jit(solution)/shard_map/middle/pallas_call | solution.py:578
  60.7 3.5 %all-to-all-start.3 = ((f32[16,4,128]{2,1,0:T(4,128)}), f32[16,4,128]{2,1,0:T(4,128)S(1)}, u32[]{:S(2)}, u32[]{:S(2)}) async-start(f32[16,4,128]{2,1,0:T(4,128)} %bitcast.9), calls=%async_computation.3 | async-start | bytes 65536 | tf_op jit(solution)/shard_map/all_to_all | solution.py:638
  64.2 3.7 %backward.5 = (f32[32,8,128]{2,1,0:T(8,128)S(1)}, f32[32,8,128]{2,1,0:T(8,128)S(1)}) custom-call(f32[32,128]{1,0:T(8,128)S(1)} %get-tuple-element.105.f_ref.refs_2_, bf16[256,32]{1,0:T(8,128)(2,1)S(1)} %get-tuple-element.82.gk_ref, bf16[256,128,128]{2,1,0:T(8,128)(2,1)} %c_hbm.7), custom_call_target="tpu_custom_call" | custom-call | flops 134217728 | bytes 8388608 | tf_op jit(solution)/shard_map/backward/pallas_call | solution.py:578
  68.0 2.9 %all-to-all-done.3 = f32[16,4,128]{2,1,0:T(4,128)S(1)} async-done(((f32[16,4,128]{2,1,0:T(4,128)}), f32[16,4,128]{2,1,0:T(4,128)S(1)}, u32[]{:S(2)}, u32[]{:S(2)}) %all-to-all-start.3) | async-done | bytes 32800 | tf_op jit(solution)/shard_map/all_to_all | solution.py:638
  70.8 0.4 phonon.1
  71.2 9.8 %all_to_all.58 = f32[16,8,128]{2,1,0:T(8,128)S(1)} all-to-all(f32[16,8,128]{2,1,0:T(8,128)S(1)} %bitcast.24), channel_id=1, replica_groups=mesh['groups'=2,'bulk'=16] {'bulk'}, dimensions={0} | all-to-all | bytes 131072 | tf_op jit(solution)/shard_map/all_to_all | solution.py:638
  81.1 4.2 %last.1 = (f32[32,128]{1,0:T(8,128)}, f32[16,128]{1,0:T(8,128)}) custom-call(f32[128,128]{1,0:T(8,128)S(1)} %bitcast.22, f32[256,128]{1,0:T(8,128)S(1)} %get-tuple-element.109.refs_0_, f32[32,128]{1,0:T(8,128)S(1)} %get-tuple-element.93.f_ref.own_ref.refs_1_, f32[32,128]{1,0:T(8,128)S(1)} %get-tuple-element.105.f_ref.refs_2_, ...), custom_call_target="tpu_custom_call" | custom-call | flops 134217728 | bytes 8388608 | tf_op jit(solution)/shard_map/last/pallas_call | solution.py:578
Async XLA Ops:
  2.2 15.7 %all-to-all-start = ((f32[8,56,128]{2,1,0:T(8,128)}), f32[8,56,128]{2,1,0:T(8,128)S(1)}, u32[]{:S(2)}, u32[]{:S(2)}) async-start(f32[8,56,128]{2,1,0:T(8,128)} %bitcast.3), calls=%async_computation | async-start | bytes 458752 | tf_op jit(solution)/shard_map/all_to_all | solution.py:652
  18.0 1.6 %collective-permute-start = (f32[448,128]{1,0:T(8,128)S(1)}, f32[448,128]{1,0:T(8,128)S(1)}, u32[]{:S(2)}, u32[]{:S(2)}) collective-permute-start(f32[448,128]{1,0:T(8,128)S(1)} %bitcast.13), channel_id=1, source_target_pairs={{0,1},{1,0},{2,3},{3,2},{4,5},{5,4},{6,7},{7,6},{8,9},{9,8},{10,11... | collective-permute-start | bytes 688136 | tf_op jit(solution)/shard_map/ppermute | solution.py:657
  24.2 12.0 %all-to-all-start.1 = ((f32[8,40,128]{2,1,0:T(8,128)}), f32[8,40,128]{2,1,0:T(8,128)S(1)}, u32[]{:S(2)}, u32[]{:S(2)}) async-start(f32[8,40,128]{2,1,0:T(8,128)} %bitcast.5), calls=%async_computation.1 | async-start | bytes 327680 | tf_op jit(solution)/shard_map/all_to_all | solution.py:652
  36.3 1.9 %collective-permute-start.1 = (f32[320,128]{1,0:T(8,128)S(1)}, f32[320,128]{1,0:T(8,128)S(1)}, u32[]{:S(2)}, u32[]{:S(2)}) collective-permute-start(f32[320,128]{1,0:T(8,128)S(1)} %bitcast.16), channel_id=1, source_target_pairs={{0,1},{1,0},{2,3},{3,2},{4,5},{5,4},{6,7},{7,6},{8,9},{9,8},{10,11... | collective-permute-start | bytes 491528 | tf_op jit(solution)/shard_map/ppermute | solution.py:657
  42.8 11.8 %all-to-all-start.2 = ((f32[8,40,128]{2,1,0:T(8,128)}), f32[8,40,128]{2,1,0:T(8,128)S(1)}, u32[]{:S(2)}, u32[]{:S(2)}) async-start(f32[8,40,128]{2,1,0:T(8,128)} %bitcast.7), calls=%async_computation.2 | async-start | bytes 327680 | tf_op jit(solution)/shard_map/all_to_all | solution.py:652
  54.6 1.6 %collective-permute-start.2 = (f32[320,128]{1,0:T(8,128)S(1)}, f32[320,128]{1,0:T(8,128)S(1)}, u32[]{:S(2)}, u32[]{:S(2)}) collective-permute-start(f32[320,128]{1,0:T(8,128)S(1)} %bitcast.19), channel_id=1, source_target_pairs={{0,1},{1,0},{2,3},{3,2},{4,5},{5,4},{6,7},{7,6},{8,9},{9,8},{10,11... | collective-permute-start | bytes 491528 | tf_op jit(solution)/shard_map/ppermute | solution.py:657
  60.7 10.1 %all-to-all-start.3 = ((f32[16,4,128]{2,1,0:T(4,128)}), f32[16,4,128]{2,1,0:T(4,128)S(1)}, u32[]{:S(2)}, u32[]{:S(2)}) async-start(f32[16,4,128]{2,1,0:T(4,128)} %bitcast.9), calls=%async_computation.3 | async-start | bytes 65536 | tf_op jit(solution)/shard_map/all_to_all | solution.py:638

commit v13 on v12

--- a/solution.py
+++ b/solution.py
@@ -119,21 +119,20 @@
         out1[base + g] = res[8:]
 
 
-def tile_products(w_ref, parts, out0, out1, after=None, carry=0):
+def tile_products(w_ref, parts, out0, out1):
     size = w_ref.shape[0] // CHUNKS
     base = 0
     for c_ref, c_hbm, sems in parts:
-        groups = c_ref.shape[0] // 8
-
-        def chunk(i, carry):
+        chunks = c_ref.shape[0] // 8 // size
+
+        def chunk(i, _):
             if c_hbm is not None:
                 chunk_copy(c_hbm, c_ref, sems, i).wait()
             chunk_products(w_ref, c_ref, i, base, out0, out1)
-            return after(base // size + i, carry) if after else carry
-
-        carry = lax.fori_loop(0, groups // size, chunk, carry)
-        base += groups
-    return carry
+            return 0
+
+        lax.fori_loop(0, chunks, chunk, 0, unroll=1 if c_hbm is not None else 2)
+        base += chunks * size
 
 
 def backward_pass(own, c_hbm, c_ref, sems, w_ref, out0, out1):
@@ -141,20 +140,10 @@
     tile_products(w_ref, [(c_ref, c_hbm, sems)], out0, out1)
 
 
-def electron_rate(sum_k_ref, far, bose, f, parts, w_ref, o0, o1):
+def electron_rate(sum_k, far, bose, f, parts, w_ref, o0, o1):
     left_sides(far * (1.0 + bose), far + bose, w_ref)
-    size = w_ref.shape[0] // CHUNKS
-
-    def after(i, totals):
-        sums = sum_k_ref[i]
-        return tuple(
-            total + add_rows(sums, out[pl.ds(i * size, size)].reshape(-1, 128))
-            for total, out in zip(totals, (o0, o1))
-        )
-
-    nothing = jnp.zeros_like(f)
-    gain, loss = tile_products(w_ref, parts, o0, o1, after, (nothing, nothing))
-    return gain - f * loss
+    tile_products(w_ref, parts, o0, o1)
+    return add_rows(sum_k, flat(o0)) - f * add_rows(sum_k, flat(o1))
 
 
 def my_core():
@@ -231,10 +220,7 @@
     gk_ref[...] = k_hot.T.astype(bf16)
     own = add_rows(gk_ref[...], f_ref[...])
     left_sides(1.0 - own, own, w_ref)
-    sums = jnp.where(used, k_hot, 0.0)
-    width = tiles // CHUNKS
-    for i in range(CHUNKS):
-        sk_ref[i] = sums[:, i * width : (i + 1) * width].astype(bf16)
+    sk_ref[...] = jnp.where(used, k_hot, 0.0).astype(bf16)
     x = iota((rows4, tiles), 0)
     row_e = (e // cap) * (2 * cap) + e % cap
     row_p = (q // cap) * (2 * cap) + cap + q % cap
@@ -423,7 +409,7 @@
     hot_ref[...] = hot
     base = n - DT * decay_ref[...] * (n - thermal_of(energy_ref))
     parts = [(held_ref, None, None), (fetched_ref, None, None), (c_ref, c_hbm, sems)]
-    rate = electron_rate(sk_ref, far, bose, f, parts, w_ref, o0, o1)
+    rate = electron_rate(sk_ref[...], far, bose, f, parts, w_ref, o0, o1)
     f1 = f + DT * rate
     e_ref[...] = rate
     f1_ref[...] = f1
@@ -477,7 +463,7 @@
     if ends:
         n2_ref, e2_ref, f3_ref = refs[:3]
         n2_ref[...] = n + (DT / 2.0) * total
-        rate = electron_rate(sk_ref, far, bose, own, parts, w_ref, o0, o1)
+        rate = electron_rate(sk_ref[...], far, bose, own, parts, w_ref, o0, o1)
         f3 = own + DT * rate
         e2_ref[...] = rate
         f3_ref[...] = f3
@@ -490,7 +476,7 @@
         n1 = n + DT * p0
         base = n + (DT / 2.0) * (p0 - decay * (n1 - thermal))
         base_ref[...] = base
-        rate = electron_rate(sk_ref, far, bose, own, parts, w_ref, o0, o1)
+        rate = electron_rate(sk_ref[...], far, bose, own, parts, w_ref, o0, o1)
         f2 = f_ref[...] + (DT / 2.0) * (e_ref[...] + rate)
         f2_ref[...] = f2
         put_broadcast(send, pick(serve_ref[...], padded(f2, base)), contributions)
@@ -558,7 +544,7 @@
     n2 = n + (DT / 2.0) * (p_ref[...] + p1)
     n2_ref[...] = n2
     parts = [(held_ref, None, None), (c_ref, c_hbm, sems)]
-    rate = electron_rate(sk_ref, far_ref[...], bose, f1_ref[...], parts, w_ref, o0, o1)
+    rate = electron_rate(sk_ref[...], far_ref[...], bose, f1_ref[...], parts, w_ref, o0, o1)
     f2 = f_ref[...] + (DT / 2.0) * (e_ref[...] + rate)
     f2_ref[...] = f2
 
@@ -662,6 +648,7 @@
         small + [lists, lists, ((chips * step_rows, 128), f32)],
         [pltpu.SemaphoreType.DMA((9,))],
         spaces={i: pltpu.HBM for i in range(9)},
+        out_spaces={9: pltpu.VMEM},
     )(
         electrons,
         phonons,
@@ -683,7 +670,7 @@
             ((tiles, 2 * rows4), bf16),
             ((tiles, rows8), bf16),
             ((tiles, kb), bf16),
-            ((CHUNKS, kb, tiles // CHUNKS), bf16),
+            ((kb, tiles), bf16),
             ((slots, tiles), bf16),
             ((rows4, tiles), bf16),
             ((rows8, 2 * tiles), bf16),
@@ -720,6 +707,7 @@
         [wide_block, k_rows, k_rows, ((rows4, 128), bf16), ((8 * devices, 128), bf16)],
         forward_scratch,
         spaces={14: pltpu.HBM},
+        out_spaces={0: pltpu.VMEM},
         **work,
     )(same, other, picks, f, n, energy, decay, pair, sk, sp, b0, b1, c_held, c_fetched, c_rest)
     share, s8, st4, st8a, st8b = call(
@@ -747,6 +735,7 @@
             outs,
             forward_scratch,
             spaces={17: pltpu.HBM},
+            out_spaces={0: pltpu.VMEM},
             **work,
         )(
             same, other, share, serve, f, e, own, n, energy, decay,

time: 85.9 us -> 84.7 us (0.986)
  Pallas kernels: 41.9 us -> 40.6 us
    pallas_call x14, Pallas kernels: 41.9 us -> 40.6 us  [run(): pl.pallas_call(kernel, out_shape=[(out_spaces or {}).get(i, jax.ShapeDtyp...]
where the time goes in v13:
time: 84.7 us; the launch traced here: 84 us
  Pallas kernels  40.6 us (48%)
  starting transfers between devices  18 us (21%)
  waiting for transfers between devices  14.1 us (17%)
  blocking collectives  9.83 us (12%)
  between operations  1.43 us (2%)
    pallas_call x14, Pallas kernels, run(): pl.pallas_call(kernel, out_shape=[(out_spaces or {}).get(i, jax.ShapeDtyp...  40.6 us
    all_to_all x3, starting transfers between devices, to_chips(): lax.all_to_all(x, 'bulk', split_axis=0, concat_axis=0, tiled=True, axis_i...  14.5 us
    all_to_all x3, waiting for transfers between devices, to_chips(): lax.all_to_all(x, 'bulk', split_axis=0, concat_axis=0, tiled=True, axis_i...  11.3 us
    all_to_all x1, blocking collectives, exchange(): return lax.all_to_all(x, 'bulk', split_axis=0, concat_axis=0, tiled=True)  9.83 us
    all_to_all x1, starting transfers between devices, exchange(): return lax.all_to_all(x, 'bulk', split_axis=0, concat_axis=0, tiled=True)  3.49 us
    all_to_all x1, waiting for transfers between devices, exchange(): return lax.all_to_all(x, 'bulk', split_axis=0, concat_axis=0, tiled=True)  2.85 us
  transfers between devices with their start and end apart: 7, of which 4 were waited for; matrix products, arithmetic and copies ran while one was open for 0% of the time, Pallas kernels for 26%

profile of v13, /device:TPU:0, one launch (start us, length us, event | category | flops | bytes accessed | tf_op | source)
XLA Modules:
  0.0 84.0 jit_solution(8396377541050312503)
XLA Ops:
  0.6 1.6 %need.1 = (f32[32,128]{1,0:T(8,128)S(1)}, f32[16,128]{1,0:T(8,128)S(1)}, f32[16,128]{1,0:T(8,128)S(1)}, f32[16,128]{1,0:T(8,128)S(1)}, s32[1,256]{1,0:T(1,128)S(...) custom-call(f32[32,128]{1,0:T(8,128)} %refs_0_.1, ...), custom_call_target="tpu_custom_call" | custom-call | tf_op jit(solution)/shard_map/need/pallas_call | solution.py:564
  2.2 7.3 %all-to-all-start = ((f32[8,56,128]{2,1,0:T(8,128)}), f32[8,56,128]{2,1,0:T(8,128)S(1)}, u32[]{:S(2)}, u32[]{:S(2)}) async-start(f32[8,56,128]{2,1,0:T(8,128)} %bitcast.3), calls=%async_computation | async-start | bytes 458752 | tf_op jit(solution)/shard_map/all_to_all | solution.py:638
  10.2 5.5 %prepare.1 = (bf16[64,128,128]{2,1,0:T(8,128)(2,1)S(1)}, bf16[192,128,128]{2,1,0:T(8,128)(2,1)}, bf16[256,128]{1,0:T(8,128)(2,1)S(1)}, bf16[256,128]{1,0:T(8,128...) custom-call(s32[1]{0:T(128)S(6)} %copy.13.count_ref, ...), custom_call_target="tpu_custom_call" | custom-call | flops 134217728 | bytes 8388608 | tf_op jit(solution)/shard_map/prepare/pallas_call | solution.py:564
  15.7 2.3 %all-to-all-done = f32[8,56,128]{2,1,0:T(8,128)S(1)} async-done(((f32[8,56,128]{2,1,0:T(8,128)}), f32[8,56,128]{2,1,0:T(8,128)S(1)}, u32[]{:S(2)}, u32[]{:S(2)}) %all-to-all-start) | async-done | bytes 229408 | tf_op jit(solution)/shard_map/all_to_all | solution.py:638
  18.0 0.0 collective-permute-start
  18.0 1.6 %fetch.3.fetched_ref = bf16[64,128,128]{2,1,0:T(8,128)(2,1)S(1)} custom-call(f32[448,128]{1,0:T(8,128)S(1)} %bitcast.14, bf16[192,128,128]{2,1,0:T(8,128)(2,1)} %get-tuple-element.79.c_hbm.refs_14_), custom_call_target="tpu_custom_call" | custom-call | bytes 2097152 | tf_op jit(solution)/shard_map/fetch/pallas_call | solution.py:564
  19.5 0.0 collective-permute-done.other_ref
  19.5 4.1 %first.1 = (f32[320,128]{1,0:T(8,128)}, f32[32,128]{1,0:T(8,128)S(1)}, f32[32,128]{1,0:T(8,128)S(1)}, bf16[64,128]{1,0:T(8,128)(2,1)S(1)}, bf16[128,128]{1,0:T(8,128)(2,1)S(1)}) custom-call(f32[448,128]{1,0:T(8,128)S(1)} %bitcast.15, f32[448,128]{1,0:T(8,128)S(1)} %collective-permute-done.other_ref, bf16[64,896]{1,0:T(8,128)(2,1)S(1)} %get-tuple-element.69.list_ref, ...), custom_call_target="tpu_custom_call" | custom-call | flops 134217728 | bytes 8388608 | tf_op jit(solution)/shard_map/first/pallas_call | solution.py:564
  23.6 3.8 %all-to-all-start.1 = ((f32[8,40,128]{2,1,0:T(8,128)}), f32[8,40,128]{2,1,0:T(8,128)S(1)}, u32[]{:S(2)}, u32[]{:S(2)}) async-start(f32[8,40,128]{2,1,0:T(8,128)} %bitcast.5), calls=%async_computation.1 | async-start | bytes 327680 | tf_op jit(solution)/shard_map/all_to_all | solution.py:638
  27.4 3.7 %backward.3 = (f32[32,8,128]{2,1,0:T(8,128)S(1)}, f32[32,8,128]{2,1,0:T(8,128)S(1)}) custom-call(f32[32,128]{1,0:T(8,128)S(1)} %get-tuple-element.81.f_ref.own_ref, bf16[256,32]{1,0:T(8,128)(2,1)S(1)} %get-tuple-element.82.gk_ref, bf16[256,128,128]{2,1,0:T(8,128)(2,1)} %c_hbm.7), custom_call_target="tpu_custom_call" | custom-call | flops 134217728 | bytes 8388608 | tf_op jit(solution)/shard_map/backward/pallas_call | solution.py:564
  31.1 4.4 %all-to-all-done.1 = f32[8,40,128]{2,1,0:T(8,128)S(1)} async-done(((f32[8,40,128]{2,1,0:T(8,128)}), f32[8,40,128]{2,1,0:T(8,128)S(1)}, u32[]{:S(2)}, u32[]{:S(2)}) %all-to-all-start.1) | async-done | bytes 163872 | tf_op jit(solution)/shard_map/all_to_all | solution.py:638
  35.5 0.0 collective-permute-start.1
  35.5 0.3 serve.1
  35.9 1.6 %fetch.4.fetched_ref = bf16[64,128,128]{2,1,0:T(8,128)(2,1)S(1)} custom-call(f32[320,128]{1,0:T(8,128)S(1)} %bitcast.17, bf16[192,128,128]{2,1,0:T(8,128)(2,1)} %get-tuple-element.79.c_hbm.refs_14_), custom_call_target="tpu_custom_call" | custom-call | bytes 2097152 | tf_op jit(solution)/shard_map/fetch/pallas_call | solution.py:564
  37.4 0.0 collective-permute-done.1.other_ref
  37.4 4.3 %middle.2 = (f32[320,128]{1,0:T(8,128)}, f32[16,128]{1,0:T(8,128)S(1)}, f32[32,128]{1,0:T(8,128)S(1)}) custom-call(f32[320,128]{1,0:T(8,128)S(1)} %bitcast.18, f32[320,128]{1,0:T(8,128)S(1)} %collective-permute-done.1.other_ref, bf16[80,512]{1,0:T(8,128)(2,1)S(1)} %get-tuple-element.88.share_ref, bf16[64,128]{1,0:T(8,128)(2,1)S(1)} %get-tuple-element.86.hot_ref.serve_ref, ...), custom_call_target="tpu_custom_call" | custom-call | flops 134217728 | bytes 8388608 | tf_op jit(solution)/shard_map/middle/pallas_call | solution.py:564
  41.8 3.4 %all-to-all-start.2 = ((f32[8,40,128]{2,1,0:T(8,128)}), f32[8,40,128]{2,1,0:T(8,128)S(1)}, u32[]{:S(2)}, u32[]{:S(2)}) async-start(f32[8,40,128]{2,1,0:T(8,128)} %bitcast.7), calls=%async_computation.2 | async-start | bytes 327680 | tf_op jit(solution)/shard_map/all_to_all | solution.py:638
  45.2 3.7 %backward.4 = (f32[32,8,128]{2,1,0:T(8,128)S(1)}, f32[32,8,128]{2,1,0:T(8,128)S(1)}) custom-call(f32[32,128]{1,0:T(8,128)S(1)} %get-tuple-element.93.f_ref.own_ref.refs_1_, bf16[256,32]{1,0:T(8,128)(2,1)S(1)} %get-tuple-element.82.gk_ref, bf16[256,128,128]{2,1,0:T(8,128)(2,1)} %c_hbm.7), custom_call_target="tpu_custom_call" | custom-call | flops 134217728 | bytes 8388608 | tf_op jit(solution)/shard_map/backward/pallas_call | solution.py:564
  48.9 4.6 %all-to-all-done.2 = f32[8,40,128]{2,1,0:T(8,128)S(1)} async-done(((f32[8,40,128]{2,1,0:T(8,128)}), f32[8,40,128]{2,1,0:T(8,128)S(1)}, u32[]{:S(2)}, u32[]{:S(2)}) %all-to-all-start.2) | async-done | bytes 163872 | tf_op jit(solution)/shard_map/all_to_all | solution.py:638
  53.5 0.0 collective-permute-start.2
  53.5 1.6 %fetch.5.fetched_ref = bf16[64,128,128]{2,1,0:T(8,128)(2,1)S(1)} custom-call(f32[320,128]{1,0:T(8,128)S(1)} %bitcast.20, bf16[192,128,128]{2,1,0:T(8,128)(2,1)} %get-tuple-element.79.c_hbm.refs_14_), custom_call_target="tpu_custom_call" | custom-call | bytes 2097152 | tf_op jit(solution)/shard_map/fetch/pallas_call | solution.py:564
  55.1 0.0 collective-permute-done.2.other_ref
  55.1 4.3 %middle.3 = (f32[64,128]{1,0:T(8,128)}, f32[16,128]{1,0:T(8,128)S(1)}, f32[32,128]{1,0:T(8,128)S(1)}, f32[32,128]{1,0:T(8,128)S(1)}) custom-call(f32[320,128]{1,0:T(8,128)S(1)} %bitcast.21, f32[320,128]{1,0:T(8,128)S(1)} %collective-permute-done.2.other_ref, bf16[80,512]{1,0:T(8,128)(2,1)S(1)} %get-tuple-element.88.share_ref, ...), custom_call_target="tpu_custom_call" | custom-call | flops 134217728 | bytes 8388608 | tf_op jit(solution)/shard_map/middle/pallas_call | solution.py:564
  59.4 3.5 %all-to-all-start.3 = ((f32[16,4,128]{2,1,0:T(4,128)}), f32[16,4,128]{2,1,0:T(4,128)S(1)}, u32[]{:S(2)}, u32[]{:S(2)}) async-start(f32[16,4,128]{2,1,0:T(4,128)} %bitcast.9), calls=%async_computation.3 | async-start | bytes 65536 | tf_op jit(solution)/shard_map/all_to_all | solution.py:624
  62.9 3.7 %backward.5 = (f32[32,8,128]{2,1,0:T(8,128)S(1)}, f32[32,8,128]{2,1,0:T(8,128)S(1)}) custom-call(f32[32,128]{1,0:T(8,128)S(1)} %get-tuple-element.105.f_ref.refs_2_, bf16[256,32]{1,0:T(8,128)(2,1)S(1)} %get-tuple-element.82.gk_ref, bf16[256,128,128]{2,1,0:T(8,128)(2,1)} %c_hbm.7), custom_call_target="tpu_custom_call" | custom-call | flops 134217728 | bytes 8388608 | tf_op jit(solution)/shard_map/backward/pallas_call | solution.py:564
  66.6 2.9 %all-to-all-done.3 = f32[16,4,128]{2,1,0:T(4,128)S(1)} async-done(((f32[16,4,128]{2,1,0:T(4,128)}), f32[16,4,128]{2,1,0:T(4,128)S(1)}, u32[]{:S(2)}, u32[]{:S(2)}) %all-to-all-start.3) | async-done | bytes 32800 | tf_op jit(solution)/shard_map/all_to_all | solution.py:624
  69.5 0.4 phonon.1
  69.9 9.8 %all_to_all.58 = f32[16,8,128]{2,1,0:T(8,128)S(1)} all-to-all(f32[16,8,128]{2,1,0:T(8,128)S(1)} %bitcast.24), channel_id=1, replica_groups=mesh['groups'=2,'bulk'=16] {'bulk'}, dimensions={0} | all-to-all | bytes 131072 | tf_op jit(solution)/shard_map/all_to_all | solution.py:624
  79.7 4.3 %last.1 = (f32[32,128]{1,0:T(8,128)}, f32[16,128]{1,0:T(8,128)}) custom-call(f32[128,128]{1,0:T(8,128)S(1)} %bitcast.22, f32[256,128]{1,0:T(8,128)S(1)} %get-tuple-element.109.refs_0_, f32[32,128]{1,0:T(8,128)S(1)} %get-tuple-element.93.f_ref.own_ref.refs_1_, f32[32,128]{1,0:T(8,128)S(1)} %get-tuple-element.105.f_ref.refs_2_, ...), custom_call_target="tpu_custom_call" | custom-call | flops 134217728 | bytes 8388608 | tf_op jit(solution)/shard_map/last/pallas_call | solution.py:564
Async XLA Ops:
  2.2 15.7 %all-to-all-start = ((f32[8,56,128]{2,1,0:T(8,128)}), f32[8,56,128]{2,1,0:T(8,128)S(1)}, u32[]{:S(2)}, u32[]{:S(2)}) async-start(f32[8,56,128]{2,1,0:T(8,128)} %bitcast.3), calls=%async_computation | async-start | bytes 458752 | tf_op jit(solution)/shard_map/all_to_all | solution.py:638
  18.0 1.6 %collective-permute-start = (f32[448,128]{1,0:T(8,128)S(1)}, f32[448,128]{1,0:T(8,128)S(1)}, u32[]{:S(2)}, u32[]{:S(2)}) collective-permute-start(f32[448,128]{1,0:T(8,128)S(1)} %bitcast.13), channel_id=1, source_target_pairs={{0,1},{1,0},{2,3},{3,2},{4,5},{5,4},{6,7},{7,6},{8,9},{9,8},{10,11... | collective-permute-start | bytes 688136 | tf_op jit(solution)/shard_map/ppermute | solution.py:643
  23.6 11.9 %all-to-all-start.1 = ((f32[8,40,128]{2,1,0:T(8,128)}), f32[8,40,128]{2,1,0:T(8,128)S(1)}, u32[]{:S(2)}, u32[]{:S(2)}) async-start(f32[8,40,128]{2,1,0:T(8,128)} %bitcast.5), calls=%async_computation.1 | async-start | bytes 327680 | tf_op jit(solution)/shard_map/all_to_all | solution.py:638
  35.5 1.9 %collective-permute-start.1 = (f32[320,128]{1,0:T(8,128)S(1)}, f32[320,128]{1,0:T(8,128)S(1)}, u32[]{:S(2)}, u32[]{:S(2)}) collective-permute-start(f32[320,128]{1,0:T(8,128)S(1)} %bitcast.16), channel_id=1, source_target_pairs={{0,1},{1,0},{2,3},{3,2},{4,5},{5,4},{6,7},{7,6},{8,9},{9,8},{10,11... | collective-permute-start | bytes 491528 | tf_op jit(solution)/shard_map/ppermute | solution.py:643
  41.8 11.8 %all-to-all-start.2 = ((f32[8,40,128]{2,1,0:T(8,128)}), f32[8,40,128]{2,1,0:T(8,128)S(1)}, u32[]{:S(2)}, u32[]{:S(2)}) async-start(f32[8,40,128]{2,1,0:T(8,128)} %bitcast.7), calls=%async_computation.2 | async-start | bytes 327680 | tf_op jit(solution)/shard_map/all_to_all | solution.py:638
  53.5 1.6 %collective-permute-start.2 = (f32[320,128]{1,0:T(8,128)S(1)}, f32[320,128]{1,0:T(8,128)S(1)}, u32[]{:S(2)}, u32[]{:S(2)}) collective-permute-start(f32[320,128]{1,0:T(8,128)S(1)} %bitcast.19), channel_id=1, source_target_pairs={{0,1},{1,0},{2,3},{3,2},{4,5},{5,4},{6,7},{7,6},{8,9},{9,8},{10,11... | collective-permute-start | bytes 491528 | tf_op jit(solution)/shard_map/ppermute | solution.py:643
  59.4 10.1 %all-to-all-start.3 = ((f32[16,4,128]{2,1,0:T(4,128)}), f32[16,4,128]{2,1,0:T(4,128)S(1)}, u32[]{:S(2)}, u32[]{:S(2)}) async-start(f32[16,4,128]{2,1,0:T(4,128)} %bitcast.9), calls=%async_computation.3 | async-start | bytes 65536 | tf_op jit(solution)/shard_map/all_to_all | solution.py:624

commit v14 on v11

--- a/solution.py
+++ b/solution.py
@@ -87,7 +87,7 @@
 
 def start_chunks(src, dst, sems):
     for i in range(sems.shape[0]):
-        chunk_copy(src, dst, sems, i).start(priority=i % 2)
+        chunk_copy(src, dst, sems, i).start()
 
 
 def start(copies):
@@ -121,7 +121,7 @@
     size = w_ref.shape[0] // CHUNKS
     base = 0
     for c_ref, c_hbm, sems in parts:
-        groups = c_ref.shape[0] // 8
+        chunks = c_ref.shape[0] // 8 // size
 
         def chunk(i, _):
             if c_hbm is not None:
@@ -129,8 +129,8 @@
             chunk_products(w_ref, c_ref, i, base, out0, out1)
             return 0
 
-        lax.fori_loop(0, groups // size, chunk, 0)
-        base += groups
+        lax.fori_loop(0, chunks, chunk, 0)
+        base += chunks * size
 
 
 def backward_pass(own, c_hbm, c_ref, sems, w_ref, out0, out1):
@@ -194,6 +194,7 @@
     sp_ref,
     sp4_ref,
     sp8_ref,
+    near_ref,
     list_ref,
     mine_ref,
     b0_ref,
@@ -237,7 +238,7 @@
         axis=1,
     ).astype(bf16)
 
-    rows, sent = list_ref.shape
+    rows, half = list_ref.shape
     slots = pneed_ref.shape[1]
     peers = slots // cap
     x = iota((rows, slots), 0)
@@ -249,10 +250,11 @@
     qn = jnp.broadcast_to(qneed_ref[...].astype(f32), (rows, slots)) + float(kb)
     col = jnp.sum(jnp.where(e_here, pn, 0.0) + jnp.where(p_here, qn, 0.0), axis=1, keepdims=True)
     mine_ref[...] = jnp.broadcast_to(col, (rows, 128))
-    start_of = block_of(iota((rows, 1), 0) // (2 * cap), peers) * (sent // peers)
-    list_ref[...] = jnp.where(
-        iota((rows, sent), 1).astype(f32) == col + start_of.astype(f32), 1.0, 0.0
-    ).astype(bf16)
+    start_of = block_of(iota((rows, 1), 0) // (2 * cap), peers) * (2 * half // peers)
+    place = col + start_of.astype(f32)
+    lane = iota((rows, half), 1).astype(f32)
+    near_ref[...] = ind(lane == place).astype(bf16)
+    list_ref[...] = ind(lane + float(half) == place).astype(bf16)
 
     size = c_ref.shape[0] // CHUNKS
     held = held_ref.shape[0] // size
@@ -278,13 +280,9 @@
         chunk_copy(t_ref, t_hbm, out_sems, i).wait()
 
 
-def blocks(same_ref, other_ref, peers, first, count):
-    step = 2 * same_ref.shape[0] // peers
-    parts = [
-        ref[b * step + first : b * step + first + count]
-        for ref in (same_ref, other_ref)
-        for b in range(peers // 2)
-    ]
+def blocks(ref, count_of_blocks, first, count):
+    step = ref.shape[0] // count_of_blocks
+    parts = [ref[b * step + first : b * step + first + count] for b in range(count_of_blocks)]
     return jnp.concatenate(parts, axis=0)
 
 
@@ -355,10 +353,35 @@
     return gain + bose * (gain - (1.0 - far) * flat(b1_ref))
 
 
+def near_rows_kernel(same_ref, list_ref, part_ref):
+    part_ref[...] = add_rows(list_ref[...], same_ref[...])
+
+
+def half_of_devices(cap, chips, weight, others, ref, share_ref):
+    rows4 = 4 * cap * chips
+    wide = share_ref.shape[1] // 2
+    x = iota((rows4, 8 * chips), 0)
+    peer = x // (2 * cap)
+    source = 8 * (peer // 2) + 2 * cap * my_core() + x % (2 * cap)
+    wanted_core = (my_core() + others) % 2
+    at = (iota((rows4, 8 * chips), 1) == source) & (peer % 2 == wanted_core)
+    heads = add_rows(jnp.where(at, 1.0, 0.0).astype(bf16), blocks(ref, chips, 0, 8))
+    tails = blocks(ref, chips, 8, wide // chips)
+    sums = add_rows(share_ref[:, others * wide : (others + 1) * wide], tails)
+    return heads + weight * sums[:rows4], sums[rows4:]
+
+
+def near_half_kernel(cap, chips, weight, same_ref, share_ref, part_ref, total_ref):
+    part, total = half_of_devices(cap, chips, weight, 0, same_ref, share_ref)
+    part_ref[...] = part
+    total_ref[...] = total
+
+
 def first_kernel(
     cap,
     same_ref,
     other_ref,
+    part_ref,
     list_ref,
     f_ref,
     n_ref,
@@ -387,10 +410,12 @@
     kb, qb = f.shape[0], n.shape[0]
     rows4 = list_ref.shape[0]
     peers = rows4 // (2 * cap)
-    got = pick(list_ref[...], jnp.concatenate([same_ref[...], other_ref[...]], axis=0))
+    got = part_ref[...] + add_rows(list_ref[...], other_ref[...])
     far, bose = gather_pair(pair_ref[...], got)
     contributions = add_rows(sp_ref[...], phonon_terms(far, bose, b0_ref, b1_ref))
-    lists = blocks(same_ref, other_ref, peers, kb + qb, 8).astype(bf16)
+    lists = jnp.concatenate(
+        [blocks(ref, peers // 2, kb + qb, 8) for ref in (same_ref, other_ref)], axis=0
+    ).astype(bf16)
     asked_ref[...] = lists
     x = iota((rows4, 8 * peers), 0)
     r = x % (2 * cap)
@@ -416,7 +441,8 @@
 def middle_kernel(
     cap,
     ends,
-    same_ref,
+    part_ref,
+    total_ref,
     other_ref,
     share_ref,
     serve_ref,
@@ -438,18 +464,11 @@
 ):
     w_ref, c_ref, sems, o0, o1 = refs[-5:]
     start_chunks(c_hbm, c_ref, sems)
-    rows4 = serve_ref.shape[0]
-    peers = rows4 // (2 * cap)
-    slots = peers * cap
-    x = iota((rows4, 8 * peers), 0)
-    source = 8 * block_of(x // (2 * cap), peers) + 2 * cap * my_core() + x % (2 * cap)
-    at = jnp.where(iota((rows4, 8 * peers), 1) == source, 1.0, 0.0).astype(bf16)
-    heads = blocks(same_ref, other_ref, peers, 0, 8)
-    tails = blocks(same_ref, other_ref, peers, 8, slots)
+    chips = serve_ref.shape[0] // (4 * cap)
     weight = DT / 2.0 if ends else DT
-    both = add_rows(share_ref[...], tails)
-    shares, total = both[:rows4], both[rows4:]
-    got = pick(at, heads) + weight * shares
+    part, total = half_of_devices(cap, chips, weight, 1, other_ref, share_ref)
+    got = part_ref[...] + part
+    total = total_ref[...] + total
     far, bose = gather_pair(pair_ref[...], got)
     terms = phonon_terms(far, bose, b0_ref, b1_ref)
     contributions = add_rows(sp_ref[...], terms)
@@ -554,8 +573,7 @@
         return pl.pallas_call(
             kernel,
             out_shape=[
-                pltpu.HBM(*o) if (out_spaces or {}).get(i) else jax.ShapeDtypeStruct(*o)
-                for i, o in enumerate(outs)
+                (out_spaces or {}).get(i, jax.ShapeDtypeStruct)(*o) for i, o in enumerate(outs)
             ],
             in_specs=specs,
             out_specs=[
@@ -648,7 +666,7 @@
         phonon_need,
     )
     same = to_chips(send)
-    c_held, c_rest, pair, gp8, gk, sk, sp, sp4, sp8, picks, mine, b0, b1 = call(
+    c_held, c_rest, pair, gp8, gk, sk, sp, sp4, sp8, near, far_picks, mine, b0, b1 = call(
         functools.partial(prepare_kernel, cap),
         "prepare",
         [
@@ -661,7 +679,8 @@
             ((slots, tiles), bf16),
             ((rows4, tiles), bf16),
             ((rows8, 2 * tiles), bf16),
-            ((rows4, devices * step_rows), bf16),
+            ((rows4, chips * step_rows), bf16),
+            ((rows4, chips * step_rows), bf16),
             ((rows4, 128), f32),
         ]
         + pass_out,
@@ -671,18 +690,19 @@
         **work,
     )(tile_count, kblock, partner, qslot, f, pneed, qneed, coupling)
     same, c_held, b0 = lax.optimization_barrier((same, c_held, b0))
-    other = between_cores(same)
     wide_block = ((chips * wide, 128), f32)
     k_rows, q_rows = ((kb, 128), f32), ((qb, 128), f32)
     forward_scratch = forward_streams + sums
+    other = between_cores(same)
+    (part,) = call(near_rows_kernel, "near_rows", [block4])(same, near)
     send, e0, f1, serve, asked = call(
         functools.partial(first_kernel, cap),
         "first",
         [wide_block, k_rows, k_rows, ((rows4, 128), bf16), ((8 * devices, 128), bf16)],
         forward_scratch,
-        spaces={13: pltpu.HBM},
+        spaces={14: pltpu.HBM},
         **work,
-    )(same, other, picks, f, n, energy, decay, pair, sk, sp, b0, b1, c_held, c_rest)
+    )(same, other, part, far_picks, f, n, energy, decay, pair, sk, sp, b0, b1, c_held, c_rest)
     share, s8, st4, st8a, st8b = call(
         functools.partial(serve_kernel, cap, kb, qb),
         "serve",
@@ -701,15 +721,19 @@
         b0, b1 = back(own, gk, coupling)
         same, b0 = lax.optimization_barrier((same, b0))
         other = between_cores(same)
+        weight = DT / 2.0 if ends else DT
+        part, total = call(
+            functools.partial(near_half_kernel, cap, chips, weight), "near_half", [block4, q_rows]
+        )(same, share)
         return call(
             functools.partial(middle_kernel, cap, ends),
             "middle",
             outs,
             forward_scratch,
-            spaces={16: pltpu.HBM},
+            spaces={17: pltpu.HBM},
             **work,
         )(
-            same, other, share, serve, f, e, own, n, energy, decay,
+            part, total, other, share, serve, f, e, own, n, energy, decay,
             pair, sk, contributions, b0, b1, c_held, c_rest,
         )
 
@@ -729,7 +753,7 @@
         last_kernel,
         "last",
         [k_rows, q_rows],
-        forward_scratch,
+        forward_streams + sums,
         spaces={15: pltpu.HBM},
         **work,
     )(

time: 85.4 us -> 82.9 us (0.971)
  Pallas kernels: 39.6 us -> 36.3 us
  waiting for transfers between devices: 15 us -> 16.8 us
    pallas_call x11 -> x14, Pallas kernels: 39.6 us -> 36.3 us  [run(): pl.pallas_call(kernel, out_shape=[(out_spaces or {}).get(i, jax.ShapeDtyp...]
    all_to_all x3, waiting for transfers between devices: 8.82 us -> 10.6 us  [to_chips(): lax.all_to_all(x, 'bulk', split_axis=0, concat_axis=0, tiled=True, axis_i...]
  transfers between devices with their start and end apart: 7 -> 7, of which waited for: 7 -> 7; matrix products, arithmetic and copies ran while one was open for 0% -> 0% of each run, Pallas kernels for 23% -> 21%
where the time goes in v14:
time: 82.9 us; the launch traced here: 82.3 us
  Pallas kernels  36.3 us (44%)
  starting transfers between devices  18 us (22%)
  waiting for transfers between devices  16.8 us (20%)
  blocking collectives  9.83 us (12%)
  between operations  1.39 us (2%)
    pallas_call x14, Pallas kernels, run(): pl.pallas_call(kernel, out_shape=[(out_spaces or {}).get(i, jax.ShapeDtyp...  36.3 us
    all_to_all x3, starting transfers between devices, to_chips(): lax.all_to_all(x, 'bulk', split_axis=0, concat_axis=0, tiled=True, axis_i...  14.5 us
    all_to_all x3, waiting for transfers between devices, to_chips(): lax.all_to_all(x, 'bulk', split_axis=0, concat_axis=0, tiled=True, axis_i...  10.6 us
    all_to_all x1, blocking collectives, exchange(): return lax.all_to_all(x, 'bulk', split_axis=0, concat_axis=0, tiled=True)  9.83 us
    all_to_all x1, starting transfers between devices, exchange(): return lax.all_to_all(x, 'bulk', split_axis=0, concat_axis=0, tiled=True)  3.5 us
    ppermute x3, waiting for transfers between devices, between_cores(): return lax.ppermute(x, 'bulk', [(i, i ^ 1) for i in range(devices)])  3.42 us
    all_to_all x1, waiting for transfers between devices, exchange(): return lax.all_to_all(x, 'bulk', split_axis=0, concat_axis=0, tiled=True)  2.85 us
  transfers between devices with their start and end apart: 7, of which 7 were waited for; matrix products, arithmetic and copies ran while one was open for 0% of the time, Pallas kernels for 21%

profile of v14, /device:TPU:0, one launch (start us, length us, event | category | flops | bytes accessed | tf_op | source)
XLA Modules:
  0.0 82.3 jit_solution(7902926622531597407)
XLA Ops:
  0.6 1.6 %need.1 = (f32[32,128]{1,0:T(8,128)S(1)}, f32[16,128]{1,0:T(8,128)S(1)}, f32[16,128]{1,0:T(8,128)S(1)}, f32[16,128]{1,0:T(8,128)S(1)}, s32[1,256]{1,0:T(1,128)S(...) custom-call(f32[32,128]{1,0:T(8,128)} %refs_0_.1, ...), custom_call_target="tpu_custom_call" | custom-call | tf_op jit(solution)/shard_map/need/pallas_call | solution.py:573
  2.2 7.3 %all-to-all-start = ((f32[8,56,128]{2,1,0:T(8,128)}), f32[8,56,128]{2,1,0:T(8,128)S(1)}, u32[]{:S(2)}, u32[]{:S(2)}) async-start(f32[8,56,128]{2,1,0:T(8,128)} %bitcast.3), calls=%async_computation | async-start | bytes 458752 | tf_op jit(solution)/shard_map/all_to_all | solution.py:644
  10.2 5.5 %prepare.1 = (bf16[64,128,128]{2,1,0:T(8,128)(2,1)S(1)}, bf16[192,128,128]{2,1,0:T(8,128)(2,1)}, bf16[256,128]{1,0:T(8,128)(2,1)S(1)}, bf16[256,128]{1,0:T(8,128...) custom-call(s32[1]{0:T(128)S(6)} %copy.13.count_ref, ...), custom_call_target="tpu_custom_call" | custom-call | flops 134217728 | bytes 8388608 | tf_op jit(solution)/shard_map/prepare/pallas_call | solution.py:573
  15.7 2.3 %all-to-all-done = f32[8,56,128]{2,1,0:T(8,128)S(1)} async-done(((f32[8,56,128]{2,1,0:T(8,128)}), f32[8,56,128]{2,1,0:T(8,128)S(1)}, u32[]{:S(2)}, u32[]{:S(2)}) %all-to-all-start) | async-done | bytes 229408 | tf_op jit(solution)/shard_map/all_to_all | solution.py:644
  18.0 0.0 collective-permute-start
  18.0 0.2 near_rows.1.part_ref
  18.1 1.3 %collective-permute-done.other_ref = f32[448,128]{1,0:T(8,128)S(1)} collective-permute-done((f32[448,128]{1,0:T(8,128)S(1)}, f32[448,128]{1,0:T(8,128)S(1)}, u32[]{:S(2)}, u32[]{:S(2)}) %collective-permute-start) | collective-permute-done | bytes 229408 | tf_op jit(solution)/shard_map/ppermute | solution.py:649
  19.5 4.3 %first.1 = (f32[320,128]{1,0:T(8,128)}, f32[32,128]{1,0:T(8,128)S(1)}, f32[32,128]{1,0:T(8,128)S(1)}, bf16[64,128]{1,0:T(8,128)(2,1)S(1)}, bf16[128,128]{1,0:T(8,128)(2,1)S(1)}) custom-call(f32[448,128]{1,0:T(8,128)S(1)} %bitcast.15, f32[448,128]{1,0:T(8,128)S(1)} %collective-permute-done.other_ref, f32[64,128]{1,0:T(8,128)S(1)} %near_rows.1.part_ref, ...), custom_call_target="tpu_custom_call" | custom-call | flops 134217728 | bytes 8388608 | tf_op jit(solution)/shard_map/first/pallas_call | solution.py:573
  23.8 3.8 %all-to-all-start.1 = ((f32[8,40,128]{2,1,0:T(8,128)}), f32[8,40,128]{2,1,0:T(8,128)S(1)}, u32[]{:S(2)}, u32[]{:S(2)}) async-start(f32[8,40,128]{2,1,0:T(8,128)} %bitcast.5), calls=%async_computation.1 | async-start | bytes 327680 | tf_op jit(solution)/shard_map/all_to_all | solution.py:644
  27.6 3.7 %backward.3 = (f32[32,8,128]{2,1,0:T(8,128)S(1)}, f32[32,8,128]{2,1,0:T(8,128)S(1)}) custom-call(f32[32,128]{1,0:T(8,128)S(1)} %get-tuple-element.87.f_ref.own_ref, bf16[256,32]{1,0:T(8,128)(2,1)S(1)} %get-tuple-element.88.gk_ref, bf16[256,128,128]{2,1,0:T(8,128)(2,1)} %c_hbm.7), custom_call_target="tpu_custom_call" | custom-call | flops 134217728 | bytes 8388608 | tf_op jit(solution)/shard_map/backward/pallas_call | solution.py:573
  31.3 4.0 %all-to-all-done.1 = f32[8,40,128]{2,1,0:T(8,128)S(1)} async-done(((f32[8,40,128]{2,1,0:T(8,128)}), f32[8,40,128]{2,1,0:T(8,128)S(1)}, u32[]{:S(2)}, u32[]{:S(2)}) %all-to-all-start.1) | async-done | bytes 163872 | tf_op jit(solution)/shard_map/all_to_all | solution.py:644
  35.4 0.0 collective-permute-start.1
  35.4 0.3 serve.1
  35.7 0.2 near_half.2
  35.9 0.9 %collective-permute-done.1.other_ref = f32[320,128]{1,0:T(8,128)S(1)} collective-permute-done((f32[320,128]{1,0:T(8,128)S(1)}, f32[320,128]{1,0:T(8,128)S(1)}, u32[]{:S(2)}, u32[]{:S(2)}) %collective-permute-start.1) | collective-permute-done | bytes 163872 | tf_op jit(solution)/shard_map/ppermute | solution.py:649
  36.7 4.4 %middle.2 = (f32[320,128]{1,0:T(8,128)}, f32[16,128]{1,0:T(8,128)S(1)}, f32[32,128]{1,0:T(8,128)S(1)}) custom-call(f32[64,128]{1,0:T(8,128)S(1)} %get-tuple-element.95.part_ref, f32[16,128]{1,0:T(8,128)S(1)} %get-tuple-element.96.total_ref, f32[320,128]{1,0:T(8,128)S(1)} %collective-permute-done.1.other_ref, ...), custom_call_target="tpu_custom_call" | custom-call | flops 134217728 | bytes 8388608 | tf_op jit(solution)/shard_map/middle/pallas_call | solution.py:573
  41.1 3.4 %all-to-all-start.2 = ((f32[8,40,128]{2,1,0:T(8,128)}), f32[8,40,128]{2,1,0:T(8,128)S(1)}, u32[]{:S(2)}, u32[]{:S(2)}) async-start(f32[8,40,128]{2,1,0:T(8,128)} %bitcast.7), calls=%async_computation.2 | async-start | bytes 327680 | tf_op jit(solution)/shard_map/all_to_all | solution.py:644
  44.5 3.7 %backward.4 = (f32[32,8,128]{2,1,0:T(8,128)S(1)}, f32[32,8,128]{2,1,0:T(8,128)S(1)}) custom-call(f32[32,128]{1,0:T(8,128)S(1)} %get-tuple-element.101.f_ref.own_ref.refs_1_, bf16[256,32]{1,0:T(8,128)(2,1)S(1)} %get-tuple-element.88.gk_ref, bf16[256,128,128]{2,1,0:T(8,128)(2,1)} %c_hbm.7), custom_call_target="tpu_custom_call" | custom-call | flops 134217728 | bytes 8388608 | tf_op jit(solution)/shard_map/backward/pallas_call | solution.py:573
  48.3 4.2 %all-to-all-done.2 = f32[8,40,128]{2,1,0:T(8,128)S(1)} async-done(((f32[8,40,128]{2,1,0:T(8,128)}), f32[8,40,128]{2,1,0:T(8,128)S(1)}, u32[]{:S(2)}, u32[]{:S(2)}) %all-to-all-start.2) | async-done | bytes 163872 | tf_op jit(solution)/shard_map/all_to_all | solution.py:644
  52.5 0.0 collective-permute-start.2
  52.5 0.2 near_half.3
  52.7 1.2 %collective-permute-done.2.other_ref = f32[320,128]{1,0:T(8,128)S(1)} collective-permute-done((f32[320,128]{1,0:T(8,128)S(1)}, f32[320,128]{1,0:T(8,128)S(1)}, u32[]{:S(2)}, u32[]{:S(2)}) %collective-permute-start.2) | collective-permute-done | bytes 163872 | tf_op jit(solution)/shard_map/ppermute | solution.py:649
  53.9 4.2 %middle.3 = (f32[64,128]{1,0:T(8,128)}, f32[16,128]{1,0:T(8,128)S(1)}, f32[32,128]{1,0:T(8,128)S(1)}, f32[32,128]{1,0:T(8,128)S(1)}) custom-call(f32[64,128]{1,0:T(8,128)S(1)} %get-tuple-element.104.part_ref, f32[16,128]{1,0:T(8,128)S(1)} %get-tuple-element.105.total_ref, f32[320,128]{1,0:T(8,128)S(1)} %collective-permute-done.2.other_ref, ...), custom_call_target="tpu_custom_call" | custom-call | flops 134217728 | bytes 8388608 | tf_op jit(solution)/shard_map/middle/pallas_call | solution.py:573
  58.1 3.5 %all-to-all-start.3 = ((f32[16,4,128]{2,1,0:T(4,128)}), f32[16,4,128]{2,1,0:T(4,128)S(1)}, u32[]{:S(2)}, u32[]{:S(2)}) async-start(f32[16,4,128]{2,1,0:T(4,128)} %bitcast.9), calls=%async_computation.3 | async-start | bytes 65536 | tf_op jit(solution)/shard_map/all_to_all | solution.py:630
  61.6 3.7 %backward.5 = (f32[32,8,128]{2,1,0:T(8,128)S(1)}, f32[32,8,128]{2,1,0:T(8,128)S(1)}) custom-call(f32[32,128]{1,0:T(8,128)S(1)} %get-tuple-element.115.f_ref.refs_2_, bf16[256,32]{1,0:T(8,128)(2,1)S(1)} %get-tuple-element.88.gk_ref, bf16[256,128,128]{2,1,0:T(8,128)(2,1)} %c_hbm.7), custom_call_target="tpu_custom_call" | custom-call | flops 134217728 | bytes 8388608 | tf_op jit(solution)/shard_map/backward/pallas_call | solution.py:573
  65.3 2.9 %all-to-all-done.3 = f32[16,4,128]{2,1,0:T(4,128)S(1)} async-done(((f32[16,4,128]{2,1,0:T(4,128)}), f32[16,4,128]{2,1,0:T(4,128)S(1)}, u32[]{:S(2)}, u32[]{:S(2)}) %all-to-all-start.3) | async-done | bytes 32800 | tf_op jit(solution)/shard_map/all_to_all | solution.py:630
  68.2 0.4 phonon.1
  68.6 9.8 %all_to_all.58 = f32[16,8,128]{2,1,0:T(8,128)S(1)} all-to-all(f32[16,8,128]{2,1,0:T(8,128)S(1)} %bitcast.22), channel_id=1, replica_groups=mesh['groups'=2,'bulk'=16] {'bulk'}, dimensions={0} | all-to-all | bytes 131072 | tf_op jit(solution)/shard_map/all_to_all | solution.py:630
  78.4 3.9 %last.1 = (f32[32,128]{1,0:T(8,128)}, f32[16,128]{1,0:T(8,128)}) custom-call(f32[128,128]{1,0:T(8,128)S(1)} %bitcast.20, f32[256,128]{1,0:T(8,128)S(1)} %get-tuple-element.119.refs_0_, f32[32,128]{1,0:T(8,128)S(1)} %get-tuple-element.101.f_ref.own_ref.refs_1_, f32[32,128]{1,0:T(8,128)S(1)} %get-tuple-element.115.f_ref.refs_2_, ...), custom_call_target="tpu_custom_call" | custom-call | flops 134217728 | bytes 8388608 | tf_op jit(solution)/shard_map/last/pallas_call | solution.py:573
Async XLA Ops:
  2.2 15.7 %all-to-all-start = ((f32[8,56,128]{2,1,0:T(8,128)}), f32[8,56,128]{2,1,0:T(8,128)S(1)}, u32[]{:S(2)}, u32[]{:S(2)}) async-start(f32[8,56,128]{2,1,0:T(8,128)} %bitcast.3), calls=%async_computation | async-start | bytes 458752 | tf_op jit(solution)/shard_map/all_to_all | solution.py:644
  18.0 1.5 %collective-permute-start = (f32[448,128]{1,0:T(8,128)S(1)}, f32[448,128]{1,0:T(8,128)S(1)}, u32[]{:S(2)}, u32[]{:S(2)}) collective-permute-start(f32[448,128]{1,0:T(8,128)S(1)} %bitcast.13), channel_id=1, source_target_pairs={{0,1},{1,0},{2,3},{3,2},{4,5},{5,4},{6,7},{7,6},{8,9},{9,8},{10,11... | collective-permute-start | bytes 688136 | tf_op jit(solution)/shard_map/ppermute | solution.py:649
  23.8 11.5 %all-to-all-start.1 = ((f32[8,40,128]{2,1,0:T(8,128)}), f32[8,40,128]{2,1,0:T(8,128)S(1)}, u32[]{:S(2)}, u32[]{:S(2)}) async-start(f32[8,40,128]{2,1,0:T(8,128)} %bitcast.5), calls=%async_computation.1 | async-start | bytes 327680 | tf_op jit(solution)/shard_map/all_to_all | solution.py:644
  35.4 1.4 %collective-permute-start.1 = (f32[320,128]{1,0:T(8,128)S(1)}, f32[320,128]{1,0:T(8,128)S(1)}, u32[]{:S(2)}, u32[]{:S(2)}) collective-permute-start(f32[320,128]{1,0:T(8,128)S(1)} %bitcast.16), channel_id=1, source_target_pairs={{0,1},{1,0},{2,3},{3,2},{4,5},{5,4},{6,7},{7,6},{8,9},{9,8},{10,11... | collective-permute-start | bytes 491528 | tf_op jit(solution)/shard_map/ppermute | solution.py:649
  41.1 11.4 %all-to-all-start.2 = ((f32[8,40,128]{2,1,0:T(8,128)}), f32[8,40,128]{2,1,0:T(8,128)S(1)}, u32[]{:S(2)}, u32[]{:S(2)}) async-start(f32[8,40,128]{2,1,0:T(8,128)} %bitcast.7), calls=%async_computation.2 | async-start | bytes 327680 | tf_op jit(solution)/shard_map/all_to_all | solution.py:644
  52.5 1.4 %collective-permute-start.2 = (f32[320,128]{1,0:T(8,128)S(1)}, f32[320,128]{1,0:T(8,128)S(1)}, u32[]{:S(2)}, u32[]{:S(2)}) collective-permute-start(f32[320,128]{1,0:T(8,128)S(1)} %bitcast.18), channel_id=1, source_target_pairs={{0,1},{1,0},{2,3},{3,2},{4,5},{5,4},{6,7},{7,6},{8,9},{9,8},{10,11... | collective-permute-start | bytes 491528 | tf_op jit(solution)/shard_map/ppermute | solution.py:649
  58.1 10.1 %all-to-all-start.3 = ((f32[16,4,128]{2,1,0:T(4,128)}), f32[16,4,128]{2,1,0:T(4,128)S(1)}, u32[]{:S(2)}, u32[]{:S(2)}) async-start(f32[16,4,128]{2,1,0:T(4,128)} %bitcast.9), calls=%async_computation.3 | async-start | bytes 65536 | tf_op jit(solution)/shard_map/all_to_all | solution.py:630

commit v15 on v14

--- a/solution.py
+++ b/solution.py
@@ -148,8 +148,24 @@
     return lax.rem(lax.axis_index("bulk"), 2)
 
 
+def place_of(chip, chips):
+    return (chip + chips - chips // 2) % chips
+
+
 def block_of(peer, peers):
-    return peer // 2 + jnp.where(peer % 2 == my_core(), 0, peers // 2)
+    chips = peers // 2
+    return place_of(peer // 2, chips) + jnp.where(peer % 2 == my_core(), 0, chips)
+
+
+def to_wire(rows, send):
+    half = rows.shape[0] // 4 * 2
+    send[: rows.shape[0] - half] = rows[half:]
+    send[rows.shape[0] - half :] = rows[:half]
+
+
+def from_wire(recv):
+    half = recv.shape[0] // 4 * 2
+    return jnp.concatenate([recv[recv.shape[0] - half :], recv[: recv.shape[0] - half]], axis=0)
 
 
 def need_kernel(cap, *refs):
@@ -342,8 +358,9 @@
 
 def put_broadcast(send, served, contributions):
     slots = contributions.shape[0]
-    for chip in range(served.shape[0] // 8):
-        at = chip * (8 + slots)
+    chips = served.shape[0] // 8
+    for chip in range(chips):
+        at = place_of(chip, chips) * (8 + slots)
         send[at : at + 8] = served[chip * 8 : chip * 8 + 8]
         send[at + 8 : at + 8 + slots] = contributions
 
@@ -362,7 +379,7 @@
     wide = share_ref.shape[1] // 2
     x = iota((rows4, 8 * chips), 0)
     peer = x // (2 * cap)
-    source = 8 * (peer // 2) + 2 * cap * my_core() + x % (2 * cap)
+    source = 8 * place_of(peer // 2, chips) + 2 * cap * my_core() + x % (2 * cap)
     wanted_core = (my_core() + others) % 2
     at = (iota((rows4, 8 * chips), 1) == source) & (peer % 2 == wanted_core)
     heads = add_rows(jnp.where(at, 1.0, 0.0).astype(bf16), blocks(ref, chips, 0, 8))
@@ -482,7 +499,7 @@
         f3 = own + DT * rate
         e2_ref[...] = rate
         f3_ref[...] = f3
-        send[...] = pick(serve_ref[...], padded(f3)) + contributions
+        to_wire(pick(serve_ref[...], padded(f3)) + contributions, send)
     else:
         base_ref, f2_ref = refs[:2]
         thermal = thermal_of(energy_ref)
@@ -521,7 +538,7 @@
     far_ref,
 ):
     n = n_ref[...]
-    got = recv[...]
+    got = from_wire(recv)
     thermal = thermal_of(energy_ref)
     rate = add_rows(st4_ref[...], got) - decay_ref[...] * (n - thermal)
     n1 = n + DT * rate
@@ -532,7 +549,7 @@
     gain = far * flat(b0_ref)
     both = jnp.concatenate([gain, gain - (1.0 - far) * flat(b1_ref)], axis=0)
     state = padded(jnp.zeros((kb, 128), f32), n1)
-    send[...] = pick(s8_ref[...], state) + add_rows(sp8_ref[...], both)
+    to_wire(pick(s8_ref[...], state) + add_rows(sp8_ref[...], both), send)
 
 
 def last_kernel(recv, *refs):
@@ -541,7 +558,7 @@
     refs = refs[15:]
     f2_ref, n2_ref, w_ref, c_ref, sems, o0, o1 = refs
     start_chunks(c_hbm, c_ref, sems)
-    got = recv[...]
+    got = from_wire(recv)
     n, n1 = n_ref[...], n1_ref[...]
     bose = add_rows(gp8_ref[...], got)
     thermal = thermal_of(energy_ref)
@@ -627,7 +644,10 @@
     work = dict(flops=2 * tiles * 16 * 128 * 128, seen=tiles * 128 * 128 * 2)
 
     def exchange(x):
-        return lax.all_to_all(x, "bulk", split_axis=0, concat_axis=0, tiled=True)
+        order = [[(i + devices // 4 * 2) % devices for i in range(devices)]]
+        return lax.all_to_all(
+            x, "bulk", split_axis=0, concat_axis=0, tiled=True, axis_index_groups=order
+        )
 
     ints = ((1, tiles), jnp.int32)
     lists = ((1, partner_need.shape[1]), jnp.int32)
@@ -638,7 +658,9 @@
     assert step_rows % 8 == 0 and slots % 8 == 0 and slots <= 128
     assert devices % 2 == 0 and cap == 2
     chips = devices // 2
-    same_core = [list(range(core, devices, 2)) for core in (0, 1)]
+    same_core = [
+        [(i + chips // 2) % chips * 2 + core for i in range(chips)] for core in (0, 1)
+    ]
 
     def to_chips(x):
         return lax.all_to_all(

time: 82.9 us -> 76.8 us (0.926)
  waiting for transfers between devices: 16.8 us -> 7.61 us
  starting transfers between devices: 18 us -> 21.7 us
  blocking collectives: 9.83 us -> 8.95 us
    all_to_all x3, waiting for transfers between devices: 10.6 us -> 3.61 us  [to_chips(): lax.all_to_all(x, 'bulk', split_axis=0, concat_axis=0, tiled=True, axis_i...]
    all_to_all x3, starting transfers between devices: 14.5 us -> 17.3 us  [to_chips(): lax.all_to_all(x, 'bulk', split_axis=0, concat_axis=0, tiled=True, axis_i...]
    all_to_all x1, waiting for transfers between devices: 2.85 us -> 0.61 us  [exchange(): lax.all_to_all(x, 'bulk', split_axis=0, concat_axis=0, tiled=True, axis_i...]
    all_to_all x1, blocking collectives: 9.83 us -> 8.95 us  [exchange(): lax.all_to_all(x, 'bulk', split_axis=0, concat_axis=0, tiled=True, axis_i...]
    all_to_all x1, starting transfers between devices: 3.5 us -> 4.37 us  [exchange(): lax.all_to_all(x, 'bulk', split_axis=0, concat_axis=0, tiled=True, axis_i...]
  transfers between devices with their start and end apart: 7 -> 7, of which waited for: 7 -> 6; matrix products, arithmetic and copies ran while one was open for 0% -> 0% of each run, Pallas kernels for 21% -> 23%
where the time goes in v15:
time: 76.8 us; the launch traced here: 76.2 us
  Pallas kernels  36.5 us (48%)
  starting transfers between devices  21.7 us (28%)
  blocking collectives  8.95 us (12%)
  waiting for transfers between devices  7.61 us (10%)
  between operations  1.39 us (2%)
    pallas_call x14, Pallas kernels, run(): pl.pallas_call(kernel, out_shape=[(out_spaces or {}).get(i, jax.ShapeDtyp...  36.5 us
    all_to_all x3, starting transfers between devices, to_chips(): lax.all_to_all(x, 'bulk', split_axis=0, concat_axis=0, tiled=True, axis_i...  17.3 us
    all_to_all x1, blocking collectives, exchange(): lax.all_to_all(x, 'bulk', split_axis=0, concat_axis=0, tiled=True, axis_i...  8.95 us
    all_to_all x1, starting transfers between devices, exchange(): lax.all_to_all(x, 'bulk', split_axis=0, concat_axis=0, tiled=True, axis_i...  4.37 us
    all_to_all x3, waiting for transfers between devices, to_chips(): lax.all_to_all(x, 'bulk', split_axis=0, concat_axis=0, tiled=True, axis_i...  3.61 us
    ppermute x3, waiting for transfers between devices, between_cores(): return lax.ppermute(x, 'bulk', [(i, i ^ 1) for i in range(devices)])  3.39 us
  transfers between devices with their start and end apart: 7, of which 6 were waited for; matrix products, arithmetic and copies ran while one was open for 0% of the time, Pallas kernels for 23%

profile of v15, /device:TPU:0, one launch (start us, length us, event | category | flops | bytes accessed | tf_op | source)
XLA Modules:
  0.0 76.2 jit_solution(1127799621229299434)
XLA Ops:
  0.6 1.6 %need.1 = (f32[32,128]{1,0:T(8,128)S(1)}, f32[16,128]{1,0:T(8,128)S(1)}, f32[16,128]{1,0:T(8,128)S(1)}, f32[16,128]{1,0:T(8,128)S(1)}, s32[1,256]{1,0:T(1,128)S(...) custom-call(f32[32,128]{1,0:T(8,128)} %refs_0_.1, ...), custom_call_target="tpu_custom_call" | custom-call | tf_op jit(solution)/shard_map/need/pallas_call | solution.py:590
  2.2 7.9 %all-to-all-start = ((f32[8,56,128]{2,1,0:T(8,128)}), f32[8,56,128]{2,1,0:T(8,128)S(1)}, u32[]{:S(2)}, u32[]{:S(2)}) async-start(f32[8,56,128]{2,1,0:T(8,128)} %bitcast.3), calls=%async_computation | async-start | bytes 458752 | tf_op jit(solution)/shard_map/all_to_all | solution.py:666
  10.7 5.6 %prepare.1 = (bf16[64,128,128]{2,1,0:T(8,128)(2,1)S(1)}, bf16[192,128,128]{2,1,0:T(8,128)(2,1)}, bf16[256,128]{1,0:T(8,128)(2,1)S(1)}, bf16[256,128]{1,0:T(8,128...) custom-call(s32[1]{0:T(128)S(6)} %copy.13.count_ref, ...), custom_call_target="tpu_custom_call" | custom-call | flops 134217728 | bytes 8388608 | tf_op jit(solution)/shard_map/prepare/pallas_call | solution.py:590
  16.4 0.0 all-to-all-done
  16.4 0.1 collective-permute-start
  16.5 0.2 near_rows.1.part_ref
  16.6 1.3 %collective-permute-done.other_ref = f32[448,128]{1,0:T(8,128)S(1)} collective-permute-done((f32[448,128]{1,0:T(8,128)S(1)}, f32[448,128]{1,0:T(8,128)S(1)}, u32[]{:S(2)}, u32[]{:S(2)}) %collective-permute-start) | collective-permute-done | bytes 229408 | tf_op jit(solution)/shard_map/ppermute | solution.py:671
  17.9 4.3 %first.1 = (f32[320,128]{1,0:T(8,128)}, f32[32,128]{1,0:T(8,128)S(1)}, f32[32,128]{1,0:T(8,128)S(1)}, bf16[64,128]{1,0:T(8,128)(2,1)S(1)}, bf16[128,128]{1,0:T(8,128)(2,1)S(1)}) custom-call(f32[448,128]{1,0:T(8,128)S(1)} %bitcast.15, f32[448,128]{1,0:T(8,128)S(1)} %collective-permute-done.other_ref, f32[64,128]{1,0:T(8,128)S(1)} %near_rows.1.part_ref, ...), custom_call_target="tpu_custom_call" | custom-call | flops 134217728 | bytes 8388608 | tf_op jit(solution)/shard_map/first/pallas_call | solution.py:590
  22.3 5.1 %all-to-all-start.1 = ((f32[8,40,128]{2,1,0:T(8,128)}), f32[8,40,128]{2,1,0:T(8,128)S(1)}, u32[]{:S(2)}, u32[]{:S(2)}) async-start(f32[8,40,128]{2,1,0:T(8,128)} %bitcast.5), calls=%async_computation.1 | async-start | bytes 327680 | tf_op jit(solution)/shard_map/all_to_all | solution.py:666
  27.4 3.7 %backward.3 = (f32[32,8,128]{2,1,0:T(8,128)S(1)}, f32[32,8,128]{2,1,0:T(8,128)S(1)}) custom-call(f32[32,128]{1,0:T(8,128)S(1)} %get-tuple-element.87.f_ref.own_ref, bf16[256,32]{1,0:T(8,128)(2,1)S(1)} %get-tuple-element.88.gk_ref, bf16[256,128,128]{2,1,0:T(8,128)(2,1)} %c_hbm.7), custom_call_target="tpu_custom_call" | custom-call | flops 134217728 | bytes 8388608 | tf_op jit(solution)/shard_map/backward/pallas_call | solution.py:590
  31.2 1.7 %all-to-all-done.1 = f32[8,40,128]{2,1,0:T(8,128)S(1)} async-done(((f32[8,40,128]{2,1,0:T(8,128)}), f32[8,40,128]{2,1,0:T(8,128)S(1)}, u32[]{:S(2)}, u32[]{:S(2)}) %all-to-all-start.1) | async-done | bytes 163872 | tf_op jit(solution)/shard_map/all_to_all | solution.py:666
  32.8 0.0 collective-permute-start.1
  32.8 0.3 serve.1
  33.1 0.2 near_half.2
  33.3 0.9 %collective-permute-done.1.other_ref = f32[320,128]{1,0:T(8,128)S(1)} collective-permute-done((f32[320,128]{1,0:T(8,128)S(1)}, f32[320,128]{1,0:T(8,128)S(1)}, u32[]{:S(2)}, u32[]{:S(2)}) %collective-permute-start.1) | collective-permute-done | bytes 163872 | tf_op jit(solution)/shard_map/ppermute | solution.py:671
  34.2 4.4 %middle.2 = (f32[320,128]{1,0:T(8,128)}, f32[16,128]{1,0:T(8,128)S(1)}, f32[32,128]{1,0:T(8,128)S(1)}) custom-call(f32[64,128]{1,0:T(8,128)S(1)} %get-tuple-element.95.part_ref, f32[16,128]{1,0:T(8,128)S(1)} %get-tuple-element.96.total_ref, f32[320,128]{1,0:T(8,128)S(1)} %collective-permute-done.1.other_ref, ...), custom_call_target="tpu_custom_call" | custom-call | flops 134217728 | bytes 8388608 | tf_op jit(solution)/shard_map/middle/pallas_call | solution.py:590
  38.6 4.3 %all-to-all-start.2 = ((f32[8,40,128]{2,1,0:T(8,128)}), f32[8,40,128]{2,1,0:T(8,128)S(1)}, u32[]{:S(2)}, u32[]{:S(2)}) async-start(f32[8,40,128]{2,1,0:T(8,128)} %bitcast.7), calls=%async_computation.2 | async-start | bytes 327680 | tf_op jit(solution)/shard_map/all_to_all | solution.py:666
  42.9 3.7 %backward.4 = (f32[32,8,128]{2,1,0:T(8,128)S(1)}, f32[32,8,128]{2,1,0:T(8,128)S(1)}) custom-call(f32[32,128]{1,0:T(8,128)S(1)} %get-tuple-element.101.f_ref.own_ref.refs_1_, bf16[256,32]{1,0:T(8,128)(2,1)S(1)} %get-tuple-element.88.gk_ref, bf16[256,128,128]{2,1,0:T(8,128)(2,1)} %c_hbm.7), custom_call_target="tpu_custom_call" | custom-call | flops 134217728 | bytes 8388608 | tf_op jit(solution)/shard_map/backward/pallas_call | solution.py:590
  46.7 1.9 %all-to-all-done.2 = f32[8,40,128]{2,1,0:T(8,128)S(1)} async-done(((f32[8,40,128]{2,1,0:T(8,128)}), f32[8,40,128]{2,1,0:T(8,128)S(1)}, u32[]{:S(2)}, u32[]{:S(2)}) %all-to-all-start.2) | async-done | bytes 163872 | tf_op jit(solution)/shard_map/all_to_all | solution.py:666
  48.6 0.0 collective-permute-start.2
  48.6 0.2 near_half.3
  48.8 1.2 %collective-permute-done.2.other_ref = f32[320,128]{1,0:T(8,128)S(1)} collective-permute-done((f32[320,128]{1,0:T(8,128)S(1)}, f32[320,128]{1,0:T(8,128)S(1)}, u32[]{:S(2)}, u32[]{:S(2)}) %collective-permute-start.2) | collective-permute-done | bytes 163872 | tf_op jit(solution)/shard_map/ppermute | solution.py:671
  50.0 4.2 %middle.3 = (f32[64,128]{1,0:T(8,128)}, f32[16,128]{1,0:T(8,128)S(1)}, f32[32,128]{1,0:T(8,128)S(1)}, f32[32,128]{1,0:T(8,128)S(1)}) custom-call(f32[64,128]{1,0:T(8,128)S(1)} %get-tuple-element.104.part_ref, f32[16,128]{1,0:T(8,128)S(1)} %get-tuple-element.105.total_ref, f32[320,128]{1,0:T(8,128)S(1)} %collective-permute-done.2.other_ref, ...), custom_call_target="tpu_custom_call" | custom-call | flops 134217728 | bytes 8388608 | tf_op jit(solution)/shard_map/middle/pallas_call | solution.py:590
  54.2 4.4 %all-to-all-start.3 = ((f32[16,4,128]{2,1,0:T(4,128)}), f32[16,4,128]{2,1,0:T(4,128)S(1)}, u32[]{:S(2)}, u32[]{:S(2)}) async-start(f32[16,4,128]{2,1,0:T(4,128)} %bitcast.9), calls=%async_computation.3 | async-start | bytes 65536 | tf_op jit(solution)/shard_map/all_to_all | solution.py:648
  58.5 3.7 %backward.5 = (f32[32,8,128]{2,1,0:T(8,128)S(1)}, f32[32,8,128]{2,1,0:T(8,128)S(1)}) custom-call(f32[32,128]{1,0:T(8,128)S(1)} %get-tuple-element.115.f_ref.refs_2_, bf16[256,32]{1,0:T(8,128)(2,1)S(1)} %get-tuple-element.88.gk_ref, bf16[256,128,128]{2,1,0:T(8,128)(2,1)} %c_hbm.7), custom_call_target="tpu_custom_call" | custom-call | flops 134217728 | bytes 8388608 | tf_op jit(solution)/shard_map/backward/pallas_call | solution.py:590
  62.3 0.6 all-to-all-done.3
  62.9 0.4 phonon.1
  63.3 9.0 %all_to_all.58 = f32[16,8,128]{2,1,0:T(8,128)S(1)} all-to-all(f32[16,8,128]{2,1,0:T(8,128)S(1)} %bitcast.22), channel_id=1, replica_groups={{8,9,10,11,12,13,14,15,0,1,2,3,4,5,6,7},{24,25,26,27,28,29,30,31,16,17,..., dimensions={0} | all-to-all | bytes 131072 | tf_op jit(solution)/shard_map/all_to_all | solution.py:648
  72.2 3.9 %last.1 = (f32[32,128]{1,0:T(8,128)}, f32[16,128]{1,0:T(8,128)}) custom-call(f32[128,128]{1,0:T(8,128)S(1)} %bitcast.20, f32[256,128]{1,0:T(8,128)S(1)} %get-tuple-element.119.refs_0_, f32[32,128]{1,0:T(8,128)S(1)} %get-tuple-element.101.f_ref.own_ref.refs_1_, f32[32,128]{1,0:T(8,128)S(1)} %get-tuple-element.115.f_ref.refs_2_, ...), custom_call_target="tpu_custom_call" | custom-call | flops 134217728 | bytes 8388608 | tf_op jit(solution)/shard_map/last/pallas_call | solution.py:590
Async XLA Ops:
  2.2 14.2 %all-to-all-start = ((f32[8,56,128]{2,1,0:T(8,128)}), f32[8,56,128]{2,1,0:T(8,128)S(1)}, u32[]{:S(2)}, u32[]{:S(2)}) async-start(f32[8,56,128]{2,1,0:T(8,128)} %bitcast.3), calls=%async_computation | async-start | bytes 458752 | tf_op jit(solution)/shard_map/all_to_all | solution.py:666
  16.4 1.6 %collective-permute-start = (f32[448,128]{1,0:T(8,128)S(1)}, f32[448,128]{1,0:T(8,128)S(1)}, u32[]{:S(2)}, u32[]{:S(2)}) collective-permute-start(f32[448,128]{1,0:T(8,128)S(1)} %bitcast.13), channel_id=1, source_target_pairs={{0,1},{1,0},{2,3},{3,2},{4,5},{5,4},{6,7},{7,6},{8,9},{9,8},{10,11... | collective-permute-start | bytes 688136 | tf_op jit(solution)/shard_map/ppermute | solution.py:671
  22.3 10.5 %all-to-all-start.1 = ((f32[8,40,128]{2,1,0:T(8,128)}), f32[8,40,128]{2,1,0:T(8,128)S(1)}, u32[]{:S(2)}, u32[]{:S(2)}) async-start(f32[8,40,128]{2,1,0:T(8,128)} %bitcast.5), calls=%async_computation.1 | async-start | bytes 327680 | tf_op jit(solution)/shard_map/all_to_all | solution.py:666
  32.8 1.4 %collective-permute-start.1 = (f32[320,128]{1,0:T(8,128)S(1)}, f32[320,128]{1,0:T(8,128)S(1)}, u32[]{:S(2)}, u32[]{:S(2)}) collective-permute-start(f32[320,128]{1,0:T(8,128)S(1)} %bitcast.16), channel_id=1, source_target_pairs={{0,1},{1,0},{2,3},{3,2},{4,5},{5,4},{6,7},{7,6},{8,9},{9,8},{10,11... | collective-permute-start | bytes 491528 | tf_op jit(solution)/shard_map/ppermute | solution.py:671
  38.6 10.0 %all-to-all-start.2 = ((f32[8,40,128]{2,1,0:T(8,128)}), f32[8,40,128]{2,1,0:T(8,128)S(1)}, u32[]{:S(2)}, u32[]{:S(2)}) async-start(f32[8,40,128]{2,1,0:T(8,128)} %bitcast.7), calls=%async_computation.2 | async-start | bytes 327680 | tf_op jit(solution)/shard_map/all_to_all | solution.py:666
  48.6 1.4 %collective-permute-start.2 = (f32[320,128]{1,0:T(8,128)S(1)}, f32[320,128]{1,0:T(8,128)S(1)}, u32[]{:S(2)}, u32[]{:S(2)}) collective-permute-start(f32[320,128]{1,0:T(8,128)S(1)} %bitcast.18), channel_id=1, source_target_pairs={{0,1},{1,0},{2,3},{3,2},{4,5},{5,4},{6,7},{7,6},{8,9},{9,8},{10,11... | collective-permute-start | bytes 491528 | tf_op jit(solution)/shard_map/ppermute | solution.py:671
  54.2 8.7 %all-to-all-start.3 = ((f32[16,4,128]{2,1,0:T(4,128)}), f32[16,4,128]{2,1,0:T(4,128)S(1)}, u32[]{:S(2)}, u32[]{:S(2)}) async-start(f32[16,4,128]{2,1,0:T(4,128)} %bitcast.9), calls=%async_computation.3 | async-start | bytes 65536 | tf_op jit(solution)/shard_map/all_to_all | solution.py:648

commit v16 on v15

--- a/solution.py
+++ b/solution.py
@@ -23,20 +23,6 @@
     return lax.dot_general(a, b, (((1,), (0,)), ((), ())), preferred_element_type=f32)
 
 
-def split(x):
-    hi = x.astype(bf16)
-    rest = x - hi.astype(f32)
-    mid = rest.astype(bf16)
-    lo = (rest - mid.astype(f32)).astype(bf16)
-    return hi, mid, lo
-
-
-def pick(onehot, x):
-    hi, mid, lo = split(x)
-    both = dot(onehot, jnp.concatenate([hi, mid], axis=1))
-    return both[:, :128] + both[:, 128:] + dot(onehot, lo)
-
-
 def add_rows(onehot, x):
     hi = x.astype(bf16)
     mid = (x - hi.astype(f32)).astype(bf16)
@@ -103,9 +89,14 @@
 
 
 def left_sides(first, second, w_ref):
-    w = stacked(first, second)
-    for g in range(w.shape[0]):
-        w_ref[g] = block_diagonal(w[g])
+    groups = w_ref.shape[0]
+    w_ref[:, :, :128] = stacked(first, second)
+
+    def spread(g, _):
+        w_ref[g] = block_diagonal(w_ref[g, :, :128])
+        return 0
+
+    lax.fori_loop(0, groups, spread, 0, unroll=4)
 
 
 def chunk_products(w_ref, c_ref, i, base, out0, out1):
@@ -141,7 +132,12 @@
 def electron_rate(sum_k, far, bose, f, parts, w_ref, o0, o1):
     left_sides(far * (1.0 + bose), far + bose, w_ref)
     tile_products(w_ref, parts, o0, o1)
-    return add_rows(sum_k, flat(o0)) - f * add_rows(sum_k, flat(o1))
+    gain, loss = flat(o0), flat(o1)
+    gain_hi, loss_hi = gain.astype(bf16), loss.astype(bf16)
+    gain_lo = (gain - gain_hi.astype(f32)).astype(bf16)
+    loss_lo = (loss - loss_hi.astype(f32)).astype(bf16)
+    sums = dot(sum_k, jnp.concatenate([gain_hi, gain_lo, loss_hi, loss_lo], axis=1))
+    return sums[:, :128] + sums[:, 128:256] - f * (sums[:, 256:384] + sums[:, 384:])
 
 
 def my_core():
@@ -452,7 +448,7 @@
     f1 = f + DT * rate
     e_ref[...] = rate
     f1_ref[...] = f1
-    put_broadcast(send, pick(hot, padded(f1, base)), contributions)
+    put_broadcast(send, add_rows(hot, padded(f1, base)), contributions)
 
 
 def middle_kernel(
@@ -499,7 +495,7 @@
         f3 = own + DT * rate
         e2_ref[...] = rate
         f3_ref[...] = f3
-        to_wire(pick(serve_ref[...], padded(f3)) + contributions, send)
+        to_wire(add_rows(serve_ref[...], padded(f3)) + contributions, send)
     else:
         base_ref, f2_ref = refs[:2]
         thermal = thermal_of(energy_ref)
@@ -511,7 +507,7 @@
         rate = electron_rate(sk_ref[...], far, bose, own, parts, w_ref, o0, o1)
         f2 = f_ref[...] + (DT / 2.0) * (e_ref[...] + rate)
         f2_ref[...] = f2
-        put_broadcast(send, pick(serve_ref[...], padded(f2, base)), contributions)
+        put_broadcast(send, add_rows(serve_ref[...], padded(f2, base)), contributions)
 
 
 def backward_kernel(f_ref, gk_ref, c_hbm, b0_ref, b1_ref, w_ref, c_ref, sems):
@@ -549,7 +545,7 @@
     gain = far * flat(b0_ref)
     both = jnp.concatenate([gain, gain - (1.0 - far) * flat(b1_ref)], axis=0)
     state = padded(jnp.zeros((kb, 128), f32), n1)
-    to_wire(pick(s8_ref[...], state) + add_rows(sp8_ref[...], both), send)
+    to_wire(add_rows(s8_ref[...], state) + add_rows(sp8_ref[...], both), send)
 
 
 def last_kernel(recv, *refs):

time: 76.8 us -> 76.6 us (level)
  no operation moved by 1% of the time
where the time goes in v16:
time: 76.6 us; the launch traced here: 76 us
  Pallas kernels  36.2 us (47%)
  starting transfers between devices  21.8 us (28%)
  blocking collectives  8.95 us (12%)
  waiting for transfers between devices  7.74 us (10%)
  between operations  1.38 us (2%)
    pallas_call x14, Pallas kernels, run(): pl.pallas_call(kernel, out_shape=[(out_spaces or {}).get(i, jax.ShapeDtyp...  36.2 us
    all_to_all x3, starting transfers between devices, to_chips(): lax.all_to_all(x, 'bulk', split_axis=0, concat_axis=0, tiled=True, axis_i...  17.3 us
    all_to_all x1, blocking collectives, exchange(): lax.all_to_all(x, 'bulk', split_axis=0, concat_axis=0, tiled=True, axis_i...  8.95 us
    all_to_all x1, starting transfers between devices, exchange(): lax.all_to_all(x, 'bulk', split_axis=0, concat_axis=0, tiled=True, axis_i...  4.36 us
    all_to_all x3, waiting for transfers between devices, to_chips(): lax.all_to_all(x, 'bulk', split_axis=0, concat_axis=0, tiled=True, axis_i...  3.74 us
    ppermute x3, waiting for transfers between devices, between_cores(): return lax.ppermute(x, 'bulk', [(i, i ^ 1) for i in range(devices)])  3.39 us
  transfers between devices with their start and end apart: 7, of which 6 were waited for; matrix products, arithmetic and copies ran while one was open for 0% of the time, Pallas kernels for 23%

profile of v16, /device:TPU:0, one launch (start us, length us, event | category | flops | bytes accessed | tf_op | source)
XLA Modules:
  0.0 76.0 jit_solution(3539194586306194595)
XLA Ops:
  0.6 1.6 %need.1 = (f32[32,128]{1,0:T(8,128)S(1)}, f32[16,128]{1,0:T(8,128)S(1)}, f32[16,128]{1,0:T(8,128)S(1)}, f32[16,128]{1,0:T(8,128)S(1)}, s32[1,256]{1,0:T(1,128)S(...) custom-call(f32[32,128]{1,0:T(8,128)} %refs_0_.1, ...), custom_call_target="tpu_custom_call" | custom-call | tf_op jit(solution)/shard_map/need/pallas_call | solution.py:586
  2.2 7.9 %all-to-all-start = ((f32[8,56,128]{2,1,0:T(8,128)}), f32[8,56,128]{2,1,0:T(8,128)S(1)}, u32[]{:S(2)}, u32[]{:S(2)}) async-start(f32[8,56,128]{2,1,0:T(8,128)} %bitcast.3), calls=%async_computation | async-start | bytes 458752 | tf_op jit(solution)/shard_map/all_to_all | solution.py:662
  10.7 5.5 %prepare.1 = (bf16[64,128,128]{2,1,0:T(8,128)(2,1)S(1)}, bf16[192,128,128]{2,1,0:T(8,128)(2,1)}, bf16[256,128]{1,0:T(8,128)(2,1)S(1)}, bf16[256,128]{1,0:T(8,128...) custom-call(s32[1]{0:T(128)S(6)} %copy.13.count_ref, ...), custom_call_target="tpu_custom_call" | custom-call | flops 134217728 | bytes 8388608 | tf_op jit(solution)/shard_map/prepare/pallas_call | solution.py:586
  16.2 0.0 all-to-all-done
  16.2 0.1 collective-permute-start
  16.3 0.2 near_rows.1.part_ref
  16.5 1.3 %collective-permute-done.other_ref = f32[448,128]{1,0:T(8,128)S(1)} collective-permute-done((f32[448,128]{1,0:T(8,128)S(1)}, f32[448,128]{1,0:T(8,128)S(1)}, u32[]{:S(2)}, u32[]{:S(2)}) %collective-permute-start) | collective-permute-done | bytes 229408 | tf_op jit(solution)/shard_map/ppermute | solution.py:667
  17.8 4.4 %first.1 = (f32[320,128]{1,0:T(8,128)}, f32[32,128]{1,0:T(8,128)S(1)}, f32[32,128]{1,0:T(8,128)S(1)}, bf16[64,128]{1,0:T(8,128)(2,1)S(1)}, bf16[128,128]{1,0:T(8,128)(2,1)S(1)}) custom-call(f32[448,128]{1,0:T(8,128)S(1)} %bitcast.15, f32[448,128]{1,0:T(8,128)S(1)} %collective-permute-done.other_ref, f32[64,128]{1,0:T(8,128)S(1)} %near_rows.1.part_ref, ...), custom_call_target="tpu_custom_call" | custom-call | flops 134217728 | bytes 8388608 | tf_op jit(solution)/shard_map/first/pallas_call | solution.py:586
  22.2 5.1 %all-to-all-start.1 = ((f32[8,40,128]{2,1,0:T(8,128)}), f32[8,40,128]{2,1,0:T(8,128)S(1)}, u32[]{:S(2)}, u32[]{:S(2)}) async-start(f32[8,40,128]{2,1,0:T(8,128)} %bitcast.5), calls=%async_computation.1 | async-start | bytes 327680 | tf_op jit(solution)/shard_map/all_to_all | solution.py:662
  27.3 3.7 %backward.3 = (f32[32,8,128]{2,1,0:T(8,128)S(1)}, f32[32,8,128]{2,1,0:T(8,128)S(1)}) custom-call(f32[32,128]{1,0:T(8,128)S(1)} %get-tuple-element.87.f_ref.own_ref, bf16[256,32]{1,0:T(8,128)(2,1)S(1)} %get-tuple-element.88.gk_ref, bf16[256,128,128]{2,1,0:T(8,128)(2,1)} %c_hbm.7), custom_call_target="tpu_custom_call" | custom-call | flops 134217728 | bytes 8388608 | tf_op jit(solution)/shard_map/backward/pallas_call | solution.py:586
  31.1 1.8 %all-to-all-done.1 = f32[8,40,128]{2,1,0:T(8,128)S(1)} async-done(((f32[8,40,128]{2,1,0:T(8,128)}), f32[8,40,128]{2,1,0:T(8,128)S(1)}, u32[]{:S(2)}, u32[]{:S(2)}) %all-to-all-start.1) | async-done | bytes 163872 | tf_op jit(solution)/shard_map/all_to_all | solution.py:662
  32.9 0.0 collective-permute-start.1
  32.9 0.3 serve.1
  33.2 0.2 near_half.2
  33.4 0.9 %collective-permute-done.1.other_ref = f32[320,128]{1,0:T(8,128)S(1)} collective-permute-done((f32[320,128]{1,0:T(8,128)S(1)}, f32[320,128]{1,0:T(8,128)S(1)}, u32[]{:S(2)}, u32[]{:S(2)}) %collective-permute-start.1) | collective-permute-done | bytes 163872 | tf_op jit(solution)/shard_map/ppermute | solution.py:667
  34.3 4.2 %middle.2 = (f32[320,128]{1,0:T(8,128)}, f32[16,128]{1,0:T(8,128)S(1)}, f32[32,128]{1,0:T(8,128)S(1)}) custom-call(f32[64,128]{1,0:T(8,128)S(1)} %get-tuple-element.95.part_ref, f32[16,128]{1,0:T(8,128)S(1)} %get-tuple-element.96.total_ref, f32[320,128]{1,0:T(8,128)S(1)} %collective-permute-done.1.other_ref, ...), custom_call_target="tpu_custom_call" | custom-call | flops 134217728 | bytes 8388608 | tf_op jit(solution)/shard_map/middle/pallas_call | solution.py:586
  38.5 4.4 %all-to-all-start.2 = ((f32[8,40,128]{2,1,0:T(8,128)}), f32[8,40,128]{2,1,0:T(8,128)S(1)}, u32[]{:S(2)}, u32[]{:S(2)}) async-start(f32[8,40,128]{2,1,0:T(8,128)} %bitcast.7), calls=%async_computation.2 | async-start | bytes 327680 | tf_op jit(solution)/shard_map/all_to_all | solution.py:662
  42.8 3.7 %backward.4 = (f32[32,8,128]{2,1,0:T(8,128)S(1)}, f32[32,8,128]{2,1,0:T(8,128)S(1)}) custom-call(f32[32,128]{1,0:T(8,128)S(1)} %get-tuple-element.101.f_ref.own_ref.refs_1_, bf16[256,32]{1,0:T(8,128)(2,1)S(1)} %get-tuple-element.88.gk_ref, bf16[256,128,128]{2,1,0:T(8,128)(2,1)} %c_hbm.7), custom_call_target="tpu_custom_call" | custom-call | flops 134217728 | bytes 8388608 | tf_op jit(solution)/shard_map/backward/pallas_call | solution.py:586
  46.6 1.9 %all-to-all-done.2 = f32[8,40,128]{2,1,0:T(8,128)S(1)} async-done(((f32[8,40,128]{2,1,0:T(8,128)}), f32[8,40,128]{2,1,0:T(8,128)S(1)}, u32[]{:S(2)}, u32[]{:S(2)}) %all-to-all-start.2) | async-done | bytes 163872 | tf_op jit(solution)/shard_map/all_to_all | solution.py:662
  48.5 0.0 collective-permute-start.2
  48.5 0.2 near_half.3
  48.7 1.2 %collective-permute-done.2.other_ref = f32[320,128]{1,0:T(8,128)S(1)} collective-permute-done((f32[320,128]{1,0:T(8,128)S(1)}, f32[320,128]{1,0:T(8,128)S(1)}, u32[]{:S(2)}, u32[]{:S(2)}) %collective-permute-start.2) | collective-permute-done | bytes 163872 | tf_op jit(solution)/shard_map/ppermute | solution.py:667
  49.9 4.1 %middle.3 = (f32[64,128]{1,0:T(8,128)}, f32[16,128]{1,0:T(8,128)S(1)}, f32[32,128]{1,0:T(8,128)S(1)}, f32[32,128]{1,0:T(8,128)S(1)}) custom-call(f32[64,128]{1,0:T(8,128)S(1)} %get-tuple-element.104.part_ref, f32[16,128]{1,0:T(8,128)S(1)} %get-tuple-element.105.total_ref, f32[320,128]{1,0:T(8,128)S(1)} %collective-permute-done.2.other_ref, ...), custom_call_target="tpu_custom_call" | custom-call | flops 134217728 | bytes 8388608 | tf_op jit(solution)/shard_map/middle/pallas_call | solution.py:586
  54.1 4.4 %all-to-all-start.3 = ((f32[16,4,128]{2,1,0:T(4,128)}), f32[16,4,128]{2,1,0:T(4,128)S(1)}, u32[]{:S(2)}, u32[]{:S(2)}) async-start(f32[16,4,128]{2,1,0:T(4,128)} %bitcast.9), calls=%async_computation.3 | async-start | bytes 65536 | tf_op jit(solution)/shard_map/all_to_all | solution.py:644
  58.4 3.7 %backward.5 = (f32[32,8,128]{2,1,0:T(8,128)S(1)}, f32[32,8,128]{2,1,0:T(8,128)S(1)}) custom-call(f32[32,128]{1,0:T(8,128)S(1)} %get-tuple-element.115.f_ref.refs_2_, bf16[256,32]{1,0:T(8,128)(2,1)S(1)} %get-tuple-element.88.gk_ref, bf16[256,128,128]{2,1,0:T(8,128)(2,1)} %c_hbm.7), custom_call_target="tpu_custom_call" | custom-call | flops 134217728 | bytes 8388608 | tf_op jit(solution)/shard_map/backward/pallas_call | solution.py:586
  62.2 0.6 all-to-all-done.3
  62.8 0.4 phonon.1
  63.1 9.0 %all_to_all.58 = f32[16,8,128]{2,1,0:T(8,128)S(1)} all-to-all(f32[16,8,128]{2,1,0:T(8,128)S(1)} %bitcast.22), channel_id=1, replica_groups={{8,9,10,11,12,13,14,15,0,1,2,3,4,5,6,7},{24,25,26,27,28,29,30,31,16,17,..., dimensions={0} | all-to-all | bytes 131072 | tf_op jit(solution)/shard_map/all_to_all | solution.py:644
  72.1 3.9 %last.1 = (f32[32,128]{1,0:T(8,128)}, f32[16,128]{1,0:T(8,128)}) custom-call(f32[128,128]{1,0:T(8,128)S(1)} %bitcast.20, f32[256,128]{1,0:T(8,128)S(1)} %get-tuple-element.119.refs_0_, f32[32,128]{1,0:T(8,128)S(1)} %get-tuple-element.101.f_ref.own_ref.refs_1_, f32[32,128]{1,0:T(8,128)S(1)} %get-tuple-element.115.f_ref.refs_2_, ...), custom_call_target="tpu_custom_call" | custom-call | flops 134217728 | bytes 8388608 | tf_op jit(solution)/shard_map/last/pallas_call | solution.py:586
Async XLA Ops:
  2.2 14.0 %all-to-all-start = ((f32[8,56,128]{2,1,0:T(8,128)}), f32[8,56,128]{2,1,0:T(8,128)S(1)}, u32[]{:S(2)}, u32[]{:S(2)}) async-start(f32[8,56,128]{2,1,0:T(8,128)} %bitcast.3), calls=%async_computation | async-start | bytes 458752 | tf_op jit(solution)/shard_map/all_to_all | solution.py:662
  16.2 1.6 %collective-permute-start = (f32[448,128]{1,0:T(8,128)S(1)}, f32[448,128]{1,0:T(8,128)S(1)}, u32[]{:S(2)}, u32[]{:S(2)}) collective-permute-start(f32[448,128]{1,0:T(8,128)S(1)} %bitcast.13), channel_id=1, source_target_pairs={{0,1},{1,0},{2,3},{3,2},{4,5},{5,4},{6,7},{7,6},{8,9},{9,8},{10,11... | collective-permute-start | bytes 688136 | tf_op jit(solution)/shard_map/ppermute | solution.py:667
  22.2 10.6 %all-to-all-start.1 = ((f32[8,40,128]{2,1,0:T(8,128)}), f32[8,40,128]{2,1,0:T(8,128)S(1)}, u32[]{:S(2)}, u32[]{:S(2)}) async-start(f32[8,40,128]{2,1,0:T(8,128)} %bitcast.5), calls=%async_computation.1 | async-start | bytes 327680 | tf_op jit(solution)/shard_map/all_to_all | solution.py:662
  32.9 1.4 %collective-permute-start.1 = (f32[320,128]{1,0:T(8,128)S(1)}, f32[320,128]{1,0:T(8,128)S(1)}, u32[]{:S(2)}, u32[]{:S(2)}) collective-permute-start(f32[320,128]{1,0:T(8,128)S(1)} %bitcast.16), channel_id=1, source_target_pairs={{0,1},{1,0},{2,3},{3,2},{4,5},{5,4},{6,7},{7,6},{8,9},{9,8},{10,11... | collective-permute-start | bytes 491528 | tf_op jit(solution)/shard_map/ppermute | solution.py:667
  38.5 10.0 %all-to-all-start.2 = ((f32[8,40,128]{2,1,0:T(8,128)}), f32[8,40,128]{2,1,0:T(8,128)S(1)}, u32[]{:S(2)}, u32[]{:S(2)}) async-start(f32[8,40,128]{2,1,0:T(8,128)} %bitcast.7), calls=%async_computation.2 | async-start | bytes 327680 | tf_op jit(solution)/shard_map/all_to_all | solution.py:662
  48.5 1.4 %collective-permute-start.2 = (f32[320,128]{1,0:T(8,128)S(1)}, f32[320,128]{1,0:T(8,128)S(1)}, u32[]{:S(2)}, u32[]{:S(2)}) collective-permute-start(f32[320,128]{1,0:T(8,128)S(1)} %bitcast.18), channel_id=1, source_target_pairs={{0,1},{1,0},{2,3},{3,2},{4,5},{5,4},{6,7},{7,6},{8,9},{9,8},{10,11... | collective-permute-start | bytes 491528 | tf_op jit(solution)/shard_map/ppermute | solution.py:667
  54.1 8.7 %all-to-all-start.3 = ((f32[16,4,128]{2,1,0:T(4,128)}), f32[16,4,128]{2,1,0:T(4,128)S(1)}, u32[]{:S(2)}, u32[]{:S(2)}) async-start(f32[16,4,128]{2,1,0:T(4,128)} %bitcast.9), calls=%async_computation.3 | async-start | bytes 65536 | tf_op jit(solution)/shard_map/all_to_all | solution.py:644

commit v17 on v16

--- a/solution.py
+++ b/solution.py
@@ -66,7 +66,7 @@
 
 
 def chunk_copy(src, dst, sems, i):
-    size = src.shape[0] // sems.shape[0]
+    size = min(src.shape[0], dst.shape[0]) // sems.shape[0]
     here = pl.ds(i * size, size)
     return pltpu.make_async_copy(src.at[here], dst.at[here], sems.at[i])
 
@@ -110,8 +110,7 @@
 
 def tile_products(w_ref, parts, out0, out1):
     size = w_ref.shape[0] // CHUNKS
-    base = 0
-    for c_ref, c_hbm, sems in parts:
+    for c_ref, c_hbm, sems, base in parts:
         chunks = c_ref.shape[0] // 8 // size
 
         def chunk(i, _):
@@ -121,12 +120,19 @@
             return 0
 
         lax.fori_loop(0, chunks, chunk, 0)
-        base += chunks * size
 
 
 def backward_pass(own, c_hbm, c_ref, sems, w_ref, out0, out1):
     left_sides(1.0 - own, own, w_ref)
-    tile_products(w_ref, [(c_ref, c_hbm, sems)], out0, out1)
+    tile_products(w_ref, [(c_ref, c_hbm, sems, 0)], out0, out1)
+
+
+def forward_parts(w_ref, held_ref, fetched_ref, c_ref, c_hbm, sems):
+    first = w_ref.shape[0] - held_ref.shape[0] // 8
+    parts = [(held_ref, None, None, first)]
+    if fetched_ref is not None:
+        parts.append((fetched_ref, None, None, first - fetched_ref.shape[0] // 8))
+    return parts + [(c_ref, c_hbm, sems, 0)]
 
 
 def electron_rate(sum_k, far, bose, f, parts, w_ref, o0, o1):
@@ -200,12 +206,10 @@
     held_ref,
     t_hbm,
     pair_ref,
-    gp8_ref,
     gk_ref,
     sk_ref,
     sp_ref,
     sp4_ref,
-    sp8_ref,
     near_ref,
     list_ref,
     mine_ref,
@@ -225,7 +229,6 @@
     e = partner_ref[...]
     q = qslot_ref[...]
     rows4 = sp4_ref.shape[0]
-    rows8 = sp8_ref.shape[0]
     ind = lambda m: jnp.where(m, 1.0, 0.0)
     k_hot = ind(iota((kb, tiles), 0) == k)
     gk_ref[...] = k_hot.T.astype(bf16)
@@ -239,17 +242,6 @@
     pair_ref[...] = jnp.concatenate([ind(x == row_e), p_hot], axis=0).T.astype(bf16)
     sp4_ref[...] = jnp.where(used, p_hot, 0.0).astype(bf16)
     sp_ref[...] = jnp.where(used, ind(iota(sp_ref.shape, 0) == q), 0.0).astype(bf16)
-    x = iota((rows8, tiles), 0)
-    row_z = (q // cap) * (4 * cap) + q % cap
-    gp8_ref[...] = ind(x == row_z).T.astype(bf16)
-    sp8_ref[...] = jnp.concatenate(
-        [
-            jnp.where(used, ind(x == row_z + cap), 0.0),
-            jnp.where(used, ind(x == row_z + 2 * cap), 0.0),
-        ],
-        axis=1,
-    ).astype(bf16)
-
     rows, half = list_ref.shape
     slots = pneed_ref.shape[1]
     peers = slots // cap
@@ -271,24 +263,26 @@
     size = c_ref.shape[0] // CHUNKS
     held = held_ref.shape[0] // size
 
-    def to_held(i, _):
+    rest = CHUNKS - held
+
+    def to_rest(i, _):
         chunk_copy(c_hbm, c_ref, in_sems, i).wait()
         chunk_products(w_ref, c_ref, i, 0, b0_ref, b1_ref)
         for t in range(size):
-            held_ref[i * size + t] = c_ref[i * size + t].T
-        return 0
-
-    def to_rest(i, _):
-        chunk_copy(c_hbm, c_ref, in_sems, held + i).wait()
-        chunk_products(w_ref, c_ref, held + i, 0, b0_ref, b1_ref)
-        for t in range(size):
-            t_ref[i * size + t] = c_ref[(held + i) * size + t].T
+            t_ref[i * size + t] = c_ref[i * size + t].T
         chunk_copy(t_ref, t_hbm, out_sems, i).start()
         return 0
 
+    def to_held(i, _):
+        chunk_copy(c_hbm, c_ref, in_sems, rest + i).wait()
+        chunk_products(w_ref, c_ref, rest + i, 0, b0_ref, b1_ref)
+        for t in range(size):
+            held_ref[i * size + t] = c_ref[(rest + i) * size + t].T
+        return 0
+
+    lax.fori_loop(0, rest, to_rest, 0)
     lax.fori_loop(0, held, to_held, 0)
-    lax.fori_loop(0, out_sems.shape[0], to_rest, 0)
-    for i in range(out_sems.shape[0]):
+    for i in range(rest):
         chunk_copy(t_ref, t_hbm, out_sems, i).wait()
 
 
@@ -302,10 +296,14 @@
     cap,
     kb,
     qb,
+    count_ref,
+    qslot_ref,
     asked_ref,
     hot_ref,
     mine_ref,
     share_ref,
+    gp8_ref,
+    sp8_ref,
     s8_ref,
     st4_ref,
     st8a_ref,
@@ -313,6 +311,20 @@
 ):
     hot = hot_ref[...]
     rows4, rows8 = hot.shape[0], s8_ref.shape[0]
+    q = qslot_ref[...]
+    tiles = q.shape[1]
+    used = iota((1, tiles), 1) < count_ref[0]
+    ind = lambda m: jnp.where(m, 1.0, 0.0)
+    x = iota((rows8, tiles), 0)
+    row_z = (q // cap) * (4 * cap) + q % cap
+    gp8_ref[...] = ind(x == row_z).T.astype(bf16)
+    sp8_ref[...] = jnp.concatenate(
+        [
+            jnp.where(used, ind(x == row_z + cap), 0.0),
+            jnp.where(used, ind(x == row_z + 2 * cap), 0.0),
+        ],
+        axis=1,
+    ).astype(bf16)
     x = iota((rows8, rows4), 0)
     y = iota((rows8, rows4), 1)
     peer, r = x // (4 * cap), x % (4 * cap)
@@ -366,8 +378,18 @@
     return gain + bose * (gain - (1.0 - far) * flat(b1_ref))
 
 
-def near_rows_kernel(same_ref, list_ref, part_ref):
+def fetch_copy(c_hbm, fetched_ref, sem):
+    count = fetched_ref.shape[0]
+    return pltpu.make_async_copy(
+        c_hbm.at[pl.ds(c_hbm.shape[0] - count, count)], fetched_ref, sem.at[0]
+    )
+
+
+def near_rows_kernel(same_ref, list_ref, c_hbm, part_ref, fetched_ref, sem):
+    copy = fetch_copy(c_hbm, fetched_ref, sem)
+    copy.start()
     part_ref[...] = add_rows(list_ref[...], same_ref[...])
+    copy.wait()
 
 
 def half_of_devices(cap, chips, weight, others, ref, share_ref):
@@ -384,10 +406,15 @@
     return heads + weight * sums[:rows4], sums[rows4:]
 
 
-def near_half_kernel(cap, chips, weight, same_ref, share_ref, part_ref, total_ref):
+def near_half_kernel(
+    cap, chips, weight, same_ref, share_ref, c_hbm, part_ref, total_ref, fetched_ref, sem
+):
+    copy = fetch_copy(c_hbm, fetched_ref, sem)
+    copy.start()
     part, total = half_of_devices(cap, chips, weight, 0, same_ref, share_ref)
     part_ref[...] = part
     total_ref[...] = total
+    copy.wait()
 
 
 def first_kernel(
@@ -406,6 +433,7 @@
     b0_ref,
     b1_ref,
     held_ref,
+    fetched_ref,
     c_hbm,
     send,
     e_ref,
@@ -443,7 +471,7 @@
     hot = jnp.where(lane.astype(f32) == col, 1.0, 0.0).astype(bf16)
     hot_ref[...] = hot
     base = n - DT * decay_ref[...] * (n - thermal_of(energy_ref))
-    parts = [(held_ref, None, None), (c_ref, c_hbm, sems)]
+    parts = forward_parts(w_ref, held_ref, fetched_ref, c_ref, c_hbm, sems)
     rate = electron_rate(sk_ref[...], far, bose, f, parts, w_ref, o0, o1)
     f1 = f + DT * rate
     e_ref[...] = rate
@@ -471,6 +499,7 @@
     b0_ref,
     b1_ref,
     held_ref,
+    fetched_ref,
     c_hbm,
     send,
     *refs,
@@ -487,7 +516,7 @@
     contributions = add_rows(sp_ref[...], terms)
     n = n_ref[...]
     own = own_ref[...]
-    parts = [(held_ref, None, None), (c_ref, c_hbm, sems)]
+    parts = forward_parts(w_ref, held_ref, fetched_ref, c_ref, c_hbm, sems)
     if ends:
         n2_ref, e2_ref, f3_ref = refs[:3]
         n2_ref[...] = n + (DT / 2.0) * total
@@ -565,7 +594,7 @@
     )
     n2 = n + (DT / 2.0) * (p_ref[...] + p1)
     n2_ref[...] = n2
-    parts = [(held_ref, None, None), (c_ref, c_hbm, sems)]
+    parts = forward_parts(w_ref, held_ref, None, c_ref, c_hbm, sems)
     rate = electron_rate(sk_ref[...], far_ref[...], bose, f1_ref[...], parts, w_ref, o0, o1)
     f2 = f_ref[...] + (DT / 2.0) * (e_ref[...] + rate)
     f2_ref[...] = f2
@@ -684,19 +713,17 @@
         phonon_need,
     )
     same = to_chips(send)
-    c_held, c_rest, pair, gp8, gk, sk, sp, sp4, sp8, near, far_picks, mine, b0, b1 = call(
+    c_held, c_rest, pair, gk, sk, sp, sp4, near, far_picks, mine, b0, b1 = call(
         functools.partial(prepare_kernel, cap),
         "prepare",
         [
             ((held, 128, 128), bf16),
             (rest, bf16),
             ((tiles, 2 * rows4), bf16),
-            ((tiles, rows8), bf16),
             ((tiles, kb), bf16),
             ((kb, tiles), bf16),
             ((slots, tiles), bf16),
             ((rows4, tiles), bf16),
-            ((rows8, 2 * tiles), bf16),
             ((rows4, chips * step_rows), bf16),
             ((rows4, chips * step_rows), bf16),
             ((rows4, 128), f32),
@@ -710,54 +737,74 @@
     same, c_held, b0 = lax.optimization_barrier((same, c_held, b0))
     wide_block = ((chips * wide, 128), f32)
     k_rows, q_rows = ((kb, 128), f32), ((qb, 128), f32)
-    forward_scratch = forward_streams + sums
+    width = tiles // CHUNKS
+    fetched = ((width, 128, 128), bf16)
+    fetch_sem = pltpu.SemaphoreType.DMA((1,))
+    short = (rest[0] - width, 128, 128)
+    short_sems = pltpu.SemaphoreType.DMA((CHUNKS - HELD_CHUNKS - 1,))
+    forward_scratch = [weights, pltpu.VMEM(short, bf16), short_sems] + sums
     other = between_cores(same)
-    (part,) = call(near_rows_kernel, "near_rows", [block4])(same, near)
+    part, c_fetched = call(
+        near_rows_kernel,
+        "near_rows",
+        [block4, fetched],
+        [fetch_sem],
+        spaces={2: pltpu.HBM},
+        out_spaces={1: pltpu.VMEM},
+    )(same, near, c_rest)
     send, e0, f1, serve, asked = call(
         functools.partial(first_kernel, cap),
         "first",
         [wide_block, k_rows, k_rows, ((rows4, 128), bf16), ((8 * devices, 128), bf16)],
         forward_scratch,
-        spaces={14: pltpu.HBM},
+        spaces={15: pltpu.HBM},
         **work,
-    )(same, other, part, far_picks, f, n, energy, decay, pair, sk, sp, b0, b1, c_held, c_rest)
-    share, s8, st4, st8a, st8b = call(
+    )(same, other, part, far_picks, f, n, energy, decay, pair, sk, sp, b0, b1, c_held, c_fetched, c_rest)
+    share, gp8, sp8, s8, st4, st8a, st8b = call(
         functools.partial(serve_kernel, cap, kb, qb),
         "serve",
         [
             ((rows4 + qb, devices * slots), bf16),
+            ((tiles, rows8), bf16),
+            ((rows8, 2 * tiles), bf16),
             ((rows8, 128), bf16),
             ((qb, rows4), bf16),
             ((qb, rows8), bf16),
             ((qb, rows8), bf16),
         ],
-    )(asked, serve, mine)
+        spaces={0: pltpu.SMEM},
+    )(tile_count, qslot, asked, serve, mine)
     back = call(backward_kernel, "backward", pass_out, streams, spaces={2: pltpu.HBM}, **work)
 
-    def middle(ends, send, outs, f, e, own, n, contributions):
+    def middle(ends, send, outs, f, e, own, n, contributions, share):
         same = to_chips(send)
         b0, b1 = back(own, gk, coupling)
-        same, b0 = lax.optimization_barrier((same, b0))
+        same, b0, share = lax.optimization_barrier((same, b0, share))
         other = between_cores(same)
         weight = DT / 2.0 if ends else DT
-        part, total = call(
-            functools.partial(near_half_kernel, cap, chips, weight), "near_half", [block4, q_rows]
-        )(same, share)
+        part, total, c_fetched = call(
+            functools.partial(near_half_kernel, cap, chips, weight),
+            "near_half",
+            [block4, q_rows, fetched],
+            [fetch_sem],
+            spaces={2: pltpu.HBM},
+            out_spaces={2: pltpu.VMEM},
+        )(same, share, c_rest)
         return call(
             functools.partial(middle_kernel, cap, ends),
             "middle",
             outs,
             forward_scratch,
-            spaces={17: pltpu.HBM},
+            spaces={18: pltpu.HBM},
             **work,
         )(
             part, total, other, share, serve, f, e, own, n, energy, decay,
-            pair, sk, contributions, b0, b1, c_held, c_rest,
+            pair, sk, contributions, b0, b1, c_held, c_fetched, c_rest,
         )
 
-    send, base, f2 = middle(False, send, [wide_block, q_rows, k_rows], f, e0, f1, n, sp)
+    send, base, f2 = middle(False, send, [wide_block, q_rows, k_rows], f, e0, f1, n, sp, share)
     send, n2, e2, f3 = middle(
-        True, send, [block4, q_rows, k_rows, k_rows], f2, e0, f2, base, sp4
+        True, send, [block4, q_rows, k_rows, k_rows], f2, e0, f2, base, sp4, share
     )
     recv = exchange(send)
     b0, b1 = back(f3, gk, coupling)

time: 76.6 us -> 76.6 us (level)
  waiting for transfers between devices: 7.74 us -> 4.79 us
  Pallas kernels: 36.2 us -> 39.1 us
    pallas_call x14, Pallas kernels: 36.2 us -> 39.1 us  [run(): pl.pallas_call(kernel, out_shape=[(out_spaces or {}).get(i, jax.ShapeDtyp...]
    ppermute x3, waiting for transfers between devices: 3.39 us -> 0.51 us  [between_cores(): return lax.ppermute(x, 'bulk', [(i, i ^ 1) for i in range(devices)])]
  transfers between devices with their start and end apart: 7 -> 7, of which waited for: 6 -> 6; matrix products, arithmetic and copies ran while one was open for 0% -> 0% of each run, Pallas kernels for 23% -> 28%
where the time goes in v17:
time: 76.6 us; the launch traced here: 75.8 us
  Pallas kernels  39.1 us (51%)
  starting transfers between devices  21.7 us (28%)
  blocking collectives  8.92 us (12%)
  waiting for transfers between devices  4.79 us (6%)
  between operations  1.41 us (2%)
    pallas_call x14, Pallas kernels, run(): pl.pallas_call(kernel, out_shape=[(out_spaces or {}).get(i, jax.ShapeDtyp...  39.1 us
    all_to_all x3, starting transfers between devices, to_chips(): lax.all_to_all(x, 'bulk', split_axis=0, concat_axis=0, tiled=True, axis_i...  17.3 us
    all_to_all x1, blocking collectives, exchange(): lax.all_to_all(x, 'bulk', split_axis=0, concat_axis=0, tiled=True, axis_i...  8.92 us
    all_to_all x1, starting transfers between devices, exchange(): lax.all_to_all(x, 'bulk', split_axis=0, concat_axis=0, tiled=True, axis_i...  4.26 us
    all_to_all x3, waiting for transfers between devices, to_chips(): lax.all_to_all(x, 'bulk', split_axis=0, concat_axis=0, tiled=True, axis_i...  3.66 us
  transfers between devices with their start and end apart: 7, of which 6 were waited for; matrix products, arithmetic and copies ran while one was open for 0% of the time, Pallas kernels for 28%

profile of v17, /device:TPU:0, one launch (start us, length us, event | category | flops | bytes accessed | tf_op | source)
XLA Modules:
  0.0 75.8 jit_solution(18383175930330370009)
XLA Ops:
  0.6 1.6 %need.1 = (f32[32,128]{1,0:T(8,128)S(1)}, f32[16,128]{1,0:T(8,128)S(1)}, f32[16,128]{1,0:T(8,128)S(1)}, f32[16,128]{1,0:T(8,128)S(1)}, s32[1,256]{1,0:T(1,128)S(...) custom-call(f32[32,128]{1,0:T(8,128)} %refs_0_.1, ...), custom_call_target="tpu_custom_call" | custom-call | tf_op jit(solution)/shard_map/need/pallas_call | solution.py:615
  2.2 7.9 %all-to-all-start = ((f32[8,56,128]{2,1,0:T(8,128)}), f32[8,56,128]{2,1,0:T(8,128)S(1)}, u32[]{:S(2)}, u32[]{:S(2)}) async-start(f32[8,56,128]{2,1,0:T(8,128)} %bitcast.3), calls=%async_computation | async-start | bytes 458752 | tf_op jit(solution)/shard_map/all_to_all | solution.py:691
  10.7 6.1 %prepare.1 = (bf16[64,128,128]{2,1,0:T(8,128)(2,1)S(1)}, bf16[192,128,128]{2,1,0:T(8,128)(2,1)}, bf16[256,128]{1,0:T(8,128)(2,1)S(1)}, bf16[256,32]{1,0:T(8,128)...) custom-call(s32[1]{0:T(128)S(6)} %copy.13.count_ref, ...), custom_call_target="tpu_custom_call" | custom-call | flops 134217728 | bytes 8388608 | tf_op jit(solution)/shard_map/prepare/pallas_call | solution.py:615
  16.9 0.0 all-to-all-done
  16.9 0.1 collective-permute-start
  16.9 1.2 %near_rows.1 = (f32[64,128]{1,0:T(8,128)S(1)}, bf16[32,128,128]{2,1,0:T(8,128)(2,1)S(1)}) custom-call(f32[448,128]{1,0:T(8,128)S(1)} %bitcast.14, bf16[64,448]{1,0:T(8,128)(2,1)S(1)} %get-tuple-element.80.list_ref, bf16[192,128,128]{2,1,0:T(8,128)(2,1)} %get-tuple-element.81.c_hbm.refs_14_), custom_call_target="tpu_custom_call" | custom-call | tf_op jit(solution)/shard_map/near_rows/pallas_call | solution.py:615
  18.2 0.2 collective-permute-done.other_ref
  18.4 4.0 %first.1 = (f32[320,128]{1,0:T(8,128)}, f32[32,128]{1,0:T(8,128)S(1)}, f32[32,128]{1,0:T(8,128)S(1)}, bf16[64,128]{1,0:T(8,128)(2,1)S(1)}, bf16[128,128]{1,0:T(8,128)(2,1)S(1)}) custom-call(f32[448,128]{1,0:T(8,128)S(1)} %bitcast.15, f32[448,128]{1,0:T(8,128)S(1)} %collective-permute-done.other_ref, f32[64,128]{1,0:T(8,128)S(1)} %get-tuple-element.82.part_ref, ...), custom_call_target="tpu_custom_call" | custom-call | flops 134217728 | bytes 8388608 | tf_op jit(solution)/shard_map/first/pallas_call | solution.py:615
  22.5 5.1 %all-to-all-start.1 = ((f32[8,40,128]{2,1,0:T(8,128)}), f32[8,40,128]{2,1,0:T(8,128)S(1)}, u32[]{:S(2)}, u32[]{:S(2)}) async-start(f32[8,40,128]{2,1,0:T(8,128)} %bitcast.5), calls=%async_computation.1 | async-start | bytes 327680 | tf_op jit(solution)/shard_map/all_to_all | solution.py:691
  27.6 0.3 serve.1
  27.9 3.7 %backward.3 = (f32[32,8,128]{2,1,0:T(8,128)S(1)}, f32[32,8,128]{2,1,0:T(8,128)S(1)}) custom-call(f32[32,128]{1,0:T(8,128)S(1)} %get-tuple-element.95.f_ref.own_ref, bf16[256,32]{1,0:T(8,128)(2,1)S(1)} %get-tuple-element.96.gk_ref, bf16[256,128,128]{2,1,0:T(8,128)(2,1)} %c_hbm.7), custom_call_target="tpu_custom_call" | custom-call | flops 134217728 | bytes 8388608 | tf_op jit(solution)/shard_map/backward/pallas_call | solution.py:615
  31.7 1.5 %all-to-all-done.1 = f32[8,40,128]{2,1,0:T(8,128)S(1)} async-done(((f32[8,40,128]{2,1,0:T(8,128)}), f32[8,40,128]{2,1,0:T(8,128)S(1)}, u32[]{:S(2)}, u32[]{:S(2)}) %all-to-all-start.1) | async-done | bytes 163872 | tf_op jit(solution)/shard_map/all_to_all | solution.py:691
  33.1 0.0 collective-permute-start.1
  33.1 1.2 %near_half.2 = (f32[64,128]{1,0:T(8,128)S(1)}, f32[16,128]{1,0:T(8,128)S(1)}, bf16[32,128,128]{2,1,0:T(8,128)(2,1)S(1)}) custom-call(f32[320,128]{1,0:T(8,128)S(1)} %bitcast.17, bf16[80,512]{1,0:T(8,128)(2,1)S(1)} %get-tuple-element.114.share_ref, bf16[192,128,128]{2,1,0:T(8,128)(2,1)} %get-tuple-element.81.c_hbm.refs_14_), custom_call_target="tpu_custom_call" | custom-call | tf_op jit(solution)/shard_map/near_half/pallas_call | solution.py:615
  34.4 0.1 collective-permute-done.1.other_ref
  34.5 4.0 %middle.2 = (f32[320,128]{1,0:T(8,128)}, f32[16,128]{1,0:T(8,128)S(1)}, f32[32,128]{1,0:T(8,128)S(1)}) custom-call(f32[64,128]{1,0:T(8,128)S(1)} %get-tuple-element.104.part_ref, f32[16,128]{1,0:T(8,128)S(1)} %get-tuple-element.105.total_ref, f32[320,128]{1,0:T(8,128)S(1)} %collective-permute-done.1.other_ref, ...), custom_call_target="tpu_custom_call" | custom-call | flops 134217728 | bytes 8388608 | tf_op jit(solution)/shard_map/middle/pallas_call | solution.py:615
  38.5 4.4 %all-to-all-start.2 = ((f32[8,40,128]{2,1,0:T(8,128)}), f32[8,40,128]{2,1,0:T(8,128)S(1)}, u32[]{:S(2)}, u32[]{:S(2)}) async-start(f32[8,40,128]{2,1,0:T(8,128)} %bitcast.7), calls=%async_computation.2 | async-start | bytes 327680 | tf_op jit(solution)/shard_map/all_to_all | solution.py:691
  42.9 3.7 %backward.4 = (f32[32,8,128]{2,1,0:T(8,128)S(1)}, f32[32,8,128]{2,1,0:T(8,128)S(1)}) custom-call(f32[32,128]{1,0:T(8,128)S(1)} %get-tuple-element.111.f_ref.own_ref.refs_1_, bf16[256,32]{1,0:T(8,128)(2,1)S(1)} %get-tuple-element.96.gk_ref, bf16[256,128,128]{2,1,0:T(8,128)(2,1)} %c_hbm.7), custom_call_target="tpu_custom_call" | custom-call | flops 134217728 | bytes 8388608 | tf_op jit(solution)/shard_map/backward/pallas_call | solution.py:615
  46.6 2.2 %all-to-all-done.2 = f32[8,40,128]{2,1,0:T(8,128)S(1)} async-done(((f32[8,40,128]{2,1,0:T(8,128)}), f32[8,40,128]{2,1,0:T(8,128)S(1)}, u32[]{:S(2)}, u32[]{:S(2)}) %all-to-all-start.2) | async-done | bytes 163872 | tf_op jit(solution)/shard_map/all_to_all | solution.py:691
  48.8 0.0 collective-permute-start.2
  48.8 1.2 %near_half.3 = (f32[64,128]{1,0:T(8,128)S(1)}, f32[16,128]{1,0:T(8,128)S(1)}, bf16[32,128,128]{2,1,0:T(8,128)(2,1)S(1)}) custom-call(f32[320,128]{1,0:T(8,128)S(1)} %bitcast.19, bf16[80,512]{1,0:T(8,128)(2,1)S(1)} %get-tuple-element.114.share_ref, bf16[192,128,128]{2,1,0:T(8,128)(2,1)} %get-tuple-element.81.c_hbm.refs_14_), custom_call_target="tpu_custom_call" | custom-call | tf_op jit(solution)/shard_map/near_half/pallas_call | solution.py:615
  50.1 0.1 collective-permute-done.2.other_ref
  50.2 3.8 %middle.3 = (f32[64,128]{1,0:T(8,128)}, f32[16,128]{1,0:T(8,128)S(1)}, f32[32,128]{1,0:T(8,128)S(1)}, f32[32,128]{1,0:T(8,128)S(1)}) custom-call(f32[64,128]{1,0:T(8,128)S(1)} %get-tuple-element.115.part_ref, f32[16,128]{1,0:T(8,128)S(1)} %get-tuple-element.116.total_ref, f32[320,128]{1,0:T(8,128)S(1)} %collective-permute-done.2.other_ref, ...), custom_call_target="tpu_custom_call" | custom-call | flops 134217728 | bytes 8388608 | tf_op jit(solution)/shard_map/middle/pallas_call | solution.py:615
  54.0 4.3 %all-to-all-start.3 = ((f32[16,4,128]{2,1,0:T(4,128)}), f32[16,4,128]{2,1,0:T(4,128)S(1)}, u32[]{:S(2)}, u32[]{:S(2)}) async-start(f32[16,4,128]{2,1,0:T(4,128)} %bitcast.9), calls=%async_computation.3 | async-start | bytes 65536 | tf_op jit(solution)/shard_map/all_to_all | solution.py:673
  58.3 3.7 %backward.5 = (f32[32,8,128]{2,1,0:T(8,128)S(1)}, f32[32,8,128]{2,1,0:T(8,128)S(1)}) custom-call(f32[32,128]{1,0:T(8,128)S(1)} %get-tuple-element.127.f_ref.refs_2_, bf16[256,32]{1,0:T(8,128)(2,1)S(1)} %get-tuple-element.96.gk_ref, bf16[256,128,128]{2,1,0:T(8,128)(2,1)} %c_hbm.7), custom_call_target="tpu_custom_call" | custom-call | flops 134217728 | bytes 8388608 | tf_op jit(solution)/shard_map/backward/pallas_call | solution.py:615
  62.0 0.6 all-to-all-done.3
  62.6 0.4 phonon.1
  63.0 8.9 %all_to_all.58 = f32[16,8,128]{2,1,0:T(8,128)S(1)} all-to-all(f32[16,8,128]{2,1,0:T(8,128)S(1)} %bitcast.22), channel_id=1, replica_groups={{8,9,10,11,12,13,14,15,0,1,2,3,4,5,6,7},{24,25,26,27,28,29,30,31,16,17,..., dimensions={0} | all-to-all | bytes 131072 | tf_op jit(solution)/shard_map/all_to_all | solution.py:673
  71.9 3.9 %last.1 = (f32[32,128]{1,0:T(8,128)}, f32[16,128]{1,0:T(8,128)}) custom-call(f32[128,128]{1,0:T(8,128)S(1)} %bitcast.20, f32[256,128]{1,0:T(8,128)S(1)} %get-tuple-element.131.refs_0_, f32[32,128]{1,0:T(8,128)S(1)} %get-tuple-element.111.f_ref.own_ref.refs_1_, f32[32,128]{1,0:T(8,128)S(1)} %get-tuple-element.127.f_ref.refs_2_, ...), custom_call_target="tpu_custom_call" | custom-call | flops 134217728 | bytes 8388608 | tf_op jit(solution)/shard_map/last/pallas_call | solution.py:615
Async XLA Ops:
  2.2 14.6 %all-to-all-start = ((f32[8,56,128]{2,1,0:T(8,128)}), f32[8,56,128]{2,1,0:T(8,128)S(1)}, u32[]{:S(2)}, u32[]{:S(2)}) async-start(f32[8,56,128]{2,1,0:T(8,128)} %bitcast.3), calls=%async_computation | async-start | bytes 458752 | tf_op jit(solution)/shard_map/all_to_all | solution.py:691
  16.9 1.6 %collective-permute-start = (f32[448,128]{1,0:T(8,128)S(1)}, f32[448,128]{1,0:T(8,128)S(1)}, u32[]{:S(2)}, u32[]{:S(2)}) collective-permute-start(f32[448,128]{1,0:T(8,128)S(1)} %bitcast.13), channel_id=1, source_target_pairs={{0,1},{1,0},{2,3},{3,2},{4,5},{5,4},{6,7},{7,6},{8,9},{9,8},{10,11... | collective-permute-start | bytes 688136 | tf_op jit(solution)/shard_map/ppermute | solution.py:696
  22.5 10.7 %all-to-all-start.1 = ((f32[8,40,128]{2,1,0:T(8,128)}), f32[8,40,128]{2,1,0:T(8,128)S(1)}, u32[]{:S(2)}, u32[]{:S(2)}) async-start(f32[8,40,128]{2,1,0:T(8,128)} %bitcast.5), calls=%async_computation.1 | async-start | bytes 327680 | tf_op jit(solution)/shard_map/all_to_all | solution.py:691
  33.1 1.4 %collective-permute-start.1 = (f32[320,128]{1,0:T(8,128)S(1)}, f32[320,128]{1,0:T(8,128)S(1)}, u32[]{:S(2)}, u32[]{:S(2)}) collective-permute-start(f32[320,128]{1,0:T(8,128)S(1)} %bitcast.16), channel_id=1, source_target_pairs={{0,1},{1,0},{2,3},{3,2},{4,5},{5,4},{6,7},{7,6},{8,9},{9,8},{10,11... | collective-permute-start | bytes 491528 | tf_op jit(solution)/shard_map/ppermute | solution.py:696
  38.5 10.3 %all-to-all-start.2 = ((f32[8,40,128]{2,1,0:T(8,128)}), f32[8,40,128]{2,1,0:T(8,128)S(1)}, u32[]{:S(2)}, u32[]{:S(2)}) async-start(f32[8,40,128]{2,1,0:T(8,128)} %bitcast.7), calls=%async_computation.2 | async-start | bytes 327680 | tf_op jit(solution)/shard_map/all_to_all | solution.py:691
  48.8 1.4 %collective-permute-start.2 = (f32[320,128]{1,0:T(8,128)S(1)}, f32[320,128]{1,0:T(8,128)S(1)}, u32[]{:S(2)}, u32[]{:S(2)}) collective-permute-start(f32[320,128]{1,0:T(8,128)S(1)} %bitcast.18), channel_id=1, source_target_pairs={{0,1},{1,0},{2,3},{3,2},{4,5},{5,4},{6,7},{7,6},{8,9},{9,8},{10,11... | collective-permute-start | bytes 491528 | tf_op jit(solution)/shard_map/ppermute | solution.py:696
  54.0 8.6 %all-to-all-start.3 = ((f32[16,4,128]{2,1,0:T(4,128)}), f32[16,4,128]{2,1,0:T(4,128)S(1)}, u32[]{:S(2)}, u32[]{:S(2)}) async-start(f32[16,4,128]{2,1,0:T(4,128)} %bitcast.9), calls=%async_computation.3 | async-start | bytes 65536 | tf_op jit(solution)/shard_map/all_to_all | solution.py:673

commit v18 on v17

--- a/solution.py
+++ b/solution.py
@@ -128,11 +128,10 @@
 
 
 def forward_parts(w_ref, held_ref, fetched_ref, c_ref, c_hbm, sems):
-    first = w_ref.shape[0] - held_ref.shape[0] // 8
-    parts = [(held_ref, None, None, first)]
+    parts = [(held_ref, None, None, 0)]
     if fetched_ref is not None:
-        parts.append((fetched_ref, None, None, first - fetched_ref.shape[0] // 8))
-    return parts + [(c_ref, c_hbm, sems, 0)]
+        parts.append((fetched_ref, None, None, w_ref.shape[0] - fetched_ref.shape[0] // 8))
+    return parts + [(c_ref, c_hbm, sems, held_ref.shape[0] // 8)]
 
 
 def electron_rate(sum_k, far, bose, f, parts, w_ref, o0, o1):
@@ -265,23 +264,23 @@
 
     rest = CHUNKS - held
 
-    def to_rest(i, _):
+    def to_held(i, _):
         chunk_copy(c_hbm, c_ref, in_sems, i).wait()
         chunk_products(w_ref, c_ref, i, 0, b0_ref, b1_ref)
         for t in range(size):
-            t_ref[i * size + t] = c_ref[i * size + t].T
+            held_ref[i * size + t] = c_ref[i * size + t].T
+        return 0
+
+    def to_rest(i, _):
+        chunk_copy(c_hbm, c_ref, in_sems, held + i).wait()
+        chunk_products(w_ref, c_ref, held + i, 0, b0_ref, b1_ref)
+        for t in range(size):
+            t_ref[i * size + t] = c_ref[(held + i) * size + t].T
         chunk_copy(t_ref, t_hbm, out_sems, i).start()
         return 0
 
-    def to_held(i, _):
-        chunk_copy(c_hbm, c_ref, in_sems, rest + i).wait()
-        chunk_products(w_ref, c_ref, rest + i, 0, b0_ref, b1_ref)
-        for t in range(size):
-            held_ref[i * size + t] = c_ref[(rest + i) * size + t].T
-        return 0
-
+    lax.fori_loop(0, held, to_held, 0)
     lax.fori_loop(0, rest, to_rest, 0)
-    lax.fori_loop(0, held, to_held, 0)
     for i in range(rest):
         chunk_copy(t_ref, t_hbm, out_sems, i).wait()
 

time: 76.6 us -> 76 us (level)
  transfers between devices with their start and end apart: 7 -> 7, of which waited for: 6 -> 6; matrix products, arithmetic and copies ran while one was open for 0% -> 0% of each run, Pallas kernels for 28% -> 27%
where the time goes in v18:
time: 76 us; the launch traced here: 75.3 us
  Pallas kernels  38.4 us (51%)
  starting transfers between devices  21.7 us (29%)
  blocking collectives  8.92 us (12%)
  waiting for transfers between devices  4.93 us (6%)
  between operations  1.41 us (2%)
    pallas_call x14, Pallas kernels, run(): pl.pallas_call(kernel, out_shape=[(out_spaces or {}).get(i, jax.ShapeDtyp...  38.4 us
    all_to_all x3, starting transfers between devices, to_chips(): lax.all_to_all(x, 'bulk', split_axis=0, concat_axis=0, tiled=True, axis_i...  17.3 us
    all_to_all x1, blocking collectives, exchange(): lax.all_to_all(x, 'bulk', split_axis=0, concat_axis=0, tiled=True, axis_i...  8.92 us
    all_to_all x1, starting transfers between devices, exchange(): lax.all_to_all(x, 'bulk', split_axis=0, concat_axis=0, tiled=True, axis_i...  4.26 us
    all_to_all x3, waiting for transfers between devices, to_chips(): lax.all_to_all(x, 'bulk', split_axis=0, concat_axis=0, tiled=True, axis_i...  3.8 us
  transfers between devices with their start and end apart: 7, of which 6 were waited for; matrix products, arithmetic and copies ran while one was open for 0% of the time, Pallas kernels for 27%

profile of v18, /device:TPU:0, one launch (start us, length us, event | category | flops | bytes accessed | tf_op | source)
XLA Modules:
  0.0 75.3 jit_solution(10920394561181694250)
XLA Ops:
  0.6 1.6 %need.1 = (f32[32,128]{1,0:T(8,128)S(1)}, f32[16,128]{1,0:T(8,128)S(1)}, f32[16,128]{1,0:T(8,128)S(1)}, f32[16,128]{1,0:T(8,128)S(1)}, s32[1,256]{1,0:T(1,128)S(...) custom-call(f32[32,128]{1,0:T(8,128)} %refs_0_.1, ...), custom_call_target="tpu_custom_call" | custom-call | tf_op jit(solution)/shard_map/need/pallas_call | solution.py:614
  2.2 7.9 %all-to-all-start = ((f32[8,56,128]{2,1,0:T(8,128)}), f32[8,56,128]{2,1,0:T(8,128)S(1)}, u32[]{:S(2)}, u32[]{:S(2)}) async-start(f32[8,56,128]{2,1,0:T(8,128)} %bitcast.3), calls=%async_computation | async-start | bytes 458752 | tf_op jit(solution)/shard_map/all_to_all | solution.py:690
  10.7 5.5 %prepare.1 = (bf16[64,128,128]{2,1,0:T(8,128)(2,1)S(1)}, bf16[192,128,128]{2,1,0:T(8,128)(2,1)}, bf16[256,128]{1,0:T(8,128)(2,1)S(1)}, bf16[256,32]{1,0:T(8,128)...) custom-call(s32[1]{0:T(128)S(6)} %copy.13.count_ref, ...), custom_call_target="tpu_custom_call" | custom-call | flops 134217728 | bytes 8388608 | tf_op jit(solution)/shard_map/prepare/pallas_call | solution.py:614
  16.2 0.0 all-to-all-done
  16.2 0.1 collective-permute-start
  16.3 1.2 %near_rows.1 = (f32[64,128]{1,0:T(8,128)S(1)}, bf16[32,128,128]{2,1,0:T(8,128)(2,1)S(1)}) custom-call(f32[448,128]{1,0:T(8,128)S(1)} %bitcast.14, bf16[64,448]{1,0:T(8,128)(2,1)S(1)} %get-tuple-element.80.list_ref, bf16[192,128,128]{2,1,0:T(8,128)(2,1)} %get-tuple-element.81.c_hbm.refs_14_), custom_call_target="tpu_custom_call" | custom-call | tf_op jit(solution)/shard_map/near_rows/pallas_call | solution.py:614
  17.5 0.2 collective-permute-done.other_ref
  17.8 4.0 %first.1 = (f32[320,128]{1,0:T(8,128)}, f32[32,128]{1,0:T(8,128)S(1)}, f32[32,128]{1,0:T(8,128)S(1)}, bf16[64,128]{1,0:T(8,128)(2,1)S(1)}, bf16[128,128]{1,0:T(8,128)(2,1)S(1)}) custom-call(f32[448,128]{1,0:T(8,128)S(1)} %bitcast.15, f32[448,128]{1,0:T(8,128)S(1)} %collective-permute-done.other_ref, f32[64,128]{1,0:T(8,128)S(1)} %get-tuple-element.82.part_ref, ...), custom_call_target="tpu_custom_call" | custom-call | flops 134217728 | bytes 8388608 | tf_op jit(solution)/shard_map/first/pallas_call | solution.py:614
  21.8 5.1 %all-to-all-start.1 = ((f32[8,40,128]{2,1,0:T(8,128)}), f32[8,40,128]{2,1,0:T(8,128)S(1)}, u32[]{:S(2)}, u32[]{:S(2)}) async-start(f32[8,40,128]{2,1,0:T(8,128)} %bitcast.5), calls=%async_computation.1 | async-start | bytes 327680 | tf_op jit(solution)/shard_map/all_to_all | solution.py:690
  26.9 0.3 serve.1
  27.3 3.7 %backward.3 = (f32[32,8,128]{2,1,0:T(8,128)S(1)}, f32[32,8,128]{2,1,0:T(8,128)S(1)}) custom-call(f32[32,128]{1,0:T(8,128)S(1)} %get-tuple-element.95.f_ref.own_ref, bf16[256,32]{1,0:T(8,128)(2,1)S(1)} %get-tuple-element.96.gk_ref, bf16[256,128,128]{2,1,0:T(8,128)(2,1)} %c_hbm.7), custom_call_target="tpu_custom_call" | custom-call | flops 134217728 | bytes 8388608 | tf_op jit(solution)/shard_map/backward/pallas_call | solution.py:614
  31.0 1.6 %all-to-all-done.1 = f32[8,40,128]{2,1,0:T(8,128)S(1)} async-done(((f32[8,40,128]{2,1,0:T(8,128)}), f32[8,40,128]{2,1,0:T(8,128)S(1)}, u32[]{:S(2)}, u32[]{:S(2)}) %all-to-all-start.1) | async-done | bytes 163872 | tf_op jit(solution)/shard_map/all_to_all | solution.py:690
  32.6 0.0 collective-permute-start.1
  32.6 1.2 %near_half.2 = (f32[64,128]{1,0:T(8,128)S(1)}, f32[16,128]{1,0:T(8,128)S(1)}, bf16[32,128,128]{2,1,0:T(8,128)(2,1)S(1)}) custom-call(f32[320,128]{1,0:T(8,128)S(1)} %bitcast.17, bf16[80,512]{1,0:T(8,128)(2,1)S(1)} %get-tuple-element.114.share_ref, bf16[192,128,128]{2,1,0:T(8,128)(2,1)} %get-tuple-element.81.c_hbm.refs_14_), custom_call_target="tpu_custom_call" | custom-call | tf_op jit(solution)/shard_map/near_half/pallas_call | solution.py:614
  33.9 0.1 collective-permute-done.1.other_ref
  34.0 4.0 %middle.2 = (f32[320,128]{1,0:T(8,128)}, f32[16,128]{1,0:T(8,128)S(1)}, f32[32,128]{1,0:T(8,128)S(1)}) custom-call(f32[64,128]{1,0:T(8,128)S(1)} %get-tuple-element.104.part_ref, f32[16,128]{1,0:T(8,128)S(1)} %get-tuple-element.105.total_ref, f32[320,128]{1,0:T(8,128)S(1)} %collective-permute-done.1.other_ref, ...), custom_call_target="tpu_custom_call" | custom-call | flops 134217728 | bytes 8388608 | tf_op jit(solution)/shard_map/middle/pallas_call | solution.py:614
  38.0 4.4 %all-to-all-start.2 = ((f32[8,40,128]{2,1,0:T(8,128)}), f32[8,40,128]{2,1,0:T(8,128)S(1)}, u32[]{:S(2)}, u32[]{:S(2)}) async-start(f32[8,40,128]{2,1,0:T(8,128)} %bitcast.7), calls=%async_computation.2 | async-start | bytes 327680 | tf_op jit(solution)/shard_map/all_to_all | solution.py:690
  42.4 3.7 %backward.4 = (f32[32,8,128]{2,1,0:T(8,128)S(1)}, f32[32,8,128]{2,1,0:T(8,128)S(1)}) custom-call(f32[32,128]{1,0:T(8,128)S(1)} %get-tuple-element.111.f_ref.own_ref.refs_1_, bf16[256,32]{1,0:T(8,128)(2,1)S(1)} %get-tuple-element.96.gk_ref, bf16[256,128,128]{2,1,0:T(8,128)(2,1)} %c_hbm.7), custom_call_target="tpu_custom_call" | custom-call | flops 134217728 | bytes 8388608 | tf_op jit(solution)/shard_map/backward/pallas_call | solution.py:614
  46.1 2.2 %all-to-all-done.2 = f32[8,40,128]{2,1,0:T(8,128)S(1)} async-done(((f32[8,40,128]{2,1,0:T(8,128)}), f32[8,40,128]{2,1,0:T(8,128)S(1)}, u32[]{:S(2)}, u32[]{:S(2)}) %all-to-all-start.2) | async-done | bytes 163872 | tf_op jit(solution)/shard_map/all_to_all | solution.py:690
  48.3 0.0 collective-permute-start.2
  48.3 1.2 %near_half.3 = (f32[64,128]{1,0:T(8,128)S(1)}, f32[16,128]{1,0:T(8,128)S(1)}, bf16[32,128,128]{2,1,0:T(8,128)(2,1)S(1)}) custom-call(f32[320,128]{1,0:T(8,128)S(1)} %bitcast.19, bf16[80,512]{1,0:T(8,128)(2,1)S(1)} %get-tuple-element.114.share_ref, bf16[192,128,128]{2,1,0:T(8,128)(2,1)} %get-tuple-element.81.c_hbm.refs_14_), custom_call_target="tpu_custom_call" | custom-call | tf_op jit(solution)/shard_map/near_half/pallas_call | solution.py:614
  49.5 0.1 collective-permute-done.2.other_ref
  49.7 3.8 %middle.3 = (f32[64,128]{1,0:T(8,128)}, f32[16,128]{1,0:T(8,128)S(1)}, f32[32,128]{1,0:T(8,128)S(1)}, f32[32,128]{1,0:T(8,128)S(1)}) custom-call(f32[64,128]{1,0:T(8,128)S(1)} %get-tuple-element.115.part_ref, f32[16,128]{1,0:T(8,128)S(1)} %get-tuple-element.116.total_ref, f32[320,128]{1,0:T(8,128)S(1)} %collective-permute-done.2.other_ref, ...), custom_call_target="tpu_custom_call" | custom-call | flops 134217728 | bytes 8388608 | tf_op jit(solution)/shard_map/middle/pallas_call | solution.py:614
  53.5 4.3 %all-to-all-start.3 = ((f32[16,4,128]{2,1,0:T(4,128)}), f32[16,4,128]{2,1,0:T(4,128)S(1)}, u32[]{:S(2)}, u32[]{:S(2)}) async-start(f32[16,4,128]{2,1,0:T(4,128)} %bitcast.9), calls=%async_computation.3 | async-start | bytes 65536 | tf_op jit(solution)/shard_map/all_to_all | solution.py:672
  57.8 3.7 %backward.5 = (f32[32,8,128]{2,1,0:T(8,128)S(1)}, f32[32,8,128]{2,1,0:T(8,128)S(1)}) custom-call(f32[32,128]{1,0:T(8,128)S(1)} %get-tuple-element.127.f_ref.refs_2_, bf16[256,32]{1,0:T(8,128)(2,1)S(1)} %get-tuple-element.96.gk_ref, bf16[256,128,128]{2,1,0:T(8,128)(2,1)} %c_hbm.7), custom_call_target="tpu_custom_call" | custom-call | flops 134217728 | bytes 8388608 | tf_op jit(solution)/shard_map/backward/pallas_call | solution.py:614
  61.5 0.6 all-to-all-done.3
  62.1 0.4 phonon.1
  62.5 8.9 %all_to_all.58 = f32[16,8,128]{2,1,0:T(8,128)S(1)} all-to-all(f32[16,8,128]{2,1,0:T(8,128)S(1)} %bitcast.22), channel_id=1, replica_groups={{8,9,10,11,12,13,14,15,0,1,2,3,4,5,6,7},{24,25,26,27,28,29,30,31,16,17,..., dimensions={0} | all-to-all | bytes 131072 | tf_op jit(solution)/shard_map/all_to_all | solution.py:672
  71.4 3.9 %last.1 = (f32[32,128]{1,0:T(8,128)}, f32[16,128]{1,0:T(8,128)}) custom-call(f32[128,128]{1,0:T(8,128)S(1)} %bitcast.20, f32[256,128]{1,0:T(8,128)S(1)} %get-tuple-element.131.refs_0_, f32[32,128]{1,0:T(8,128)S(1)} %get-tuple-element.111.f_ref.own_ref.refs_1_, f32[32,128]{1,0:T(8,128)S(1)} %get-tuple-element.127.f_ref.refs_2_, ...), custom_call_target="tpu_custom_call" | custom-call | flops 134217728 | bytes 8388608 | tf_op jit(solution)/shard_map/last/pallas_call | solution.py:614
Async XLA Ops:
  2.2 14.0 %all-to-all-start = ((f32[8,56,128]{2,1,0:T(8,128)}), f32[8,56,128]{2,1,0:T(8,128)S(1)}, u32[]{:S(2)}, u32[]{:S(2)}) async-start(f32[8,56,128]{2,1,0:T(8,128)} %bitcast.3), calls=%async_computation | async-start | bytes 458752 | tf_op jit(solution)/shard_map/all_to_all | solution.py:690
  16.2 1.6 %collective-permute-start = (f32[448,128]{1,0:T(8,128)S(1)}, f32[448,128]{1,0:T(8,128)S(1)}, u32[]{:S(2)}, u32[]{:S(2)}) collective-permute-start(f32[448,128]{1,0:T(8,128)S(1)} %bitcast.13), channel_id=1, source_target_pairs={{0,1},{1,0},{2,3},{3,2},{4,5},{5,4},{6,7},{7,6},{8,9},{9,8},{10,11... | collective-permute-start | bytes 688136 | tf_op jit(solution)/shard_map/ppermute | solution.py:695
  21.8 10.8 %all-to-all-start.1 = ((f32[8,40,128]{2,1,0:T(8,128)}), f32[8,40,128]{2,1,0:T(8,128)S(1)}, u32[]{:S(2)}, u32[]{:S(2)}) async-start(f32[8,40,128]{2,1,0:T(8,128)} %bitcast.5), calls=%async_computation.1 | async-start | bytes 327680 | tf_op jit(solution)/shard_map/all_to_all | solution.py:690
  32.6 1.4 %collective-permute-start.1 = (f32[320,128]{1,0:T(8,128)S(1)}, f32[320,128]{1,0:T(8,128)S(1)}, u32[]{:S(2)}, u32[]{:S(2)}) collective-permute-start(f32[320,128]{1,0:T(8,128)S(1)} %bitcast.16), channel_id=1, source_target_pairs={{0,1},{1,0},{2,3},{3,2},{4,5},{5,4},{6,7},{7,6},{8,9},{9,8},{10,11... | collective-permute-start | bytes 491528 | tf_op jit(solution)/shard_map/ppermute | solution.py:695
  38.0 10.3 %all-to-all-start.2 = ((f32[8,40,128]{2,1,0:T(8,128)}), f32[8,40,128]{2,1,0:T(8,128)S(1)}, u32[]{:S(2)}, u32[]{:S(2)}) async-start(f32[8,40,128]{2,1,0:T(8,128)} %bitcast.7), calls=%async_computation.2 | async-start | bytes 327680 | tf_op jit(solution)/shard_map/all_to_all | solution.py:690
  48.3 1.4 %collective-permute-start.2 = (f32[320,128]{1,0:T(8,128)S(1)}, f32[320,128]{1,0:T(8,128)S(1)}, u32[]{:S(2)}, u32[]{:S(2)}) collective-permute-start(f32[320,128]{1,0:T(8,128)S(1)} %bitcast.18), channel_id=1, source_target_pairs={{0,1},{1,0},{2,3},{3,2},{4,5},{5,4},{6,7},{7,6},{8,9},{9,8},{10,11... | collective-permute-start | bytes 491528 | tf_op jit(solution)/shard_map/ppermute | solution.py:695
  53.5 8.6 %all-to-all-start.3 = ((f32[16,4,128]{2,1,0:T(4,128)}), f32[16,4,128]{2,1,0:T(4,128)S(1)}, u32[]{:S(2)}, u32[]{:S(2)}) async-start(f32[16,4,128]{2,1,0:T(4,128)} %bitcast.9), calls=%async_computation.3 | async-start | bytes 65536 | tf_op jit(solution)/shard_map/all_to_all | solution.py:672

commit v19 on v18

--- a/solution.py
+++ b/solution.py
@@ -149,13 +149,15 @@
     return lax.rem(lax.axis_index("bulk"), 2)
 
 
-def place_of(chip, chips):
-    return (chip + chips - chips // 2) % chips
+def place_of(chip, chips, core):
+    up = (chip + chips // 2) % chips
+    down = (chips // 2 - 1 - chip + chips) % chips
+    return jnp.where(core == 0, up, down)
 
 
 def block_of(peer, peers):
     chips = peers // 2
-    return place_of(peer // 2, chips) + jnp.where(peer % 2 == my_core(), 0, chips)
+    return place_of(peer // 2, chips, peer % 2) + jnp.where(peer % 2 == my_core(), 0, chips)
 
 
 def to_wire(rows, send):
@@ -367,9 +369,9 @@
     slots = contributions.shape[0]
     chips = served.shape[0] // 8
     for chip in range(chips):
-        at = place_of(chip, chips) * (8 + slots)
-        send[at : at + 8] = served[chip * 8 : chip * 8 + 8]
-        send[at + 8 : at + 8 + slots] = contributions
+        at = pl.multiple_of(place_of(chip, chips, my_core()) * (8 + slots), 8)
+        send[pl.ds(at, 8)] = served[chip * 8 : chip * 8 + 8]
+        send[chip * (8 + slots) + 8 : (chip + 1) * (8 + slots)] = contributions
 
 
 def phonon_terms(far, bose, b0_ref, b1_ref):
@@ -396,7 +398,7 @@
     wide = share_ref.shape[1] // 2
     x = iota((rows4, 8 * chips), 0)
     peer = x // (2 * cap)
-    source = 8 * place_of(peer // 2, chips) + 2 * cap * my_core() + x % (2 * cap)
+    source = 8 * place_of(peer // 2, chips, peer % 2) + 2 * cap * my_core() + x % (2 * cap)
     wanted_core = (my_core() + others) % 2
     at = (iota((rows4, 8 * chips), 1) == source) & (peer % 2 == wanted_core)
     heads = add_rows(jnp.where(at, 1.0, 0.0).astype(bf16), blocks(ref, chips, 0, 8))
@@ -683,7 +685,8 @@
     assert devices % 2 == 0 and cap == 2
     chips = devices // 2
     same_core = [
-        [(i + chips // 2) % chips * 2 + core for i in range(chips)] for core in (0, 1)
+        [(i + chips // 2) % chips * 2 for i in range(chips)],
+        [(chips // 2 - 1 - i) % chips * 2 + 1 for i in range(chips)],
     ]
 
     def to_chips(x):

time: 76 us -> 76.3 us (level)
  transfers between devices with their start and end apart: 7 -> 7, of which waited for: 6 -> 7; matrix products, arithmetic and copies ran while one was open for 0% -> 0% of each run, Pallas kernels for 27% -> 27%
where the time goes in v19:
time: 76.3 us; the launch traced here: 75.6 us
  Pallas kernels  38.6 us (51%)
  starting transfers between devices  21.1 us (28%)
  blocking collectives  8.93 us (12%)
  waiting for transfers between devices  5.52 us (7%)
  between operations  1.39 us (2%)
    pallas_call x14, Pallas kernels, run(): pl.pallas_call(kernel, out_shape=[(out_spaces or {}).get(i, jax.ShapeDtyp...  38.6 us
    all_to_all x3, starting transfers between devices, to_chips(): lax.all_to_all(x, 'bulk', split_axis=0, concat_axis=0, tiled=True, axis_i...  16.8 us
    all_to_all x1, blocking collectives, exchange(): lax.all_to_all(x, 'bulk', split_axis=0, concat_axis=0, tiled=True, axis_i...  8.93 us
    all_to_all x3, waiting for transfers between devices, to_chips(): lax.all_to_all(x, 'bulk', split_axis=0, concat_axis=0, tiled=True, axis_i...  4.48 us
    all_to_all x1, starting transfers between devices, exchange(): lax.all_to_all(x, 'bulk', split_axis=0, concat_axis=0, tiled=True, axis_i...  4.26 us
  transfers between devices with their start and end apart: 7, of which 7 were waited for; matrix products, arithmetic and copies ran while one was open for 0% of the time, Pallas kernels for 27%

profile of v19, /device:TPU:0, one launch (start us, length us, event | category | flops | bytes accessed | tf_op | source)
XLA Modules:
  0.0 75.6 jit_solution(6894179711843317443)
XLA Ops:
  0.6 1.6 %need.1 = (f32[32,128]{1,0:T(8,128)S(1)}, f32[16,128]{1,0:T(8,128)S(1)}, f32[16,128]{1,0:T(8,128)S(1)}, f32[16,128]{1,0:T(8,128)S(1)}, s32[1,256]{1,0:T(1,128)S(...) custom-call(f32[32,128]{1,0:T(8,128)} %refs_0_.1, ...), custom_call_target="tpu_custom_call" | custom-call | tf_op jit(solution)/shard_map/need/pallas_call | solution.py:616
  2.2 7.9 %all-to-all-start = ((f32[8,56,128]{2,1,0:T(8,128)}), f32[8,56,128]{2,1,0:T(8,128)S(1)}, u32[]{:S(2)}, u32[]{:S(2)}) async-start(f32[8,56,128]{2,1,0:T(8,128)} %bitcast.3), calls=%async_computation | async-start | bytes 458752 | tf_op jit(solution)/shard_map/all_to_all | solution.py:693
  10.7 5.5 %prepare.1 = (bf16[64,128,128]{2,1,0:T(8,128)(2,1)S(1)}, bf16[192,128,128]{2,1,0:T(8,128)(2,1)}, bf16[256,128]{1,0:T(8,128)(2,1)S(1)}, bf16[256,32]{1,0:T(8,128)...) custom-call(s32[1]{0:T(128)S(6)} %copy.13.count_ref, ...), custom_call_target="tpu_custom_call" | custom-call | flops 134217728 | bytes 8388608 | tf_op jit(solution)/shard_map/prepare/pallas_call | solution.py:616
  16.2 0.5 all-to-all-done
  16.7 0.1 collective-permute-start
  16.8 1.2 %near_rows.1 = (f32[64,128]{1,0:T(8,128)S(1)}, bf16[32,128,128]{2,1,0:T(8,128)(2,1)S(1)}) custom-call(f32[448,128]{1,0:T(8,128)S(1)} %bitcast.14, bf16[64,448]{1,0:T(8,128)(2,1)S(1)} %get-tuple-element.80.list_ref, bf16[192,128,128]{2,1,0:T(8,128)(2,1)} %get-tuple-element.81.c_hbm.refs_14_), custom_call_target="tpu_custom_call" | custom-call | tf_op jit(solution)/shard_map/near_rows/pallas_call | solution.py:616
  18.0 0.1 collective-permute-done.other_ref
  18.2 4.2 %first.1 = (f32[320,128]{1,0:T(8,128)}, f32[32,128]{1,0:T(8,128)S(1)}, f32[32,128]{1,0:T(8,128)S(1)}, bf16[64,128]{1,0:T(8,128)(2,1)S(1)}, bf16[128,128]{1,0:T(8,128)(2,1)S(1)}) custom-call(f32[448,128]{1,0:T(8,128)S(1)} %bitcast.15, f32[448,128]{1,0:T(8,128)S(1)} %collective-permute-done.other_ref, f32[64,128]{1,0:T(8,128)S(1)} %get-tuple-element.82.part_ref, ...), custom_call_target="tpu_custom_call" | custom-call | flops 134217728 | bytes 8388608 | tf_op jit(solution)/shard_map/first/pallas_call | solution.py:616
  22.4 4.7 %all-to-all-start.1 = ((f32[8,40,128]{2,1,0:T(8,128)}), f32[8,40,128]{2,1,0:T(8,128)S(1)}, u32[]{:S(2)}, u32[]{:S(2)}) async-start(f32[8,40,128]{2,1,0:T(8,128)} %bitcast.5), calls=%async_computation.1 | async-start | bytes 327680 | tf_op jit(solution)/shard_map/all_to_all | solution.py:693
  27.1 0.3 serve.1
  27.4 3.7 %backward.3 = (f32[32,8,128]{2,1,0:T(8,128)S(1)}, f32[32,8,128]{2,1,0:T(8,128)S(1)}) custom-call(f32[32,128]{1,0:T(8,128)S(1)} %get-tuple-element.95.f_ref.own_ref, bf16[256,32]{1,0:T(8,128)(2,1)S(1)} %get-tuple-element.96.gk_ref, bf16[256,128,128]{2,1,0:T(8,128)(2,1)} %c_hbm.7), custom_call_target="tpu_custom_call" | custom-call | flops 134217728 | bytes 8388608 | tf_op jit(solution)/shard_map/backward/pallas_call | solution.py:616
  31.2 1.4 %all-to-all-done.1 = f32[8,40,128]{2,1,0:T(8,128)S(1)} async-done(((f32[8,40,128]{2,1,0:T(8,128)}), f32[8,40,128]{2,1,0:T(8,128)S(1)}, u32[]{:S(2)}, u32[]{:S(2)}) %all-to-all-start.1) | async-done | bytes 163872 | tf_op jit(solution)/shard_map/all_to_all | solution.py:693
  32.6 0.0 collective-permute-start.1
  32.6 1.2 %near_half.2 = (f32[64,128]{1,0:T(8,128)S(1)}, f32[16,128]{1,0:T(8,128)S(1)}, bf16[32,128,128]{2,1,0:T(8,128)(2,1)S(1)}) custom-call(f32[320,128]{1,0:T(8,128)S(1)} %bitcast.17, bf16[80,512]{1,0:T(8,128)(2,1)S(1)} %get-tuple-element.114.share_ref, bf16[192,128,128]{2,1,0:T(8,128)(2,1)} %get-tuple-element.81.c_hbm.refs_14_), custom_call_target="tpu_custom_call" | custom-call | tf_op jit(solution)/shard_map/near_half/pallas_call | solution.py:616
  33.9 0.1 collective-permute-done.1.other_ref
  34.0 4.0 %middle.2 = (f32[320,128]{1,0:T(8,128)}, f32[16,128]{1,0:T(8,128)S(1)}, f32[32,128]{1,0:T(8,128)S(1)}) custom-call(f32[64,128]{1,0:T(8,128)S(1)} %get-tuple-element.104.part_ref, f32[16,128]{1,0:T(8,128)S(1)} %get-tuple-element.105.total_ref, f32[320,128]{1,0:T(8,128)S(1)} %collective-permute-done.1.other_ref, ...), custom_call_target="tpu_custom_call" | custom-call | flops 134217728 | bytes 8388608 | tf_op jit(solution)/shard_map/middle/pallas_call | solution.py:616
  38.0 4.2 %all-to-all-start.2 = ((f32[8,40,128]{2,1,0:T(8,128)}), f32[8,40,128]{2,1,0:T(8,128)S(1)}, u32[]{:S(2)}, u32[]{:S(2)}) async-start(f32[8,40,128]{2,1,0:T(8,128)} %bitcast.7), calls=%async_computation.2 | async-start | bytes 327680 | tf_op jit(solution)/shard_map/all_to_all | solution.py:693
  42.2 3.7 %backward.4 = (f32[32,8,128]{2,1,0:T(8,128)S(1)}, f32[32,8,128]{2,1,0:T(8,128)S(1)}) custom-call(f32[32,128]{1,0:T(8,128)S(1)} %get-tuple-element.111.f_ref.own_ref.refs_1_, bf16[256,32]{1,0:T(8,128)(2,1)S(1)} %get-tuple-element.96.gk_ref, bf16[256,128,128]{2,1,0:T(8,128)(2,1)} %c_hbm.7), custom_call_target="tpu_custom_call" | custom-call | flops 134217728 | bytes 8388608 | tf_op jit(solution)/shard_map/backward/pallas_call | solution.py:616
  45.9 2.6 %all-to-all-done.2 = f32[8,40,128]{2,1,0:T(8,128)S(1)} async-done(((f32[8,40,128]{2,1,0:T(8,128)}), f32[8,40,128]{2,1,0:T(8,128)S(1)}, u32[]{:S(2)}, u32[]{:S(2)}) %all-to-all-start.2) | async-done | bytes 163872 | tf_op jit(solution)/shard_map/all_to_all | solution.py:693
  48.5 0.0 collective-permute-start.2
  48.5 1.2 %near_half.3 = (f32[64,128]{1,0:T(8,128)S(1)}, f32[16,128]{1,0:T(8,128)S(1)}, bf16[32,128,128]{2,1,0:T(8,128)(2,1)S(1)}) custom-call(f32[320,128]{1,0:T(8,128)S(1)} %bitcast.19, bf16[80,512]{1,0:T(8,128)(2,1)S(1)} %get-tuple-element.114.share_ref, bf16[192,128,128]{2,1,0:T(8,128)(2,1)} %get-tuple-element.81.c_hbm.refs_14_), custom_call_target="tpu_custom_call" | custom-call | tf_op jit(solution)/shard_map/near_half/pallas_call | solution.py:616
  49.8 0.1 collective-permute-done.2.other_ref
  49.9 3.8 %middle.3 = (f32[64,128]{1,0:T(8,128)}, f32[16,128]{1,0:T(8,128)S(1)}, f32[32,128]{1,0:T(8,128)S(1)}, f32[32,128]{1,0:T(8,128)S(1)}) custom-call(f32[64,128]{1,0:T(8,128)S(1)} %get-tuple-element.115.part_ref, f32[16,128]{1,0:T(8,128)S(1)} %get-tuple-element.116.total_ref, f32[320,128]{1,0:T(8,128)S(1)} %collective-permute-done.2.other_ref, ...), custom_call_target="tpu_custom_call" | custom-call | flops 134217728 | bytes 8388608 | tf_op jit(solution)/shard_map/middle/pallas_call | solution.py:616
  53.7 4.3 %all-to-all-start.3 = ((f32[16,4,128]{2,1,0:T(4,128)}), f32[16,4,128]{2,1,0:T(4,128)S(1)}, u32[]{:S(2)}, u32[]{:S(2)}) async-start(f32[16,4,128]{2,1,0:T(4,128)} %bitcast.9), calls=%async_computation.3 | async-start | bytes 65536 | tf_op jit(solution)/shard_map/all_to_all | solution.py:674
  58.0 3.7 %backward.5 = (f32[32,8,128]{2,1,0:T(8,128)S(1)}, f32[32,8,128]{2,1,0:T(8,128)S(1)}) custom-call(f32[32,128]{1,0:T(8,128)S(1)} %get-tuple-element.127.f_ref.refs_2_, bf16[256,32]{1,0:T(8,128)(2,1)S(1)} %get-tuple-element.96.gk_ref, bf16[256,128,128]{2,1,0:T(8,128)(2,1)} %c_hbm.7), custom_call_target="tpu_custom_call" | custom-call | flops 134217728 | bytes 8388608 | tf_op jit(solution)/shard_map/backward/pallas_call | solution.py:616
  61.7 0.6 all-to-all-done.3
  62.4 0.4 phonon.1
  62.7 8.9 %all_to_all.58 = f32[16,8,128]{2,1,0:T(8,128)S(1)} all-to-all(f32[16,8,128]{2,1,0:T(8,128)S(1)} %bitcast.22), channel_id=1, replica_groups={{8,9,10,11,12,13,14,15,0,1,2,3,4,5,6,7},{24,25,26,27,28,29,30,31,16,17,..., dimensions={0} | all-to-all | bytes 131072 | tf_op jit(solution)/shard_map/all_to_all | solution.py:674
  71.7 3.9 %last.1 = (f32[32,128]{1,0:T(8,128)}, f32[16,128]{1,0:T(8,128)}) custom-call(f32[128,128]{1,0:T(8,128)S(1)} %bitcast.20, f32[256,128]{1,0:T(8,128)S(1)} %get-tuple-element.131.refs_0_, f32[32,128]{1,0:T(8,128)S(1)} %get-tuple-element.111.f_ref.own_ref.refs_1_, f32[32,128]{1,0:T(8,128)S(1)} %get-tuple-element.127.f_ref.refs_2_, ...), custom_call_target="tpu_custom_call" | custom-call | flops 134217728 | bytes 8388608 | tf_op jit(solution)/shard_map/last/pallas_call | solution.py:616
Async XLA Ops:
  2.2 14.5 %all-to-all-start = ((f32[8,56,128]{2,1,0:T(8,128)}), f32[8,56,128]{2,1,0:T(8,128)S(1)}, u32[]{:S(2)}, u32[]{:S(2)}) async-start(f32[8,56,128]{2,1,0:T(8,128)} %bitcast.3), calls=%async_computation | async-start | bytes 458752 | tf_op jit(solution)/shard_map/all_to_all | solution.py:693
  16.7 1.5 %collective-permute-start = (f32[448,128]{1,0:T(8,128)S(1)}, f32[448,128]{1,0:T(8,128)S(1)}, u32[]{:S(2)}, u32[]{:S(2)}) collective-permute-start(f32[448,128]{1,0:T(8,128)S(1)} %bitcast.13), channel_id=1, source_target_pairs={{0,1},{1,0},{2,3},{3,2},{4,5},{5,4},{6,7},{7,6},{8,9},{9,8},{10,11... | collective-permute-start | bytes 688136 | tf_op jit(solution)/shard_map/ppermute | solution.py:698
  22.4 10.2 %all-to-all-start.1 = ((f32[8,40,128]{2,1,0:T(8,128)}), f32[8,40,128]{2,1,0:T(8,128)S(1)}, u32[]{:S(2)}, u32[]{:S(2)}) async-start(f32[8,40,128]{2,1,0:T(8,128)} %bitcast.5), calls=%async_computation.1 | async-start | bytes 327680 | tf_op jit(solution)/shard_map/all_to_all | solution.py:693
  32.6 1.4 %collective-permute-start.1 = (f32[320,128]{1,0:T(8,128)S(1)}, f32[320,128]{1,0:T(8,128)S(1)}, u32[]{:S(2)}, u32[]{:S(2)}) collective-permute-start(f32[320,128]{1,0:T(8,128)S(1)} %bitcast.16), channel_id=1, source_target_pairs={{0,1},{1,0},{2,3},{3,2},{4,5},{5,4},{6,7},{7,6},{8,9},{9,8},{10,11... | collective-permute-start | bytes 491528 | tf_op jit(solution)/shard_map/ppermute | solution.py:698
  38.0 10.5 %all-to-all-start.2 = ((f32[8,40,128]{2,1,0:T(8,128)}), f32[8,40,128]{2,1,0:T(8,128)S(1)}, u32[]{:S(2)}, u32[]{:S(2)}) async-start(f32[8,40,128]{2,1,0:T(8,128)} %bitcast.7), calls=%async_computation.2 | async-start | bytes 327680 | tf_op jit(solution)/shard_map/all_to_all | solution.py:693
  48.5 1.4 %collective-permute-start.2 = (f32[320,128]{1,0:T(8,128)S(1)}, f32[320,128]{1,0:T(8,128)S(1)}, u32[]{:S(2)}, u32[]{:S(2)}) collective-permute-start(f32[320,128]{1,0:T(8,128)S(1)} %bitcast.18), channel_id=1, source_target_pairs={{0,1},{1,0},{2,3},{3,2},{4,5},{5,4},{6,7},{7,6},{8,9},{9,8},{10,11... | collective-permute-start | bytes 491528 | tf_op jit(solution)/shard_map/ppermute | solution.py:698
  53.7 8.6 %all-to-all-start.3 = ((f32[16,4,128]{2,1,0:T(4,128)}), f32[16,4,128]{2,1,0:T(4,128)S(1)}, u32[]{:S(2)}, u32[]{:S(2)}) async-start(f32[16,4,128]{2,1,0:T(4,128)} %bitcast.9), calls=%async_computation.3 | async-start | bytes 65536 | tf_op jit(solution)/shard_map/all_to_all | solution.py:674

commit v20 on v18

--- a/solution.py
+++ b/solution.py
@@ -53,7 +53,7 @@
 
 
 def row_is(r):
-    return iota((16, 128), 0) % 8 == r
+    return iota((32, 128), 0) % 8 == r
 
 
 def padded(*parts):
@@ -89,27 +89,30 @@
 
 
 def left_sides(first, second, w_ref):
-    groups = w_ref.shape[0]
-    w_ref[:, :, :128] = stacked(first, second)
+    pairs = w_ref.shape[0]
+    w_ref[:, :, :128] = stacked(first, second).reshape(pairs, 32, 128)
 
     def spread(g, _):
         w_ref[g] = block_diagonal(w_ref[g, :, :128])
         return 0
 
-    lax.fori_loop(0, groups, spread, 0, unroll=4)
+    lax.fori_loop(0, pairs, spread, 0, unroll=2)
 
 
 def chunk_products(w_ref, c_ref, i, base, out0, out1):
-    size = w_ref.shape[0] // CHUNKS
-    for k in range(size):
+    size = out0.shape[0] // CHUNKS
+    for k in range(0, size, 2):
         g = i * size + k
-        res = dot(w_ref[base + g], c_ref[pl.ds(g * 8, 8)].reshape(1024, 128))
-        out0[base + g] = res[:8]
-        out1[base + g] = res[8:]
+        tiles = [c_ref[pl.ds((g + j) * 8, 8)].reshape(1024, 128) for j in (0, 1)]
+        res = dot(w_ref[(base + g) // 2], jnp.concatenate(tiles, axis=1))
+        for j in (0, 1):
+            own = res[16 * j : 16 * (j + 1), 128 * j : 128 * (j + 1)]
+            out0[base + g + j] = own[:8]
+            out1[base + g + j] = own[8:]
 
 
 def tile_products(w_ref, parts, out0, out1):
-    size = w_ref.shape[0] // CHUNKS
+    size = out0.shape[0] // CHUNKS
     for c_ref, c_hbm, sems, base in parts:
         chunks = c_ref.shape[0] // 8 // size
 
@@ -130,7 +133,7 @@
 def forward_parts(w_ref, held_ref, fetched_ref, c_ref, c_hbm, sems):
     parts = [(held_ref, None, None, 0)]
     if fetched_ref is not None:
-        parts.append((fetched_ref, None, None, w_ref.shape[0] - fetched_ref.shape[0] // 8))
+        parts.append((fetched_ref, None, None, 2 * w_ref.shape[0] - fetched_ref.shape[0] // 8))
     return parts + [(c_ref, c_hbm, sems, held_ref.shape[0] // 8)]
 
 
@@ -655,7 +658,7 @@
     rows8 = devices * 4 * cap
     groups = tiles // 8
     held = HELD_CHUNKS * (tiles // CHUNKS)
-    weights = pltpu.VMEM((groups, 16, 1024), bf16)
+    weights = pltpu.VMEM((groups // 2, 32, 1024), bf16)
     streams = [weights, pltpu.VMEM(coupling.shape, bf16), pltpu.SemaphoreType.DMA((CHUNKS,))]
     rest = (tiles - held, 128, 128)
     rest_sems = pltpu.SemaphoreType.DMA((CHUNKS - HELD_CHUNKS,))

time: 76 us -> 76.2 us (level)
  transfers between devices with their start and end apart: 7 -> 7, of which waited for: 6 -> 7; matrix products, arithmetic and copies ran while one was open for 0% -> 0% of each run, Pallas kernels for 27% -> 27%
where the time goes in v20:
time: 76.2 us; the launch traced here: 75.5 us
  Pallas kernels  38.5 us (51%)
  starting transfers between devices  21.6 us (28%)
  blocking collectives  8.96 us (12%)
  waiting for transfers between devices  5.13 us (7%)
  between operations  1.39 us (2%)
    pallas_call x14, Pallas kernels, run(): pl.pallas_call(kernel, out_shape=[(out_spaces or {}).get(i, jax.ShapeDtyp...  38.5 us
    all_to_all x3, starting transfers between devices, to_chips(): lax.all_to_all(x, 'bulk', split_axis=0, concat_axis=0, tiled=True, axis_i...  17.3 us
    all_to_all x1, blocking collectives, exchange(): lax.all_to_all(x, 'bulk', split_axis=0, concat_axis=0, tiled=True, axis_i...  8.96 us
    all_to_all x1, starting transfers between devices, exchange(): lax.all_to_all(x, 'bulk', split_axis=0, concat_axis=0, tiled=True, axis_i...  4.27 us
    all_to_all x3, waiting for transfers between devices, to_chips(): lax.all_to_all(x, 'bulk', split_axis=0, concat_axis=0, tiled=True, axis_i...  4.01 us
  transfers between devices with their start and end apart: 7, of which 7 were waited for; matrix products, arithmetic and copies ran while one was open for 0% of the time, Pallas kernels for 27%

profile of v20, /device:TPU:0, one launch (start us, length us, event | category | flops | bytes accessed | tf_op | source)
XLA Modules:
  0.0 75.5 jit_solution(1552260111240215263)
XLA Ops:
  0.6 1.6 %need.1 = (f32[32,128]{1,0:T(8,128)S(1)}, f32[16,128]{1,0:T(8,128)S(1)}, f32[16,128]{1,0:T(8,128)S(1)}, f32[16,128]{1,0:T(8,128)S(1)}, s32[1,256]{1,0:T(1,128)S(...) custom-call(f32[32,128]{1,0:T(8,128)} %refs_0_.1, ...), custom_call_target="tpu_custom_call" | custom-call | tf_op jit(solution)/shard_map/need/pallas_call | solution.py:617
  2.2 7.9 %all-to-all-start = ((f32[8,56,128]{2,1,0:T(8,128)}), f32[8,56,128]{2,1,0:T(8,128)S(1)}, u32[]{:S(2)}, u32[]{:S(2)}) async-start(f32[8,56,128]{2,1,0:T(8,128)} %bitcast.3), calls=%async_computation | async-start | bytes 458752 | tf_op jit(solution)/shard_map/all_to_all | solution.py:693
  10.7 5.3 %prepare.1 = (bf16[64,128,128]{2,1,0:T(8,128)(2,1)S(1)}, bf16[192,128,128]{2,1,0:T(8,128)(2,1)}, bf16[256,128]{1,0:T(8,128)(2,1)S(1)}, bf16[256,32]{1,0:T(8,128)...) custom-call(s32[1]{0:T(128)S(6)} %copy.13.count_ref, ...), custom_call_target="tpu_custom_call" | custom-call | flops 134217728 | bytes 8388608 | tf_op jit(solution)/shard_map/prepare/pallas_call | solution.py:617
  16.0 0.1 all-to-all-done
  16.1 0.0 collective-permute-start
  16.1 1.2 %near_rows.1 = (f32[64,128]{1,0:T(8,128)S(1)}, bf16[32,128,128]{2,1,0:T(8,128)(2,1)S(1)}) custom-call(f32[448,128]{1,0:T(8,128)S(1)} %bitcast.14, bf16[64,448]{1,0:T(8,128)(2,1)S(1)} %get-tuple-element.80.list_ref, bf16[192,128,128]{2,1,0:T(8,128)(2,1)} %get-tuple-element.81.c_hbm.refs_14_), custom_call_target="tpu_custom_call" | custom-call | tf_op jit(solution)/shard_map/near_rows/pallas_call | solution.py:617
  17.4 0.2 collective-permute-done.other_ref
  17.6 4.0 %first.1 = (f32[320,128]{1,0:T(8,128)}, f32[32,128]{1,0:T(8,128)S(1)}, f32[32,128]{1,0:T(8,128)S(1)}, bf16[64,128]{1,0:T(8,128)(2,1)S(1)}, bf16[128,128]{1,0:T(8,128)(2,1)S(1)}) custom-call(f32[448,128]{1,0:T(8,128)S(1)} %bitcast.15, f32[448,128]{1,0:T(8,128)S(1)} %collective-permute-done.other_ref, f32[64,128]{1,0:T(8,128)S(1)} %get-tuple-element.82.part_ref, ...), custom_call_target="tpu_custom_call" | custom-call | flops 134217728 | bytes 8388608 | tf_op jit(solution)/shard_map/first/pallas_call | solution.py:617
  21.7 5.1 %all-to-all-start.1 = ((f32[8,40,128]{2,1,0:T(8,128)}), f32[8,40,128]{2,1,0:T(8,128)S(1)}, u32[]{:S(2)}, u32[]{:S(2)}) async-start(f32[8,40,128]{2,1,0:T(8,128)} %bitcast.5), calls=%async_computation.1 | async-start | bytes 327680 | tf_op jit(solution)/shard_map/all_to_all | solution.py:693
  26.8 0.3 serve.1
  27.1 3.8 %backward.3 = (f32[32,8,128]{2,1,0:T(8,128)S(1)}, f32[32,8,128]{2,1,0:T(8,128)S(1)}) custom-call(f32[32,128]{1,0:T(8,128)S(1)} %get-tuple-element.95.f_ref.own_ref, bf16[256,32]{1,0:T(8,128)(2,1)S(1)} %get-tuple-element.96.gk_ref, bf16[256,128,128]{2,1,0:T(8,128)(2,1)} %c_hbm.7), custom_call_target="tpu_custom_call" | custom-call | flops 134217728 | bytes 8388608 | tf_op jit(solution)/shard_map/backward/pallas_call | solution.py:617
  30.9 1.7 %all-to-all-done.1 = f32[8,40,128]{2,1,0:T(8,128)S(1)} async-done(((f32[8,40,128]{2,1,0:T(8,128)}), f32[8,40,128]{2,1,0:T(8,128)S(1)}, u32[]{:S(2)}, u32[]{:S(2)}) %all-to-all-start.1) | async-done | bytes 163872 | tf_op jit(solution)/shard_map/all_to_all | solution.py:693
  32.6 0.0 collective-permute-start.1
  32.6 1.2 %near_half.2 = (f32[64,128]{1,0:T(8,128)S(1)}, f32[16,128]{1,0:T(8,128)S(1)}, bf16[32,128,128]{2,1,0:T(8,128)(2,1)S(1)}) custom-call(f32[320,128]{1,0:T(8,128)S(1)} %bitcast.17, bf16[80,512]{1,0:T(8,128)(2,1)S(1)} %get-tuple-element.114.share_ref, bf16[192,128,128]{2,1,0:T(8,128)(2,1)} %get-tuple-element.81.c_hbm.refs_14_), custom_call_target="tpu_custom_call" | custom-call | tf_op jit(solution)/shard_map/near_half/pallas_call | solution.py:617
  33.9 0.1 collective-permute-done.1.other_ref
  34.0 4.0 %middle.2 = (f32[320,128]{1,0:T(8,128)}, f32[16,128]{1,0:T(8,128)S(1)}, f32[32,128]{1,0:T(8,128)S(1)}) custom-call(f32[64,128]{1,0:T(8,128)S(1)} %get-tuple-element.104.part_ref, f32[16,128]{1,0:T(8,128)S(1)} %get-tuple-element.105.total_ref, f32[320,128]{1,0:T(8,128)S(1)} %collective-permute-done.1.other_ref, ...), custom_call_target="tpu_custom_call" | custom-call | flops 134217728 | bytes 8388608 | tf_op jit(solution)/shard_map/middle/pallas_call | solution.py:617
  38.0 4.3 %all-to-all-start.2 = ((f32[8,40,128]{2,1,0:T(8,128)}), f32[8,40,128]{2,1,0:T(8,128)S(1)}, u32[]{:S(2)}, u32[]{:S(2)}) async-start(f32[8,40,128]{2,1,0:T(8,128)} %bitcast.7), calls=%async_computation.2 | async-start | bytes 327680 | tf_op jit(solution)/shard_map/all_to_all | solution.py:693
  42.4 3.8 %backward.4 = (f32[32,8,128]{2,1,0:T(8,128)S(1)}, f32[32,8,128]{2,1,0:T(8,128)S(1)}) custom-call(f32[32,128]{1,0:T(8,128)S(1)} %get-tuple-element.111.f_ref.own_ref.refs_1_, bf16[256,32]{1,0:T(8,128)(2,1)S(1)} %get-tuple-element.96.gk_ref, bf16[256,128,128]{2,1,0:T(8,128)(2,1)} %c_hbm.7), custom_call_target="tpu_custom_call" | custom-call | flops 134217728 | bytes 8388608 | tf_op jit(solution)/shard_map/backward/pallas_call | solution.py:617
  46.2 2.1 %all-to-all-done.2 = f32[8,40,128]{2,1,0:T(8,128)S(1)} async-done(((f32[8,40,128]{2,1,0:T(8,128)}), f32[8,40,128]{2,1,0:T(8,128)S(1)}, u32[]{:S(2)}, u32[]{:S(2)}) %all-to-all-start.2) | async-done | bytes 163872 | tf_op jit(solution)/shard_map/all_to_all | solution.py:693
  48.3 0.0 collective-permute-start.2
  48.3 1.2 %near_half.3 = (f32[64,128]{1,0:T(8,128)S(1)}, f32[16,128]{1,0:T(8,128)S(1)}, bf16[32,128,128]{2,1,0:T(8,128)(2,1)S(1)}) custom-call(f32[320,128]{1,0:T(8,128)S(1)} %bitcast.19, bf16[80,512]{1,0:T(8,128)(2,1)S(1)} %get-tuple-element.114.share_ref, bf16[192,128,128]{2,1,0:T(8,128)(2,1)} %get-tuple-element.81.c_hbm.refs_14_), custom_call_target="tpu_custom_call" | custom-call | tf_op jit(solution)/shard_map/near_half/pallas_call | solution.py:617
  49.6 0.1 collective-permute-done.2.other_ref
  49.7 3.9 %middle.3 = (f32[64,128]{1,0:T(8,128)}, f32[16,128]{1,0:T(8,128)S(1)}, f32[32,128]{1,0:T(8,128)S(1)}, f32[32,128]{1,0:T(8,128)S(1)}) custom-call(f32[64,128]{1,0:T(8,128)S(1)} %get-tuple-element.115.part_ref, f32[16,128]{1,0:T(8,128)S(1)} %get-tuple-element.116.total_ref, f32[320,128]{1,0:T(8,128)S(1)} %collective-permute-done.2.other_ref, ...), custom_call_target="tpu_custom_call" | custom-call | flops 134217728 | bytes 8388608 | tf_op jit(solution)/shard_map/middle/pallas_call | solution.py:617
  53.6 4.3 %all-to-all-start.3 = ((f32[16,4,128]{2,1,0:T(4,128)}), f32[16,4,128]{2,1,0:T(4,128)S(1)}, u32[]{:S(2)}, u32[]{:S(2)}) async-start(f32[16,4,128]{2,1,0:T(4,128)} %bitcast.9), calls=%async_computation.3 | async-start | bytes 65536 | tf_op jit(solution)/shard_map/all_to_all | solution.py:675
  57.9 3.8 %backward.5 = (f32[32,8,128]{2,1,0:T(8,128)S(1)}, f32[32,8,128]{2,1,0:T(8,128)S(1)}) custom-call(f32[32,128]{1,0:T(8,128)S(1)} %get-tuple-element.127.f_ref.refs_2_, bf16[256,32]{1,0:T(8,128)(2,1)S(1)} %get-tuple-element.96.gk_ref, bf16[256,128,128]{2,1,0:T(8,128)(2,1)} %c_hbm.7), custom_call_target="tpu_custom_call" | custom-call | flops 134217728 | bytes 8388608 | tf_op jit(solution)/shard_map/backward/pallas_call | solution.py:617
  61.6 0.6 all-to-all-done.3
  62.2 0.4 phonon.1
  62.6 9.0 %all_to_all.58 = f32[16,8,128]{2,1,0:T(8,128)S(1)} all-to-all(f32[16,8,128]{2,1,0:T(8,128)S(1)} %bitcast.22), channel_id=1, replica_groups={{8,9,10,11,12,13,14,15,0,1,2,3,4,5,6,7},{24,25,26,27,28,29,30,31,16,17,..., dimensions={0} | all-to-all | bytes 131072 | tf_op jit(solution)/shard_map/all_to_all | solution.py:675
  71.6 3.9 %last.1 = (f32[32,128]{1,0:T(8,128)}, f32[16,128]{1,0:T(8,128)}) custom-call(f32[128,128]{1,0:T(8,128)S(1)} %bitcast.20, f32[256,128]{1,0:T(8,128)S(1)} %get-tuple-element.131.refs_0_, f32[32,128]{1,0:T(8,128)S(1)} %get-tuple-element.111.f_ref.own_ref.refs_1_, f32[32,128]{1,0:T(8,128)S(1)} %get-tuple-element.127.f_ref.refs_2_, ...), custom_call_target="tpu_custom_call" | custom-call | flops 134217728 | bytes 8388608 | tf_op jit(solution)/shard_map/last/pallas_call | solution.py:617
Async XLA Ops:
  2.2 13.9 %all-to-all-start = ((f32[8,56,128]{2,1,0:T(8,128)}), f32[8,56,128]{2,1,0:T(8,128)S(1)}, u32[]{:S(2)}, u32[]{:S(2)}) async-start(f32[8,56,128]{2,1,0:T(8,128)} %bitcast.3), calls=%async_computation | async-start | bytes 458752 | tf_op jit(solution)/shard_map/all_to_all | solution.py:693
  16.1 1.5 %collective-permute-start = (f32[448,128]{1,0:T(8,128)S(1)}, f32[448,128]{1,0:T(8,128)S(1)}, u32[]{:S(2)}, u32[]{:S(2)}) collective-permute-start(f32[448,128]{1,0:T(8,128)S(1)} %bitcast.13), channel_id=1, source_target_pairs={{0,1},{1,0},{2,3},{3,2},{4,5},{5,4},{6,7},{7,6},{8,9},{9,8},{10,11... | collective-permute-start | bytes 688136 | tf_op jit(solution)/shard_map/ppermute | solution.py:698
  21.7 10.9 %all-to-all-start.1 = ((f32[8,40,128]{2,1,0:T(8,128)}), f32[8,40,128]{2,1,0:T(8,128)S(1)}, u32[]{:S(2)}, u32[]{:S(2)}) async-start(f32[8,40,128]{2,1,0:T(8,128)} %bitcast.5), calls=%async_computation.1 | async-start | bytes 327680 | tf_op jit(solution)/shard_map/all_to_all | solution.py:693
  32.6 1.4 %collective-permute-start.1 = (f32[320,128]{1,0:T(8,128)S(1)}, f32[320,128]{1,0:T(8,128)S(1)}, u32[]{:S(2)}, u32[]{:S(2)}) collective-permute-start(f32[320,128]{1,0:T(8,128)S(1)} %bitcast.16), channel_id=1, source_target_pairs={{0,1},{1,0},{2,3},{3,2},{4,5},{5,4},{6,7},{7,6},{8,9},{9,8},{10,11... | collective-permute-start | bytes 491528 | tf_op jit(solution)/shard_map/ppermute | solution.py:698
  38.0 10.2 %all-to-all-start.2 = ((f32[8,40,128]{2,1,0:T(8,128)}), f32[8,40,128]{2,1,0:T(8,128)S(1)}, u32[]{:S(2)}, u32[]{:S(2)}) async-start(f32[8,40,128]{2,1,0:T(8,128)} %bitcast.7), calls=%async_computation.2 | async-start | bytes 327680 | tf_op jit(solution)/shard_map/all_to_all | solution.py:693
  48.3 1.4 %collective-permute-start.2 = (f32[320,128]{1,0:T(8,128)S(1)}, f32[320,128]{1,0:T(8,128)S(1)}, u32[]{:S(2)}, u32[]{:S(2)}) collective-permute-start(f32[320,128]{1,0:T(8,128)S(1)} %bitcast.18), channel_id=1, source_target_pairs={{0,1},{1,0},{2,3},{3,2},{4,5},{5,4},{6,7},{7,6},{8,9},{9,8},{10,11... | collective-permute-start | bytes 491528 | tf_op jit(solution)/shard_map/ppermute | solution.py:698
  53.6 8.6 %all-to-all-start.3 = ((f32[16,4,128]{2,1,0:T(4,128)}), f32[16,4,128]{2,1,0:T(4,128)S(1)}, u32[]{:S(2)}, u32[]{:S(2)}) async-start(f32[16,4,128]{2,1,0:T(4,128)} %bitcast.9), calls=%async_computation.3 | async-start | bytes 65536 | tf_op jit(solution)/shard_map/all_to_all | solution.py:675

commit v21 on v18

--- a/solution.py
+++ b/solution.py
@@ -96,16 +96,20 @@
         w_ref[g] = block_diagonal(w_ref[g, :, :128])
         return 0
 
-    lax.fori_loop(0, groups, spread, 0, unroll=4)
+    lax.fori_loop(0, groups, spread, 0, unroll=2)
 
 
 def chunk_products(w_ref, c_ref, i, base, out0, out1):
     size = w_ref.shape[0] // CHUNKS
-    for k in range(size):
+
+    def group(k, _):
         g = i * size + k
         res = dot(w_ref[base + g], c_ref[pl.ds(g * 8, 8)].reshape(1024, 128))
         out0[base + g] = res[:8]
         out1[base + g] = res[8:]
+        return 0
+
+    lax.fori_loop(0, size, group, 0, unroll=2)
 
 
 def tile_products(w_ref, parts, out0, out1):

time: 76 us -> 81.5 us (1.072)
  Pallas kernels: 38.4 us -> 45.2 us
  waiting for transfers between devices: 4.93 us -> 3.09 us
    pallas_call x14, Pallas kernels: 38.4 us -> 45.2 us  [run(): pl.pallas_call(kernel, out_shape=[(out_spaces or {}).get(i, jax.ShapeDtyp...]
    all_to_all x3, waiting for transfers between devices: 3.8 us -> 2.52 us  [to_chips(): lax.all_to_all(x, 'bulk', split_axis=0, concat_axis=0, tiled=True, axis_i...]
  transfers between devices with their start and end apart: 7 -> 7, of which waited for: 6 -> 6; matrix products, arithmetic and copies ran while one was open for 0% -> 0% of each run, Pallas kernels for 27% -> 30%
where the time goes in v21:
time: 81.5 us; the launch traced here: 80.8 us
  Pallas kernels  45.2 us (55%)
  starting transfers between devices  21.7 us (27%)
  blocking collectives  9.49 us (12%)
  waiting for transfers between devices  3.09 us (4%)
  between operations  1.41 us (2%)
    pallas_call x14, Pallas kernels, run(): pl.pallas_call(kernel, out_shape=[(out_spaces or {}).get(i, jax.ShapeDtyp...  45.2 us
    all_to_all x3, starting transfers between devices, to_chips(): lax.all_to_all(x, 'bulk', split_axis=0, concat_axis=0, tiled=True, axis_i...  17.3 us
    all_to_all x1, blocking collectives, exchange(): lax.all_to_all(x, 'bulk', split_axis=0, concat_axis=0, tiled=True, axis_i...  9.49 us
    all_to_all x1, starting transfers between devices, exchange(): lax.all_to_all(x, 'bulk', split_axis=0, concat_axis=0, tiled=True, axis_i...  4.26 us
    all_to_all x3, waiting for transfers between devices, to_chips(): lax.all_to_all(x, 'bulk', split_axis=0, concat_axis=0, tiled=True, axis_i...  2.52 us
  transfers between devices with their start and end apart: 7, of which 6 were waited for; matrix products, arithmetic and copies ran while one was open for 0% of the time, Pallas kernels for 30%

profile of v21, /device:TPU:0, one launch (start us, length us, event | category | flops | bytes accessed | tf_op | source)
XLA Modules:
  0.0 80.8 jit_solution(15199618621688654488)
XLA Ops:
  0.6 1.6 %need.1 = (f32[32,128]{1,0:T(8,128)S(1)}, f32[16,128]{1,0:T(8,128)S(1)}, f32[16,128]{1,0:T(8,128)S(1)}, f32[16,128]{1,0:T(8,128)S(1)}, s32[1,256]{1,0:T(1,128)S(...) custom-call(f32[32,128]{1,0:T(8,128)} %refs_0_.1, ...), custom_call_target="tpu_custom_call" | custom-call | tf_op jit(solution)/shard_map/need/pallas_call | solution.py:618
  2.2 7.9 %all-to-all-start = ((f32[8,56,128]{2,1,0:T(8,128)}), f32[8,56,128]{2,1,0:T(8,128)S(1)}, u32[]{:S(2)}, u32[]{:S(2)}) async-start(f32[8,56,128]{2,1,0:T(8,128)} %bitcast.3), calls=%async_computation | async-start | bytes 458752 | tf_op jit(solution)/shard_map/all_to_all | solution.py:694
  10.7 7.5 %prepare.1 = (bf16[64,128,128]{2,1,0:T(8,128)(2,1)S(1)}, bf16[192,128,128]{2,1,0:T(8,128)(2,1)}, bf16[256,128]{1,0:T(8,128)(2,1)S(1)}, bf16[256,32]{1,0:T(8,128)...) custom-call(s32[1]{0:T(128)S(6)} %copy.13.count_ref, ...), custom_call_target="tpu_custom_call" | custom-call | flops 134217728 | bytes 8388608 | tf_op jit(solution)/shard_map/prepare/pallas_call | solution.py:618
  18.3 0.0 all-to-all-done
  18.3 0.1 collective-permute-start
  18.4 1.2 %near_rows.1 = (f32[64,128]{1,0:T(8,128)S(1)}, bf16[32,128,128]{2,1,0:T(8,128)(2,1)S(1)}) custom-call(f32[448,128]{1,0:T(8,128)S(1)} %bitcast.14, bf16[64,448]{1,0:T(8,128)(2,1)S(1)} %get-tuple-element.80.list_ref, bf16[192,128,128]{2,1,0:T(8,128)(2,1)} %get-tuple-element.81.c_hbm.refs_14_), custom_call_target="tpu_custom_call" | custom-call | tf_op jit(solution)/shard_map/near_rows/pallas_call | solution.py:618
  19.6 0.2 collective-permute-done.other_ref
  19.8 4.9 %first.1 = (f32[320,128]{1,0:T(8,128)}, f32[32,128]{1,0:T(8,128)S(1)}, f32[32,128]{1,0:T(8,128)S(1)}, bf16[64,128]{1,0:T(8,128)(2,1)S(1)}, bf16[128,128]{1,0:T(8,128)(2,1)S(1)}) custom-call(f32[448,128]{1,0:T(8,128)S(1)} %bitcast.15, f32[448,128]{1,0:T(8,128)S(1)} %collective-permute-done.other_ref, f32[64,128]{1,0:T(8,128)S(1)} %get-tuple-element.82.part_ref, ...), custom_call_target="tpu_custom_call" | custom-call | flops 134217728 | bytes 8388608 | tf_op jit(solution)/shard_map/first/pallas_call | solution.py:618
  24.7 5.1 %all-to-all-start.1 = ((f32[8,40,128]{2,1,0:T(8,128)}), f32[8,40,128]{2,1,0:T(8,128)S(1)}, u32[]{:S(2)}, u32[]{:S(2)}) async-start(f32[8,40,128]{2,1,0:T(8,128)} %bitcast.5), calls=%async_computation.1 | async-start | bytes 327680 | tf_op jit(solution)/shard_map/all_to_all | solution.py:694
  29.9 0.3 serve.1
  30.2 4.3 %backward.3 = (f32[32,8,128]{2,1,0:T(8,128)S(1)}, f32[32,8,128]{2,1,0:T(8,128)S(1)}) custom-call(f32[32,128]{1,0:T(8,128)S(1)} %get-tuple-element.95.f_ref.own_ref, bf16[256,32]{1,0:T(8,128)(2,1)S(1)} %get-tuple-element.96.gk_ref, bf16[256,128,128]{2,1,0:T(8,128)(2,1)} %c_hbm.7), custom_call_target="tpu_custom_call" | custom-call | flops 134217728 | bytes 8388608 | tf_op jit(solution)/shard_map/backward/pallas_call | solution.py:618
  34.5 0.9 %all-to-all-done.1 = f32[8,40,128]{2,1,0:T(8,128)S(1)} async-done(((f32[8,40,128]{2,1,0:T(8,128)}), f32[8,40,128]{2,1,0:T(8,128)S(1)}, u32[]{:S(2)}, u32[]{:S(2)}) %all-to-all-start.1) | async-done | bytes 163872 | tf_op jit(solution)/shard_map/all_to_all | solution.py:694
  35.4 0.0 collective-permute-start.1
  35.4 1.2 %near_half.2 = (f32[64,128]{1,0:T(8,128)S(1)}, f32[16,128]{1,0:T(8,128)S(1)}, bf16[32,128,128]{2,1,0:T(8,128)(2,1)S(1)}) custom-call(f32[320,128]{1,0:T(8,128)S(1)} %bitcast.17, bf16[80,512]{1,0:T(8,128)(2,1)S(1)} %get-tuple-element.114.share_ref, bf16[192,128,128]{2,1,0:T(8,128)(2,1)} %get-tuple-element.81.c_hbm.refs_14_), custom_call_target="tpu_custom_call" | custom-call | tf_op jit(solution)/shard_map/near_half/pallas_call | solution.py:618
  36.7 0.1 collective-permute-done.1.other_ref
  36.8 4.8 %middle.2 = (f32[320,128]{1,0:T(8,128)}, f32[16,128]{1,0:T(8,128)S(1)}, f32[32,128]{1,0:T(8,128)S(1)}) custom-call(f32[64,128]{1,0:T(8,128)S(1)} %get-tuple-element.104.part_ref, f32[16,128]{1,0:T(8,128)S(1)} %get-tuple-element.105.total_ref, f32[320,128]{1,0:T(8,128)S(1)} %collective-permute-done.1.other_ref, ...), custom_call_target="tpu_custom_call" | custom-call | flops 134217728 | bytes 8388608 | tf_op jit(solution)/shard_map/middle/pallas_call | solution.py:618
  41.6 4.4 %all-to-all-start.2 = ((f32[8,40,128]{2,1,0:T(8,128)}), f32[8,40,128]{2,1,0:T(8,128)S(1)}, u32[]{:S(2)}, u32[]{:S(2)}) async-start(f32[8,40,128]{2,1,0:T(8,128)} %bitcast.7), calls=%async_computation.2 | async-start | bytes 327680 | tf_op jit(solution)/shard_map/all_to_all | solution.py:694
  46.0 4.3 %backward.4 = (f32[32,8,128]{2,1,0:T(8,128)S(1)}, f32[32,8,128]{2,1,0:T(8,128)S(1)}) custom-call(f32[32,128]{1,0:T(8,128)S(1)} %get-tuple-element.111.f_ref.own_ref.refs_1_, bf16[256,32]{1,0:T(8,128)(2,1)S(1)} %get-tuple-element.96.gk_ref, bf16[256,128,128]{2,1,0:T(8,128)(2,1)} %c_hbm.7), custom_call_target="tpu_custom_call" | custom-call | flops 134217728 | bytes 8388608 | tf_op jit(solution)/shard_map/backward/pallas_call | solution.py:618
  50.3 1.6 %all-to-all-done.2 = f32[8,40,128]{2,1,0:T(8,128)S(1)} async-done(((f32[8,40,128]{2,1,0:T(8,128)}), f32[8,40,128]{2,1,0:T(8,128)S(1)}, u32[]{:S(2)}, u32[]{:S(2)}) %all-to-all-start.2) | async-done | bytes 163872 | tf_op jit(solution)/shard_map/all_to_all | solution.py:694
  51.9 0.0 collective-permute-start.2
  51.9 1.2 %near_half.3 = (f32[64,128]{1,0:T(8,128)S(1)}, f32[16,128]{1,0:T(8,128)S(1)}, bf16[32,128,128]{2,1,0:T(8,128)(2,1)S(1)}) custom-call(f32[320,128]{1,0:T(8,128)S(1)} %bitcast.19, bf16[80,512]{1,0:T(8,128)(2,1)S(1)} %get-tuple-element.114.share_ref, bf16[192,128,128]{2,1,0:T(8,128)(2,1)} %get-tuple-element.81.c_hbm.refs_14_), custom_call_target="tpu_custom_call" | custom-call | tf_op jit(solution)/shard_map/near_half/pallas_call | solution.py:618
  53.1 0.1 collective-permute-done.2.other_ref
  53.3 4.7 %middle.3 = (f32[64,128]{1,0:T(8,128)}, f32[16,128]{1,0:T(8,128)S(1)}, f32[32,128]{1,0:T(8,128)S(1)}, f32[32,128]{1,0:T(8,128)S(1)}) custom-call(f32[64,128]{1,0:T(8,128)S(1)} %get-tuple-element.115.part_ref, f32[16,128]{1,0:T(8,128)S(1)} %get-tuple-element.116.total_ref, f32[320,128]{1,0:T(8,128)S(1)} %collective-permute-done.2.other_ref, ...), custom_call_target="tpu_custom_call" | custom-call | flops 134217728 | bytes 8388608 | tf_op jit(solution)/shard_map/middle/pallas_call | solution.py:618
  58.0 4.3 %all-to-all-start.3 = ((f32[16,4,128]{2,1,0:T(4,128)}), f32[16,4,128]{2,1,0:T(4,128)S(1)}, u32[]{:S(2)}, u32[]{:S(2)}) async-start(f32[16,4,128]{2,1,0:T(4,128)} %bitcast.9), calls=%async_computation.3 | async-start | bytes 65536 | tf_op jit(solution)/shard_map/all_to_all | solution.py:676
  62.3 4.3 %backward.5 = (f32[32,8,128]{2,1,0:T(8,128)S(1)}, f32[32,8,128]{2,1,0:T(8,128)S(1)}) custom-call(f32[32,128]{1,0:T(8,128)S(1)} %get-tuple-element.127.f_ref.refs_2_, bf16[256,32]{1,0:T(8,128)(2,1)S(1)} %get-tuple-element.96.gk_ref, bf16[256,128,128]{2,1,0:T(8,128)(2,1)} %c_hbm.7), custom_call_target="tpu_custom_call" | custom-call | flops 134217728 | bytes 8388608 | tf_op jit(solution)/shard_map/backward/pallas_call | solution.py:618
  66.6 0.1 all-to-all-done.3
  66.6 0.4 phonon.1
  67.0 9.5 %all_to_all.58 = f32[16,8,128]{2,1,0:T(8,128)S(1)} all-to-all(f32[16,8,128]{2,1,0:T(8,128)S(1)} %bitcast.22), channel_id=1, replica_groups={{8,9,10,11,12,13,14,15,0,1,2,3,4,5,6,7},{24,25,26,27,28,29,30,31,16,17,..., dimensions={0} | all-to-all | bytes 131072 | tf_op jit(solution)/shard_map/all_to_all | solution.py:676
  76.5 4.3 %last.1 = (f32[32,128]{1,0:T(8,128)}, f32[16,128]{1,0:T(8,128)}) custom-call(f32[128,128]{1,0:T(8,128)S(1)} %bitcast.20, f32[256,128]{1,0:T(8,128)S(1)} %get-tuple-element.131.refs_0_, f32[32,128]{1,0:T(8,128)S(1)} %get-tuple-element.111.f_ref.own_ref.refs_1_, f32[32,128]{1,0:T(8,128)S(1)} %get-tuple-element.127.f_ref.refs_2_, ...), custom_call_target="tpu_custom_call" | custom-call | flops 134217728 | bytes 8388608 | tf_op jit(solution)/shard_map/last/pallas_call | solution.py:618
Async XLA Ops:
  2.2 16.0 %all-to-all-start = ((f32[8,56,128]{2,1,0:T(8,128)}), f32[8,56,128]{2,1,0:T(8,128)S(1)}, u32[]{:S(2)}, u32[]{:S(2)}) async-start(f32[8,56,128]{2,1,0:T(8,128)} %bitcast.3), calls=%async_computation | async-start | bytes 458752 | tf_op jit(solution)/shard_map/all_to_all | solution.py:694
  18.3 1.6 %collective-permute-start = (f32[448,128]{1,0:T(8,128)S(1)}, f32[448,128]{1,0:T(8,128)S(1)}, u32[]{:S(2)}, u32[]{:S(2)}) collective-permute-start(f32[448,128]{1,0:T(8,128)S(1)} %bitcast.13), channel_id=1, source_target_pairs={{0,1},{1,0},{2,3},{3,2},{4,5},{5,4},{6,7},{7,6},{8,9},{9,8},{10,11... | collective-permute-start | bytes 688136 | tf_op jit(solution)/shard_map/ppermute | solution.py:699
  24.7 10.7 %all-to-all-start.1 = ((f32[8,40,128]{2,1,0:T(8,128)}), f32[8,40,128]{2,1,0:T(8,128)S(1)}, u32[]{:S(2)}, u32[]{:S(2)}) async-start(f32[8,40,128]{2,1,0:T(8,128)} %bitcast.5), calls=%async_computation.1 | async-start | bytes 327680 | tf_op jit(solution)/shard_map/all_to_all | solution.py:694
  35.4 1.4 %collective-permute-start.1 = (f32[320,128]{1,0:T(8,128)S(1)}, f32[320,128]{1,0:T(8,128)S(1)}, u32[]{:S(2)}, u32[]{:S(2)}) collective-permute-start(f32[320,128]{1,0:T(8,128)S(1)} %bitcast.16), channel_id=1, source_target_pairs={{0,1},{1,0},{2,3},{3,2},{4,5},{5,4},{6,7},{7,6},{8,9},{9,8},{10,11... | collective-permute-start | bytes 491528 | tf_op jit(solution)/shard_map/ppermute | solution.py:699
  41.6 10.3 %all-to-all-start.2 = ((f32[8,40,128]{2,1,0:T(8,128)}), f32[8,40,128]{2,1,0:T(8,128)S(1)}, u32[]{:S(2)}, u32[]{:S(2)}) async-start(f32[8,40,128]{2,1,0:T(8,128)} %bitcast.7), calls=%async_computation.2 | async-start | bytes 327680 | tf_op jit(solution)/shard_map/all_to_all | solution.py:694
  51.9 1.4 %collective-permute-start.2 = (f32[320,128]{1,0:T(8,128)S(1)}, f32[320,128]{1,0:T(8,128)S(1)}, u32[]{:S(2)}, u32[]{:S(2)}) collective-permute-start(f32[320,128]{1,0:T(8,128)S(1)} %bitcast.18), channel_id=1, source_target_pairs={{0,1},{1,0},{2,3},{3,2},{4,5},{5,4},{6,7},{7,6},{8,9},{9,8},{10,11... | collective-permute-start | bytes 491528 | tf_op jit(solution)/shard_map/ppermute | solution.py:699
  58.0 8.6 %all-to-all-start.3 = ((f32[16,4,128]{2,1,0:T(4,128)}), f32[16,4,128]{2,1,0:T(4,128)S(1)}, u32[]{:S(2)}, u32[]{:S(2)}) async-start(f32[16,4,128]{2,1,0:T(4,128)} %bitcast.9), calls=%async_computation.3 | async-start | bytes 65536 | tf_op jit(solution)/shard_map/all_to_all | solution.py:676

commit v22 on v18

--- a/solution.py
+++ b/solution.py
@@ -10,6 +10,7 @@
 DT = 0.05
 CHUNKS = 8
 HELD_CHUNKS = 2
+SHORT_CHUNKS = 4
 f32 = jnp.float32
 bf16 = jnp.bfloat16
 VMEM_LIMIT = 48 * 1024 * 1024
@@ -99,8 +100,7 @@
     lax.fori_loop(0, groups, spread, 0, unroll=4)
 
 
-def chunk_products(w_ref, c_ref, i, base, out0, out1):
-    size = w_ref.shape[0] // CHUNKS
+def chunk_products(w_ref, c_ref, i, base, out0, out1, size):
     for k in range(size):
         g = i * size + k
         res = dot(w_ref[base + g], c_ref[pl.ds(g * 8, 8)].reshape(1024, 128))
@@ -109,17 +109,19 @@
 
 
 def tile_products(w_ref, parts, out0, out1):
-    size = w_ref.shape[0] // CHUNKS
     for c_ref, c_hbm, sems, base in parts:
-        chunks = c_ref.shape[0] // 8 // size
+        groups = c_ref.shape[0] // 8
+        if c_hbm is None:
+            chunk_products(w_ref, c_ref, 0, base, out0, out1, groups)
+            continue
+        size = groups // sems.shape[0]
 
         def chunk(i, _):
-            if c_hbm is not None:
-                chunk_copy(c_hbm, c_ref, sems, i).wait()
-            chunk_products(w_ref, c_ref, i, base, out0, out1)
+            chunk_copy(c_hbm, c_ref, sems, i).wait()
+            chunk_products(w_ref, c_ref, i, base, out0, out1, size)
             return 0
 
-        lax.fori_loop(0, chunks, chunk, 0)
+        lax.fori_loop(0, sems.shape[0], chunk, 0)
 
 
 def backward_pass(own, c_hbm, c_ref, sems, w_ref, out0, out1):
@@ -266,14 +268,14 @@
 
     def to_held(i, _):
         chunk_copy(c_hbm, c_ref, in_sems, i).wait()
-        chunk_products(w_ref, c_ref, i, 0, b0_ref, b1_ref)
+        chunk_products(w_ref, c_ref, i, 0, b0_ref, b1_ref, size // 8)
         for t in range(size):
             held_ref[i * size + t] = c_ref[i * size + t].T
         return 0
 
     def to_rest(i, _):
         chunk_copy(c_hbm, c_ref, in_sems, held + i).wait()
-        chunk_products(w_ref, c_ref, held + i, 0, b0_ref, b1_ref)
+        chunk_products(w_ref, c_ref, held + i, 0, b0_ref, b1_ref, size // 8)
         for t in range(size):
             t_ref[i * size + t] = c_ref[(held + i) * size + t].T
         chunk_copy(t_ref, t_hbm, out_sems, i).start()
@@ -740,7 +742,7 @@
     fetched = ((width, 128, 128), bf16)
     fetch_sem = pltpu.SemaphoreType.DMA((1,))
     short = (rest[0] - width, 128, 128)
-    short_sems = pltpu.SemaphoreType.DMA((CHUNKS - HELD_CHUNKS - 1,))
+    short_sems = pltpu.SemaphoreType.DMA((SHORT_CHUNKS,))
     forward_scratch = [weights, pltpu.VMEM(short, bf16), short_sems] + sums
     other = between_cores(same)
     part, c_fetched = call(

time: 76 us -> 76.2 us (level)
  no operation moved by 1% of the time
where the time goes in v22:
time: 76.2 us; the launch traced here: 75.5 us
  Pallas kernels  38.5 us (51%)
  starting transfers between devices  21.7 us (28%)
  blocking collectives  8.93 us (12%)
  waiting for transfers between devices  4.93 us (6%)
  between operations  1.41 us (2%)
    pallas_call x14, Pallas kernels, run(): pl.pallas_call(kernel, out_shape=[(out_spaces or {}).get(i, jax.ShapeDtyp...  38.5 us
    all_to_all x3, starting transfers between devices, to_chips(): lax.all_to_all(x, 'bulk', split_axis=0, concat_axis=0, tiled=True, axis_i...  17.3 us
    all_to_all x1, blocking collectives, exchange(): lax.all_to_all(x, 'bulk', split_axis=0, concat_axis=0, tiled=True, axis_i...  8.93 us
    all_to_all x1, starting transfers between devices, exchange(): lax.all_to_all(x, 'bulk', split_axis=0, concat_axis=0, tiled=True, axis_i...  4.26 us
    all_to_all x3, waiting for transfers between devices, to_chips(): lax.all_to_all(x, 'bulk', split_axis=0, concat_axis=0, tiled=True, axis_i...  3.8 us
  transfers between devices with their start and end apart: 7, of which 6 were waited for; matrix products, arithmetic and copies ran while one was open for 0% of the time, Pallas kernels for 27%

profile of v22, /device:TPU:0, one launch (start us, length us, event | category | flops | bytes accessed | tf_op | source)
XLA Modules:
  0.0 75.5 jit_solution(7203628440631193093)
XLA Ops:
  0.6 1.6 %need.1 = (f32[32,128]{1,0:T(8,128)S(1)}, f32[16,128]{1,0:T(8,128)S(1)}, f32[16,128]{1,0:T(8,128)S(1)}, f32[16,128]{1,0:T(8,128)S(1)}, s32[1,256]{1,0:T(1,128)S(...) custom-call(f32[32,128]{1,0:T(8,128)} %refs_0_.1, ...), custom_call_target="tpu_custom_call" | custom-call | tf_op jit(solution)/shard_map/need/pallas_call | solution.py:616
  2.2 7.9 %all-to-all-start = ((f32[8,56,128]{2,1,0:T(8,128)}), f32[8,56,128]{2,1,0:T(8,128)S(1)}, u32[]{:S(2)}, u32[]{:S(2)}) async-start(f32[8,56,128]{2,1,0:T(8,128)} %bitcast.3), calls=%async_computation | async-start | bytes 458752 | tf_op jit(solution)/shard_map/all_to_all | solution.py:692
  10.7 5.5 %prepare.1 = (bf16[64,128,128]{2,1,0:T(8,128)(2,1)S(1)}, bf16[192,128,128]{2,1,0:T(8,128)(2,1)}, bf16[256,128]{1,0:T(8,128)(2,1)S(1)}, bf16[256,32]{1,0:T(8,128)...) custom-call(s32[1]{0:T(128)S(6)} %copy.13.count_ref, ...), custom_call_target="tpu_custom_call" | custom-call | flops 134217728 | bytes 8388608 | tf_op jit(solution)/shard_map/prepare/pallas_call | solution.py:616
  16.2 0.0 all-to-all-done
  16.2 0.1 collective-permute-start
  16.3 1.2 %near_rows.1 = (f32[64,128]{1,0:T(8,128)S(1)}, bf16[32,128,128]{2,1,0:T(8,128)(2,1)S(1)}) custom-call(f32[448,128]{1,0:T(8,128)S(1)} %bitcast.14, bf16[64,448]{1,0:T(8,128)(2,1)S(1)} %get-tuple-element.80.list_ref, bf16[192,128,128]{2,1,0:T(8,128)(2,1)} %get-tuple-element.81.c_hbm.refs_14_), custom_call_target="tpu_custom_call" | custom-call | tf_op jit(solution)/shard_map/near_rows/pallas_call | solution.py:616
  17.5 0.2 collective-permute-done.other_ref
  17.8 4.1 %first.1 = (f32[320,128]{1,0:T(8,128)}, f32[32,128]{1,0:T(8,128)S(1)}, f32[32,128]{1,0:T(8,128)S(1)}, bf16[64,128]{1,0:T(8,128)(2,1)S(1)}, bf16[128,128]{1,0:T(8,128)(2,1)S(1)}) custom-call(f32[448,128]{1,0:T(8,128)S(1)} %bitcast.15, f32[448,128]{1,0:T(8,128)S(1)} %collective-permute-done.other_ref, f32[64,128]{1,0:T(8,128)S(1)} %get-tuple-element.82.part_ref, ...), custom_call_target="tpu_custom_call" | custom-call | flops 134217728 | bytes 8388608 | tf_op jit(solution)/shard_map/first/pallas_call | solution.py:616
  21.8 5.1 %all-to-all-start.1 = ((f32[8,40,128]{2,1,0:T(8,128)}), f32[8,40,128]{2,1,0:T(8,128)S(1)}, u32[]{:S(2)}, u32[]{:S(2)}) async-start(f32[8,40,128]{2,1,0:T(8,128)} %bitcast.5), calls=%async_computation.1 | async-start | bytes 327680 | tf_op jit(solution)/shard_map/all_to_all | solution.py:692
  27.0 0.3 serve.1
  27.3 3.7 %backward.3 = (f32[32,8,128]{2,1,0:T(8,128)S(1)}, f32[32,8,128]{2,1,0:T(8,128)S(1)}) custom-call(f32[32,128]{1,0:T(8,128)S(1)} %get-tuple-element.95.f_ref.own_ref, bf16[256,32]{1,0:T(8,128)(2,1)S(1)} %get-tuple-element.96.gk_ref, bf16[256,128,128]{2,1,0:T(8,128)(2,1)} %c_hbm.7), custom_call_target="tpu_custom_call" | custom-call | flops 134217728 | bytes 8388608 | tf_op jit(solution)/shard_map/backward/pallas_call | solution.py:616
  31.0 1.6 %all-to-all-done.1 = f32[8,40,128]{2,1,0:T(8,128)S(1)} async-done(((f32[8,40,128]{2,1,0:T(8,128)}), f32[8,40,128]{2,1,0:T(8,128)S(1)}, u32[]{:S(2)}, u32[]{:S(2)}) %all-to-all-start.1) | async-done | bytes 163872 | tf_op jit(solution)/shard_map/all_to_all | solution.py:692
  32.6 0.0 collective-permute-start.1
  32.6 1.2 %near_half.2 = (f32[64,128]{1,0:T(8,128)S(1)}, f32[16,128]{1,0:T(8,128)S(1)}, bf16[32,128,128]{2,1,0:T(8,128)(2,1)S(1)}) custom-call(f32[320,128]{1,0:T(8,128)S(1)} %bitcast.17, bf16[80,512]{1,0:T(8,128)(2,1)S(1)} %get-tuple-element.114.share_ref, bf16[192,128,128]{2,1,0:T(8,128)(2,1)} %get-tuple-element.81.c_hbm.refs_14_), custom_call_target="tpu_custom_call" | custom-call | tf_op jit(solution)/shard_map/near_half/pallas_call | solution.py:616
  33.9 0.1 collective-permute-done.1.other_ref
  34.0 4.0 %middle.2 = (f32[320,128]{1,0:T(8,128)}, f32[16,128]{1,0:T(8,128)S(1)}, f32[32,128]{1,0:T(8,128)S(1)}) custom-call(f32[64,128]{1,0:T(8,128)S(1)} %get-tuple-element.104.part_ref, f32[16,128]{1,0:T(8,128)S(1)} %get-tuple-element.105.total_ref, f32[320,128]{1,0:T(8,128)S(1)} %collective-permute-done.1.other_ref, ...), custom_call_target="tpu_custom_call" | custom-call | flops 134217728 | bytes 8388608 | tf_op jit(solution)/shard_map/middle/pallas_call | solution.py:616
  38.1 4.4 %all-to-all-start.2 = ((f32[8,40,128]{2,1,0:T(8,128)}), f32[8,40,128]{2,1,0:T(8,128)S(1)}, u32[]{:S(2)}, u32[]{:S(2)}) async-start(f32[8,40,128]{2,1,0:T(8,128)} %bitcast.7), calls=%async_computation.2 | async-start | bytes 327680 | tf_op jit(solution)/shard_map/all_to_all | solution.py:692
  42.5 3.7 %backward.4 = (f32[32,8,128]{2,1,0:T(8,128)S(1)}, f32[32,8,128]{2,1,0:T(8,128)S(1)}) custom-call(f32[32,128]{1,0:T(8,128)S(1)} %get-tuple-element.111.f_ref.own_ref.refs_1_, bf16[256,32]{1,0:T(8,128)(2,1)S(1)} %get-tuple-element.96.gk_ref, bf16[256,128,128]{2,1,0:T(8,128)(2,1)} %c_hbm.7), custom_call_target="tpu_custom_call" | custom-call | flops 134217728 | bytes 8388608 | tf_op jit(solution)/shard_map/backward/pallas_call | solution.py:616
  46.2 2.2 %all-to-all-done.2 = f32[8,40,128]{2,1,0:T(8,128)S(1)} async-done(((f32[8,40,128]{2,1,0:T(8,128)}), f32[8,40,128]{2,1,0:T(8,128)S(1)}, u32[]{:S(2)}, u32[]{:S(2)}) %all-to-all-start.2) | async-done | bytes 163872 | tf_op jit(solution)/shard_map/all_to_all | solution.py:692
  48.4 0.0 collective-permute-start.2
  48.4 1.2 %near_half.3 = (f32[64,128]{1,0:T(8,128)S(1)}, f32[16,128]{1,0:T(8,128)S(1)}, bf16[32,128,128]{2,1,0:T(8,128)(2,1)S(1)}) custom-call(f32[320,128]{1,0:T(8,128)S(1)} %bitcast.19, bf16[80,512]{1,0:T(8,128)(2,1)S(1)} %get-tuple-element.114.share_ref, bf16[192,128,128]{2,1,0:T(8,128)(2,1)} %get-tuple-element.81.c_hbm.refs_14_), custom_call_target="tpu_custom_call" | custom-call | tf_op jit(solution)/shard_map/near_half/pallas_call | solution.py:616
  49.6 0.1 collective-permute-done.2.other_ref
  49.8 3.9 %middle.3 = (f32[64,128]{1,0:T(8,128)}, f32[16,128]{1,0:T(8,128)S(1)}, f32[32,128]{1,0:T(8,128)S(1)}, f32[32,128]{1,0:T(8,128)S(1)}) custom-call(f32[64,128]{1,0:T(8,128)S(1)} %get-tuple-element.115.part_ref, f32[16,128]{1,0:T(8,128)S(1)} %get-tuple-element.116.total_ref, f32[320,128]{1,0:T(8,128)S(1)} %collective-permute-done.2.other_ref, ...), custom_call_target="tpu_custom_call" | custom-call | flops 134217728 | bytes 8388608 | tf_op jit(solution)/shard_map/middle/pallas_call | solution.py:616
  53.6 4.3 %all-to-all-start.3 = ((f32[16,4,128]{2,1,0:T(4,128)}), f32[16,4,128]{2,1,0:T(4,128)S(1)}, u32[]{:S(2)}, u32[]{:S(2)}) async-start(f32[16,4,128]{2,1,0:T(4,128)} %bitcast.9), calls=%async_computation.3 | async-start | bytes 65536 | tf_op jit(solution)/shard_map/all_to_all | solution.py:674
  57.9 3.7 %backward.5 = (f32[32,8,128]{2,1,0:T(8,128)S(1)}, f32[32,8,128]{2,1,0:T(8,128)S(1)}) custom-call(f32[32,128]{1,0:T(8,128)S(1)} %get-tuple-element.127.f_ref.refs_2_, bf16[256,32]{1,0:T(8,128)(2,1)S(1)} %get-tuple-element.96.gk_ref, bf16[256,128,128]{2,1,0:T(8,128)(2,1)} %c_hbm.7), custom_call_target="tpu_custom_call" | custom-call | flops 134217728 | bytes 8388608 | tf_op jit(solution)/shard_map/backward/pallas_call | solution.py:616
  61.6 0.6 all-to-all-done.3
  62.3 0.4 phonon.1
  62.6 8.9 %all_to_all.58 = f32[16,8,128]{2,1,0:T(8,128)S(1)} all-to-all(f32[16,8,128]{2,1,0:T(8,128)S(1)} %bitcast.22), channel_id=1, replica_groups={{8,9,10,11,12,13,14,15,0,1,2,3,4,5,6,7},{24,25,26,27,28,29,30,31,16,17,..., dimensions={0} | all-to-all | bytes 131072 | tf_op jit(solution)/shard_map/all_to_all | solution.py:674
  71.6 3.9 %last.1 = (f32[32,128]{1,0:T(8,128)}, f32[16,128]{1,0:T(8,128)}) custom-call(f32[128,128]{1,0:T(8,128)S(1)} %bitcast.20, f32[256,128]{1,0:T(8,128)S(1)} %get-tuple-element.131.refs_0_, f32[32,128]{1,0:T(8,128)S(1)} %get-tuple-element.111.f_ref.own_ref.refs_1_, f32[32,128]{1,0:T(8,128)S(1)} %get-tuple-element.127.f_ref.refs_2_, ...), custom_call_target="tpu_custom_call" | custom-call | flops 134217728 | bytes 8388608 | tf_op jit(solution)/shard_map/last/pallas_call | solution.py:616
Async XLA Ops:
  2.2 14.0 %all-to-all-start = ((f32[8,56,128]{2,1,0:T(8,128)}), f32[8,56,128]{2,1,0:T(8,128)S(1)}, u32[]{:S(2)}, u32[]{:S(2)}) async-start(f32[8,56,128]{2,1,0:T(8,128)} %bitcast.3), calls=%async_computation | async-start | bytes 458752 | tf_op jit(solution)/shard_map/all_to_all | solution.py:692
  16.2 1.6 %collective-permute-start = (f32[448,128]{1,0:T(8,128)S(1)}, f32[448,128]{1,0:T(8,128)S(1)}, u32[]{:S(2)}, u32[]{:S(2)}) collective-permute-start(f32[448,128]{1,0:T(8,128)S(1)} %bitcast.13), channel_id=1, source_target_pairs={{0,1},{1,0},{2,3},{3,2},{4,5},{5,4},{6,7},{7,6},{8,9},{9,8},{10,11... | collective-permute-start | bytes 688136 | tf_op jit(solution)/shard_map/ppermute | solution.py:697
  21.8 10.8 %all-to-all-start.1 = ((f32[8,40,128]{2,1,0:T(8,128)}), f32[8,40,128]{2,1,0:T(8,128)S(1)}, u32[]{:S(2)}, u32[]{:S(2)}) async-start(f32[8,40,128]{2,1,0:T(8,128)} %bitcast.5), calls=%async_computation.1 | async-start | bytes 327680 | tf_op jit(solution)/shard_map/all_to_all | solution.py:692
  32.6 1.4 %collective-permute-start.1 = (f32[320,128]{1,0:T(8,128)S(1)}, f32[320,128]{1,0:T(8,128)S(1)}, u32[]{:S(2)}, u32[]{:S(2)}) collective-permute-start(f32[320,128]{1,0:T(8,128)S(1)} %bitcast.16), channel_id=1, source_target_pairs={{0,1},{1,0},{2,3},{3,2},{4,5},{5,4},{6,7},{7,6},{8,9},{9,8},{10,11... | collective-permute-start | bytes 491528 | tf_op jit(solution)/shard_map/ppermute | solution.py:697
  38.1 10.3 %all-to-all-start.2 = ((f32[8,40,128]{2,1,0:T(8,128)}), f32[8,40,128]{2,1,0:T(8,128)S(1)}, u32[]{:S(2)}, u32[]{:S(2)}) async-start(f32[8,40,128]{2,1,0:T(8,128)} %bitcast.7), calls=%async_computation.2 | async-start | bytes 327680 | tf_op jit(solution)/shard_map/all_to_all | solution.py:692
  48.4 1.4 %collective-permute-start.2 = (f32[320,128]{1,0:T(8,128)S(1)}, f32[320,128]{1,0:T(8,128)S(1)}, u32[]{:S(2)}, u32[]{:S(2)}) collective-permute-start(f32[320,128]{1,0:T(8,128)S(1)} %bitcast.18), channel_id=1, source_target_pairs={{0,1},{1,0},{2,3},{3,2},{4,5},{5,4},{6,7},{7,6},{8,9},{9,8},{10,11... | collective-permute-start | bytes 491528 | tf_op jit(solution)/shard_map/ppermute | solution.py:697
  53.6 8.6 %all-to-all-start.3 = ((f32[16,4,128]{2,1,0:T(4,128)}), f32[16,4,128]{2,1,0:T(4,128)S(1)}, u32[]{:S(2)}, u32[]{:S(2)}) async-start(f32[16,4,128]{2,1,0:T(4,128)} %bitcast.9), calls=%async_computation.3 | async-start | bytes 65536 | tf_op jit(solution)/shard_map/all_to_all | solution.py:674

commit v23 on v22

--- a/solution.py
+++ b/solution.py
@@ -10,7 +10,7 @@
 DT = 0.05
 CHUNKS = 8
 HELD_CHUNKS = 2
-SHORT_CHUNKS = 4
+SHORT_CHUNKS = 3
 f32 = jnp.float32
 bf16 = jnp.bfloat16
 VMEM_LIMIT = 48 * 1024 * 1024
@@ -738,7 +738,7 @@
     same, c_held, b0 = lax.optimization_barrier((same, c_held, b0))
     wide_block = ((chips * wide, 128), f32)
     k_rows, q_rows = ((kb, 128), f32), ((qb, 128), f32)
-    width = tiles // CHUNKS
+    width = 3 * (tiles // CHUNKS) // 2
     fetched = ((width, 128, 128), bf16)
     fetch_sem = pltpu.SemaphoreType.DMA((1,))
     short = (rest[0] - width, 128, 128)

time: 76.2 us -> 76.4 us (level)
  transfers between devices with their start and end apart: 7 -> 7, of which waited for: 6 -> 3; matrix products, arithmetic and copies ran while one was open for 0% -> 0% of each run, Pallas kernels for 27% -> 28%
where the time goes in v23:
time: 76.4 us; the launch traced here: 75.7 us
  Pallas kernels  38.9 us (51%)
  starting transfers between devices  21.6 us (28%)
  blocking collectives  8.93 us (12%)
  waiting for transfers between devices  4.81 us (6%)
  between operations  1.42 us (2%)
    pallas_call x14, Pallas kernels, run(): pl.pallas_call(kernel, out_shape=[(out_spaces or {}).get(i, jax.ShapeDtyp...  38.9 us
    all_to_all x3, starting transfers between devices, to_chips(): lax.all_to_all(x, 'bulk', split_axis=0, concat_axis=0, tiled=True, axis_i...  17.2 us
    all_to_all x1, blocking collectives, exchange(): lax.all_to_all(x, 'bulk', split_axis=0, concat_axis=0, tiled=True, axis_i...  8.93 us
    all_to_all x1, starting transfers between devices, exchange(): lax.all_to_all(x, 'bulk', split_axis=0, concat_axis=0, tiled=True, axis_i...  4.35 us
    all_to_all x3, waiting for transfers between devices, to_chips(): lax.all_to_all(x, 'bulk', split_axis=0, concat_axis=0, tiled=True, axis_i...  4.13 us
  transfers between devices with their start and end apart: 7, of which 3 were waited for; matrix products, arithmetic and copies ran while one was open for 0% of the time, Pallas kernels for 28%

profile of v23, /device:TPU:0, one launch (start us, length us, event | category | flops | bytes accessed | tf_op | source)
XLA Modules:
  0.0 75.7 jit_solution(15800652883181837132)
XLA Ops:
  0.6 1.6 %need.1 = (f32[32,128]{1,0:T(8,128)S(1)}, f32[16,128]{1,0:T(8,128)S(1)}, f32[16,128]{1,0:T(8,128)S(1)}, f32[16,128]{1,0:T(8,128)S(1)}, s32[1,256]{1,0:T(1,128)S(...) custom-call(f32[32,128]{1,0:T(8,128)} %refs_0_.1, ...), custom_call_target="tpu_custom_call" | custom-call | tf_op jit(solution)/shard_map/need/pallas_call | solution.py:616
  2.2 7.9 %all-to-all-start = ((f32[8,56,128]{2,1,0:T(8,128)}), f32[8,56,128]{2,1,0:T(8,128)S(1)}, u32[]{:S(2)}, u32[]{:S(2)}) async-start(f32[8,56,128]{2,1,0:T(8,128)} %bitcast.3), calls=%async_computation | async-start | bytes 458752 | tf_op jit(solution)/shard_map/all_to_all | solution.py:692
  10.7 5.5 %prepare.1 = (bf16[64,128,128]{2,1,0:T(8,128)(2,1)S(1)}, bf16[192,128,128]{2,1,0:T(8,128)(2,1)}, bf16[256,128]{1,0:T(8,128)(2,1)S(1)}, bf16[256,32]{1,0:T(8,128)...) custom-call(s32[1]{0:T(128)S(6)} %copy.13.count_ref, ...), custom_call_target="tpu_custom_call" | custom-call | flops 134217728 | bytes 8388608 | tf_op jit(solution)/shard_map/prepare/pallas_call | solution.py:616
  16.2 0.0 all-to-all-done
  16.2 0.1 collective-permute-start
  16.3 1.4 %near_rows.1 = (f32[64,128]{1,0:T(8,128)S(1)}, bf16[48,128,128]{2,1,0:T(8,128)(2,1)S(1)}) custom-call(f32[448,128]{1,0:T(8,128)S(1)} %bitcast.14, bf16[64,448]{1,0:T(8,128)(2,1)S(1)} %get-tuple-element.80.list_ref, bf16[192,128,128]{2,1,0:T(8,128)(2,1)} %get-tuple-element.81.c_hbm.refs_14_), custom_call_target="tpu_custom_call" | custom-call | tf_op jit(solution)/shard_map/near_rows/pallas_call | solution.py:616
  17.7 0.0 collective-permute-done.other_ref
  17.8 4.1 %first.1 = (f32[320,128]{1,0:T(8,128)}, f32[32,128]{1,0:T(8,128)S(1)}, f32[32,128]{1,0:T(8,128)S(1)}, bf16[64,128]{1,0:T(8,128)(2,1)S(1)}, bf16[128,128]{1,0:T(8,128)(2,1)S(1)}) custom-call(f32[448,128]{1,0:T(8,128)S(1)} %bitcast.15, f32[448,128]{1,0:T(8,128)S(1)} %collective-permute-done.other_ref, f32[64,128]{1,0:T(8,128)S(1)} %get-tuple-element.82.part_ref, ...), custom_call_target="tpu_custom_call" | custom-call | flops 134217728 | bytes 8388608 | tf_op jit(solution)/shard_map/first/pallas_call | solution.py:616
  21.9 5.1 %all-to-all-start.1 = ((f32[8,40,128]{2,1,0:T(8,128)}), f32[8,40,128]{2,1,0:T(8,128)S(1)}, u32[]{:S(2)}, u32[]{:S(2)}) async-start(f32[8,40,128]{2,1,0:T(8,128)} %bitcast.5), calls=%async_computation.1 | async-start | bytes 327680 | tf_op jit(solution)/shard_map/all_to_all | solution.py:692
  27.0 0.3 serve.1
  27.3 3.7 %backward.3 = (f32[32,8,128]{2,1,0:T(8,128)S(1)}, f32[32,8,128]{2,1,0:T(8,128)S(1)}) custom-call(f32[32,128]{1,0:T(8,128)S(1)} %get-tuple-element.95.f_ref.own_ref, bf16[256,32]{1,0:T(8,128)(2,1)S(1)} %get-tuple-element.96.gk_ref, bf16[256,128,128]{2,1,0:T(8,128)(2,1)} %c_hbm.7), custom_call_target="tpu_custom_call" | custom-call | flops 134217728 | bytes 8388608 | tf_op jit(solution)/shard_map/backward/pallas_call | solution.py:616
  31.1 1.8 %all-to-all-done.1 = f32[8,40,128]{2,1,0:T(8,128)S(1)} async-done(((f32[8,40,128]{2,1,0:T(8,128)}), f32[8,40,128]{2,1,0:T(8,128)S(1)}, u32[]{:S(2)}, u32[]{:S(2)}) %all-to-all-start.1) | async-done | bytes 163872 | tf_op jit(solution)/shard_map/all_to_all | solution.py:692
  32.9 0.0 collective-permute-start.1
  32.9 1.4 %near_half.2 = (f32[64,128]{1,0:T(8,128)S(1)}, f32[16,128]{1,0:T(8,128)S(1)}, bf16[48,128,128]{2,1,0:T(8,128)(2,1)S(1)}) custom-call(f32[320,128]{1,0:T(8,128)S(1)} %bitcast.17, bf16[80,512]{1,0:T(8,128)(2,1)S(1)} %get-tuple-element.114.share_ref, bf16[192,128,128]{2,1,0:T(8,128)(2,1)} %get-tuple-element.81.c_hbm.refs_14_), custom_call_target="tpu_custom_call" | custom-call | tf_op jit(solution)/shard_map/near_half/pallas_call | solution.py:616
  34.3 0.0 collective-permute-done.1.other_ref
  34.3 3.9 %middle.2 = (f32[320,128]{1,0:T(8,128)}, f32[16,128]{1,0:T(8,128)S(1)}, f32[32,128]{1,0:T(8,128)S(1)}) custom-call(f32[64,128]{1,0:T(8,128)S(1)} %get-tuple-element.104.part_ref, f32[16,128]{1,0:T(8,128)S(1)} %get-tuple-element.105.total_ref, f32[320,128]{1,0:T(8,128)S(1)} %collective-permute-done.1.other_ref, ...), custom_call_target="tpu_custom_call" | custom-call | flops 134217728 | bytes 8388608 | tf_op jit(solution)/shard_map/middle/pallas_call | solution.py:616
  38.3 4.3 %all-to-all-start.2 = ((f32[8,40,128]{2,1,0:T(8,128)}), f32[8,40,128]{2,1,0:T(8,128)S(1)}, u32[]{:S(2)}, u32[]{:S(2)}) async-start(f32[8,40,128]{2,1,0:T(8,128)} %bitcast.7), calls=%async_computation.2 | async-start | bytes 327680 | tf_op jit(solution)/shard_map/all_to_all | solution.py:692
  42.5 3.7 %backward.4 = (f32[32,8,128]{2,1,0:T(8,128)S(1)}, f32[32,8,128]{2,1,0:T(8,128)S(1)}) custom-call(f32[32,128]{1,0:T(8,128)S(1)} %get-tuple-element.111.f_ref.own_ref.refs_1_, bf16[256,32]{1,0:T(8,128)(2,1)S(1)} %get-tuple-element.96.gk_ref, bf16[256,128,128]{2,1,0:T(8,128)(2,1)} %c_hbm.7), custom_call_target="tpu_custom_call" | custom-call | flops 134217728 | bytes 8388608 | tf_op jit(solution)/shard_map/backward/pallas_call | solution.py:616
  46.2 2.3 %all-to-all-done.2 = f32[8,40,128]{2,1,0:T(8,128)S(1)} async-done(((f32[8,40,128]{2,1,0:T(8,128)}), f32[8,40,128]{2,1,0:T(8,128)S(1)}, u32[]{:S(2)}, u32[]{:S(2)}) %all-to-all-start.2) | async-done | bytes 163872 | tf_op jit(solution)/shard_map/all_to_all | solution.py:692
  48.6 0.0 collective-permute-start.2
  48.6 1.4 %near_half.3 = (f32[64,128]{1,0:T(8,128)S(1)}, f32[16,128]{1,0:T(8,128)S(1)}, bf16[48,128,128]{2,1,0:T(8,128)(2,1)S(1)}) custom-call(f32[320,128]{1,0:T(8,128)S(1)} %bitcast.19, bf16[80,512]{1,0:T(8,128)(2,1)S(1)} %get-tuple-element.114.share_ref, bf16[192,128,128]{2,1,0:T(8,128)(2,1)} %get-tuple-element.81.c_hbm.refs_14_), custom_call_target="tpu_custom_call" | custom-call | tf_op jit(solution)/shard_map/near_half/pallas_call | solution.py:616
  50.0 0.0 collective-permute-done.2.other_ref
  50.0 3.7 %middle.3 = (f32[64,128]{1,0:T(8,128)}, f32[16,128]{1,0:T(8,128)S(1)}, f32[32,128]{1,0:T(8,128)S(1)}, f32[32,128]{1,0:T(8,128)S(1)}) custom-call(f32[64,128]{1,0:T(8,128)S(1)} %get-tuple-element.115.part_ref, f32[16,128]{1,0:T(8,128)S(1)} %get-tuple-element.116.total_ref, f32[320,128]{1,0:T(8,128)S(1)} %collective-permute-done.2.other_ref, ...), custom_call_target="tpu_custom_call" | custom-call | flops 134217728 | bytes 8388608 | tf_op jit(solution)/shard_map/middle/pallas_call | solution.py:616
  53.8 4.3 %all-to-all-start.3 = ((f32[16,4,128]{2,1,0:T(4,128)}), f32[16,4,128]{2,1,0:T(4,128)S(1)}, u32[]{:S(2)}, u32[]{:S(2)}) async-start(f32[16,4,128]{2,1,0:T(4,128)} %bitcast.9), calls=%async_computation.3 | async-start | bytes 65536 | tf_op jit(solution)/shard_map/all_to_all | solution.py:674
  58.1 3.7 %backward.5 = (f32[32,8,128]{2,1,0:T(8,128)S(1)}, f32[32,8,128]{2,1,0:T(8,128)S(1)}) custom-call(f32[32,128]{1,0:T(8,128)S(1)} %get-tuple-element.127.f_ref.refs_2_, bf16[256,32]{1,0:T(8,128)(2,1)S(1)} %get-tuple-element.96.gk_ref, bf16[256,128,128]{2,1,0:T(8,128)(2,1)} %c_hbm.7), custom_call_target="tpu_custom_call" | custom-call | flops 134217728 | bytes 8388608 | tf_op jit(solution)/shard_map/backward/pallas_call | solution.py:616
  61.9 0.6 all-to-all-done.3
  62.5 0.4 phonon.1
  62.9 8.9 %all_to_all.58 = f32[16,8,128]{2,1,0:T(8,128)S(1)} all-to-all(f32[16,8,128]{2,1,0:T(8,128)S(1)} %bitcast.22), channel_id=1, replica_groups={{8,9,10,11,12,13,14,15,0,1,2,3,4,5,6,7},{24,25,26,27,28,29,30,31,16,17,..., dimensions={0} | all-to-all | bytes 131072 | tf_op jit(solution)/shard_map/all_to_all | solution.py:674
  71.8 3.9 %last.1 = (f32[32,128]{1,0:T(8,128)}, f32[16,128]{1,0:T(8,128)}) custom-call(f32[128,128]{1,0:T(8,128)S(1)} %bitcast.20, f32[256,128]{1,0:T(8,128)S(1)} %get-tuple-element.131.refs_0_, f32[32,128]{1,0:T(8,128)S(1)} %get-tuple-element.111.f_ref.own_ref.refs_1_, f32[32,128]{1,0:T(8,128)S(1)} %get-tuple-element.127.f_ref.refs_2_, ...), custom_call_target="tpu_custom_call" | custom-call | flops 134217728 | bytes 8388608 | tf_op jit(solution)/shard_map/last/pallas_call | solution.py:616
Async XLA Ops:
  2.2 14.0 %all-to-all-start = ((f32[8,56,128]{2,1,0:T(8,128)}), f32[8,56,128]{2,1,0:T(8,128)S(1)}, u32[]{:S(2)}, u32[]{:S(2)}) async-start(f32[8,56,128]{2,1,0:T(8,128)} %bitcast.3), calls=%async_computation | async-start | bytes 458752 | tf_op jit(solution)/shard_map/all_to_all | solution.py:692
  16.2 1.6 %collective-permute-start = (f32[448,128]{1,0:T(8,128)S(1)}, f32[448,128]{1,0:T(8,128)S(1)}, u32[]{:S(2)}, u32[]{:S(2)}) collective-permute-start(f32[448,128]{1,0:T(8,128)S(1)} %bitcast.13), channel_id=1, source_target_pairs={{0,1},{1,0},{2,3},{3,2},{4,5},{5,4},{6,7},{7,6},{8,9},{9,8},{10,11... | collective-permute-start | bytes 688136 | tf_op jit(solution)/shard_map/ppermute | solution.py:697
  21.9 11.0 %all-to-all-start.1 = ((f32[8,40,128]{2,1,0:T(8,128)}), f32[8,40,128]{2,1,0:T(8,128)S(1)}, u32[]{:S(2)}, u32[]{:S(2)}) async-start(f32[8,40,128]{2,1,0:T(8,128)} %bitcast.5), calls=%async_computation.1 | async-start | bytes 327680 | tf_op jit(solution)/shard_map/all_to_all | solution.py:692
  32.9 1.4 %collective-permute-start.1 = (f32[320,128]{1,0:T(8,128)S(1)}, f32[320,128]{1,0:T(8,128)S(1)}, u32[]{:S(2)}, u32[]{:S(2)}) collective-permute-start(f32[320,128]{1,0:T(8,128)S(1)} %bitcast.16), channel_id=1, source_target_pairs={{0,1},{1,0},{2,3},{3,2},{4,5},{5,4},{6,7},{7,6},{8,9},{9,8},{10,11... | collective-permute-start | bytes 491528 | tf_op jit(solution)/shard_map/ppermute | solution.py:697
  38.3 10.3 %all-to-all-start.2 = ((f32[8,40,128]{2,1,0:T(8,128)}), f32[8,40,128]{2,1,0:T(8,128)S(1)}, u32[]{:S(2)}, u32[]{:S(2)}) async-start(f32[8,40,128]{2,1,0:T(8,128)} %bitcast.7), calls=%async_computation.2 | async-start | bytes 327680 | tf_op jit(solution)/shard_map/all_to_all | solution.py:692
  48.6 1.4 %collective-permute-start.2 = (f32[320,128]{1,0:T(8,128)S(1)}, f32[320,128]{1,0:T(8,128)S(1)}, u32[]{:S(2)}, u32[]{:S(2)}) collective-permute-start(f32[320,128]{1,0:T(8,128)S(1)} %bitcast.18), channel_id=1, source_target_pairs={{0,1},{1,0},{2,3},{3,2},{4,5},{5,4},{6,7},{7,6},{8,9},{9,8},{10,11... | collective-permute-start | bytes 491528 | tf_op jit(solution)/shard_map/ppermute | solution.py:697
  53.8 8.7 %all-to-all-start.3 = ((f32[16,4,128]{2,1,0:T(4,128)}), f32[16,4,128]{2,1,0:T(4,128)S(1)}, u32[]{:S(2)}, u32[]{:S(2)}) async-start(f32[16,4,128]{2,1,0:T(4,128)} %bitcast.9), calls=%async_computation.3 | async-start | bytes 65536 | tf_op jit(solution)/shard_map/all_to_all | solution.py:674

commit v24 on v18

--- a/solution.py
+++ b/solution.py
@@ -171,14 +171,15 @@
 
 def need_kernel(cap, *refs):
     ins, outs = refs[:9], refs[9:]
-    *small, pneed_ref, qneed_ref, send_ref, sems = outs
+    *small, pneed_ref, qneed_ref, send_hbm, sems, block_ref, out_sems = outs
     copies = [
         pltpu.make_async_copy(src, dst, sems.at[i])
         for i, (src, dst) in enumerate(zip(ins, [*small, pneed_ref, qneed_ref]))
     ]
     start(copies)
     slots = pneed_ref.shape[1]
-    step = send_ref.shape[0] // (slots // cap // 2)
+    chips = slots // cap // 2
+    step = send_hbm.shape[0] // chips
     for copy in copies:
         copy.wait()
     f, n = small[0][...], small[1][...]
@@ -187,9 +188,16 @@
     lists = jnp.where(row == 0, own_p, jnp.where(row == 1, own_q, 0.0))
     if slots < 128:
         lists = jnp.concatenate([lists, jnp.zeros((8, 128 - slots), f32)], axis=1)
-    block = jnp.concatenate([f, n, lists], axis=0)
-    for chip in range(slots // cap // 2):
-        send_ref[chip * step : (chip + 1) * step] = block
+    block_ref[...] = jnp.concatenate([f, n, lists], axis=0)
+    copies = [
+        pltpu.make_async_copy(
+            block_ref, send_hbm.at[pl.ds(chip * step, step)], out_sems.at[chip]
+        )
+        for chip in range(chips)
+    ]
+    start(copies)
+    for copy in copies:
+        copy.wait()
 
 
 def prepare_kernel(
@@ -698,8 +706,13 @@
         functools.partial(need_kernel, cap),
         "need",
         small + [lists, lists, ((chips * step_rows, 128), f32)],
-        [pltpu.SemaphoreType.DMA((9,))],
+        [
+            pltpu.SemaphoreType.DMA((9,)),
+            pltpu.VMEM((step_rows, 128), f32),
+            pltpu.SemaphoreType.DMA((chips,)),
+        ],
         spaces={i: pltpu.HBM for i in range(9)},
+        out_spaces={9: pltpu.HBM},
     )(
         electrons,
         phonons,

time: 76 us -> 76.1 us (level)
  no operation moved by 1% of the time
where the time goes in v24:
time: 76.1 us; the launch traced here: 75.4 us
  Pallas kernels  38.5 us (51%)
  starting transfers between devices  21.7 us (29%)
  blocking collectives  8.93 us (12%)
  waiting for transfers between devices  4.93 us (6%)
  between operations  1.41 us (2%)
    pallas_call x14, Pallas kernels, run(): pl.pallas_call(kernel, out_shape=[(out_spaces or {}).get(i, jax.ShapeDtyp...  38.5 us
    all_to_all x3, starting transfers between devices, to_chips(): lax.all_to_all(x, 'bulk', split_axis=0, concat_axis=0, tiled=True, axis_i...  17.3 us
    all_to_all x1, blocking collectives, exchange(): lax.all_to_all(x, 'bulk', split_axis=0, concat_axis=0, tiled=True, axis_i...  8.93 us
    all_to_all x1, starting transfers between devices, exchange(): lax.all_to_all(x, 'bulk', split_axis=0, concat_axis=0, tiled=True, axis_i...  4.26 us
    all_to_all x3, waiting for transfers between devices, to_chips(): lax.all_to_all(x, 'bulk', split_axis=0, concat_axis=0, tiled=True, axis_i...  3.8 us
  transfers between devices with their start and end apart: 7, of which 6 were waited for; matrix products, arithmetic and copies ran while one was open for 0% of the time, Pallas kernels for 27%

profile of v24, /device:TPU:0, one launch (start us, length us, event | category | flops | bytes accessed | tf_op | source)
XLA Modules:
  0.0 75.4 jit_solution(8263986487279832703)
XLA Ops:
  0.6 1.6 %need.1 = (f32[32,128]{1,0:T(8,128)S(1)}, f32[16,128]{1,0:T(8,128)S(1)}, f32[16,128]{1,0:T(8,128)S(1)}, f32[16,128]{1,0:T(8,128)S(1)}, s32[1,256]{1,0:T(1,128)S(...) custom-call(f32[32,128]{1,0:T(8,128)} %refs_0_.1, ...), custom_call_target="tpu_custom_call" | custom-call | tf_op jit(solution)/shard_map/need/pallas_call | solution.py:622
  2.3 7.9 %all-to-all-start = ((f32[8,56,128]{2,1,0:T(8,128)}), f32[8,56,128]{2,1,0:T(8,128)S(1)}, u32[]{:S(2)}, u32[]{:S(2)}) async-start(f32[8,56,128]{2,1,0:T(8,128)} %bitcast.23), calls=%async_computation | async-start | bytes 458752 | tf_op jit(solution)/shard_map/all_to_all | solution.py:698
  10.8 5.5 %prepare.1 = (bf16[64,128,128]{2,1,0:T(8,128)(2,1)S(1)}, bf16[192,128,128]{2,1,0:T(8,128)(2,1)}, bf16[256,128]{1,0:T(8,128)(2,1)S(1)}, bf16[256,32]{1,0:T(8,128)...) custom-call(s32[1]{0:T(128)S(6)} %copy.13.count_ref, ...), custom_call_target="tpu_custom_call" | custom-call | flops 134217728 | bytes 8388608 | tf_op jit(solution)/shard_map/prepare/pallas_call | solution.py:622
  16.3 0.0 all-to-all-done
  16.3 0.1 collective-permute-start
  16.3 1.2 %near_rows.1 = (f32[64,128]{1,0:T(8,128)S(1)}, bf16[32,128,128]{2,1,0:T(8,128)(2,1)S(1)}) custom-call(f32[448,128]{1,0:T(8,128)S(1)} %bitcast.14, bf16[64,448]{1,0:T(8,128)(2,1)S(1)} %get-tuple-element.80.list_ref, bf16[192,128,128]{2,1,0:T(8,128)(2,1)} %get-tuple-element.81.c_hbm.refs_14_), custom_call_target="tpu_custom_call" | custom-call | tf_op jit(solution)/shard_map/near_rows/pallas_call | solution.py:622
  17.6 0.2 collective-permute-done.other_ref
  17.8 4.0 %first.1 = (f32[320,128]{1,0:T(8,128)}, f32[32,128]{1,0:T(8,128)S(1)}, f32[32,128]{1,0:T(8,128)S(1)}, bf16[64,128]{1,0:T(8,128)(2,1)S(1)}, bf16[128,128]{1,0:T(8,128)(2,1)S(1)}) custom-call(f32[448,128]{1,0:T(8,128)S(1)} %bitcast.15, f32[448,128]{1,0:T(8,128)S(1)} %collective-permute-done.other_ref, f32[64,128]{1,0:T(8,128)S(1)} %get-tuple-element.82.part_ref, ...), custom_call_target="tpu_custom_call" | custom-call | flops 134217728 | bytes 8388608 | tf_op jit(solution)/shard_map/first/pallas_call | solution.py:622
  21.9 5.1 %all-to-all-start.1 = ((f32[8,40,128]{2,1,0:T(8,128)}), f32[8,40,128]{2,1,0:T(8,128)S(1)}, u32[]{:S(2)}, u32[]{:S(2)}) async-start(f32[8,40,128]{2,1,0:T(8,128)} %bitcast.5), calls=%async_computation.1 | async-start | bytes 327680 | tf_op jit(solution)/shard_map/all_to_all | solution.py:698
  27.0 0.3 serve.1
  27.3 3.7 %backward.3 = (f32[32,8,128]{2,1,0:T(8,128)S(1)}, f32[32,8,128]{2,1,0:T(8,128)S(1)}) custom-call(f32[32,128]{1,0:T(8,128)S(1)} %get-tuple-element.95.f_ref.own_ref, bf16[256,32]{1,0:T(8,128)(2,1)S(1)} %get-tuple-element.96.gk_ref, bf16[256,128,128]{2,1,0:T(8,128)(2,1)} %c_hbm.7), custom_call_target="tpu_custom_call" | custom-call | flops 134217728 | bytes 8388608 | tf_op jit(solution)/shard_map/backward/pallas_call | solution.py:622
  31.1 1.6 %all-to-all-done.1 = f32[8,40,128]{2,1,0:T(8,128)S(1)} async-done(((f32[8,40,128]{2,1,0:T(8,128)}), f32[8,40,128]{2,1,0:T(8,128)S(1)}, u32[]{:S(2)}, u32[]{:S(2)}) %all-to-all-start.1) | async-done | bytes 163872 | tf_op jit(solution)/shard_map/all_to_all | solution.py:698
  32.7 0.0 collective-permute-start.1
  32.7 1.2 %near_half.2 = (f32[64,128]{1,0:T(8,128)S(1)}, f32[16,128]{1,0:T(8,128)S(1)}, bf16[32,128,128]{2,1,0:T(8,128)(2,1)S(1)}) custom-call(f32[320,128]{1,0:T(8,128)S(1)} %bitcast.17, bf16[80,512]{1,0:T(8,128)(2,1)S(1)} %get-tuple-element.114.share_ref, bf16[192,128,128]{2,1,0:T(8,128)(2,1)} %get-tuple-element.81.c_hbm.refs_14_), custom_call_target="tpu_custom_call" | custom-call | tf_op jit(solution)/shard_map/near_half/pallas_call | solution.py:622
  33.9 0.1 collective-permute-done.1.other_ref
  34.1 4.0 %middle.2 = (f32[320,128]{1,0:T(8,128)}, f32[16,128]{1,0:T(8,128)S(1)}, f32[32,128]{1,0:T(8,128)S(1)}) custom-call(f32[64,128]{1,0:T(8,128)S(1)} %get-tuple-element.104.part_ref, f32[16,128]{1,0:T(8,128)S(1)} %get-tuple-element.105.total_ref, f32[320,128]{1,0:T(8,128)S(1)} %collective-permute-done.1.other_ref, ...), custom_call_target="tpu_custom_call" | custom-call | flops 134217728 | bytes 8388608 | tf_op jit(solution)/shard_map/middle/pallas_call | solution.py:622
  38.1 4.4 %all-to-all-start.2 = ((f32[8,40,128]{2,1,0:T(8,128)}), f32[8,40,128]{2,1,0:T(8,128)S(1)}, u32[]{:S(2)}, u32[]{:S(2)}) async-start(f32[8,40,128]{2,1,0:T(8,128)} %bitcast.7), calls=%async_computation.2 | async-start | bytes 327680 | tf_op jit(solution)/shard_map/all_to_all | solution.py:698
  42.4 3.7 %backward.4 = (f32[32,8,128]{2,1,0:T(8,128)S(1)}, f32[32,8,128]{2,1,0:T(8,128)S(1)}) custom-call(f32[32,128]{1,0:T(8,128)S(1)} %get-tuple-element.111.f_ref.own_ref.refs_1_, bf16[256,32]{1,0:T(8,128)(2,1)S(1)} %get-tuple-element.96.gk_ref, bf16[256,128,128]{2,1,0:T(8,128)(2,1)} %c_hbm.7), custom_call_target="tpu_custom_call" | custom-call | flops 134217728 | bytes 8388608 | tf_op jit(solution)/shard_map/backward/pallas_call | solution.py:622
  46.2 2.2 %all-to-all-done.2 = f32[8,40,128]{2,1,0:T(8,128)S(1)} async-done(((f32[8,40,128]{2,1,0:T(8,128)}), f32[8,40,128]{2,1,0:T(8,128)S(1)}, u32[]{:S(2)}, u32[]{:S(2)}) %all-to-all-start.2) | async-done | bytes 163872 | tf_op jit(solution)/shard_map/all_to_all | solution.py:698
  48.3 0.0 collective-permute-start.2
  48.4 1.2 %near_half.3 = (f32[64,128]{1,0:T(8,128)S(1)}, f32[16,128]{1,0:T(8,128)S(1)}, bf16[32,128,128]{2,1,0:T(8,128)(2,1)S(1)}) custom-call(f32[320,128]{1,0:T(8,128)S(1)} %bitcast.19, bf16[80,512]{1,0:T(8,128)(2,1)S(1)} %get-tuple-element.114.share_ref, bf16[192,128,128]{2,1,0:T(8,128)(2,1)} %get-tuple-element.81.c_hbm.refs_14_), custom_call_target="tpu_custom_call" | custom-call | tf_op jit(solution)/shard_map/near_half/pallas_call | solution.py:622
  49.6 0.1 collective-permute-done.2.other_ref
  49.7 3.8 %middle.3 = (f32[64,128]{1,0:T(8,128)}, f32[16,128]{1,0:T(8,128)S(1)}, f32[32,128]{1,0:T(8,128)S(1)}, f32[32,128]{1,0:T(8,128)S(1)}) custom-call(f32[64,128]{1,0:T(8,128)S(1)} %get-tuple-element.115.part_ref, f32[16,128]{1,0:T(8,128)S(1)} %get-tuple-element.116.total_ref, f32[320,128]{1,0:T(8,128)S(1)} %collective-permute-done.2.other_ref, ...), custom_call_target="tpu_custom_call" | custom-call | flops 134217728 | bytes 8388608 | tf_op jit(solution)/shard_map/middle/pallas_call | solution.py:622
  53.6 4.3 %all-to-all-start.3 = ((f32[16,4,128]{2,1,0:T(4,128)}), f32[16,4,128]{2,1,0:T(4,128)S(1)}, u32[]{:S(2)}, u32[]{:S(2)}) async-start(f32[16,4,128]{2,1,0:T(4,128)} %bitcast.9), calls=%async_computation.3 | async-start | bytes 65536 | tf_op jit(solution)/shard_map/all_to_all | solution.py:680
  57.8 3.7 %backward.5 = (f32[32,8,128]{2,1,0:T(8,128)S(1)}, f32[32,8,128]{2,1,0:T(8,128)S(1)}) custom-call(f32[32,128]{1,0:T(8,128)S(1)} %get-tuple-element.127.f_ref.refs_2_, bf16[256,32]{1,0:T(8,128)(2,1)S(1)} %get-tuple-element.96.gk_ref, bf16[256,128,128]{2,1,0:T(8,128)(2,1)} %c_hbm.7), custom_call_target="tpu_custom_call" | custom-call | flops 134217728 | bytes 8388608 | tf_op jit(solution)/shard_map/backward/pallas_call | solution.py:622
  61.6 0.6 all-to-all-done.3
  62.2 0.4 phonon.1
  62.6 8.9 %all_to_all.58 = f32[16,8,128]{2,1,0:T(8,128)S(1)} all-to-all(f32[16,8,128]{2,1,0:T(8,128)S(1)} %bitcast.22), channel_id=1, replica_groups={{8,9,10,11,12,13,14,15,0,1,2,3,4,5,6,7},{24,25,26,27,28,29,30,31,16,17,..., dimensions={0} | all-to-all | bytes 131072 | tf_op jit(solution)/shard_map/all_to_all | solution.py:680
  71.5 3.9 %last.1 = (f32[32,128]{1,0:T(8,128)}, f32[16,128]{1,0:T(8,128)}) custom-call(f32[128,128]{1,0:T(8,128)S(1)} %bitcast.20, f32[256,128]{1,0:T(8,128)S(1)} %get-tuple-element.131.refs_0_, f32[32,128]{1,0:T(8,128)S(1)} %get-tuple-element.111.f_ref.own_ref.refs_1_, f32[32,128]{1,0:T(8,128)S(1)} %get-tuple-element.127.f_ref.refs_2_, ...), custom_call_target="tpu_custom_call" | custom-call | flops 134217728 | bytes 8388608 | tf_op jit(solution)/shard_map/last/pallas_call | solution.py:622
Async XLA Ops:
  2.3 14.0 %all-to-all-start = ((f32[8,56,128]{2,1,0:T(8,128)}), f32[8,56,128]{2,1,0:T(8,128)S(1)}, u32[]{:S(2)}, u32[]{:S(2)}) async-start(f32[8,56,128]{2,1,0:T(8,128)} %bitcast.23), calls=%async_computation | async-start | bytes 458752 | tf_op jit(solution)/shard_map/all_to_all | solution.py:698
  16.3 1.6 %collective-permute-start = (f32[448,128]{1,0:T(8,128)S(1)}, f32[448,128]{1,0:T(8,128)S(1)}, u32[]{:S(2)}, u32[]{:S(2)}) collective-permute-start(f32[448,128]{1,0:T(8,128)S(1)} %bitcast.13), channel_id=1, source_target_pairs={{0,1},{1,0},{2,3},{3,2},{4,5},{5,4},{6,7},{7,6},{8,9},{9,8},{10,11... | collective-permute-start | bytes 688136 | tf_op jit(solution)/shard_map/ppermute | solution.py:703
  21.9 10.8 %all-to-all-start.1 = ((f32[8,40,128]{2,1,0:T(8,128)}), f32[8,40,128]{2,1,0:T(8,128)S(1)}, u32[]{:S(2)}, u32[]{:S(2)}) async-start(f32[8,40,128]{2,1,0:T(8,128)} %bitcast.5), calls=%async_computation.1 | async-start | bytes 327680 | tf_op jit(solution)/shard_map/all_to_all | solution.py:698
  32.7 1.4 %collective-permute-start.1 = (f32[320,128]{1,0:T(8,128)S(1)}, f32[320,128]{1,0:T(8,128)S(1)}, u32[]{:S(2)}, u32[]{:S(2)}) collective-permute-start(f32[320,128]{1,0:T(8,128)S(1)} %bitcast.16), channel_id=1, source_target_pairs={{0,1},{1,0},{2,3},{3,2},{4,5},{5,4},{6,7},{7,6},{8,9},{9,8},{10,11... | collective-permute-start | bytes 491528 | tf_op jit(solution)/shard_map/ppermute | solution.py:703
  38.1 10.3 %all-to-all-start.2 = ((f32[8,40,128]{2,1,0:T(8,128)}), f32[8,40,128]{2,1,0:T(8,128)S(1)}, u32[]{:S(2)}, u32[]{:S(2)}) async-start(f32[8,40,128]{2,1,0:T(8,128)} %bitcast.7), calls=%async_computation.2 | async-start | bytes 327680 | tf_op jit(solution)/shard_map/all_to_all | solution.py:698
  48.3 1.4 %collective-permute-start.2 = (f32[320,128]{1,0:T(8,128)S(1)}, f32[320,128]{1,0:T(8,128)S(1)}, u32[]{:S(2)}, u32[]{:S(2)}) collective-permute-start(f32[320,128]{1,0:T(8,128)S(1)} %bitcast.18), channel_id=1, source_target_pairs={{0,1},{1,0},{2,3},{3,2},{4,5},{5,4},{6,7},{7,6},{8,9},{9,8},{10,11... | collective-permute-start | bytes 491528 | tf_op jit(solution)/shard_map/ppermute | solution.py:703
  53.6 8.6 %all-to-all-start.3 = ((f32[16,4,128]{2,1,0:T(4,128)}), f32[16,4,128]{2,1,0:T(4,128)S(1)}, u32[]{:S(2)}, u32[]{:S(2)}) async-start(f32[16,4,128]{2,1,0:T(4,128)} %bitcast.9), calls=%async_computation.3 | async-start | bytes 65536 | tf_op jit(solution)/shard_map/all_to_all | solution.py:680
